TPU v7x, 1024 devices: a whole 4x4x32 slice. The times are simulated.
1024 devices in a mesh: row: 32 (over z), col: 32 (over x, y, core).
Axes of the slice: x: 4, y: 4, z: 32, core: 2. Of those that a mesh axis runs over, the one named last changes fastest.
Arguments:
- values: bfloat16 [128, 32, 128, 128], P('row', 'col'), may hold values from -0.1875 to 0.1875
- column_slot_index: int32 [128, 32], P('row', 'col'), may hold values from 0 to 3
- branches: int32 [2], replicated, may hold values from 0 to 1, as said below
Outputs:
- purified: bfloat16 [128, 32, 128, 128], P('row', 'col')
Inputs may be any that keep to these rules, and one draw needn't show every extreme that they name: column_slot_index[i, c] places block row i's single nonzero block among the 4 block columns of col index c. Branch 0 squares, branch 1 takes 2 X - X X; consecutive steps take different branches.
All inputs are finite; a program needn't handle non-finite values.
Results may differ from a plain program's by a relative error of at most 0.0051.
Values may be sent and summed in bfloat16 or wider, within the bound.
No kernel may reach another device: no remote copies, remote signals or barrier semaphores. Data moves between devices by JAX's collectives and lax.ppermute only.
A program may use at most 32 MiB of HBM per device.

v0:
```python
import jax
import jax.numpy as jnp
from jax import lax
from jax.sharding import PartitionSpec as P

BPD = 4
STEPS = 2


def body(values, column_slot_index, branches):
    state = values
    own_ids = column_slot_index[:, 0]
    for step in range(STEPS):
        below, lower_block_index = (
            lax.all_gather(state, "row", axis=0, tiled=True),
            lax.all_gather(column_slot_index, "row", axis=0, tiled=True),
        )
        below_blocks = below[:, 0]
        below_pos = lower_block_index[:, 0]
        block_strip, panel_ids = (
            lax.all_gather(state, "col", axis=1, tiled=True),
            lax.all_gather(column_slot_index, "col", axis=1, tiled=True),
        )
        count = block_strip.shape[1]
        slots = jnp.arange(count, dtype=jnp.int32)
        desired_trace = slots[None, :] * BPD + panel_ids
        selected_blocks = jnp.take(below_blocks, desired_trace, axis=0)
        match = jnp.take(below_pos, desired_trace, axis=0) == own_ids[:, None]
        selected_blocks = jnp.where(
            match[:, :, None, None], selected_blocks, jnp.zeros_like(selected_blocks)
        )
        matrix_square = jnp.einsum(
            "jlut,jlto->juo", block_strip, selected_blocks, preferred_element_type=jnp.float32
        )
        twice_density = 2.0 * state[:, 0].astype(jnp.float32) - matrix_square
        newer = jnp.where(branches[step] == 1, twice_density, matrix_square)
        state = newer.astype(jnp.bfloat16)[:, None]
    return state


def solution(mesh):
    in_specs = (P("row", "col", None, None), P("row", "col"), P())
    out_specs = P("row", "col", None, None)
    return jax.shard_map(body, mesh=mesh, in_specs=in_specs, out_specs=out_specs, check_vma=False)
```

profile of v0, /device:TPU:4, one launch (start us, length us, event | category | flops | bytes accessed | tf_op | source)
XLA Modules:
  0.0 505.1 jit_solution(10814274939253786433)
XLA Ops:
  6.5 0.0 all-gather.8.cloned.1.call-start
  6.5 0.7 all-gather.8.cloned.1.call-update
  7.3 0.0 all-gather.10.cloned.1.call-start
  7.3 0.7 all-gather.10.cloned.1.call-update
  8.0 0.0 all-gather.12.cloned.1.call-start
  8.1 1.0 copy.20
  9.1 29.5 %all-gather.2 = s32[32,1,4]{2,1,0:T(1,128)S(1)} all-gather(s32[1,1,4]{2,1,0:T(1,128)} %bitcast.55), channel_id=1, replica_groups=mesh['row'=32,'col'=32] {'col'}, dimensions={0}, use_global_device_ids=true | all-gather | bytes 528 | tf_op jit(solution)/shard_map/all_gather | solution.py:22
  38.6 0.1 copy.21
  38.7 0.1 reshape.66
  38.8 1.3 dynamic-slice
  40.7 0.8 bitcast_dynamic-update-slice_fusion
  41.5 37.5 %all-reduce = s32[128]{0:T(128)S(1)} all-reduce(s32[128]{0:T(128)S(1)} %bitcast_dynamic-update-slice_fusion), channel_id=1, replica_groups=mesh['row'=32,'col'=32] {'row'}, use_global_device_ids=true, to_apply=%add | all-reduce | flops 128 | bytes 1024 | tf_op jit(solution)/shard_map/squeeze | solution.py:19
  79.0 1.2 gather_fusion
  80.2 0.1 reshape.69
  80.3 1.3 fusion.37
  82.3 0.7 select_compare_fusion
  83.0 78.7 %all-gather.8.cloned.1.call-done = bf16[128,1,128,128]{3,2,1,0:T(8,128)(2,1)} async-done(((bf16[4,1,128,128]{3,2,1,0:T(8,128)(2,1)}), bf16[128,1,128,128]{3,2,1,0:T(8,128)(2,1)}) %all-gather.8.cloned.1.call-update) | async-done | bytes 4194320 | tf_op jit(solution)/shard_map/all_gather | solution.py:15
  161.7 5.2 %gather_fusion.1 = bf16[128,128,128]{2,1,0:T(8,128)(2,1)} fusion(bf16[128,128,128]{2,1,0:T(8,128)(2,1)} %bitcast.50, s32[1024]{0:T(1024)S(1)} %pad_clamp_fusion), kind=kCustom, calls=%fused_computation.1.clone | custom fusion | bytes 8389120 | tf_op jit(solution)/shard_map/jit(_take)/gather | solution.py:27
  166.9 71.0 %all-gather.10.cloned.1.call-done = bf16[4,32,128,128]{3,2,1,0:T(8,128)(2,1)} async-done(((bf16[4,1,128,128]{3,2,1,0:T(8,128)(2,1)}), bf16[4,32,128,128]{3,2,1,0:T(8,128)(2,1)}) %all-gather.10.cloned.1.call-update) | async-done | bytes 4194320 | tf_op jit(solution)/shard_map/all_gather | solution.py:21
  237.9 7.9 %copy.30 = bf16[4,32,128,128]{2,1,3,0:T(8,128)(2,1)} copy(bf16[4,32,128,128]{3,2,1,0:T(8,128)(2,1)} %all-gather.10.cloned.1.call-done) | data formatting | bytes 8388608 | tf_op jit(solution)/shard_map/all_gather | solution.py:21
  245.8 7.7 %fusion.30 = bf16[4,128,128]{1,2,0:T(8,128)(2,1)} fusion(bf16[4,32,128,128]{2,1,3,0:T(8,128)(2,1)} %copy.30, bf16[4,32,128,128]{3,2,1,0:T(8,128)(2,1)} %bitcast.51, pred[4,32]{1,0:T(4,128)(4,1)S(1)} %get-tuple-element.8, pred[4,32]{1,0:T(4,128)(4,1)S(1)} %get-tuple-element.6, bf16[4,1,128,128]{2,3,0,1:T(8,128)(2,1)S(1)} %copy.20, pred[]{:T(512)} %bitcast.1), kind=kOutput, calls=%fused_computation.23 | convolution fusion | flops 541392896 | bytes 8651009 | tf_op jit(solution)/shard_map/jlut,jlto->juo/dot_general | solution.py:32
  253.5 0.0 all-gather.12.cloned.1.call-update
  253.6 0.0 all-gather.14.cloned.1.call-start
  253.6 1.7 copy.24
  255.3 0.0 all-gather.14.cloned.1.call-update
  255.9 82.0 %all-gather.12.cloned.1.call-done = bf16[4,4096,128]{1,2,0:T(8,128)(2,1)} async-done(((bf16[4,128,128]{1,2,0:T(8,128)(2,1)}), bf16[4,4096,128]{1,2,0:T(8,128)(2,1)}) %all-gather.12.cloned.1.call-update) | async-done | bytes 4194320 | tf_op jit(solution)/shard_map/all_gather | solution.py:21
  337.8 5.4 %copy.35 = bf16[64,8,32,128]{3,2,1,0:T(8,128)(2,1)} copy(bf16[64,8,32,128]{3,1,2,0:T(8,128)(2,1)} %bitcast.53) | data formatting | bytes 8388608
  343.3 0.0 copy-start
  343.3 142.2 %all-gather.14.cloned.1.call-done = bf16[128,128,128]{2,1,0:T(8,128)(2,1)} async-done(((bf16[4,128,128]{2,1,0:T(8,128)(2,1)}), bf16[128,128,128]{2,1,0:T(8,128)(2,1)}) %all-gather.14.cloned.1.call-update) | async-done | bytes 4194320 | tf_op jit(solution)/shard_map/all_gather | solution.py:15
  485.4 5.2 %gather_fusion.2 = bf16[128,128,128]{2,1,0:T(8,128)(2,1)} fusion(bf16[128,128,128]{2,1,0:T(8,128)(2,1)} %all-gather.14.cloned.1.call-done, s32[1024]{0:T(1024)S(1)} %pad_clamp_fusion), kind=kCustom, calls=%fused_computation.2.clone | custom fusion | bytes 8389120 | tf_op jit(solution)/shard_map/jit(_take)/gather | solution.py:27
  490.7 0.0 copy-done
  490.7 7.1 %fusion.25 = bf16[4,1,128,128]{2,3,0,1:T(8,128)(2,1)S(1)} fusion(bf16[4,32,128,128]{2,1,3,0:T(8,128)(2,1)} %bitcast.54, bf16[4,32,128,128]{3,2,1,0:T(8,128)(2,1)} %bitcast.52, pred[4,32]{1,0:T(4,128)(4,1)S(1)} %get-tuple-element.8, pred[4,32]{1,0:T(4,128)(4,1)S(1)} %get-tuple-element.6, bf16[4,128,128]{1,2,0:T(8,128)(2,1)S(1)} %copy-done, pred[]{:T(512)} %bitcast), kind=kOutput, calls=%fused_computation.21 | convolution fusion | flops 541392896 | bytes 8651009 | tf_op jit(solution)/shard_map/jlut,jlto->juo/dot_general | solution.py:32
  497.8 0.8 copy.28
  (4 shorter events, 0.0 us)
Async XLA Ops:
  6.5 155.1 %all-gather.8.cloned.1.call-start = ((), (), s32[]{:S(2)}) async-start(), calls=%async_computation | async-start | bytes 4325376 | tf_op jit(solution)/shard_map/all_gather | solution.py:15
  7.3 230.6 %all-gather.10.cloned.1.call-start = ((), (), s32[]{:S(2)}) async-start(), calls=%async_computation.1 | async-start | bytes 4325376 | tf_op jit(solution)/shard_map/all_gather | solution.py:21
  8.0 329.8 %all-gather.12.cloned.1.call-start = ((), (), s32[]{:S(2)}) async-start(), calls=%async_computation.2 | async-start | bytes 4325376 | tf_op jit(solution)/shard_map/all_gather | solution.py:21
  253.6 231.9 %all-gather.14.cloned.1.call-start = ((), (), s32[]{:S(2)}) async-start(), calls=%async_computation.3 | async-start | bytes 4325376 | tf_op jit(solution)/shard_map/all_gather | solution.py:15
  343.3 147.4 %copy-start = (bf16[4,128,128]{1,2,0:T(8,128)(2,1)S(1)}, bf16[4,128,128]{1,2,0:T(8,128)(2,1)}, u32[]{:S(2)}) copy-start(bf16[4,128,128]{1,2,0:T(8,128)(2,1)} %fusion.30) | copy-start | bytes 393220
Sparse Core Ops, SparseCore 0:
  10.0 151.6 all-gather.7
  166.1 71.7 all-gather.9
  253.7 84.1 all-gather.11
  340.4 145.0 all-gather.13
where the time goes:
time: 506 us; the launch traced here: 505 us
  waiting for transfers between devices  375 us (74%)
  blocking collectives  67 us (13%)
  local copies, waits for them, and re-layouts  32.1 us (6%)
  between operations  15.1 us (3%)
  matrix products  14.8 us (3%)
    all_gather x2, waiting for transfers between devices, body(): lax.all_gather(state, 'row', axis=0, tiled=True)  221 us
    all_gather x2, waiting for transfers between devices, body(): lax.all_gather(state, 'col', axis=1, tiled=True)  153 us
    squeeze x1, blocking collectives, body(): below_pos = lower_block_index[:, 0]  37.5 us
    all_gather x1, blocking collectives, body(): lax.all_gather(column_slot_index, 'col', axis=1, tiled=True)  29.5 us
    dot_general x2, matrix products, body(): jnp.einsum('jlut,jlto->juo', block_strip, selected_blocks, preferred_elem...  14.8 us
    gather x2, local copies, waits for them, and re-layouts, body(): selected_blocks = jnp.take(below_blocks, desired_trace, axis=0)  10.5 us
  transfers between devices with their start and end apart: 4, of which 4 were waited for; matrix products, arithmetic and copies ran while one was open for 4% of the time, Pallas kernels for 0%

commit v1 on v0

v1 whole, which is shorter than its diff:
```python
import functools

import jax
import jax.numpy as jnp
from jax import lax
from jax.experimental import pallas as pl
from jax.experimental.pallas import tpu as pltpu
from jax.sharding import Mesh, PartitionSpec as P

BPD = 4
STEPS = 2
BS = 128
ROWS = 4 * BS
AXES = ("zh", "zl", "x", "y", "core")
SIZES = (8, 4, 4, 4, 2)
BATCHES = ((0, 1, 7, 2, 6), (3, 5, 4))
RING = (0, 1, 3, 2)


def shift(size, by):
    return [(i, (i + by) % size) for i in range(size)]


def swap_pairs():
    pairs = []
    for zh in range(8):
        for zl in range(4):
            for x in range(4):
                for w in range(8):
                    pairs.append((((zh * 4 + zl) * 4 + x) * 8 + w, ((zh * 4 + x) * 4 + zl) * 8 + w))
    return pairs


def ring4(part, axis):
    one = lax.ppermute(part, axis, shift(4, 1))
    three = lax.ppermute(part, axis, shift(4, -1))
    half = part.shape[0] // 32 * 16
    two_a = lax.ppermute(one[:half], axis, shift(4, 1))
    two_b = lax.ppermute(three[half:], axis, shift(4, -1))
    return [part, one, three, two_a, two_b]


def kernel(rows, a_sizes, b_sizes, branch, tab, sa, sb, own, *refs):
    a_parts, refs = refs[: len(a_sizes)], refs[len(a_sizes) :]
    b_parts, refs = refs[: len(b_sizes)], refs[len(b_sizes) :]
    out, a_all, b_all, acc, sems = refs
    copies = []
    for parts, sizes, whole in ((a_parts, a_sizes, a_all), (b_parts, b_sizes, b_all)):
        at = 0
        for part, size in zip(parts, sizes):
            copies.append(
                pltpu.make_async_copy(part, whole.at[pl.ds(at, size)], sems.at[len(copies)])
            )
            at += size
    for copy in copies:
        copy.start()
    acc[...] = jnp.zeros_like(acc)
    mine = [sa[tab[64] * 4 + j] for j in range(4)]
    for copy in copies:
        copy.wait()

    def step(p, carry):
        la, lb = tab[p], tab[32 + p]
        for j in range(4):
            m = sa[la * 4 + j]

            @pl.when(sb[lb * 4 + m] == mine[j])
            def _():
                left = a_all[pl.ds(pl.multiple_of(la * rows + j * BS, 16), BS), :]
                right = b_all[pl.ds(pl.multiple_of(lb * rows + m * BS, 16), BS), :]
                acc[j * BS : (j + 1) * BS, :] += jnp.dot(
                    left, right, preferred_element_type=jnp.float32
                )

        return carry

    lax.fori_loop(0, 32, step, 0)
    square = acc[...]
    twice = 2.0 * own[...].astype(jnp.float32) - square
    out[...] = jnp.where(branch[0] == 1, twice, square).astype(out.dtype)


def multiply(branch, tab, sa, sb, own, a_parts, b_parts, rows):
    a_sizes = [q.shape[0] for q in a_parts]
    b_sizes = [q.shape[0] for q in b_parts]
    smem = pl.BlockSpec(memory_space=pltpu.SMEM)
    vmem = pl.BlockSpec(memory_space=pltpu.VMEM)
    anywhere = pl.BlockSpec(memory_space=pl.ANY)
    return pl.pallas_call(
        functools.partial(kernel, rows, a_sizes, b_sizes),
        out_shape=jax.ShapeDtypeStruct((ROWS, BS), jnp.bfloat16),
        in_specs=[smem] * 4 + [vmem] + [anywhere] * (len(a_parts) + len(b_parts)),
        out_specs=vmem,
        scratch_shapes=[
            pltpu.VMEM((32 * rows, BS), jnp.bfloat16),
            pltpu.VMEM((32 * rows, BS), jnp.bfloat16),
            pltpu.VMEM((ROWS, BS), jnp.float32),
            pltpu.SemaphoreType.DMA((len(a_parts) + len(b_parts),)),
        ],
        compiler_params=pltpu.CompilerParams(vmem_limit_bytes=24 * 1024 * 1024),
        cost_estimate=pl.CostEstimate(
            flops=2 * 128 * BS**3, bytes_accessed=64 * ROWS * BS * 2, transcendentals=0
        ),
    )(branch, tab, sa, sb, own, *a_parts, *b_parts)


def slots_of(parts, rows):
    found, at = [], 0
    for part in parts:
        size = part.shape[0]
        first = -(-(at - ROWS) // rows)
        for unit in range(max(first, 0), 32):
            row = unit * rows + ROWS - at
            if row >= size:
                break
            if row >= 0:
                found.append(part[row, :4])
        at += size
    return jnp.concatenate(found).astype(jnp.int32)


def places(zh, zl, x, y, core):
    p = jnp.arange(32, dtype=jnp.int32)
    ring = jnp.array([0, 1, 3, 2], jnp.int32)

    def pick(table, index):
        out = jnp.zeros_like(index)
        for k, value in enumerate(table):
            out = jnp.where(index == k, value, out)
        return out

    del ring
    order = [RING.index(k) for k in range(4)]
    la = ((p % 2) ^ core) * 16 + pick(order, (y - p // 2 % 4) % 4) * 4 + p // 8
    dz, dx = (zh - p // 4) % 8, pick(order, (x - p % 4) % 4)
    first, second = BATCHES
    at_first = pick([first.index(k) if k in first else 0 for k in range(8)], dz)
    at_second = pick([second.index(k) if k in second else 0 for k in range(8)], dz)
    is_first = pick([int(k in first) for k in range(8)], dz)
    n1, n2 = len(first), len(second)
    lb = jnp.where(is_first == 1, dx * n1 + at_first, 4 * n1 + dx * n2 + at_second)
    return jnp.concatenate([la, lb, jnp.full((1,), zl, jnp.int32)])


def gather(unit):
    at = {0: unit}
    for hop in (1, 2, 3):
        at[hop] = lax.ppermute(at[hop - 1], "zh", shift(8, 1))
        at[8 - hop] = lax.ppermute(at[(9 - hop) % 8], "zh", shift(8, -1))
    at[4] = lax.ppermute(at[3], "zh", shift(8, 1))
    near = lax.all_gather(unit, "zl", axis=0, tiled=True)
    half = ring4(near, "y")
    half = jnp.concatenate(half)
    other = lax.ppermute(half, "core", shift(2, 1))
    b_parts = []
    for batch in BATCHES:
        b_parts += ring4(jnp.concatenate([at[k] for k in batch]), "x")
    return [half, other], b_parts


def body(values, column_slot_index, branches):
    where = [lax.axis_index(name) for name in AXES]
    tab = places(*where)
    flat = values.reshape(ROWS, BS)
    tail = jnp.pad(column_slot_index[:, 0].astype(jnp.bfloat16)[None], ((0, 15), (0, BS - 4)))
    unit = lax.ppermute(jnp.concatenate([flat, tail]), AXES, swap_pairs())
    sa = sb = None
    for step in range(STEPS):
        rows = unit.shape[0]
        a_parts, b_parts = gather(unit)
        if step == 0:
            sa, sb = slots_of(a_parts, rows), slots_of(b_parts, rows)
        own = unit[:ROWS]
        unit = multiply(branches[step : step + 1], tab, sa, sb, own, a_parts, b_parts, rows)
    out = lax.ppermute(unit, AXES, swap_pairs())
    return out.reshape(values.shape)


def solution(mesh):
    fine = Mesh(mesh.devices.reshape(SIZES), AXES)
    split = (("zh", "zl"), ("x", "y", "core"))
    in_specs = (P(*split, None, None), P(*split), P())
    return jax.shard_map(
        body, mesh=fine, in_specs=in_specs, out_specs=P(*split, None, None), check_vma=False
    )
```

time: 506 us -> 386 us (0.76)
  the two profiles are of different devices: /device:TPU:4 before, /device:TPU:10 now
where the time goes in v1:
time: 386 us; the launch traced here: 384 us
  starting transfers between devices  177 us (46%)
  waiting for transfers between devices  94.7 us (25%)
  local copies, waits for them, and re-layouts  59.7 us (15%)
  blocking collectives  31.7 us (8%)
  Pallas kernels  16.8 us (4%)
    ppermute x6, starting transfers between devices, gather(): at[8 - hop] = lax.ppermute(at[(9 - hop) % 8], 'zh', shift(8, -1))  44 us
    ppermute x6, starting transfers between devices, gather(): at[hop] = lax.ppermute(at[hop - 1], 'zh', shift(8, 1))  38.3 us
    all_gather x2, blocking collectives, gather(): near = lax.all_gather(unit, 'zl', axis=0, tiled=True)  31.7 us
    concatenate x2, local copies, waits for them, and re-layouts, slots_of(): return jnp.concatenate(found).astype(jnp.int32)  31.7 us
    ppermute x6, starting transfers between devices, ring4(): one = lax.ppermute(part, axis, shift(4, 1))  25.5 us
    ppermute x6, starting transfers between devices, ring4(): two_a = lax.ppermute(one[:half], axis, shift(4, 1))  23.2 us
    ppermute x6, waiting for transfers between devices, gather(): at[8 - hop] = lax.ppermute(at[(9 - hop) % 8], 'zh', shift(8, -1))  23 us
    ppermute x6, waiting for transfers between devices, gather(): at[hop] = lax.ppermute(at[hop - 1], 'zh', shift(8, 1))  17 us
  transfers between devices with their start and end apart: 42, of which 22 were waited for; matrix products, arithmetic and copies ran while one was open for 8% of the time, Pallas kernels for 0%

profile of v1, /device:TPU:10, one launch (start us, length us, event | category | flops | bytes accessed | tf_op | source)
XLA Modules:
  0.0 384.0 jit_solution(7930382704943331604)
XLA Ops:
  1.6 3.8 collective-permute-start
  6.8 8.7 %collective-permute-done = bf16[528,128]{1,0:T(8,128)(2,1)S(1)} collective-permute-done((bf16[528,128]{1,0:T(8,128)(2,1)S(1)}, bf16[528,128]{1,0:T(8,128)(2,1)S(1)}, u32[]{:S(2)}, u32[]{:S(2)}) %collective-permute-start) | collective-permute-done | bytes 135200 | tf_op jit(solution)/shard_map/ppermute | solution.py:166
  15.5 16.7 %all_gather.6 = bf16[2112,128]{1,0:T(8,128)(2,1)S(1)} all-gather(bf16[528,128]{1,0:T(8,128)(2,1)S(1)} %collective-permute-done), channel_id=1, replica_groups=mesh['zh'=8,'zl'=4,'x'=4,'y'=4,'core'=2] {'zl'}, dimensions={0}, use_global_device_ids=true | all-gather | bytes 675840 | tf_op jit(solution)/shard_map/all_gather | solution.py:151
  32.8 3.5 collective-permute-start.1
  36.3 2.4 collective-permute-start.2
  38.7 9.1 %collective-permute-start.6 = (bf16[528,128]{1,0:T(8,128)(2,1)S(1)}, bf16[528,128]{1,0:T(8,128)(2,1)S(1)}, u32[]{:S(2)}, u32[]{:S(2)}) collective-permute-start(bf16[528,128]{1,0:T(8,128)(2,1)S(1)} %collective-permute-done), channel_id=1, source_target_pairs={{0,128},{128,256},{256,384},{384,512},{512,640},{640,768},{768,896... | collective-permute-start | bytes 405512 | tf_op jit(solution)/shard_map/ppermute | solution.py:148
  48.3 11.5 %collective-permute-start.7 = (bf16[528,128]{1,0:T(8,128)(2,1)S(1)}, bf16[528,128]{1,0:T(8,128)(2,1)S(1)}, u32[]{:S(2)}, u32[]{:S(2)}) collective-permute-start(bf16[528,128]{1,0:T(8,128)(2,1)S(1)} %collective-permute-done), channel_id=1, source_target_pairs={{0,896},{128,0},{256,128},{384,256},{512,384},{640,512},{768,640},... | collective-permute-start | bytes 405512 | tf_op jit(solution)/shard_map/ppermute | solution.py:149
  61.3 3.0 collective-permute-start.8
  67.4 12.9 %collective-permute-start.9 = (bf16[528,128]{1,0:T(8,128)(2,1)S(1)}, bf16[528,128]{1,0:T(8,128)(2,1)S(1)}, u32[]{:S(2)}, u32[]{:S(2)}) collective-permute-start(bf16[528,128]{1,0:T(8,128)(2,1)S(1)} %collective-permute-done.7), channel_id=1, source_target_pairs={{0,896},{128,0},{256,128},{384,256},{512,384},{640,512},{768,640},... | collective-permute-start | bytes 405512 | tf_op jit(solution)/shard_map/ppermute | solution.py:149
  80.3 3.6 collective-permute-done.8
  83.9 2.0 collective-permute-done.9
  85.9 2.1 collective-permute-start.10
  88.0 3.7 collective-permute-start.11
  92.3 7.4 %collective-permute-start.14 = (bf16[528,128]{1,0:T(8,128)(2,1)S(1)}, bf16[528,128]{1,0:T(8,128)(2,1)S(1)}, u32[]{:S(2)}, u32[]{:S(2)}) collective-permute-start(bf16[528,128]{1,0:T(8,128)(2,1)S(1)} %collective-permute-done.8), channel_id=1, source_target_pairs={{0,128},{128,256},{256,384},{384,512},{512,640},{640,768},{768,896... | collective-permute-start | bytes 405512 | tf_op jit(solution)/shard_map/ppermute | solution.py:148
  100.3 7.9 %collective-permute-done.14 = bf16[528,128]{1,0:T(8,128)(2,1)S(1)} collective-permute-done((bf16[528,128]{1,0:T(8,128)(2,1)S(1)}, bf16[528,128]{1,0:T(8,128)(2,1)S(1)}, u32[]{:S(2)}, u32[]{:S(2)}) %collective-permute-start.14) | collective-permute-done | bytes 135200 | tf_op jit(solution)/shard_map/ppermute | solution.py:148
  108.2 4.1 %collective-permute-start.15 = (bf16[528,128]{1,0:T(8,128)(2,1)S(1)}, bf16[528,128]{1,0:T(8,128)(2,1)S(1)}, u32[]{:S(2)}, u32[]{:S(2)}) collective-permute-start(bf16[528,128]{1,0:T(8,128)(2,1)S(1)} %collective-permute-done.9), channel_id=1, source_target_pairs={{0,896},{128,0},{256,128},{384,256},{512,384},{640,512},{768,640},... | collective-permute-start | bytes 405512 | tf_op jit(solution)/shard_map/ppermute | solution.py:149
  112.8 11.7 %collective-permute-done.15 = bf16[528,128]{1,0:T(8,128)(2,1)S(1)} collective-permute-done((bf16[528,128]{1,0:T(8,128)(2,1)S(1)}, bf16[528,128]{1,0:T(8,128)(2,1)S(1)}, u32[]{:S(2)}, u32[]{:S(2)}) %collective-permute-start.15) | collective-permute-done | bytes 135200 | tf_op jit(solution)/shard_map/ppermute | solution.py:149
  124.5 5.1 %collective-permute-start.16 = (bf16[528,128]{1,0:T(8,128)(2,1)S(1)}, bf16[528,128]{1,0:T(8,128)(2,1)S(1)}, u32[]{:S(2)}, u32[]{:S(2)}) collective-permute-start(bf16[528,128]{1,0:T(8,128)(2,1)S(1)} %collective-permute-done.14), channel_id=1, source_target_pairs={{0,128},{128,256},{256,384},{384,512},{512,640},{640,768},{768,896... | collective-permute-start | bytes 405512 | tf_op jit(solution)/shard_map/ppermute | solution.py:150
  130.2 3.5 collective-permute-start.3
  133.7 2.4 collective-permute-start.4
  136.0 2.3 collective-permute-done.16
  138.4 4.7 %collective-permute-start.17 = (bf16[1584,128]{1,0:T(8,128)(2,1)S(1)}, bf16[1584,128]{1,0:T(8,128)(2,1)S(1)}, u32[]{:S(2)}, u32[]{:S(2)}) collective-permute-start(bf16[1584,128]{1,0:T(8,128)(2,1)S(1)} %constant_dynamic-update-slice_fusion.10.refs_7_), channel_id=1, source_target_pairs={{0,8},{8,16},{16,24},{24,0},{1,9},{9,17},{17,25},{25,1},{2,10},{10... | collective-permute-start | bytes 1216520 | tf_op jit(solution)/shard_map/ppermute | solution.py:35
  147.1 1.9 collective-permute-start.5
  150.2 3.9 %collective-permute-start.12 = (bf16[1312,128]{1,0:T(8,128)(2,1)S(1)}, bf16[1312,128]{1,0:T(8,128)(2,1)S(1)}, u32[]{:S(2)}, u32[]{:S(2)}) collective-permute-start(bf16[1312,128]{1,0:T(8,128)(2,1)S(1)} %slice.365), channel_id=1, source_target_pairs={{0,8},{8,16},{16,24},{24,0},{1,9},{9,17},{17,25},{25,1},{2,10},{10... | collective-permute-start | bytes 1007624 | tf_op jit(solution)/shard_map/ppermute | solution.py:38
  154.1 1.9 collective-permute-start.13
  156.1 3.9 %collective-permute-start.19 = (bf16[784,128]{1,0:T(8,128)(2,1)S(1)}, bf16[784,128]{1,0:T(8,128)(2,1)S(1)}, u32[]{:S(2)}, u32[]{:S(2)}) collective-permute-start(bf16[784,128]{1,0:T(8,128)(2,1)S(1)} %slice.381), channel_id=1, source_target_pairs={{0,8},{8,16},{16,24},{24,0},{1,9},{9,17},{17,25},{25,1},{2,10},{10... | collective-permute-start | bytes 602120 | tf_op jit(solution)/shard_map/ppermute | solution.py:38
  160.1 1.9 collective-permute-start.20
  163.7 2.9 collective-permute-done.19.refs_10_
  167.8 2.7 collective-permute-done.20.refs_11_
  174.4 15.5 %concatenate.36 = bf16[128]{0:T(256)(128)(2,1)} concatenate(bf16[4]{0:T(256)(128)(2,1)} %slice_bitcast_fusion.31, bf16[4]{0:T(256)(128)(2,1)} %slice_bitcast_fusion.30, bf16[4]{0:T(256)(128)(2,1)} %slice_bitcast_fusion.29, bf16[4]{0:T(256)(128)(2,1)} %slice_bitcast_fusion.28, bf16[4]{0:T(256)(128)(2,1)} %slice_bitcast_fusion.27, bf16[4]{0:T(256)(128)(2,1)S(1)} %get-tuple-element.30, ...), dimensions={0} | concatenate | bytes 512 | tf_op jit(solution)/shard_map/concatenate | solution.py:119
  191.9 16.2 %concatenate.33 = bf16[128]{0:T(256)(128)(2,1)} concatenate(bf16[4]{0:T(256)(128)(2,1)} %get-tuple-element.42, bf16[4]{0:T(256)(128)(2,1)} %get-tuple-element.41, bf16[4]{0:T(256)(128)(2,1)} %get-tuple-element.40, bf16[4]{0:T(256)(128)(2,1)} %get-tuple-element.39, bf16[4]{0:T(256)(128)(2,1)} %get-tuple-element.38, bf16[4]{0:T(256)(128)(2,1)} %get-tuple-element.37, ...), dimensions={0} | concatenate | bytes 512 | tf_op jit(solution)/shard_map/concatenate | solution.py:119
  217.6 8.4 %shard_map.37.own = bf16[512,128]{1,0:T(8,128)(2,1)S(1)} custom-call(s32[1]{0:T(128)} %get-tuple-element.60.branch, s32[65]{0:T(128)S(1)} %pad_add_fusion.tab, s32[128]{0:T(128)S(1)} %convert_element_type.23.sa, s32[128]{0:T(128)S(1)} %convert_element_type.24.sb, bf16[512,128]{1,0:T(8,128)(2,1)S(1)} %copy-done.8, ...), custom_call_target="tpu_custom_call" | custom-call | flops 536870912 | bytes 8388608 | tf_op jit(solution)/shard_map/pallas_call | solution.py:89
  226.0 15.0 %all_gather.7 = bf16[2048,128]{1,0:T(8,128)(2,1)S(1)} all-gather(bf16[512,128]{1,0:T(8,128)(2,1)S(1)} %shard_map.37.own), channel_id=1, replica_groups=mesh['zh'=8,'zl'=4,'x'=4,'y'=4,'core'=2] {'zl'}, dimensions={0}, use_global_device_ids=true | all-gather | bytes 655360 | tf_op jit(solution)/shard_map/all_gather | solution.py:151
  241.0 4.2 %collective-permute-start.21 = (bf16[2048,128]{1,0:T(8,128)(2,1)S(1)}, bf16[2048,128]{1,0:T(8,128)(2,1)S(1)}, u32[]{:S(2)}, u32[]{:S(2)}) collective-permute-start(bf16[2048,128]{1,0:T(8,128)(2,1)S(1)} %all_gather.7), channel_id=1, source_target_pairs={{0,2},{2,4},{4,6},{6,0},{1,3},{3,5},{5,7},{7,1},{8,10},{10,12},{12... | collective-permute-start | bytes 1572872 | tf_op jit(solution)/shard_map/ppermute | solution.py:35
  245.2 1.9 collective-permute-start.22
  247.2 5.7 %collective-permute-done.21 = bf16[2048,128]{1,0:T(8,128)(2,1)S(1)} collective-permute-done((bf16[2048,128]{1,0:T(8,128)(2,1)S(1)}, bf16[2048,128]{1,0:T(8,128)(2,1)S(1)}, u32[]{:S(2)}, u32[]{:S(2)}) %collective-permute-start.21) | collective-permute-done | bytes 524320 | tf_op jit(solution)/shard_map/ppermute | solution.py:35
  252.9 4.4 %collective-permute-start.23 = (bf16[1024,128]{1,0:T(8,128)(2,1)S(1)}, bf16[1024,128]{1,0:T(8,128)(2,1)S(1)}, u32[]{:S(2)}, u32[]{:S(2)}) collective-permute-start(bf16[1024,128]{1,0:T(8,128)(2,1)S(1)} %slice.387), channel_id=1, source_target_pairs={{0,2},{2,4},{4,6},{6,0},{1,3},{3,5},{5,7},{7,1},{8,10},{10,12},{12... | collective-permute-start | bytes 786440 | tf_op jit(solution)/shard_map/ppermute | solution.py:38
  257.3 1.9 collective-permute-start.24
  261.2 4.4 %collective-permute-done.24 = bf16[1024,128]{1,0:T(8,128)(2,1)S(1)} collective-permute-done((bf16[1024,128]{1,0:T(8,128)(2,1)S(1)}, bf16[1024,128]{1,0:T(8,128)(2,1)S(1)}, u32[]{:S(2)}, u32[]{:S(2)}) %collective-permute-start.24) | collective-permute-done | bytes 262176 | tf_op jit(solution)/shard_map/ppermute | solution.py:39
  267.6 5.2 %collective-permute-start.26 = (bf16[512,128]{1,0:T(8,128)(2,1)S(1)}, bf16[512,128]{1,0:T(8,128)(2,1)S(1)}, u32[]{:S(2)}, u32[]{:S(2)}) collective-permute-start(bf16[512,128]{1,0:T(8,128)(2,1)S(1)} %shard_map.37.own), channel_id=1, source_target_pairs={{0,128},{128,256},{256,384},{384,512},{512,640},{640,768},{768,896... | collective-permute-start | bytes 393224 | tf_op jit(solution)/shard_map/ppermute | solution.py:148
  272.8 4.5 %collective-permute-start.27 = (bf16[512,128]{1,0:T(8,128)(2,1)S(1)}, bf16[512,128]{1,0:T(8,128)(2,1)S(1)}, u32[]{:S(2)}, u32[]{:S(2)}) collective-permute-start(bf16[512,128]{1,0:T(8,128)(2,1)S(1)} %shard_map.37.own), channel_id=1, source_target_pairs={{0,896},{128,0},{256,128},{384,256},{512,384},{640,512},{768,640},... | collective-permute-start | bytes 393224 | tf_op jit(solution)/shard_map/ppermute | solution.py:149
  277.4 4.8 %collective-permute-done.26 = bf16[512,128]{1,0:T(8,128)(2,1)S(1)} collective-permute-done((bf16[512,128]{1,0:T(8,128)(2,1)S(1)}, bf16[512,128]{1,0:T(8,128)(2,1)S(1)}, u32[]{:S(2)}, u32[]{:S(2)}) %collective-permute-start.26) | collective-permute-done | bytes 131104 | tf_op jit(solution)/shard_map/ppermute | solution.py:148
  282.2 7.3 %collective-permute-start.28 = (bf16[512,128]{1,0:T(8,128)(2,1)S(1)}, bf16[512,128]{1,0:T(8,128)(2,1)S(1)}, u32[]{:S(2)}, u32[]{:S(2)}) collective-permute-start(bf16[512,128]{1,0:T(8,128)(2,1)S(1)} %collective-permute-done.26), channel_id=1, source_target_pairs={{0,128},{128,256},{256,384},{384,512},{512,640},{640,768},{768,896... | collective-permute-start | bytes 393224 | tf_op jit(solution)/shard_map/ppermute | solution.py:148
  291.2 3.5 collective-permute-start.29
  294.7 6.3 %collective-permute-start.34 = (bf16[512,128]{1,0:T(8,128)(2,1)S(1)}, bf16[512,128]{1,0:T(8,128)(2,1)S(1)}, u32[]{:S(2)}, u32[]{:S(2)}) collective-permute-start(bf16[512,128]{1,0:T(8,128)(2,1)S(1)} %collective-permute-done.28), channel_id=1, source_target_pairs={{0,128},{128,256},{256,384},{384,512},{512,640},{640,768},{768,896... | collective-permute-start | bytes 393224 | tf_op jit(solution)/shard_map/ppermute | solution.py:148
  301.0 2.4 collective-permute-done.29
  303.5 7.3 %collective-permute-start.30 = (bf16[2560,128]{1,0:T(8,128)(2,1)S(1)}, bf16[2560,128]{1,0:T(8,128)(2,1)S(1)}, u32[]{:S(2)}, u32[]{:S(2)}) collective-permute-start(bf16[2560,128]{1,0:T(8,128)(2,1)S(1)} %constant_dynamic-update-slice_fusion.18.refs_2_), channel_id=1, source_target_pairs={{0,8},{8,16},{16,24},{24,0},{1,9},{9,17},{17,25},{25,1},{2,10},{10... | collective-permute-start | bytes 1966088 | tf_op jit(solution)/shard_map/ppermute | solution.py:35
  310.7 1.9 collective-permute-start.31
  312.7 7.6 %collective-permute-start.35 = (bf16[512,128]{1,0:T(8,128)(2,1)S(1)}, bf16[512,128]{1,0:T(8,128)(2,1)S(1)}, u32[]{:S(2)}, u32[]{:S(2)}) collective-permute-start(bf16[512,128]{1,0:T(8,128)(2,1)S(1)} %collective-permute-done.29), channel_id=1, source_target_pairs={{0,896},{128,0},{256,128},{384,256},{512,384},{640,512},{768,640},... | collective-permute-start | bytes 393224 | tf_op jit(solution)/shard_map/ppermute | solution.py:149
  320.3 2.2 collective-permute-start.36
  322.5 3.3 collective-permute-done.35
  325.8 8.2 %collective-permute-done.36 = bf16[512,128]{1,0:T(8,128)(2,1)S(1)} collective-permute-done((bf16[512,128]{1,0:T(8,128)(2,1)S(1)}, bf16[512,128]{1,0:T(8,128)(2,1)S(1)}, u32[]{:S(2)}, u32[]{:S(2)}) %collective-permute-start.36) | collective-permute-done | bytes 131104 | tf_op jit(solution)/shard_map/ppermute | solution.py:150
  334.0 3.7 collective-permute-start.37
  337.8 2.1 collective-permute-start.38
  339.9 3.7 collective-permute-start.32
  343.7 2.1 collective-permute-start.33
  345.8 2.1 collective-permute-done.37.refs_8_
  347.9 3.7 collective-permute-start.39
  351.7 2.1 collective-permute-start.40
  353.8 4.4 %collective-permute-done.39.refs_10_ = bf16[768,128]{1,0:T(8,128)(2,1)S(1)} collective-permute-done((bf16[768,128]{1,0:T(8,128)(2,1)S(1)}, bf16[768,128]{1,0:T(8,128)(2,1)S(1)}, u32[]{:S(2)}, u32[]{:S(2)}) %collective-permute-start.39) | collective-permute-done | bytes 196640 | tf_op jit(solution)/shard_map/ppermute | solution.py:38
  358.2 3.4 collective-permute-done.40.refs_11_
  361.6 8.4 %shard_map.38 = bf16[512,128]{1,0:T(8,128)(2,1)S(1)} custom-call(s32[1]{0:T(128)} %get-tuple-element.61.branch, s32[65]{0:T(128)S(1)} %pad_add_fusion.tab, s32[128]{0:T(128)S(1)} %convert_element_type.23.sa, s32[128]{0:T(128)S(1)} %convert_element_type.24.sb, bf16[512,128]{1,0:T(8,128)(2,1)S(1)} %shard_map.37.own, ...), custom_call_target="tpu_custom_call" | custom-call | flops 536870912 | bytes 8388608 | tf_op jit(solution)/shard_map/pallas_call | solution.py:89
  370.0 5.3 %collective-permute-start.41 = (bf16[512,128]{1,0:T(8,128)(2,1)S(1)}, bf16[512,128]{1,0:T(8,128)(2,1)S(1)}, u32[]{:S(2)}, u32[]{:S(2)}) collective-permute-start(bf16[512,128]{1,0:T(8,128)(2,1)S(1)} %shard_map.38), channel_id=1, source_target_pairs={{0,0},{1,1},{2,2},{3,3},{4,4},{5,5},{6,6},{7,7},{8,32},{9,33},{10,... | collective-permute-start | bytes 393224 | tf_op jit(solution)/shard_map/ppermute | solution.py:175
  375.3 8.0 %collective-permute-done.41 = bf16[512,128]{1,0:T(8,128)(2,1)S(1)} collective-permute-done((bf16[512,128]{1,0:T(8,128)(2,1)S(1)}, bf16[512,128]{1,0:T(8,128)(2,1)S(1)}, u32[]{:S(2)}, u32[]{:S(2)}) %collective-permute-start.41) | collective-permute-done | bytes 131104 | tf_op jit(solution)/shard_map/ppermute | solution.py:175
  (129 shorter events, 40.9 us)
Async XLA Ops:
  1.6 13.9 %collective-permute-start = (bf16[528,128]{1,0:T(8,128)(2,1)S(1)}, bf16[528,128]{1,0:T(8,128)(2,1)S(1)}, u32[]{:S(2)}, u32[]{:S(2)}) collective-permute-start(bf16[528,128]{1,0:T(8,128)(2,1)S(1)} %fusion.1), channel_id=1, source_target_pairs={{0,0},{1,1},{2,2},{3,3},{4,4},{5,5},{6,6},{7,7},{8,32},{9,33},{10,... | collective-permute-start | bytes 405512 | tf_op jit(solution)/shard_map/ppermute | solution.py:166
  32.8 97.3 %collective-permute-start.1 = (bf16[2112,128]{1,0:T(8,128)(2,1)S(1)}, bf16[2112,128]{1,0:T(8,128)(2,1)S(1)}, u32[]{:S(2)}, u32[]{:S(2)}) collective-permute-start(bf16[2112,128]{1,0:T(8,128)(2,1)S(1)} %all_gather.6), channel_id=1, source_target_pairs={{0,2},{2,4},{4,6},{6,0},{1,3},{3,5},{5,7},{7,1},{8,10},{10,12},{12... | collective-permute-start | bytes 1622024 | tf_op jit(solution)/shard_map/ppermute | solution.py:35
  36.3 97.4 %collective-permute-start.2 = (bf16[2112,128]{1,0:T(8,128)(2,1)S(1)}, bf16[2112,128]{1,0:T(8,128)(2,1)S(1)}, u32[]{:S(2)}, u32[]{:S(2)}) collective-permute-start(bf16[2112,128]{1,0:T(8,128)(2,1)S(1)} %all_gather.6), channel_id=1, source_target_pairs={{0,6},{2,0},{4,2},{6,4},{1,7},{3,1},{5,3},{7,5},{8,14},{10,8},{12,... | collective-permute-start | bytes 1622024 | tf_op jit(solution)/shard_map/ppermute | solution.py:36
  38.7 22.6 %collective-permute-start.6 = (bf16[528,128]{1,0:T(8,128)(2,1)S(1)}, bf16[528,128]{1,0:T(8,128)(2,1)S(1)}, u32[]{:S(2)}, u32[]{:S(2)}) collective-permute-start(bf16[528,128]{1,0:T(8,128)(2,1)S(1)} %collective-permute-done), channel_id=1, source_target_pairs={{0,128},{128,256},{256,384},{384,512},{512,640},{640,768},{768,896... | collective-permute-start | bytes 405512 | tf_op jit(solution)/shard_map/ppermute | solution.py:148
  48.3 18.4 %collective-permute-start.7 = (bf16[528,128]{1,0:T(8,128)(2,1)S(1)}, bf16[528,128]{1,0:T(8,128)(2,1)S(1)}, u32[]{:S(2)}, u32[]{:S(2)}) collective-permute-start(bf16[528,128]{1,0:T(8,128)(2,1)S(1)} %collective-permute-done), channel_id=1, source_target_pairs={{0,896},{128,0},{256,128},{384,256},{512,384},{640,512},{768,640},... | collective-permute-start | bytes 405512 | tf_op jit(solution)/shard_map/ppermute | solution.py:149
  61.3 22.6 %collective-permute-start.8 = (bf16[528,128]{1,0:T(8,128)(2,1)S(1)}, bf16[528,128]{1,0:T(8,128)(2,1)S(1)}, u32[]{:S(2)}, u32[]{:S(2)}) collective-permute-start(bf16[528,128]{1,0:T(8,128)(2,1)S(1)} %collective-permute-done.6), channel_id=1, source_target_pairs={{0,128},{128,256},{256,384},{384,512},{512,640},{640,768},{768,896... | collective-permute-start | bytes 405512 | tf_op jit(solution)/shard_map/ppermute | solution.py:148
  67.4 18.5 %collective-permute-start.9 = (bf16[528,128]{1,0:T(8,128)(2,1)S(1)}, bf16[528,128]{1,0:T(8,128)(2,1)S(1)}, u32[]{:S(2)}, u32[]{:S(2)}) collective-permute-start(bf16[528,128]{1,0:T(8,128)(2,1)S(1)} %collective-permute-done.7), channel_id=1, source_target_pairs={{0,896},{128,0},{256,128},{384,256},{512,384},{640,512},{768,640},... | collective-permute-start | bytes 405512 | tf_op jit(solution)/shard_map/ppermute | solution.py:149
  85.9 61.1 %copy-start = (bf16[2640,128]{1,0:T(8,128)(2,1)}, bf16[2640,128]{1,0:T(8,128)(2,1)S(1)}, u32[]{:S(2)}) copy-start(bf16[2640,128]{1,0:T(8,128)(2,1)S(1)} %constant_dynamic-update-slice_fusion.5.refs_2_) | copy-start | bytes 2027524
  85.9 64.2 %collective-permute-start.10 = (bf16[2640,128]{1,0:T(8,128)(2,1)S(1)}, bf16[2640,128]{1,0:T(8,128)(2,1)S(1)}, u32[]{:S(2)}, u32[]{:S(2)}) collective-permute-start(bf16[2640,128]{1,0:T(8,128)(2,1)S(1)} %constant_dynamic-update-slice_fusion.5.refs_2_), channel_id=1, source_target_pairs={{0,8},{8,16},{16,24},{24,0},{1,9},{9,17},{17,25},{25,1},{2,10},{10... | collective-permute-start | bytes 2027528 | tf_op jit(solution)/shard_map/ppermute | solution.py:35
  88.0 66.1 %collective-permute-start.11 = (bf16[2640,128]{1,0:T(8,128)(2,1)S(1)}, bf16[2640,128]{1,0:T(8,128)(2,1)S(1)}, u32[]{:S(2)}, u32[]{:S(2)}) collective-permute-start(bf16[2640,128]{1,0:T(8,128)(2,1)S(1)} %constant_dynamic-update-slice_fusion.5.refs_2_), channel_id=1, source_target_pairs={{0,24},{8,0},{16,8},{24,16},{1,25},{9,1},{17,9},{25,17},{2,26},{10... | collective-permute-start | bytes 2027528 | tf_op jit(solution)/shard_map/ppermute | solution.py:36
  92.3 15.9 %collective-permute-start.14 = (bf16[528,128]{1,0:T(8,128)(2,1)S(1)}, bf16[528,128]{1,0:T(8,128)(2,1)S(1)}, u32[]{:S(2)}, u32[]{:S(2)}) collective-permute-start(bf16[528,128]{1,0:T(8,128)(2,1)S(1)} %collective-permute-done.8), channel_id=1, source_target_pairs={{0,128},{128,256},{256,384},{384,512},{512,640},{640,768},{768,896... | collective-permute-start | bytes 405512 | tf_op jit(solution)/shard_map/ppermute | solution.py:148
  108.2 16.3 %collective-permute-start.15 = (bf16[528,128]{1,0:T(8,128)(2,1)S(1)}, bf16[528,128]{1,0:T(8,128)(2,1)S(1)}, u32[]{:S(2)}, u32[]{:S(2)}) collective-permute-start(bf16[528,128]{1,0:T(8,128)(2,1)S(1)} %collective-permute-done.9), channel_id=1, source_target_pairs={{0,896},{128,0},{256,128},{384,256},{512,384},{640,512},{768,640},... | collective-permute-start | bytes 405512 | tf_op jit(solution)/shard_map/ppermute | solution.py:149
  124.5 13.9 %collective-permute-start.16 = (bf16[528,128]{1,0:T(8,128)(2,1)S(1)}, bf16[528,128]{1,0:T(8,128)(2,1)S(1)}, u32[]{:S(2)}, u32[]{:S(2)}) collective-permute-start(bf16[528,128]{1,0:T(8,128)(2,1)S(1)} %collective-permute-done.14), channel_id=1, source_target_pairs={{0,128},{128,256},{256,384},{384,512},{512,640},{640,768},{768,896... | collective-permute-start | bytes 405512 | tf_op jit(solution)/shard_map/ppermute | solution.py:150
  130.2 14.9 %collective-permute-start.3 = (bf16[1056,128]{1,0:T(8,128)(2,1)S(1)}, bf16[1056,128]{1,0:T(8,128)(2,1)S(1)}, u32[]{:S(2)}, u32[]{:S(2)}) collective-permute-start(bf16[1056,128]{1,0:T(8,128)(2,1)S(1)} %slice.328), channel_id=1, source_target_pairs={{0,2},{2,4},{4,6},{6,0},{1,3},{3,5},{5,7},{7,1},{8,10},{10,12},{12... | collective-permute-start | bytes 811016 | tf_op jit(solution)/shard_map/ppermute | solution.py:38
  133.7 13.3 %collective-permute-start.4 = (bf16[1056,128]{1,0:T(8,128)(2,1)S(1)}, bf16[1056,128]{1,0:T(8,128)(2,1)S(1)}, u32[]{:S(2)}, u32[]{:S(2)}) collective-permute-start(bf16[1056,128]{1,0:T(8,128)(2,1)S(1)} %slice.331), channel_id=1, source_target_pairs={{0,6},{2,0},{4,2},{6,4},{1,7},{3,1},{5,3},{7,5},{8,14},{10,8},{12,... | collective-permute-start | bytes 811016 | tf_op jit(solution)/shard_map/ppermute | solution.py:39
  138.4 15.7 %copy-start.6 = (bf16[1584,128]{1,0:T(8,128)(2,1)}, bf16[1584,128]{1,0:T(8,128)(2,1)S(1)}, u32[]{:S(2)}) copy-start(bf16[1584,128]{1,0:T(8,128)(2,1)S(1)} %constant_dynamic-update-slice_fusion.10.refs_7_) | copy-start | bytes 1216516
  138.4 17.7 %collective-permute-start.17 = (bf16[1584,128]{1,0:T(8,128)(2,1)S(1)}, bf16[1584,128]{1,0:T(8,128)(2,1)S(1)}, u32[]{:S(2)}, u32[]{:S(2)}) collective-permute-start(bf16[1584,128]{1,0:T(8,128)(2,1)S(1)} %constant_dynamic-update-slice_fusion.10.refs_7_), channel_id=1, source_target_pairs={{0,8},{8,16},{16,24},{24,0},{1,9},{9,17},{17,25},{25,1},{2,10},{10... | collective-permute-start | bytes 1216520 | tf_op jit(solution)/shard_map/ppermute | solution.py:35
  145.0 15.0 %collective-permute-start.18 = (bf16[1584,128]{1,0:T(8,128)(2,1)S(1)}, bf16[1584,128]{1,0:T(8,128)(2,1)S(1)}, u32[]{:S(2)}, u32[]{:S(2)}) collective-permute-start(bf16[1584,128]{1,0:T(8,128)(2,1)S(1)} %constant_dynamic-update-slice_fusion.10.refs_7_), channel_id=1, source_target_pairs={{0,24},{8,0},{16,8},{24,16},{1,25},{9,1},{17,9},{25,17},{2,26},{10... | collective-permute-start | bytes 1216520 | tf_op jit(solution)/shard_map/ppermute | solution.py:36
  147.1 43.5 %collective-permute-start.5 = (bf16[8448,128]{1,0:T(8,128)(2,1)S(1)}, bf16[8448,128]{1,0:T(8,128)(2,1)}, u32[]{:S(2)}, u32[]{:S(2)}) collective-permute-start(bf16[8448,128]{1,0:T(8,128)(2,1)S(1)} %constant_dynamic-update-slice_fusion.refs_0_), channel_id=1, source_target_pairs={{0,1},{1,0},{2,3},{3,2},{4,5},{5,4},{6,7},{7,6},{8,9},{9,8},{10,11... | collective-permute-start | bytes 6488072 | tf_op jit(solution)/shard_map/ppermute | solution.py:154
  150.2 21.6 %collective-permute-start.12 = (bf16[1312,128]{1,0:T(8,128)(2,1)S(1)}, bf16[1312,128]{1,0:T(8,128)(2,1)S(1)}, u32[]{:S(2)}, u32[]{:S(2)}) collective-permute-start(bf16[1312,128]{1,0:T(8,128)(2,1)S(1)} %slice.365), channel_id=1, source_target_pairs={{0,8},{8,16},{16,24},{24,0},{1,9},{9,17},{17,25},{25,1},{2,10},{10... | collective-permute-start | bytes 1007624 | tf_op jit(solution)/shard_map/ppermute | solution.py:38
  154.1 18.9 %collective-permute-start.13 = (bf16[1328,128]{1,0:T(8,128)(2,1)S(1)}, bf16[1328,128]{1,0:T(8,128)(2,1)S(1)}, u32[]{:S(2)}, u32[]{:S(2)}) collective-permute-start(bf16[1328,128]{1,0:T(8,128)(2,1)S(1)} %slice.368), channel_id=1, source_target_pairs={{0,24},{8,0},{16,8},{24,16},{1,25},{9,1},{17,9},{25,17},{2,26},{10... | collective-permute-start | bytes 1019912 | tf_op jit(solution)/shard_map/ppermute | solution.py:39
  156.1 7.6 %copy-start.4 = (bf16[1584,128]{1,0:T(8,128)(2,1)}, bf16[1584,128]{1,0:T(8,128)(2,1)S(1)}, u32[]{:S(2)}) copy-start(bf16[1584,128]{1,0:T(8,128)(2,1)S(1)} %collective-permute-done.17.refs_8_) | copy-start | bytes 1216516
  156.1 10.5 %collective-permute-start.19 = (bf16[784,128]{1,0:T(8,128)(2,1)S(1)}, bf16[784,128]{1,0:T(8,128)(2,1)S(1)}, u32[]{:S(2)}, u32[]{:S(2)}) collective-permute-start(bf16[784,128]{1,0:T(8,128)(2,1)S(1)} %slice.381), channel_id=1, source_target_pairs={{0,8},{8,16},{16,24},{24,0},{1,9},{9,17},{17,25},{25,1},{2,10},{10... | collective-permute-start | bytes 602120 | tf_op jit(solution)/shard_map/ppermute | solution.py:38
  160.1 3.1 copy-start.2
  160.1 10.4 %collective-permute-start.20 = (bf16[800,128]{1,0:T(8,128)(2,1)S(1)}, bf16[800,128]{1,0:T(8,128)(2,1)S(1)}, u32[]{:S(2)}, u32[]{:S(2)}) collective-permute-start(bf16[800,128]{1,0:T(8,128)(2,1)S(1)} %slice.383), channel_id=1, source_target_pairs={{0,24},{8,0},{16,8},{24,16},{1,25},{9,1},{17,9},{25,17},{2,26},{10... | collective-permute-start | bytes 614408 | tf_op jit(solution)/shard_map/ppermute | solution.py:39
  167.2 0.7 copy-start.15
  171.1 0.7 copy-start.13
  172.3 0.7 copy-start.11
  173.7 0.7 copy-start.9
  208.8 1.1 copy-start.1
  209.8 1.0 copy-start.3
  210.8 1.0 copy-start.5
  211.8 1.0 copy-start.7
  212.8 0.9 copy-start.8
  213.8 1.0 copy-start.10
  214.7 1.0 copy-start.12
  215.7 0.9 copy-start.14
  216.6 0.9 copy-start.16
  241.0 11.9 %collective-permute-start.21 = (bf16[2048,128]{1,0:T(8,128)(2,1)S(1)}, bf16[2048,128]{1,0:T(8,128)(2,1)S(1)}, u32[]{:S(2)}, u32[]{:S(2)}) collective-permute-start(bf16[2048,128]{1,0:T(8,128)(2,1)S(1)} %all_gather.7), channel_id=1, source_target_pairs={{0,2},{2,4},{4,6},{6,0},{1,3},{3,5},{5,7},{7,1},{8,10},{10,12},{12... | collective-permute-start | bytes 1572872 | tf_op jit(solution)/shard_map/ppermute | solution.py:35
  245.2 12.1 %collective-permute-start.22 = (bf16[2048,128]{1,0:T(8,128)(2,1)S(1)}, bf16[2048,128]{1,0:T(8,128)(2,1)S(1)}, u32[]{:S(2)}, u32[]{:S(2)}) collective-permute-start(bf16[2048,128]{1,0:T(8,128)(2,1)S(1)} %all_gather.7), channel_id=1, source_target_pairs={{0,6},{2,0},{4,2},{6,4},{1,7},{3,1},{5,3},{7,5},{8,14},{10,8},{12,... | collective-permute-start | bytes 1572872 | tf_op jit(solution)/shard_map/ppermute | solution.py:36
  252.9 8.3 %collective-permute-start.23 = (bf16[1024,128]{1,0:T(8,128)(2,1)S(1)}, bf16[1024,128]{1,0:T(8,128)(2,1)S(1)}, u32[]{:S(2)}, u32[]{:S(2)}) collective-permute-start(bf16[1024,128]{1,0:T(8,128)(2,1)S(1)} %slice.387), channel_id=1, source_target_pairs={{0,2},{2,4},{4,6},{6,0},{1,3},{3,5},{5,7},{7,1},{8,10},{10,12},{12... | collective-permute-start | bytes 786440 | tf_op jit(solution)/shard_map/ppermute | solution.py:38
  257.3 8.3 %collective-permute-start.24 = (bf16[1024,128]{1,0:T(8,128)(2,1)S(1)}, bf16[1024,128]{1,0:T(8,128)(2,1)S(1)}, u32[]{:S(2)}, u32[]{:S(2)}) collective-permute-start(bf16[1024,128]{1,0:T(8,128)(2,1)S(1)} %slice.388), channel_id=1, source_target_pairs={{0,6},{2,0},{4,2},{6,4},{1,7},{3,1},{5,3},{7,5},{8,14},{10,8},{12,... | collective-permute-start | bytes 786440 | tf_op jit(solution)/shard_map/ppermute | solution.py:39
  265.6 96.0 %collective-permute-start.25 = (bf16[8192,128]{1,0:T(8,128)(2,1)S(1)}, bf16[8192,128]{1,0:T(8,128)(2,1)S(1)}, u32[]{:S(2)}, u32[]{:S(2)}) collective-permute-start(bf16[8192,128]{1,0:T(8,128)(2,1)S(1)} %constant_dynamic-update-slice_fusion.13.refs_0_), channel_id=1, source_target_pairs={{0,1},{1,0},{2,3},{3,2},{4,5},{5,4},{6,7},{7,6},{8,9},{9,8},{10,11... | collective-permute-start | bytes 6291464 | tf_op jit(solution)/shard_map/ppermute | solution.py:154
  267.6 14.6 %collective-permute-start.26 = (bf16[512,128]{1,0:T(8,128)(2,1)S(1)}, bf16[512,128]{1,0:T(8,128)(2,1)S(1)}, u32[]{:S(2)}, u32[]{:S(2)}) collective-permute-start(bf16[512,128]{1,0:T(8,128)(2,1)S(1)} %shard_map.37.own), channel_id=1, source_target_pairs={{0,128},{128,256},{256,384},{384,512},{512,640},{640,768},{768,896... | collective-permute-start | bytes 393224 | tf_op jit(solution)/shard_map/ppermute | solution.py:148
  272.8 18.4 %collective-permute-start.27 = (bf16[512,128]{1,0:T(8,128)(2,1)S(1)}, bf16[512,128]{1,0:T(8,128)(2,1)S(1)}, u32[]{:S(2)}, u32[]{:S(2)}) collective-permute-start(bf16[512,128]{1,0:T(8,128)(2,1)S(1)} %shard_map.37.own), channel_id=1, source_target_pairs={{0,896},{128,0},{256,128},{384,256},{512,384},{640,512},{768,640},... | collective-permute-start | bytes 393224 | tf_op jit(solution)/shard_map/ppermute | solution.py:149
  282.2 12.5 %collective-permute-start.28 = (bf16[512,128]{1,0:T(8,128)(2,1)S(1)}, bf16[512,128]{1,0:T(8,128)(2,1)S(1)}, u32[]{:S(2)}, u32[]{:S(2)}) collective-permute-start(bf16[512,128]{1,0:T(8,128)(2,1)S(1)} %collective-permute-done.26), channel_id=1, source_target_pairs={{0,128},{128,256},{256,384},{384,512},{512,640},{640,768},{768,896... | collective-permute-start | bytes 393224 | tf_op jit(solution)/shard_map/ppermute | solution.py:148
  291.2 12.3 %collective-permute-start.29 = (bf16[512,128]{1,0:T(8,128)(2,1)S(1)}, bf16[512,128]{1,0:T(8,128)(2,1)S(1)}, u32[]{:S(2)}, u32[]{:S(2)}) collective-permute-start(bf16[512,128]{1,0:T(8,128)(2,1)S(1)} %collective-permute-done.27), channel_id=1, source_target_pairs={{0,896},{128,0},{256,128},{384,256},{512,384},{640,512},{768,640},... | collective-permute-start | bytes 393224 | tf_op jit(solution)/shard_map/ppermute | solution.py:149
  294.7 25.5 %collective-permute-start.34 = (bf16[512,128]{1,0:T(8,128)(2,1)S(1)}, bf16[512,128]{1,0:T(8,128)(2,1)S(1)}, u32[]{:S(2)}, u32[]{:S(2)}) collective-permute-start(bf16[512,128]{1,0:T(8,128)(2,1)S(1)} %collective-permute-done.28), channel_id=1, source_target_pairs={{0,128},{128,256},{256,384},{384,512},{512,640},{640,768},{768,896... | collective-permute-start | bytes 393224 | tf_op jit(solution)/shard_map/ppermute | solution.py:148
  303.5 36.4 %collective-permute-start.30 = (bf16[2560,128]{1,0:T(8,128)(2,1)S(1)}, bf16[2560,128]{1,0:T(8,128)(2,1)S(1)}, u32[]{:S(2)}, u32[]{:S(2)}) collective-permute-start(bf16[2560,128]{1,0:T(8,128)(2,1)S(1)} %constant_dynamic-update-slice_fusion.18.refs_2_), channel_id=1, source_target_pairs={{0,8},{8,16},{16,24},{24,0},{1,9},{9,17},{17,25},{25,1},{2,10},{10... | collective-permute-start | bytes 1966088 | tf_op jit(solution)/shard_map/ppermute | solution.py:35
  310.7 32.9 %collective-permute-start.31 = (bf16[2560,128]{1,0:T(8,128)(2,1)S(1)}, bf16[2560,128]{1,0:T(8,128)(2,1)S(1)}, u32[]{:S(2)}, u32[]{:S(2)}) collective-permute-start(bf16[2560,128]{1,0:T(8,128)(2,1)S(1)} %constant_dynamic-update-slice_fusion.18.refs_2_), channel_id=1, source_target_pairs={{0,24},{8,0},{16,8},{24,16},{1,25},{9,1},{17,9},{25,17},{2,26},{10... | collective-permute-start | bytes 1966088 | tf_op jit(solution)/shard_map/ppermute | solution.py:36
  312.7 13.1 %collective-permute-start.35 = (bf16[512,128]{1,0:T(8,128)(2,1)S(1)}, bf16[512,128]{1,0:T(8,128)(2,1)S(1)}, u32[]{:S(2)}, u32[]{:S(2)}) collective-permute-start(bf16[512,128]{1,0:T(8,128)(2,1)S(1)} %collective-permute-done.29), channel_id=1, source_target_pairs={{0,896},{128,0},{256,128},{384,256},{512,384},{640,512},{768,640},... | collective-permute-start | bytes 393224 | tf_op jit(solution)/shard_map/ppermute | solution.py:149
  320.3 13.8 %collective-permute-start.36 = (bf16[512,128]{1,0:T(8,128)(2,1)S(1)}, bf16[512,128]{1,0:T(8,128)(2,1)S(1)}, u32[]{:S(2)}, u32[]{:S(2)}) collective-permute-start(bf16[512,128]{1,0:T(8,128)(2,1)S(1)} %collective-permute-done.34), channel_id=1, source_target_pairs={{0,128},{128,256},{256,384},{384,512},{512,640},{640,768},{768,896... | collective-permute-start | bytes 393224 | tf_op jit(solution)/shard_map/ppermute | solution.py:150
  334.0 13.9 %collective-permute-start.37 = (bf16[1536,128]{1,0:T(8,128)(2,1)S(1)}, bf16[1536,128]{1,0:T(8,128)(2,1)S(1)}, u32[]{:S(2)}, u32[]{:S(2)}) collective-permute-start(bf16[1536,128]{1,0:T(8,128)(2,1)S(1)} %constant_dynamic-update-slice_fusion.23.refs_7_), channel_id=1, source_target_pairs={{0,8},{8,16},{16,24},{24,0},{1,9},{9,17},{17,25},{25,1},{2,10},{10... | collective-permute-start | bytes 1179656 | tf_op jit(solution)/shard_map/ppermute | solution.py:35
  337.8 13.9 %collective-permute-start.38 = (bf16[1536,128]{1,0:T(8,128)(2,1)S(1)}, bf16[1536,128]{1,0:T(8,128)(2,1)S(1)}, u32[]{:S(2)}, u32[]{:S(2)}) collective-permute-start(bf16[1536,128]{1,0:T(8,128)(2,1)S(1)} %constant_dynamic-update-slice_fusion.23.refs_7_), channel_id=1, source_target_pairs={{0,24},{8,0},{16,8},{24,16},{1,25},{9,1},{17,9},{25,17},{2,26},{10... | collective-permute-start | bytes 1179656 | tf_op jit(solution)/shard_map/ppermute | solution.py:36
  339.9 21.7 %collective-permute-start.32 = (bf16[1280,128]{1,0:T(8,128)(2,1)S(1)}, bf16[1280,128]{1,0:T(8,128)(2,1)S(1)}, u32[]{:S(2)}, u32[]{:S(2)}) collective-permute-start(bf16[1280,128]{1,0:T(8,128)(2,1)S(1)} %slice.389), channel_id=1, source_target_pairs={{0,8},{8,16},{16,24},{24,0},{1,9},{9,17},{17,25},{25,1},{2,10},{10... | collective-permute-start | bytes 983048 | tf_op jit(solution)/shard_map/ppermute | solution.py:38
  343.7 17.9 %collective-permute-start.33 = (bf16[1280,128]{1,0:T(8,128)(2,1)S(1)}, bf16[1280,128]{1,0:T(8,128)(2,1)S(1)}, u32[]{:S(2)}, u32[]{:S(2)}) collective-permute-start(bf16[1280,128]{1,0:T(8,128)(2,1)S(1)} %slice.390), channel_id=1, source_target_pairs={{0,24},{8,0},{16,8},{24,16},{1,25},{9,1},{17,9},{25,17},{2,26},{10... | collective-permute-start | bytes 983048 | tf_op jit(solution)/shard_map/ppermute | solution.py:39
  347.9 10.3 %collective-permute-start.39 = (bf16[768,128]{1,0:T(8,128)(2,1)S(1)}, bf16[768,128]{1,0:T(8,128)(2,1)S(1)}, u32[]{:S(2)}, u32[]{:S(2)}) collective-permute-start(bf16[768,128]{1,0:T(8,128)(2,1)S(1)} %slice.391), channel_id=1, source_target_pairs={{0,8},{8,16},{16,24},{24,0},{1,9},{9,17},{17,25},{25,1},{2,10},{10... | collective-permute-start | bytes 589832 | tf_op jit(solution)/shard_map/ppermute | solution.py:38
  351.7 9.9 %collective-permute-start.40 = (bf16[768,128]{1,0:T(8,128)(2,1)S(1)}, bf16[768,128]{1,0:T(8,128)(2,1)S(1)}, u32[]{:S(2)}, u32[]{:S(2)}) collective-permute-start(bf16[768,128]{1,0:T(8,128)(2,1)S(1)} %slice.392), channel_id=1, source_target_pairs={{0,24},{8,0},{16,8},{24,16},{1,25},{9,1},{17,9},{25,17},{2,26},{10... | collective-permute-start | bytes 589832 | tf_op jit(solution)/shard_map/ppermute | solution.py:39
  370.0 13.3 %collective-permute-start.41 = (bf16[512,128]{1,0:T(8,128)(2,1)S(1)}, bf16[512,128]{1,0:T(8,128)(2,1)S(1)}, u32[]{:S(2)}, u32[]{:S(2)}) collective-permute-start(bf16[512,128]{1,0:T(8,128)(2,1)S(1)} %shard_map.38), channel_id=1, source_target_pairs={{0,0},{1,1},{2,2},{3,3},{4,4},{5,5},{6,6},{7,7},{8,32},{9,33},{10,... | collective-permute-start | bytes 393224 | tf_op jit(solution)/shard_map/ppermute | solution.py:175

commit v2 on v0

v2 whole, which is shorter than its diff:
```python
import functools

import jax
import jax.numpy as jnp
import numpy as np
from jax import lax
from jax.experimental import pallas as pl
from jax.experimental.pallas import tpu as pltpu
from jax.sharding import Mesh, PartitionSpec as P

STEPS = 2
BS = 128
ROWS = 4 * BS
TAIL = 16
AXES = ("zh", "zl", "x", "y", "core")
SIZES = (8, 4, 4, 4, 2)
BATCHES = ((0, 1, 7, 2, 6), (3, 5), (4,))


def shift(size, by):
    return [(i, (i + by) % size) for i in range(size)]


def swap_pairs(by=0):
    pairs = []
    for i in range(1024):
        zh, zl, x, y, core = np.unravel_index(i, SIZES)
        pairs.append((i, int(np.ravel_multi_index(((zh + by) % 8, x, zl, y, core), SIZES))))
    return pairs


def ring4(batch, rows):
    offsets, units = batch
    part = jnp.concatenate(units) if len(units) > 1 else units[0]
    one = lax.ppermute(part, "x", shift(4, 1))
    three = lax.ppermute(part, "x", shift(4, -1))
    placed = [(part, 0, offsets), (one, 1, offsets), (three, 3, offsets)]
    if len(units) == 1:
        placed.append((lax.ppermute(part, "x", shift(4, 2)), 2, offsets))
    else:
        cut = len(units) // 2
        placed.append((lax.ppermute(one[: cut * rows], "x", shift(4, 1)), 2, offsets[:cut]))
        placed.append((lax.ppermute(three[cut * rows :], "x", shift(4, -1)), 2, offsets[cut:]))
    return placed


def kernel(rows, units, first, branch, tab, *refs):
    slots_in, refs = (None, refs) if first else (refs[0], refs[1:])
    own, a_all, refs = refs[0], refs[1], refs[2:]
    parts, refs = refs[: len(units)], refs[len(units) :]
    if first:
        out, slots_out, acc, slots, sem = refs
        for k in range(32):
            row = a_all[k * rows + ROWS : (k + 1) * rows, :].astype(jnp.float32)[0:1]
            slots_out[k : k + 1, :] = row.astype(jnp.int32)
        at = 32
        for part, n in zip(parts, units):
            for k in range(n):
                row = part[k * rows + ROWS : (k + 1) * rows, :].astype(jnp.float32)[0:1]
                slots_out[at : at + 1, :] = row.astype(jnp.int32)
                at += 1
        copy = pltpu.make_async_copy(slots_out, slots, sem)
        copy.start()
        acc[...] = jnp.zeros_like(acc)
        copy.wait()
    else:
        out, acc = refs
        slots = slots_in
        acc[...] = jnp.zeros_like(acc)
    mine = [slots[tab[32], j] for j in range(4)]

    def unit(part, start, k, carry):
        la = tab[start + k]
        for j in range(4):
            m = slots[la, j]

            @pl.when(slots[32 + start + k, m] == mine[j])
            def _():
                left = a_all[pl.ds(pl.multiple_of(la * rows + j * BS, 16), BS), :]
                right = part[pl.ds(pl.multiple_of(k * rows + m * BS, 16), BS), :]
                acc[j * BS : (j + 1) * BS, :] += jnp.dot(
                    left, right, preferred_element_type=jnp.float32
                )

        return carry

    at = 0
    for part, n in zip(parts, units):
        if n == 1:
            unit(part, at, 0, 0)
        else:
            lax.fori_loop(0, n, functools.partial(unit, part, at), 0)
        at += n
    square = acc[...]
    twice = 2.0 * own[:ROWS, :].astype(jnp.float32) - square
    out[...] = jnp.where(branch[0] == 1, twice, square).astype(out.dtype)


def multiply(branch, tab, slots, own, a_all, parts):
    first, rows = slots is None, own.shape[0]
    units = [part.shape[0] // rows for part in parts]
    smem = pl.BlockSpec(memory_space=pltpu.SMEM)
    vmem = pl.BlockSpec(memory_space=pltpu.VMEM)
    out_shape = [jax.ShapeDtypeStruct((ROWS, BS), jnp.bfloat16)]
    scratch = [pltpu.VMEM((ROWS, BS), jnp.float32)]
    if first:
        out_shape.append(jax.ShapeDtypeStruct((64, BS), jnp.int32))
        scratch += [pltpu.SMEM((64, BS), jnp.int32), pltpu.SemaphoreType.DMA]
    done = pl.pallas_call(
        functools.partial(kernel, rows, units, first),
        out_shape=out_shape,
        in_specs=[smem] * (2 if first else 3) + [vmem] * (2 + len(parts)),
        out_specs=[vmem] * len(out_shape),
        scratch_shapes=scratch,
        compiler_params=pltpu.CompilerParams(vmem_limit_bytes=24 * 1024 * 1024),
        cost_estimate=pl.CostEstimate(
            flops=2 * 128 * BS**3, bytes_accessed=64 * ROWS * BS * 2, transcendentals=0
        ),
    )(branch, tab, *([] if first else [slots]), own, a_all, *parts)
    return done[0], done[1] if first else slots


def gather(unit, up, down):
    near = lax.all_gather(unit, "zl", axis=0, tiled=True)
    a_all = lax.all_gather(near, ("y", "core"), axis=0, tiled=True)
    at = {0: unit, 1: up, 7: down}
    for hop in (2, 3):
        at[hop] = lax.ppermute(at[hop - 1], "zh", shift(8, 1))
        at[8 - hop] = lax.ppermute(at[9 - hop], "zh", shift(8, -1))
    at[4] = lax.ppermute(at[3], "zh", shift(8, 1))
    placed = []
    for offsets in BATCHES:
        placed += ring4((offsets, [at[k] for k in offsets]), unit.shape[0])
    return a_all, placed


def table(placed):
    zh, zl, x, y, core = (lax.axis_index(name) for name in AXES)
    dz = np.concatenate([np.array(offsets) for _, _, offsets in placed])
    dx = np.concatenate([np.full(len(offsets), d) for _, d, offsets in placed])
    p = (zh - dz) % 8 * 4 + (x - dx) % 4
    la = p % 8 * 4 + p // 8
    return jnp.concatenate([la, jnp.reshape((y * 2 + core) * 4 + zl, (1,))]).astype(jnp.int32)


def body(values, column_slot_index, branches):
    flat = values.reshape(ROWS, BS)
    tail = column_slot_index[:, 0].astype(jnp.bfloat16)[None]
    start = jnp.concatenate([flat, jnp.pad(tail, ((0, TAIL - 1), (0, BS - 4)))])
    unit, up, down = (lax.ppermute(start, AXES, swap_pairs(by)) for by in (0, 1, -1))
    slots = None
    for step in range(STEPS):
        if step:
            up, down = (lax.ppermute(unit, "zh", shift(8, by)) for by in (1, -1))
        a_all, placed = gather(unit, up, down)
        unit, slots = multiply(
            branches[step : step + 1], table(placed), slots, unit, a_all, [q for q, _, _ in placed]
        )
    return lax.ppermute(unit, AXES, swap_pairs()).reshape(values.shape)


def solution(mesh):
    fine = Mesh(mesh.devices.reshape(SIZES), AXES)
    split = (("zh", "zl"), ("x", "y", "core"))
    in_specs = (P(*split, None, None), P(*split), P())
    return jax.shard_map(
        body, mesh=fine, in_specs=in_specs, out_specs=P(*split, None, None), check_vma=False
    )
```

time: 506 us -> 341 us (0.67)
  the two profiles are of different devices: /device:TPU:4 before, /device:TPU:64 now
where the time goes in v2:
time: 341 us; the launch traced here: 340 us
  starting transfers between devices  167 us (49%)
  waiting for transfers between devices  87.7 us (26%)
  blocking collectives  33.1 us (10%)
  local copies, waits for them, and re-layouts  21.6 us (6%)
  Pallas kernels  14.3 us (4%)
  between operations  14 us (4%)
    all_gather x2, blocking collectives, gather(): near = lax.all_gather(unit, 'zl', axis=0, tiled=True)  33.1 us
    ppermute x3, starting transfers between devices, body(): lax.ppermute(start, AXES, swap_pairs(by))  29.1 us
    ppermute x6, starting transfers between devices, ring4(): three = lax.ppermute(part, 'x', shift(4, -1))  29 us
    ppermute x4, starting transfers between devices, gather(): at[hop] = lax.ppermute(at[hop - 1], 'zh', shift(8, 1))  27.7 us
    ppermute x4, waiting for transfers between devices, gather(): at[8 - hop] = lax.ppermute(at[9 - hop], 'zh', shift(8, -1))  27.4 us
    ppermute x3, waiting for transfers between devices, body(): lax.ppermute(start, AXES, swap_pairs(by))  20 us
    unnamed x57, local copies, waits for them, and re-layouts  19.3 us
    ppermute x4, starting transfers between devices, ring4(): lax.ppermute(three[cut * rows:], 'x', shift(4, -1))  16.8 us
  transfers between devices with their start and end apart: 40, of which 17 were waited for; matrix products, arithmetic and copies ran while one was open for 1% of the time, Pallas kernels for 0%

profile of v2, /device:TPU:64, one launch (start us, length us, event | category | flops | bytes accessed | tf_op | source)
XLA Modules:
  0.0 339.7 jit_solution(17305194435608462220)
XLA Ops:
  7.2 0.9 fusion.1
  8.2 4.0 %collective-permute-start = (bf16[528,128]{1,0:T(8,128)(2,1)S(1)}, bf16[528,128]{1,0:T(8,128)(2,1)S(1)}, u32[]{:S(2)}, u32[]{:S(2)}) collective-permute-start(bf16[528,128]{1,0:T(8,128)(2,1)S(1)} %fusion.1), channel_id=1, source_target_pairs={{0,0},{1,1},{2,2},{3,3},{4,4},{5,5},{6,6},{7,7},{8,32},{9,33},{10,... | collective-permute-start | bytes 405512 | tf_op jit(solution)/shard_map/ppermute | solution.py:150
  12.2 9.0 %collective-permute-done.refs_0_ = bf16[528,128]{1,0:T(8,128)(2,1)S(1)} collective-permute-done((bf16[528,128]{1,0:T(8,128)(2,1)S(1)}, bf16[528,128]{1,0:T(8,128)(2,1)S(1)}, u32[]{:S(2)}, u32[]{:S(2)}) %collective-permute-start) | collective-permute-done | bytes 135200 | tf_op jit(solution)/shard_map/ppermute | solution.py:150
  21.2 15.0 %all_gather.12 = bf16[2112,128]{1,0:T(8,128)(2,1)} all-gather(bf16[528,128]{1,0:T(8,128)(2,1)S(1)} %collective-permute-done.refs_0_), channel_id=1, replica_groups=mesh['zh'=8,'zl'=4,'x'=4,'y'=4,'core'=2] {'zl'}, dimensions={0}, use_global_device_ids=true | all-gather | bytes 675840 | tf_op jit(solution)/shard_map/all_gather | solution.py:124
  36.3 11.8 %collective-permute-start.1 = (bf16[528,128]{1,0:T(8,128)(2,1)S(1)}, bf16[528,128]{1,0:T(8,128)(2,1)S(1)}, u32[]{:S(2)}, u32[]{:S(2)}) collective-permute-start(bf16[528,128]{1,0:T(8,128)(2,1)S(1)} %fusion.1), channel_id=1, source_target_pairs={{0,128},{1,129},{2,130},{3,131},{4,132},{5,133},{6,134},{7,135},{8... | collective-permute-start | bytes 405512 | tf_op jit(solution)/shard_map/ppermute | solution.py:150
  48.1 13.3 %collective-permute-start.2 = (bf16[528,128]{1,0:T(8,128)(2,1)S(1)}, bf16[528,128]{1,0:T(8,128)(2,1)S(1)}, u32[]{:S(2)}, u32[]{:S(2)}) collective-permute-start(bf16[528,128]{1,0:T(8,128)(2,1)S(1)} %fusion.1), channel_id=1, source_target_pairs={{0,896},{1,897},{2,898},{3,899},{4,900},{5,901},{6,902},{7,903},{8... | collective-permute-start | bytes 405512 | tf_op jit(solution)/shard_map/ppermute | solution.py:150
  61.4 7.7 %collective-permute-done.1 = bf16[528,128]{1,0:T(8,128)(2,1)S(1)} collective-permute-done((bf16[528,128]{1,0:T(8,128)(2,1)S(1)}, bf16[528,128]{1,0:T(8,128)(2,1)S(1)}, u32[]{:S(2)}, u32[]{:S(2)}) %collective-permute-start.1) | collective-permute-done | bytes 135200 | tf_op jit(solution)/shard_map/ppermute | solution.py:150
  69.1 1.9 collective-permute-start.3
  71.1 3.3 collective-permute-done.2
  74.3 4.6 %collective-permute-start.4 = (bf16[528,128]{1,0:T(8,128)(2,1)S(1)}, bf16[528,128]{1,0:T(8,128)(2,1)S(1)}, u32[]{:S(2)}, u32[]{:S(2)}) collective-permute-start(bf16[528,128]{1,0:T(8,128)(2,1)S(1)} %collective-permute-done.2), channel_id=1, source_target_pairs={{0,896},{128,0},{256,128},{384,256},{512,384},{640,512},{768,640},... | collective-permute-start | bytes 405512 | tf_op jit(solution)/shard_map/ppermute | solution.py:129
  78.9 3.9 %collective-permute-done.3 = bf16[528,128]{1,0:T(8,128)(2,1)S(1)} collective-permute-done((bf16[528,128]{1,0:T(8,128)(2,1)S(1)}, bf16[528,128]{1,0:T(8,128)(2,1)S(1)}, u32[]{:S(2)}, u32[]{:S(2)}) %collective-permute-start.3) | collective-permute-done | bytes 135200 | tf_op jit(solution)/shard_map/ppermute | solution.py:128
  82.8 4.1 %collective-permute-done.4 = bf16[528,128]{1,0:T(8,128)(2,1)S(1)} collective-permute-done((bf16[528,128]{1,0:T(8,128)(2,1)S(1)}, bf16[528,128]{1,0:T(8,128)(2,1)S(1)}, u32[]{:S(2)}, u32[]{:S(2)}) %collective-permute-start.4) | collective-permute-done | bytes 135200 | tf_op jit(solution)/shard_map/ppermute | solution.py:129
  86.9 5.4 %collective-permute-start.5 = (bf16[2640,128]{1,0:T(8,128)(2,1)S(1)}, bf16[2640,128]{1,0:T(8,128)(2,1)S(1)}, u32[]{:S(2)}, u32[]{:S(2)}) collective-permute-start(bf16[2640,128]{1,0:T(8,128)(2,1)S(1)} %constant_dynamic-update-slice_fusion.refs_2_), channel_id=1, source_target_pairs={{0,8},{8,16},{16,24},{24,0},{1,9},{9,17},{17,25},{25,1},{2,10},{10... | collective-permute-start | bytes 2027528 | tf_op jit(solution)/shard_map/ppermute | solution.py:35
  92.3 3.9 %collective-permute-start.6 = (bf16[2640,128]{1,0:T(8,128)(2,1)S(1)}, bf16[2640,128]{1,0:T(8,128)(2,1)S(1)}, u32[]{:S(2)}, u32[]{:S(2)}) collective-permute-start(bf16[2640,128]{1,0:T(8,128)(2,1)S(1)} %constant_dynamic-update-slice_fusion.refs_2_), channel_id=1, source_target_pairs={{0,24},{8,0},{16,8},{24,16},{1,25},{9,1},{17,9},{25,17},{2,26},{10... | collective-permute-start | bytes 2027528 | tf_op jit(solution)/shard_map/ppermute | solution.py:36
  96.2 11.2 %collective-permute-start.9 = (bf16[528,128]{1,0:T(8,128)(2,1)S(1)}, bf16[528,128]{1,0:T(8,128)(2,1)S(1)}, u32[]{:S(2)}, u32[]{:S(2)}) collective-permute-start(bf16[528,128]{1,0:T(8,128)(2,1)S(1)} %collective-permute-done.3), channel_id=1, source_target_pairs={{0,128},{128,256},{256,384},{384,512},{512,640},{640,768},{768,896... | collective-permute-start | bytes 405512 | tf_op jit(solution)/shard_map/ppermute | solution.py:128
  107.4 1.9 collective-permute-start.10
  109.3 3.5 %collective-permute-done.9 = bf16[528,128]{1,0:T(8,128)(2,1)S(1)} collective-permute-done((bf16[528,128]{1,0:T(8,128)(2,1)S(1)}, bf16[528,128]{1,0:T(8,128)(2,1)S(1)}, u32[]{:S(2)}, u32[]{:S(2)}) %collective-permute-start.9) | collective-permute-done | bytes 135200 | tf_op jit(solution)/shard_map/ppermute | solution.py:128
  112.8 9.9 %collective-permute-done.10 = bf16[528,128]{1,0:T(8,128)(2,1)S(1)} collective-permute-done((bf16[528,128]{1,0:T(8,128)(2,1)S(1)}, bf16[528,128]{1,0:T(8,128)(2,1)S(1)}, u32[]{:S(2)}, u32[]{:S(2)}) %collective-permute-start.10) | collective-permute-done | bytes 135200 | tf_op jit(solution)/shard_map/ppermute | solution.py:129
  122.7 1.9 collective-permute-start.11
  124.6 4.9 %collective-permute-start.15 = (bf16[528,128]{1,0:T(8,128)(2,1)S(1)}, bf16[528,128]{1,0:T(8,128)(2,1)}, u32[]{:S(2)}, u32[]{:S(2)}) collective-permute-start(bf16[528,128]{1,0:T(8,128)(2,1)S(1)} %collective-permute-done.9), channel_id=1, source_target_pairs={{0,128},{128,256},{256,384},{384,512},{512,640},{640,768},{768,896... | collective-permute-start | bytes 405512 | tf_op jit(solution)/shard_map/ppermute | solution.py:130
  129.6 5.1 %collective-permute-start.12 = (bf16[1056,128]{1,0:T(8,128)(2,1)S(1)}, bf16[1056,128]{1,0:T(8,128)(2,1)S(1)}, u32[]{:S(2)}, u32[]{:S(2)}) collective-permute-start(bf16[1056,128]{1,0:T(8,128)(2,1)S(1)} %constant_dynamic-update-slice_fusion.5.refs_7_), channel_id=1, source_target_pairs={{0,24},{8,0},{16,8},{24,16},{1,25},{9,1},{17,9},{25,17},{2,26},{10... | collective-permute-start | bytes 811016 | tf_op jit(solution)/shard_map/ppermute | solution.py:36
  134.7 2.5 collective-permute-done.15.refs_12_
  137.2 1.9 collective-permute-start.16
  139.2 5.1 %collective-permute-start.17 = (bf16[528,128]{1,0:T(8,128)(2,1)}, bf16[528,128]{1,0:T(8,128)(2,1)}, u32[]{:S(2)}, u32[]{:S(2)}) collective-permute-start(bf16[528,128]{1,0:T(8,128)(2,1)} %collective-permute-done.15.refs_12_), channel_id=1, source_target_pairs={{0,24},{8,0},{16,8},{24,16},{1,25},{9,1},{17,9},{25,17},{2,26},{10... | collective-permute-start | bytes 405512 | tf_op jit(solution)/shard_map/ppermute | solution.py:36
  145.0 1.9 collective-permute-start.7
  147.7 5.1 %collective-permute-start.8 = (bf16[1584,128]{1,0:T(8,128)(2,1)}, bf16[1584,128]{1,0:T(8,128)(2,1)S(1)}, u32[]{:S(2)}, u32[]{:S(2)}) collective-permute-start(bf16[1584,128]{1,0:T(8,128)(2,1)} %slice.41), channel_id=1, source_target_pairs={{0,24},{8,0},{16,8},{24,16},{1,25},{9,1},{17,9},{25,17},{2,26},{10... | collective-permute-start | bytes 1216520 | tf_op jit(solution)/shard_map/ppermute | solution.py:43
  152.9 2.4 collective-permute-start.18
  155.4 2.3 collective-permute-start.13
  157.7 4.8 %collective-permute-start.14 = (bf16[528,128]{1,0:T(8,128)(2,1)S(1)}, bf16[528,128]{1,0:T(8,128)(2,1)S(1)}, u32[]{:S(2)}, u32[]{:S(2)}) collective-permute-start(bf16[528,128]{1,0:T(8,128)(2,1)S(1)} %slice.43), channel_id=1, source_target_pairs={{0,24},{8,0},{16,8},{24,16},{1,25},{9,1},{17,9},{25,17},{2,26},{10... | collective-permute-start | bytes 405512 | tf_op jit(solution)/shard_map/ppermute | solution.py:43
  165.9 2.2 copy-done
  168.1 0.9 copy-done.5
  169.0 0.9 copy-done.7
  170.8 7.7 %shard_map.73 = (bf16[512,128]{1,0:T(8,128)(2,1)S(1)}, s32[64,128]{1,0:T(8,128)S(1)}) custom-call(s32[1]{0:T(128)} %get-tuple-element.9.branch, s32[33]{0:T(128)S(1)} %pad_add_fusion.tab, bf16[528,128]{1,0:T(8,128)(2,1)S(1)} %collective-permute-done.refs_0_, bf16[16896,128]{1,0:T(8,128)(2,1)S(1)} %copy-done, ...), custom_call_target="tpu_custom_call" | custom-call | flops 536870912 | bytes 8388608 | tf_op jit(solution)/shard_map/pallas_call | solution.py:109
  178.6 18.2 %all_gather.14 = bf16[2048,128]{1,0:T(8,128)(2,1)} all-gather(bf16[512,128]{1,0:T(8,128)(2,1)S(1)} %get-tuple-element.8.refs_1_), channel_id=1, replica_groups=mesh['zh'=8,'zl'=4,'x'=4,'y'=4,'core'=2] {'zl'}, dimensions={0}, use_global_device_ids=true | all-gather | bytes 655360 | tf_op jit(solution)/shard_map/all_gather | solution.py:124
  196.8 6.2 %collective-permute-start.19 = (bf16[512,128]{1,0:T(8,128)(2,1)S(1)}, bf16[512,128]{1,0:T(8,128)(2,1)S(1)}, u32[]{:S(2)}, u32[]{:S(2)}) collective-permute-start(bf16[512,128]{1,0:T(8,128)(2,1)S(1)} %get-tuple-element.8.refs_1_), channel_id=1, source_target_pairs={{0,128},{128,256},{256,384},{384,512},{512,640},{640,768},{768,896... | collective-permute-start | bytes 393224 | tf_op jit(solution)/shard_map/ppermute | solution.py:154
  202.9 3.6 %collective-permute-start.20 = (bf16[512,128]{1,0:T(8,128)(2,1)S(1)}, bf16[512,128]{1,0:T(8,128)(2,1)S(1)}, u32[]{:S(2)}, u32[]{:S(2)}) collective-permute-start(bf16[512,128]{1,0:T(8,128)(2,1)S(1)} %get-tuple-element.8.refs_1_), channel_id=1, source_target_pairs={{0,896},{128,0},{256,128},{384,256},{512,384},{640,512},{768,640},... | collective-permute-start | bytes 393224 | tf_op jit(solution)/shard_map/ppermute | solution.py:154
  206.6 3.2 collective-permute-done.19
  209.8 6.2 %collective-permute-start.21 = (bf16[512,128]{1,0:T(8,128)(2,1)S(1)}, bf16[512,128]{1,0:T(8,128)(2,1)S(1)}, u32[]{:S(2)}, u32[]{:S(2)}) collective-permute-start(bf16[512,128]{1,0:T(8,128)(2,1)S(1)} %collective-permute-done.19), channel_id=1, source_target_pairs={{0,128},{128,256},{256,384},{384,512},{512,640},{640,768},{768,896... | collective-permute-start | bytes 393224 | tf_op jit(solution)/shard_map/ppermute | solution.py:128
  216.0 3.5 %collective-permute-done.20 = bf16[512,128]{1,0:T(8,128)(2,1)S(1)} collective-permute-done((bf16[512,128]{1,0:T(8,128)(2,1)S(1)}, bf16[512,128]{1,0:T(8,128)(2,1)S(1)}, u32[]{:S(2)}, u32[]{:S(2)}) %collective-permute-start.20) | collective-permute-done | bytes 131104 | tf_op jit(solution)/shard_map/ppermute | solution.py:154
  219.5 3.9 %collective-permute-start.22 = (bf16[512,128]{1,0:T(8,128)(2,1)S(1)}, bf16[512,128]{1,0:T(8,128)(2,1)S(1)}, u32[]{:S(2)}, u32[]{:S(2)}) collective-permute-start(bf16[512,128]{1,0:T(8,128)(2,1)S(1)} %collective-permute-done.20), channel_id=1, source_target_pairs={{0,896},{128,0},{256,128},{384,256},{512,384},{640,512},{768,640},... | collective-permute-start | bytes 393224 | tf_op jit(solution)/shard_map/ppermute | solution.py:129
  223.6 6.9 %collective-permute-done.22 = bf16[512,128]{1,0:T(8,128)(2,1)S(1)} collective-permute-done((bf16[512,128]{1,0:T(8,128)(2,1)S(1)}, bf16[512,128]{1,0:T(8,128)(2,1)S(1)}, u32[]{:S(2)}, u32[]{:S(2)}) %collective-permute-start.22) | collective-permute-done | bytes 131104 | tf_op jit(solution)/shard_map/ppermute | solution.py:129
  230.5 4.6 %collective-permute-start.24 = (bf16[2560,128]{1,0:T(8,128)(2,1)S(1)}, bf16[2560,128]{1,0:T(8,128)(2,1)S(1)}, u32[]{:S(2)}, u32[]{:S(2)}) collective-permute-start(bf16[2560,128]{1,0:T(8,128)(2,1)S(1)} %constant_dynamic-update-slice_fusion.7.refs_3_), channel_id=1, source_target_pairs={{0,24},{8,0},{16,8},{24,16},{1,25},{9,1},{17,9},{25,17},{2,26},{10... | collective-permute-start | bytes 1966088 | tf_op jit(solution)/shard_map/ppermute | solution.py:36
  235.0 1.9 collective-permute-start.23
  237.0 8.4 %collective-permute-start.27 = (bf16[512,128]{1,0:T(8,128)(2,1)S(1)}, bf16[512,128]{1,0:T(8,128)(2,1)S(1)}, u32[]{:S(2)}, u32[]{:S(2)}) collective-permute-start(bf16[512,128]{1,0:T(8,128)(2,1)S(1)} %collective-permute-done.21), channel_id=1, source_target_pairs={{0,128},{128,256},{256,384},{384,512},{512,640},{640,768},{768,896... | collective-permute-start | bytes 393224 | tf_op jit(solution)/shard_map/ppermute | solution.py:128
  245.4 1.9 collective-permute-start.28
  247.3 3.5 %collective-permute-done.27 = bf16[512,128]{1,0:T(8,128)(2,1)S(1)} collective-permute-done((bf16[512,128]{1,0:T(8,128)(2,1)S(1)}, bf16[512,128]{1,0:T(8,128)(2,1)S(1)}, u32[]{:S(2)}, u32[]{:S(2)}) %collective-permute-start.27) | collective-permute-done | bytes 131104 | tf_op jit(solution)/shard_map/ppermute | solution.py:128
  250.8 6.6 %collective-permute-done.28 = bf16[512,128]{1,0:T(8,128)(2,1)S(1)} collective-permute-done((bf16[512,128]{1,0:T(8,128)(2,1)S(1)}, bf16[512,128]{1,0:T(8,128)(2,1)S(1)}, u32[]{:S(2)}, u32[]{:S(2)}) %collective-permute-start.28) | collective-permute-done | bytes 131104 | tf_op jit(solution)/shard_map/ppermute | solution.py:129
  257.4 1.9 collective-permute-start.29
  259.3 5.1 %collective-permute-start.30 = (bf16[1024,128]{1,0:T(8,128)(2,1)S(1)}, bf16[1024,128]{1,0:T(8,128)(2,1)S(1)}, u32[]{:S(2)}, u32[]{:S(2)}) collective-permute-start(bf16[1024,128]{1,0:T(8,128)(2,1)S(1)} %constant_dynamic-update-slice_fusion.12.refs_8_), channel_id=1, source_target_pairs={{0,24},{8,0},{16,8},{24,16},{1,25},{9,1},{17,9},{25,17},{2,26},{10... | collective-permute-start | bytes 786440 | tf_op jit(solution)/shard_map/ppermute | solution.py:36
  264.5 4.1 %collective-permute-start.33 = (bf16[512,128]{1,0:T(8,128)(2,1)S(1)}, bf16[512,128]{1,0:T(8,128)(2,1)S(1)}, u32[]{:S(2)}, u32[]{:S(2)}) collective-permute-start(bf16[512,128]{1,0:T(8,128)(2,1)S(1)} %collective-permute-done.27), channel_id=1, source_target_pairs={{0,128},{128,256},{256,384},{384,512},{512,640},{640,768},{768,896... | collective-permute-start | bytes 393224 | tf_op jit(solution)/shard_map/ppermute | solution.py:130
  268.7 3.9 %collective-permute-start.26 = (bf16[1536,128]{1,0:T(8,128)(2,1)S(1)}, bf16[1536,128]{1,0:T(8,128)(2,1)S(1)}, u32[]{:S(2)}, u32[]{:S(2)}) collective-permute-start(bf16[1536,128]{1,0:T(8,128)(2,1)S(1)} %slice.45), channel_id=1, source_target_pairs={{0,24},{8,0},{16,8},{24,16},{1,25},{9,1},{17,9},{25,17},{2,26},{10... | collective-permute-start | bytes 1179656 | tf_op jit(solution)/shard_map/ppermute | solution.py:43
  272.6 8.0 %collective-permute-done.33.refs_13_ = bf16[512,128]{1,0:T(8,128)(2,1)S(1)} collective-permute-done((bf16[512,128]{1,0:T(8,128)(2,1)S(1)}, bf16[512,128]{1,0:T(8,128)(2,1)S(1)}, u32[]{:S(2)}, u32[]{:S(2)}) %collective-permute-start.33) | collective-permute-done | bytes 131104 | tf_op jit(solution)/shard_map/ppermute | solution.py:130
  280.7 1.9 collective-permute-start.34
  282.6 5.1 %collective-permute-start.35 = (bf16[512,128]{1,0:T(8,128)(2,1)S(1)}, bf16[512,128]{1,0:T(8,128)(2,1)S(1)}, u32[]{:S(2)}, u32[]{:S(2)}) collective-permute-start(bf16[512,128]{1,0:T(8,128)(2,1)S(1)} %collective-permute-done.33.refs_13_), channel_id=1, source_target_pairs={{0,24},{8,0},{16,8},{24,16},{1,25},{9,1},{17,9},{25,17},{2,26},{10... | collective-permute-start | bytes 393224 | tf_op jit(solution)/shard_map/ppermute | solution.py:36
  287.8 1.9 collective-permute-start.25
  289.7 3.8 %collective-permute-start.36 = (bf16[512,128]{1,0:T(8,128)(2,1)S(1)}, bf16[512,128]{1,0:T(8,128)(2,1)S(1)}, u32[]{:S(2)}, u32[]{:S(2)}) collective-permute-start(bf16[512,128]{1,0:T(8,128)(2,1)S(1)} %collective-permute-done.33.refs_13_), channel_id=1, source_target_pairs={{0,16},{8,24},{16,0},{24,8},{1,17},{9,25},{17,1},{25,9},{2,18},{10... | collective-permute-start | bytes 393224 | tf_op jit(solution)/shard_map/ppermute | solution.py:39
  294.2 4.1 %collective-permute-start.31 = (bf16[512,128]{1,0:T(8,128)(2,1)S(1)}, bf16[512,128]{1,0:T(8,128)(2,1)S(1)}, u32[]{:S(2)}, u32[]{:S(2)}) collective-permute-start(bf16[512,128]{1,0:T(8,128)(2,1)S(1)} %slice.46), channel_id=1, source_target_pairs={{0,8},{8,16},{16,24},{24,0},{1,9},{9,17},{17,25},{25,1},{2,10},{10... | collective-permute-start | bytes 393224 | tf_op jit(solution)/shard_map/ppermute | solution.py:42
  299.0 3.0 collective-permute-start.32
  303.3 2.6 collective-permute-done.32.refs_12_
  307.2 2.2 copy-done.1
  309.4 0.9 copy-done.3
  314.9 6.6 %shard_map.74 = bf16[512,128]{1,0:T(8,128)(2,1)S(1)} custom-call(s32[1]{0:T(128)} %get-tuple-element.10.branch, s32[33]{0:T(128)S(1)} %pad_add_fusion.tab, s32[64,128]{1,0:T(8,128)S(1)} %get-tuple-element.7.refs_0_, bf16[512,128]{1,0:T(8,128)(2,1)S(1)} %get-tuple-element.8.refs_1_, bf16[16384,128]{1,0:T(8,128)(2,1)S(1)} %copy-done.1, ...), custom_call_target="tpu_custom_call" | custom-call | flops 536870912 | bytes 8388608 | tf_op jit(solution)/shard_map/pallas_call | solution.py:109
  321.5 1.9 collective-permute-start.37
  323.4 8.8 %collective-permute-done.37 = bf16[512,128]{1,0:T(8,128)(2,1)S(1)} collective-permute-done((bf16[512,128]{1,0:T(8,128)(2,1)S(1)}, bf16[512,128]{1,0:T(8,128)(2,1)S(1)}, u32[]{:S(2)}, u32[]{:S(2)}) %collective-permute-start.37) | collective-permute-done | bytes 131104 | tf_op jit(solution)/shard_map/ppermute | solution.py:159
  (96 shorter events, 16.1 us)
Async XLA Ops:
  6.5 146.3 %copy-start.21 = (s32[32]{0:T(128)S(1)}, s32[32]{0:T(128)}, u32[]{:S(2)}) copy-start(s32[32]{0:T(128)} %constant.101) | copy-start | bytes 388
  6.5 146.3 %copy-start.22 = (s32[32]{0:T(128)S(1)}, s32[32]{0:T(128)}, u32[]{:S(2)}) copy-start(s32[32]{0:T(128)} %constant.100) | copy-start | bytes 388
  6.5 156.0 %copy-start.20 = (s32[2]{0:T(128)S(1)}, s32[2]{0:T(128)}, u32[]{:S(2)}) copy-start(s32[2]{0:T(128)} %param.9) | copy-start | bytes 28
  6.5 159.3 %all-gather.3.cloned.1.call-start = ((), (), s32[]{:S(2)}) async-start(), calls=%async_computation | async-start | bytes 4866048 | tf_op jit(solution)/shard_map/all_gather | solution.py:125
  8.2 13.1 %collective-permute-start = (bf16[528,128]{1,0:T(8,128)(2,1)S(1)}, bf16[528,128]{1,0:T(8,128)(2,1)S(1)}, u32[]{:S(2)}, u32[]{:S(2)}) collective-permute-start(bf16[528,128]{1,0:T(8,128)(2,1)S(1)} %fusion.1), channel_id=1, source_target_pairs={{0,0},{1,1},{2,2},{3,3},{4,4},{5,5},{6,6},{7,7},{8,32},{9,33},{10,... | collective-permute-start | bytes 405512 | tf_op jit(solution)/shard_map/ppermute | solution.py:150
  36.2 271.0 %all-gather.5.cloned.1.call-start = ((), (), s32[]{:S(2)}) async-start(), calls=%async_computation.1 | async-start | bytes 4718592 | tf_op jit(solution)/shard_map/all_gather | solution.py:125
  36.3 32.9 %collective-permute-start.1 = (bf16[528,128]{1,0:T(8,128)(2,1)S(1)}, bf16[528,128]{1,0:T(8,128)(2,1)S(1)}, u32[]{:S(2)}, u32[]{:S(2)}) collective-permute-start(bf16[528,128]{1,0:T(8,128)(2,1)S(1)} %fusion.1), channel_id=1, source_target_pairs={{0,128},{1,129},{2,130},{3,131},{4,132},{5,133},{6,134},{7,135},{8... | collective-permute-start | bytes 405512 | tf_op jit(solution)/shard_map/ppermute | solution.py:150
  48.1 26.2 %collective-permute-start.2 = (bf16[528,128]{1,0:T(8,128)(2,1)S(1)}, bf16[528,128]{1,0:T(8,128)(2,1)S(1)}, u32[]{:S(2)}, u32[]{:S(2)}) collective-permute-start(bf16[528,128]{1,0:T(8,128)(2,1)S(1)} %fusion.1), channel_id=1, source_target_pairs={{0,896},{1,897},{2,898},{3,899},{4,900},{5,901},{6,902},{7,903},{8... | collective-permute-start | bytes 405512 | tf_op jit(solution)/shard_map/ppermute | solution.py:150
  69.1 13.7 %collective-permute-start.3 = (bf16[528,128]{1,0:T(8,128)(2,1)S(1)}, bf16[528,128]{1,0:T(8,128)(2,1)S(1)}, u32[]{:S(2)}, u32[]{:S(2)}) collective-permute-start(bf16[528,128]{1,0:T(8,128)(2,1)S(1)} %collective-permute-done.1), channel_id=1, source_target_pairs={{0,128},{128,256},{256,384},{384,512},{512,640},{640,768},{768,896... | collective-permute-start | bytes 405512 | tf_op jit(solution)/shard_map/ppermute | solution.py:128
  74.3 12.6 %collective-permute-start.4 = (bf16[528,128]{1,0:T(8,128)(2,1)S(1)}, bf16[528,128]{1,0:T(8,128)(2,1)S(1)}, u32[]{:S(2)}, u32[]{:S(2)}) collective-permute-start(bf16[528,128]{1,0:T(8,128)(2,1)S(1)} %collective-permute-done.2), channel_id=1, source_target_pairs={{0,896},{128,0},{256,128},{384,256},{512,384},{640,512},{768,640},... | collective-permute-start | bytes 405512 | tf_op jit(solution)/shard_map/ppermute | solution.py:129
  86.9 52.2 %collective-permute-start.5 = (bf16[2640,128]{1,0:T(8,128)(2,1)S(1)}, bf16[2640,128]{1,0:T(8,128)(2,1)S(1)}, u32[]{:S(2)}, u32[]{:S(2)}) collective-permute-start(bf16[2640,128]{1,0:T(8,128)(2,1)S(1)} %constant_dynamic-update-slice_fusion.refs_2_), channel_id=1, source_target_pairs={{0,8},{8,16},{16,24},{24,0},{1,9},{9,17},{17,25},{25,1},{2,10},{10... | collective-permute-start | bytes 2027528 | tf_op jit(solution)/shard_map/ppermute | solution.py:35
  92.3 52.7 %collective-permute-start.6 = (bf16[2640,128]{1,0:T(8,128)(2,1)S(1)}, bf16[2640,128]{1,0:T(8,128)(2,1)S(1)}, u32[]{:S(2)}, u32[]{:S(2)}) collective-permute-start(bf16[2640,128]{1,0:T(8,128)(2,1)S(1)} %constant_dynamic-update-slice_fusion.refs_2_), channel_id=1, source_target_pairs={{0,24},{8,0},{16,8},{24,16},{1,25},{9,1},{17,9},{25,17},{2,26},{10... | collective-permute-start | bytes 2027528 | tf_op jit(solution)/shard_map/ppermute | solution.py:36
  96.2 16.6 %collective-permute-start.9 = (bf16[528,128]{1,0:T(8,128)(2,1)S(1)}, bf16[528,128]{1,0:T(8,128)(2,1)S(1)}, u32[]{:S(2)}, u32[]{:S(2)}) collective-permute-start(bf16[528,128]{1,0:T(8,128)(2,1)S(1)} %collective-permute-done.3), channel_id=1, source_target_pairs={{0,128},{128,256},{256,384},{384,512},{512,640},{640,768},{768,896... | collective-permute-start | bytes 405512 | tf_op jit(solution)/shard_map/ppermute | solution.py:128
  107.4 15.3 %collective-permute-start.10 = (bf16[528,128]{1,0:T(8,128)(2,1)S(1)}, bf16[528,128]{1,0:T(8,128)(2,1)S(1)}, u32[]{:S(2)}, u32[]{:S(2)}) collective-permute-start(bf16[528,128]{1,0:T(8,128)(2,1)S(1)} %collective-permute-done.4), channel_id=1, source_target_pairs={{0,896},{128,0},{256,128},{384,256},{512,384},{640,512},{768,640},... | collective-permute-start | bytes 405512 | tf_op jit(solution)/shard_map/ppermute | solution.py:129
  122.7 25.0 %collective-permute-start.11 = (bf16[1056,128]{1,0:T(8,128)(2,1)S(1)}, bf16[1056,128]{1,0:T(8,128)(2,1)S(1)}, u32[]{:S(2)}, u32[]{:S(2)}) collective-permute-start(bf16[1056,128]{1,0:T(8,128)(2,1)S(1)} %constant_dynamic-update-slice_fusion.5.refs_7_), channel_id=1, source_target_pairs={{0,8},{8,16},{16,24},{24,0},{1,9},{9,17},{17,25},{25,1},{2,10},{10... | collective-permute-start | bytes 811016 | tf_op jit(solution)/shard_map/ppermute | solution.py:35
  124.6 12.6 %collective-permute-start.15 = (bf16[528,128]{1,0:T(8,128)(2,1)S(1)}, bf16[528,128]{1,0:T(8,128)(2,1)}, u32[]{:S(2)}, u32[]{:S(2)}) collective-permute-start(bf16[528,128]{1,0:T(8,128)(2,1)S(1)} %collective-permute-done.9), channel_id=1, source_target_pairs={{0,128},{128,256},{256,384},{384,512},{512,640},{640,768},{768,896... | collective-permute-start | bytes 405512 | tf_op jit(solution)/shard_map/ppermute | solution.py:130
  129.6 23.4 %collective-permute-start.12 = (bf16[1056,128]{1,0:T(8,128)(2,1)S(1)}, bf16[1056,128]{1,0:T(8,128)(2,1)S(1)}, u32[]{:S(2)}, u32[]{:S(2)}) collective-permute-start(bf16[1056,128]{1,0:T(8,128)(2,1)S(1)} %constant_dynamic-update-slice_fusion.5.refs_7_), channel_id=1, source_target_pairs={{0,24},{8,0},{16,8},{24,16},{1,25},{9,1},{17,9},{25,17},{2,26},{10... | collective-permute-start | bytes 811016 | tf_op jit(solution)/shard_map/ppermute | solution.py:36
  137.2 18.2 %collective-permute-start.16 = (bf16[528,128]{1,0:T(8,128)(2,1)}, bf16[528,128]{1,0:T(8,128)(2,1)}, u32[]{:S(2)}, u32[]{:S(2)}) collective-permute-start(bf16[528,128]{1,0:T(8,128)(2,1)} %collective-permute-done.15.refs_12_), channel_id=1, source_target_pairs={{0,8},{8,16},{16,24},{24,0},{1,9},{9,17},{17,25},{25,1},{2,10},{10... | collective-permute-start | bytes 405512 | tf_op jit(solution)/shard_map/ppermute | solution.py:35
  139.2 18.5 %collective-permute-start.17 = (bf16[528,128]{1,0:T(8,128)(2,1)}, bf16[528,128]{1,0:T(8,128)(2,1)}, u32[]{:S(2)}, u32[]{:S(2)}) collective-permute-start(bf16[528,128]{1,0:T(8,128)(2,1)} %collective-permute-done.15.refs_12_), channel_id=1, source_target_pairs={{0,24},{8,0},{16,8},{24,16},{1,25},{9,1},{17,9},{25,17},{2,26},{10... | collective-permute-start | bytes 405512 | tf_op jit(solution)/shard_map/ppermute | solution.py:36
  145.0 20.8 %collective-permute-start.7 = (bf16[1056,128]{1,0:T(8,128)(2,1)}, bf16[1056,128]{1,0:T(8,128)(2,1)}, u32[]{:S(2)}, u32[]{:S(2)}) collective-permute-start(bf16[1056,128]{1,0:T(8,128)(2,1)} %slice.40), channel_id=1, source_target_pairs={{0,8},{8,16},{16,24},{24,0},{1,9},{9,17},{17,25},{25,1},{2,10},{10... | collective-permute-start | bytes 811016 | tf_op jit(solution)/shard_map/ppermute | solution.py:42
  147.7 18.1 %collective-permute-start.8 = (bf16[1584,128]{1,0:T(8,128)(2,1)}, bf16[1584,128]{1,0:T(8,128)(2,1)S(1)}, u32[]{:S(2)}, u32[]{:S(2)}) collective-permute-start(bf16[1584,128]{1,0:T(8,128)(2,1)} %slice.41), channel_id=1, source_target_pairs={{0,24},{8,0},{16,8},{24,16},{1,25},{9,1},{17,9},{25,17},{2,26},{10... | collective-permute-start | bytes 1216520 | tf_op jit(solution)/shard_map/ppermute | solution.py:43
  152.9 10.2 %collective-permute-start.18 = (bf16[528,128]{1,0:T(8,128)(2,1)}, bf16[528,128]{1,0:T(8,128)(2,1)S(1)}, u32[]{:S(2)}, u32[]{:S(2)}) collective-permute-start(bf16[528,128]{1,0:T(8,128)(2,1)} %collective-permute-done.15.refs_12_), channel_id=1, source_target_pairs={{0,16},{8,24},{16,0},{24,8},{1,17},{9,25},{17,1},{25,9},{2,18},{10... | collective-permute-start | bytes 405512 | tf_op jit(solution)/shard_map/ppermute | solution.py:39
  155.4 8.4 %collective-permute-start.13 = (bf16[528,128]{1,0:T(8,128)(2,1)S(1)}, bf16[528,128]{1,0:T(8,128)(2,1)S(1)}, u32[]{:S(2)}, u32[]{:S(2)}) collective-permute-start(bf16[528,128]{1,0:T(8,128)(2,1)S(1)} %slice.42), channel_id=1, source_target_pairs={{0,8},{8,16},{16,24},{24,0},{1,9},{9,17},{17,25},{25,1},{2,10},{10... | collective-permute-start | bytes 405512 | tf_op jit(solution)/shard_map/ppermute | solution.py:42
  157.7 7.5 %collective-permute-start.14 = (bf16[528,128]{1,0:T(8,128)(2,1)S(1)}, bf16[528,128]{1,0:T(8,128)(2,1)S(1)}, u32[]{:S(2)}, u32[]{:S(2)}) collective-permute-start(bf16[528,128]{1,0:T(8,128)(2,1)S(1)} %slice.43), channel_id=1, source_target_pairs={{0,24},{8,0},{16,8},{24,16},{1,25},{9,1},{17,9},{25,17},{2,26},{10... | collective-permute-start | bytes 405512 | tf_op jit(solution)/shard_map/ppermute | solution.py:43
  163.2 0.6 copy-start.4
  163.8 0.6 copy-start.6
  165.2 0.7 copy-start.8
  165.9 2.2 copy-start
  168.1 0.9 copy-start.5
  169.0 0.9 copy-start.7
  169.9 0.9 copy-start.9
  196.8 13.0 %collective-permute-start.19 = (bf16[512,128]{1,0:T(8,128)(2,1)S(1)}, bf16[512,128]{1,0:T(8,128)(2,1)S(1)}, u32[]{:S(2)}, u32[]{:S(2)}) collective-permute-start(bf16[512,128]{1,0:T(8,128)(2,1)S(1)} %get-tuple-element.8.refs_1_), channel_id=1, source_target_pairs={{0,128},{128,256},{256,384},{384,512},{512,640},{640,768},{768,896... | collective-permute-start | bytes 393224 | tf_op jit(solution)/shard_map/ppermute | solution.py:154
  202.9 16.6 %collective-permute-start.20 = (bf16[512,128]{1,0:T(8,128)(2,1)S(1)}, bf16[512,128]{1,0:T(8,128)(2,1)S(1)}, u32[]{:S(2)}, u32[]{:S(2)}) collective-permute-start(bf16[512,128]{1,0:T(8,128)(2,1)S(1)} %get-tuple-element.8.refs_1_), channel_id=1, source_target_pairs={{0,896},{128,0},{256,128},{384,256},{512,384},{640,512},{768,640},... | collective-permute-start | bytes 393224 | tf_op jit(solution)/shard_map/ppermute | solution.py:154
  209.8 13.7 %collective-permute-start.21 = (bf16[512,128]{1,0:T(8,128)(2,1)S(1)}, bf16[512,128]{1,0:T(8,128)(2,1)S(1)}, u32[]{:S(2)}, u32[]{:S(2)}) collective-permute-start(bf16[512,128]{1,0:T(8,128)(2,1)S(1)} %collective-permute-done.19), channel_id=1, source_target_pairs={{0,128},{128,256},{256,384},{384,512},{512,640},{640,768},{768,896... | collective-permute-start | bytes 393224 | tf_op jit(solution)/shard_map/ppermute | solution.py:128
  219.5 10.9 %collective-permute-start.22 = (bf16[512,128]{1,0:T(8,128)(2,1)S(1)}, bf16[512,128]{1,0:T(8,128)(2,1)S(1)}, u32[]{:S(2)}, u32[]{:S(2)}) collective-permute-start(bf16[512,128]{1,0:T(8,128)(2,1)S(1)} %collective-permute-done.20), channel_id=1, source_target_pairs={{0,896},{128,0},{256,128},{384,256},{512,384},{640,512},{768,640},... | collective-permute-start | bytes 393224 | tf_op jit(solution)/shard_map/ppermute | solution.py:129
  230.5 38.2 %collective-permute-start.24 = (bf16[2560,128]{1,0:T(8,128)(2,1)S(1)}, bf16[2560,128]{1,0:T(8,128)(2,1)S(1)}, u32[]{:S(2)}, u32[]{:S(2)}) collective-permute-start(bf16[2560,128]{1,0:T(8,128)(2,1)S(1)} %constant_dynamic-update-slice_fusion.7.refs_3_), channel_id=1, source_target_pairs={{0,24},{8,0},{16,8},{24,16},{1,25},{9,1},{17,9},{25,17},{2,26},{10... | collective-permute-start | bytes 1966088 | tf_op jit(solution)/shard_map/ppermute | solution.py:36
  235.0 47.5 %collective-permute-start.23 = (bf16[2560,128]{1,0:T(8,128)(2,1)S(1)}, bf16[2560,128]{1,0:T(8,128)(2,1)S(1)}, u32[]{:S(2)}, u32[]{:S(2)}) collective-permute-start(bf16[2560,128]{1,0:T(8,128)(2,1)S(1)} %constant_dynamic-update-slice_fusion.7.refs_3_), channel_id=1, source_target_pairs={{0,8},{8,16},{16,24},{24,0},{1,9},{9,17},{17,25},{25,1},{2,10},{10... | collective-permute-start | bytes 1966088 | tf_op jit(solution)/shard_map/ppermute | solution.py:35
  237.0 13.8 %collective-permute-start.27 = (bf16[512,128]{1,0:T(8,128)(2,1)S(1)}, bf16[512,128]{1,0:T(8,128)(2,1)S(1)}, u32[]{:S(2)}, u32[]{:S(2)}) collective-permute-start(bf16[512,128]{1,0:T(8,128)(2,1)S(1)} %collective-permute-done.21), channel_id=1, source_target_pairs={{0,128},{128,256},{256,384},{384,512},{512,640},{640,768},{768,896... | collective-permute-start | bytes 393224 | tf_op jit(solution)/shard_map/ppermute | solution.py:128
  245.4 12.0 %collective-permute-start.28 = (bf16[512,128]{1,0:T(8,128)(2,1)S(1)}, bf16[512,128]{1,0:T(8,128)(2,1)S(1)}, u32[]{:S(2)}, u32[]{:S(2)}) collective-permute-start(bf16[512,128]{1,0:T(8,128)(2,1)S(1)} %collective-permute-done.22), channel_id=1, source_target_pairs={{0,896},{128,0},{256,128},{384,256},{512,384},{640,512},{768,640},... | collective-permute-start | bytes 393224 | tf_op jit(solution)/shard_map/ppermute | solution.py:129
  257.4 30.3 %collective-permute-start.29 = (bf16[1024,128]{1,0:T(8,128)(2,1)S(1)}, bf16[1024,128]{1,0:T(8,128)(2,1)S(1)}, u32[]{:S(2)}, u32[]{:S(2)}) collective-permute-start(bf16[1024,128]{1,0:T(8,128)(2,1)S(1)} %constant_dynamic-update-slice_fusion.12.refs_8_), channel_id=1, source_target_pairs={{0,8},{8,16},{16,24},{24,0},{1,9},{9,17},{17,25},{25,1},{2,10},{10... | collective-permute-start | bytes 786440 | tf_op jit(solution)/shard_map/ppermute | solution.py:35
  259.3 30.4 %collective-permute-start.30 = (bf16[1024,128]{1,0:T(8,128)(2,1)S(1)}, bf16[1024,128]{1,0:T(8,128)(2,1)S(1)}, u32[]{:S(2)}, u32[]{:S(2)}) collective-permute-start(bf16[1024,128]{1,0:T(8,128)(2,1)S(1)} %constant_dynamic-update-slice_fusion.12.refs_8_), channel_id=1, source_target_pairs={{0,24},{8,0},{16,8},{24,16},{1,25},{9,1},{17,9},{25,17},{2,26},{10... | collective-permute-start | bytes 786440 | tf_op jit(solution)/shard_map/ppermute | solution.py:36
  264.5 16.2 %collective-permute-start.33 = (bf16[512,128]{1,0:T(8,128)(2,1)S(1)}, bf16[512,128]{1,0:T(8,128)(2,1)S(1)}, u32[]{:S(2)}, u32[]{:S(2)}) collective-permute-start(bf16[512,128]{1,0:T(8,128)(2,1)S(1)} %collective-permute-done.27), channel_id=1, source_target_pairs={{0,128},{128,256},{256,384},{384,512},{512,640},{640,768},{768,896... | collective-permute-start | bytes 393224 | tf_op jit(solution)/shard_map/ppermute | solution.py:130
  268.7 38.5 %collective-permute-start.26 = (bf16[1536,128]{1,0:T(8,128)(2,1)S(1)}, bf16[1536,128]{1,0:T(8,128)(2,1)S(1)}, u32[]{:S(2)}, u32[]{:S(2)}) collective-permute-start(bf16[1536,128]{1,0:T(8,128)(2,1)S(1)} %slice.45), channel_id=1, source_target_pairs={{0,24},{8,0},{16,8},{24,16},{1,25},{9,1},{17,9},{25,17},{2,26},{10... | collective-permute-start | bytes 1179656 | tf_op jit(solution)/shard_map/ppermute | solution.py:43
  280.7 12.9 %collective-permute-start.34 = (bf16[512,128]{1,0:T(8,128)(2,1)S(1)}, bf16[512,128]{1,0:T(8,128)(2,1)S(1)}, u32[]{:S(2)}, u32[]{:S(2)}) collective-permute-start(bf16[512,128]{1,0:T(8,128)(2,1)S(1)} %collective-permute-done.33.refs_13_), channel_id=1, source_target_pairs={{0,8},{8,16},{16,24},{24,0},{1,9},{9,17},{17,25},{25,1},{2,10},{10... | collective-permute-start | bytes 393224 | tf_op jit(solution)/shard_map/ppermute | solution.py:35
  282.6 15.7 %collective-permute-start.35 = (bf16[512,128]{1,0:T(8,128)(2,1)S(1)}, bf16[512,128]{1,0:T(8,128)(2,1)S(1)}, u32[]{:S(2)}, u32[]{:S(2)}) collective-permute-start(bf16[512,128]{1,0:T(8,128)(2,1)S(1)} %collective-permute-done.33.refs_13_), channel_id=1, source_target_pairs={{0,24},{8,0},{16,8},{24,16},{1,25},{9,1},{17,9},{25,17},{2,26},{10... | collective-permute-start | bytes 393224 | tf_op jit(solution)/shard_map/ppermute | solution.py:36
  287.8 18.7 %collective-permute-start.25 = (bf16[1024,128]{1,0:T(8,128)(2,1)S(1)}, bf16[1024,128]{1,0:T(8,128)(2,1)S(1)}, u32[]{:S(2)}, u32[]{:S(2)}) collective-permute-start(bf16[1024,128]{1,0:T(8,128)(2,1)S(1)} %slice.44), channel_id=1, source_target_pairs={{0,8},{8,16},{16,24},{24,0},{1,9},{9,17},{17,25},{25,1},{2,10},{10... | collective-permute-start | bytes 786440 | tf_op jit(solution)/shard_map/ppermute | solution.py:42
  289.7 12.2 %collective-permute-start.36 = (bf16[512,128]{1,0:T(8,128)(2,1)S(1)}, bf16[512,128]{1,0:T(8,128)(2,1)S(1)}, u32[]{:S(2)}, u32[]{:S(2)}) collective-permute-start(bf16[512,128]{1,0:T(8,128)(2,1)S(1)} %collective-permute-done.33.refs_13_), channel_id=1, source_target_pairs={{0,16},{8,24},{16,0},{24,8},{1,17},{9,25},{17,1},{25,9},{2,18},{10... | collective-permute-start | bytes 393224 | tf_op jit(solution)/shard_map/ppermute | solution.py:39
  293.6 0.7 copy-start.10
  294.2 8.4 %collective-permute-start.31 = (bf16[512,128]{1,0:T(8,128)(2,1)S(1)}, bf16[512,128]{1,0:T(8,128)(2,1)S(1)}, u32[]{:S(2)}, u32[]{:S(2)}) collective-permute-start(bf16[512,128]{1,0:T(8,128)(2,1)S(1)} %slice.46), channel_id=1, source_target_pairs={{0,8},{8,16},{16,24},{24,0},{1,9},{9,17},{17,25},{25,1},{2,10},{10... | collective-permute-start | bytes 393224 | tf_op jit(solution)/shard_map/ppermute | solution.py:42
  298.3 0.7 copy-start.12
  299.0 6.8 %collective-permute-start.32 = (bf16[512,128]{1,0:T(8,128)(2,1)S(1)}, bf16[512,128]{1,0:T(8,128)(2,1)S(1)}, u32[]{:S(2)}, u32[]{:S(2)}) collective-permute-start(bf16[512,128]{1,0:T(8,128)(2,1)S(1)} %slice.47), channel_id=1, source_target_pairs={{0,24},{8,0},{16,8},{24,16},{1,25},{9,1},{17,9},{25,17},{2,26},{10... | collective-permute-start | bytes 393224 | tf_op jit(solution)/shard_map/ppermute | solution.py:43
  301.9 0.6 copy-start.14
  302.6 0.7 copy-start.16
  305.8 0.7 copy-start.18
  306.5 0.7 copy-start.2
  307.2 2.2 copy-start.1
  309.4 0.9 copy-start.3
  310.3 0.9 copy-start.11
  311.3 0.9 copy-start.13
  312.2 0.9 copy-start.15
  313.1 0.9 copy-start.17
  314.0 0.9 copy-start.19
  321.5 10.7 %collective-permute-start.37 = (bf16[512,128]{1,0:T(8,128)(2,1)S(1)}, bf16[512,128]{1,0:T(8,128)(2,1)S(1)}, u32[]{:S(2)}, u32[]{:S(2)}) collective-permute-start(bf16[512,128]{1,0:T(8,128)(2,1)S(1)} %shard_map.74), channel_id=1, source_target_pairs={{0,0},{1,1},{2,2},{3,3},{4,4},{5,5},{6,6},{7,7},{8,32},{9,33},{10,... | collective-permute-start | bytes 393224 | tf_op jit(solution)/shard_map/ppermute | solution.py:159
Sparse Core Ops, SparseCore 0:
  36.3 58.9 all-gather.2
  196.9 46.1 all-gather.4

commit v3 on v2

v3 whole, which is shorter than its diff:
```python
import functools

import jax
import jax.numpy as jnp
import numpy as np
from jax import lax
from jax.experimental import pallas as pl
from jax.experimental.pallas import tpu as pltpu
from jax.sharding import Mesh, PartitionSpec as P

STEPS = 2
BS = 128
ROWS = 4 * BS
TAIL = 16
AXES = ("zh", "zl", "x1", "x0", "y", "core")
SIZES = (8, 4, 2, 2, 4, 2)


def swap(zh, zl, x1, x0, y, core):
    return zh, x0 * 2 + core, x1, zl // 2, y, zl % 2


def hop(zh, zl, x1, x0, y, core):
    return (zh + 1 - 2 * core) % 8, zl, x1, x0, y, core


def flip(zh, zl, x1, x0, y, core):
    return zh, zl, x1, x0, y, 1 - core


def move(part, *steps):
    pairs = []
    for i in range(1024):
        place = tuple(int(k) for k in np.unravel_index(i, SIZES))
        for step in steps:
            place = step(*place)
        pairs.append((i, int(np.ravel_multi_index(place, SIZES))))
    return lax.ppermute(part, AXES, pairs)


def exchange(part, axis):
    return lax.ppermute(part, axis, [(0, 1), (1, 0)])


def kernel(rows, units, first, branch, tab, *refs):
    slots, refs = (None, refs) if first else (refs[0], refs[1:])
    own, a_hbm, refs = refs[0], refs[1], refs[2:]
    parts, refs = refs[: len(units)], refs[len(units) :]
    if first:
        out, slots_out, a_all, b_all, acc, sems, slots, sem = refs
    else:
        out, a_all, b_all, acc, sems = refs
    copies = [pltpu.make_async_copy(a_hbm, a_all, sems.at[0])]
    at = 0
    for part, n in zip(parts, units):
        copies.append(
            pltpu.make_async_copy(
                part, b_all.at[pl.ds(at * rows, n * rows)], sems.at[len(copies)]
            )
        )
        at += n
    for copy in copies:
        copy.start()
    nothing = 32 * rows
    b_all[nothing : nothing + BS, :] = jnp.zeros((BS, BS), jnp.bfloat16)
    acc[...] = jnp.zeros_like(acc)
    for copy in copies:
        copy.wait()
    if first:
        for base, whole in ((0, a_all), (32, b_all)):
            for k in range(32):
                row = whole[k * rows + ROWS : (k + 1) * rows, :].astype(jnp.float32)[0:1]
                slots_out[base + k : base + k + 1, :] = row.astype(jnp.int32)
        copy = pltpu.make_async_copy(slots_out, slots, sem)
        copy.start()
        copy.wait()
    mine = [slots[tab[32], j] for j in range(4)]

    def pair(t, carry):
        las = [tab[2 * t + k] for k in range(2)]
        for j in range(4):
            lefts, rights = [], []
            for k in range(2):
                m = slots[las[k], j]
                hit = slots[32 + 2 * t + k, m] == mine[j]
                right = jnp.where(hit, (2 * t + k) * rows + m * BS, nothing)
                rights.append(b_all[pl.ds(pl.multiple_of(right, 16), BS), :])
                left = las[k] * rows + j * BS
                lefts.append(a_all[pl.ds(pl.multiple_of(left, 16), BS), :])
            acc[j * BS : (j + 1) * BS, :] += jnp.dot(
                jnp.concatenate(lefts, 1),
                jnp.concatenate(rights, 0),
                preferred_element_type=jnp.float32,
            )
        return carry

    lax.fori_loop(0, 16, pair, 0)
    square = acc[...]
    twice = 2.0 * own[:ROWS, :].astype(jnp.float32) - square
    out[...] = jnp.where(branch[0] == 1, twice, square).astype(out.dtype)


def multiply(branch, tab, slots, own, a_all, parts):
    first, rows = slots is None, own.shape[0]
    units = [part.shape[0] // rows for part in parts]
    smem = pl.BlockSpec(memory_space=pltpu.SMEM)
    vmem = pl.BlockSpec(memory_space=pltpu.VMEM)
    anywhere = pl.BlockSpec(memory_space=pl.ANY)
    out_shape = [jax.ShapeDtypeStruct((ROWS, BS), jnp.bfloat16)]
    scratch = [
        pltpu.VMEM((32 * rows, BS), jnp.bfloat16),
        pltpu.VMEM((32 * rows + BS, BS), jnp.bfloat16),
        pltpu.VMEM((ROWS, BS), jnp.float32),
        pltpu.SemaphoreType.DMA((1 + len(parts),)),
    ]
    if first:
        out_shape.append(jax.ShapeDtypeStruct((64, BS), jnp.int32))
        scratch += [pltpu.SMEM((64, BS), jnp.int32), pltpu.SemaphoreType.DMA]
    done = pl.pallas_call(
        functools.partial(kernel, rows, units, first),
        out_shape=out_shape,
        in_specs=[smem] * (2 if first else 3) + [vmem] + [anywhere] * (1 + len(parts)),
        out_specs=[vmem] * len(out_shape),
        scratch_shapes=scratch,
        compiler_params=pltpu.CompilerParams(vmem_limit_bytes=16 * 1024 * 1024),
        cost_estimate=pl.CostEstimate(
            flops=2 * 128 * BS**3, bytes_accessed=64 * ROWS * BS * 2, transcendentals=0
        ),
    )(branch, tab, *([] if first else [slots]), own, a_all, *parts)
    return done[0], done[1] if first else slots


def gather(unit, sibling, hop1):
    rows = unit.shape[0]
    near = [unit]
    for by in (1, 2, 3):
        near.append(lax.ppermute(unit, "zl", [(i, (i + by) % 4) for i in range(4)]))
    a_all = lax.all_gather(jnp.concatenate(near), ("x1", "y"), axis=0, tiled=True)
    both = jnp.concatenate([unit, sibling])
    hops = [hop1]
    for _ in range(2):
        hops.append(move(hops[-1], hop))
    hops.append(move(hops[-1][:rows], hop))
    placed = [
        (both, [(0, 0, 0), (0, 0, 1)]),
        (exchange(both, "x0"), [(0, 1, 0), (0, 1, 1)]),
    ]
    for k, got in enumerate(hops, 1):
        line = jnp.concatenate([got, exchange(got, "x0")])
        names = [(k, f, w) for f in (0, 1) for w in range(2 if k < 4 else 1)]
        placed.append((line, names))
        placed.append((exchange(line, "core"), [(-h, f, 1 - w) for h, f, w in names]))
    return a_all, placed


def table(placed):
    zh, zl, x1, x0, y, core = (lax.axis_index(name) for name in AXES)
    names = np.concatenate([np.array(n) for _, n in placed])
    up = (1 - 2 * core) * names[:, 0]
    p = (zh - up) % 8 * 4 + (x0 ^ names[:, 1]) * 2 + (core ^ names[:, 2])
    low = p // 8 % 2 * 2 + p % 2
    la = (p // 16 * 4 + p // 2 % 4) * 4 + (zl - low) % 4
    return jnp.concatenate([la, jnp.reshape((x1 * 4 + y) * 4, (1,))]).astype(jnp.int32)


def body(values, column_slot_index, branches):
    flat = values.reshape(ROWS, BS)
    tail = column_slot_index[:, 0].astype(jnp.bfloat16)[None]
    start = jnp.concatenate([flat, jnp.pad(tail, ((0, TAIL - 1), (0, BS - 4)))])
    unit, sibling = move(start, swap), move(start, swap, flip)
    hop1 = jnp.concatenate([move(start, swap, hop), move(start, swap, flip, hop)])
    slots = None
    for step in range(STEPS):
        if step:
            sibling = exchange(unit, "core")
            hop1 = move(jnp.concatenate([unit, sibling]), hop)
        a_all, placed = gather(unit, sibling, hop1)
        unit, slots = multiply(
            branches[step : step + 1], table(placed), slots, unit, a_all, [q for q, _ in placed]
        )
    return move(unit, swap).reshape(values.shape)


def solution(mesh):
    fine = Mesh(mesh.devices.reshape(SIZES), AXES)
    split = (("zh", "zl"), ("x1", "x0", "y", "core"))
    in_specs = (P(*split, None, None), P(*split), P())
    return jax.shard_map(
        body, mesh=fine, in_specs=in_specs, out_specs=P(*split, None, None), check_vma=False
    )
```

time: 341 us -> 339 us (level)
  the two profiles are of different devices: /device:TPU:64 before, /device:TPU:1 now
where the time goes in v3:
time: 339 us; the launch traced here: 336 us
  starting transfers between devices  170 us (50%)
  waiting for transfers between devices  123 us (36%)
  Pallas kernels  14.2 us (4%)
  between operations  14 us (4%)
  local copies, waits for them, and re-layouts  11.4 us (3%)
  other arithmetic  3.39 us (1%)
    ppermute x12, starting transfers between devices, move(): return lax.ppermute(part, AXES, pairs)  85.5 us
    ppermute x19, starting transfers between devices, exchange(): return lax.ppermute(part, axis, [(0, 1), (1, 0)])  58.4 us
    ppermute x12, waiting for transfers between devices, move(): return lax.ppermute(part, AXES, pairs)  55.3 us
    ppermute x6, starting transfers between devices, gather(): near.append(lax.ppermute(unit, 'zl', [(i, (i + by) % 4) for i in range(4)]))  26.4 us
    ppermute x19, waiting for transfers between devices, exchange(): return lax.ppermute(part, axis, [(0, 1), (1, 0)])  26.4 us
    all_gather x2, waiting for transfers between devices, gather(): lax.all_gather(jnp.concatenate(near), ('x1', 'y'), axis=0, tiled=True)  24.4 us
    ppermute x6, waiting for transfers between devices, gather(): near.append(lax.ppermute(unit, 'zl', [(i, (i + by) % 4) for i in range(4)]))  16.8 us
    pallas_call x2, Pallas kernels, multiply(): pl.pallas_call(functools.partial(kernel, rows, units, first), out_shape=o...  14.2 us
  transfers between devices with their start and end apart: 39, of which 19 were waited for; matrix products, arithmetic and copies ran while one was open for 0% of the time, Pallas kernels for 0%

profile of v3, /device:TPU:1, one launch (start us, length us, event | category | flops | bytes accessed | tf_op | source)
XLA Modules:
  0.0 336.3 jit_solution(10678905101374720252)
XLA Ops:
  7.2 0.9 fusion.1
  8.1 4.9 %collective-permute-start = (bf16[528,128]{1,0:T(8,128)(2,1)S(1)}, bf16[528,128]{1,0:T(8,128)(2,1)S(1)}, u32[]{:S(2)}, u32[]{:S(2)}) collective-permute-start(bf16[528,128]{1,0:T(8,128)(2,1)S(1)} %fusion.1), channel_id=1, source_target_pairs={{0,0},{1,32},{2,2},{3,34},{4,4},{5,36},{6,6},{7,38},{8,64},{9,96},... | collective-permute-start | bytes 405512 | tf_op jit(solution)/shard_map/ppermute | solution.py:38
  13.1 2.7 collective-permute-done.refs_0_
  15.7 10.6 %collective-permute-start.3 = (bf16[528,128]{1,0:T(8,128)(2,1)S(1)}, bf16[528,128]{1,0:T(8,128)(2,1)S(1)}, u32[]{:S(2)}, u32[]{:S(2)}) collective-permute-start(bf16[528,128]{1,0:T(8,128)(2,1)S(1)} %collective-permute-done.refs_0_), channel_id=1, source_target_pairs={{0,96},{32,0},{64,32},{96,64},{1,97},{33,1},{65,33},{97,65},{2,98}... | collective-permute-start | bytes 405512 | tf_op jit(solution)/shard_map/ppermute | solution.py:137
  26.3 1.9 collective-permute-start.2
  28.2 2.2 collective-permute-start.1
  30.5 8.5 %collective-permute-done.2 = bf16[528,128]{1,0:T(8,128)(2,1)S(1)} collective-permute-done((bf16[528,128]{1,0:T(8,128)(2,1)S(1)}, bf16[528,128]{1,0:T(8,128)(2,1)S(1)}, u32[]{:S(2)}, u32[]{:S(2)}) %collective-permute-start.2) | collective-permute-done | bytes 135200 | tf_op jit(solution)/shard_map/ppermute | solution.py:137
  39.0 0.9 pad_maximum_fusion
  39.9 9.3 %collective-permute-start.6 = (bf16[528,128]{1,0:T(8,128)(2,1)S(1)}, bf16[528,128]{1,0:T(8,128)(2,1)S(1)}, u32[]{:S(2)}, u32[]{:S(2)}) collective-permute-start(bf16[528,128]{1,0:T(8,128)(2,1)S(1)} %fusion.1), channel_id=1, source_target_pairs={{0,128},{1,160},{2,130},{3,162},{4,132},{5,164},{6,134},{7,166},{8... | collective-permute-start | bytes 405512 | tf_op jit(solution)/shard_map/ppermute | solution.py:38
  49.2 12.9 %collective-permute-start.7 = (bf16[528,128]{1,0:T(8,128)(2,1)S(1)}, bf16[528,128]{1,0:T(8,128)(2,1)S(1)}, u32[]{:S(2)}, u32[]{:S(2)}) collective-permute-start(bf16[528,128]{1,0:T(8,128)(2,1)S(1)} %fusion.1), channel_id=1, source_target_pairs={{0,897},{1,929},{2,899},{3,931},{4,901},{5,933},{6,903},{7,935},{8... | collective-permute-start | bytes 405512 | tf_op jit(solution)/shard_map/ppermute | solution.py:38
  62.1 7.7 %collective-permute-done.7 = bf16[528,128]{1,0:T(8,128)(2,1)S(1)} collective-permute-done((bf16[528,128]{1,0:T(8,128)(2,1)S(1)}, bf16[528,128]{1,0:T(8,128)(2,1)S(1)}, u32[]{:S(2)}, u32[]{:S(2)}) %collective-permute-start.7) | collective-permute-done | bytes 135200 | tf_op jit(solution)/shard_map/ppermute | solution.py:38
  69.9 7.6 %collective-permute-start.10 = (bf16[1056,128]{1,0:T(8,128)(2,1)S(1)}, bf16[1056,128]{1,0:T(8,128)(2,1)S(1)}, u32[]{:S(2)}, u32[]{:S(2)}) collective-permute-start(bf16[1056,128]{1,0:T(8,128)(2,1)S(1)} %get-tuple-element.9), channel_id=1, source_target_pairs={{0,128},{1,897},{2,130},{3,899},{4,132},{5,901},{6,134},{7,903},{8... | collective-permute-start | bytes 811016 | tf_op jit(solution)/shard_map/ppermute | solution.py:38
  77.5 1.9 collective-permute-start.8
  79.4 2.4 collective-permute-start.4
  81.9 2.0 collective-permute-done.4
  83.9 13.8 %collective-permute-start.5 = (bf16[1056,128]{1,0:T(8,128)(2,1)S(1)}, bf16[1056,128]{1,0:T(8,128)(2,1)}, u32[]{:S(2)}, u32[]{:S(2)}) collective-permute-start(bf16[1056,128]{1,0:T(8,128)(2,1)S(1)} %constant_dynamic-update-slice_fusion.refs_2_), channel_id=1, source_target_pairs={{0,8},{8,0},{1,9},{9,1},{2,10},{10,2},{3,11},{11,3},{4,12},{12,4},... | collective-permute-start | bytes 811016 | tf_op jit(solution)/shard_map/ppermute | solution.py:42
  97.7 14.8 %collective-permute-start.13 = (bf16[1056,128]{1,0:T(8,128)(2,1)S(1)}, bf16[1056,128]{1,0:T(8,128)(2,1)S(1)}, u32[]{:S(2)}, u32[]{:S(2)}) collective-permute-start(bf16[1056,128]{1,0:T(8,128)(2,1)S(1)} %collective-permute-done.10), channel_id=1, source_target_pairs={{0,128},{1,897},{2,130},{3,899},{4,132},{5,901},{6,134},{7,903},{8... | collective-permute-start | bytes 811016 | tf_op jit(solution)/shard_map/ppermute | solution.py:38
  112.4 1.9 collective-permute-start.11
  114.4 1.9 collective-permute-start.9
  116.4 7.8 %collective-permute-done.13 = bf16[1056,128]{1,0:T(8,128)(2,1)S(1)} collective-permute-done((bf16[1056,128]{1,0:T(8,128)(2,1)S(1)}, bf16[1056,128]{1,0:T(8,128)(2,1)S(1)}, u32[]{:S(2)}, u32[]{:S(2)}) %collective-permute-start.13) | collective-permute-done | bytes 270368 | tf_op jit(solution)/shard_map/ppermute | solution.py:38
  124.3 7.9 %collective-permute-start.16 = (bf16[528,128]{1,0:T(8,128)(2,1)S(1)}, bf16[528,128]{1,0:T(8,128)(2,1)S(1)}, u32[]{:S(2)}, u32[]{:S(2)}) collective-permute-start(bf16[528,128]{1,0:T(8,128)(2,1)S(1)} %slice.16), channel_id=1, source_target_pairs={{0,128},{1,897},{2,130},{3,899},{4,132},{5,901},{6,134},{7,903},{8... | collective-permute-start | bytes 405512 | tf_op jit(solution)/shard_map/ppermute | solution.py:38
  132.2 1.9 collective-permute-start.12
  134.1 2.0 collective-permute-start.14
  136.2 3.3 collective-permute-start.17
  139.5 10.6 %collective-permute-done.14 = bf16[1056,128]{1,0:T(8,128)(2,1)S(1)} collective-permute-done((bf16[1056,128]{1,0:T(8,128)(2,1)S(1)}, bf16[1056,128]{1,0:T(8,128)(2,1)S(1)}, u32[]{:S(2)}, u32[]{:S(2)}) %collective-permute-start.14) | collective-permute-done | bytes 270368 | tf_op jit(solution)/shard_map/ppermute | solution.py:42
  150.1 3.5 %collective-permute-start.15 = (bf16[2112,128]{1,0:T(8,128)(2,1)S(1)}, bf16[2112,128]{1,0:T(8,128)(2,1)}, u32[]{:S(2)}, u32[]{:S(2)}) collective-permute-start(bf16[2112,128]{1,0:T(8,128)(2,1)S(1)} %constant_dynamic-update-slice_fusion.9.refs_8_), channel_id=1, source_target_pairs={{0,1},{1,0},{2,3},{3,2},{4,5},{5,4},{6,7},{7,6},{8,9},{9,8},{10,11... | collective-permute-start | bytes 1622024 | tf_op jit(solution)/shard_map/ppermute | solution.py:42
  154.4 2.5 collective-permute-start.18
  158.2 5.1 %all-gather.3.cloned.1.call-done.refs_1_ = bf16[16896,128]{1,0:T(8,128)(2,1)} async-done(((bf16[2112,128]{1,0:T(8,128)(2,1)}), bf16[16896,128]{1,0:T(8,128)(2,1)}) %all-gather.3.cloned.1.call-update) | async-done | bytes 4325392 | tf_op jit(solution)/shard_map/all_gather | solution.py:138
  163.3 2.2 copy-done
  165.5 8.1 %shard_map.91 = (bf16[512,128]{1,0:T(8,128)(2,1)S(1)}, s32[64,128]{1,0:T(8,128)S(1)}) custom-call(s32[1]{0:T(128)} %get-tuple-element.13.branch, s32[33]{0:T(128)S(1)} %pad_add_fusion.tab, bf16[528,128]{1,0:T(8,128)(2,1)S(1)} %collective-permute-done.refs_0_, bf16[16896,128]{1,0:T(8,128)(2,1)S(1)} %copy-done, ...), custom_call_target="tpu_custom_call" | custom-call | flops 536870912 | bytes 8388608 | tf_op jit(solution)/shard_map/pallas_call | solution.py:119
  173.6 7.5 %collective-permute-start.21 = (bf16[512,128]{1,0:T(8,128)(2,1)S(1)}, bf16[512,128]{1,0:T(8,128)(2,1)S(1)}, u32[]{:S(2)}, u32[]{:S(2)}) collective-permute-start(bf16[512,128]{1,0:T(8,128)(2,1)S(1)} %get-tuple-element.8.refs_1_), channel_id=1, source_target_pairs={{0,96},{32,0},{64,32},{96,64},{1,97},{33,1},{65,33},{97,65},{2,98}... | collective-permute-start | bytes 393224 | tf_op jit(solution)/shard_map/ppermute | solution.py:137
  181.1 1.9 collective-permute-start.20
  183.0 2.4 collective-permute-start.19
  185.4 8.3 %collective-permute-done.20 = bf16[512,128]{1,0:T(8,128)(2,1)S(1)} collective-permute-done((bf16[512,128]{1,0:T(8,128)(2,1)S(1)}, bf16[512,128]{1,0:T(8,128)(2,1)S(1)}, u32[]{:S(2)}, u32[]{:S(2)}) %collective-permute-start.20) | collective-permute-done | bytes 131104 | tf_op jit(solution)/shard_map/ppermute | solution.py:137
  193.7 0.8 pad_maximum_fusion.1
  194.6 2.5 collective-permute-start.22
  197.1 0.9 collective-permute-done.22
  198.1 8.0 %collective-permute-start.24 = (bf16[1024,128]{1,0:T(8,128)(2,1)S(1)}, bf16[1024,128]{1,0:T(8,128)(2,1)S(1)}, u32[]{:S(2)}, u32[]{:S(2)}) collective-permute-start(bf16[1024,128]{1,0:T(8,128)(2,1)S(1)} %constant_dynamic-update-slice_fusion.13.refs_3_), channel_id=1, source_target_pairs={{0,128},{1,897},{2,130},{3,899},{4,132},{5,901},{6,134},{7,903},{8... | collective-permute-start | bytes 786440 | tf_op jit(solution)/shard_map/ppermute | solution.py:38
  206.1 11.6 %collective-permute-done.24 = bf16[1024,128]{1,0:T(8,128)(2,1)S(1)} collective-permute-done((bf16[1024,128]{1,0:T(8,128)(2,1)S(1)}, bf16[1024,128]{1,0:T(8,128)(2,1)S(1)}, u32[]{:S(2)}, u32[]{:S(2)}) %collective-permute-start.24) | collective-permute-done | bytes 262176 | tf_op jit(solution)/shard_map/ppermute | solution.py:38
  217.7 6.8 %collective-permute-start.27 = (bf16[1024,128]{1,0:T(8,128)(2,1)S(1)}, bf16[1024,128]{1,0:T(8,128)(2,1)S(1)}, u32[]{:S(2)}, u32[]{:S(2)}) collective-permute-start(bf16[1024,128]{1,0:T(8,128)(2,1)S(1)} %collective-permute-done.24), channel_id=1, source_target_pairs={{0,128},{1,897},{2,130},{3,899},{4,132},{5,901},{6,134},{7,903},{8... | collective-permute-start | bytes 786440 | tf_op jit(solution)/shard_map/ppermute | solution.py:38
  224.4 2.2 collective-permute-start.25
  226.7 7.3 %collective-permute-done.27 = bf16[1024,128]{1,0:T(8,128)(2,1)S(1)} collective-permute-done((bf16[1024,128]{1,0:T(8,128)(2,1)S(1)}, bf16[1024,128]{1,0:T(8,128)(2,1)S(1)}, u32[]{:S(2)}, u32[]{:S(2)}) %collective-permute-start.27) | collective-permute-done | bytes 262176 | tf_op jit(solution)/shard_map/ppermute | solution.py:38
  234.0 3.0 collective-permute-start.30
  237.0 2.2 collective-permute-start.28
  239.3 1.9 collective-permute-start.26
  241.2 9.1 %collective-permute-done.30 = bf16[1024,128]{1,0:T(8,128)(2,1)S(1)} collective-permute-done((bf16[1024,128]{1,0:T(8,128)(2,1)S(1)}, bf16[1024,128]{1,0:T(8,128)(2,1)S(1)}, u32[]{:S(2)}, u32[]{:S(2)}) %collective-permute-start.30) | collective-permute-done | bytes 262176 | tf_op jit(solution)/shard_map/ppermute | solution.py:38
  250.3 2.2 collective-permute-start.31
  252.5 1.9 collective-permute-start.33
  254.5 5.6 %collective-permute-start.29 = (bf16[2048,128]{1,0:T(8,128)(2,1)S(1)}, bf16[2048,128]{1,0:T(8,128)(2,1)S(1)}, u32[]{:S(2)}, u32[]{:S(2)}) collective-permute-start(bf16[2048,128]{1,0:T(8,128)(2,1)S(1)} %constant_dynamic-update-slice_fusion.17.refs_7_), channel_id=1, source_target_pairs={{0,1},{1,0},{2,3},{3,2},{4,5},{5,4},{6,7},{7,6},{8,9},{9,8},{10,11... | collective-permute-start | bytes 1572872 | tf_op jit(solution)/shard_map/ppermute | solution.py:42
  260.2 1.9 collective-permute-start.32
  262.1 2.9 collective-permute-done.33
  265.0 3.1 collective-permute-start.34
  268.1 2.2 collective-permute-start.23
  270.3 5.0 %collective-permute-done.34 = bf16[512,128]{1,0:T(8,128)(2,1)S(1)} collective-permute-done((bf16[512,128]{1,0:T(8,128)(2,1)S(1)}, bf16[512,128]{1,0:T(8,128)(2,1)S(1)}, u32[]{:S(2)}, u32[]{:S(2)}) %collective-permute-start.34) | collective-permute-done | bytes 131104 | tf_op jit(solution)/shard_map/ppermute | solution.py:42
  275.3 1.9 collective-permute-start.35
  277.3 8.6 %collective-permute-done.23.refs_4_ = bf16[1024,128]{1,0:T(8,128)(2,1)S(1)} collective-permute-done((bf16[1024,128]{1,0:T(8,128)(2,1)S(1)}, bf16[1024,128]{1,0:T(8,128)(2,1)S(1)}, u32[]{:S(2)}, u32[]{:S(2)}) %collective-permute-start.23) | collective-permute-done | bytes 262176 | tf_op jit(solution)/shard_map/ppermute | solution.py:42
  288.1 19.3 %all-gather.5.cloned.1.call-done.refs_2_ = bf16[16384,128]{1,0:T(8,128)(2,1)} async-done(((bf16[2048,128]{1,0:T(8,128)(2,1)}), bf16[16384,128]{1,0:T(8,128)(2,1)}) %all-gather.5.cloned.1.call-update) | async-done | bytes 4194320 | tf_op jit(solution)/shard_map/all_gather | solution.py:138
  307.3 2.2 copy-done.1
  309.5 1.0 copy-done.3
  310.6 0.9 copy-done.5
  311.5 0.9 copy-done.7
  312.5 6.2 %shard_map.92 = bf16[512,128]{1,0:T(8,128)(2,1)S(1)} custom-call(s32[1]{0:T(128)} %get-tuple-element.14.branch, s32[33]{0:T(128)S(1)} %pad_add_fusion.tab, s32[64,128]{1,0:T(8,128)S(1)} %get-tuple-element.7.refs_0_, bf16[512,128]{1,0:T(8,128)(2,1)S(1)} %get-tuple-element.8.refs_1_, bf16[16384,128]{1,0:T(8,128)(2,1)S(1)} %copy-done.1, ...), custom_call_target="tpu_custom_call" | custom-call | flops 536870912 | bytes 8388608 | tf_op jit(solution)/shard_map/pallas_call | solution.py:119
  318.6 6.0 %collective-permute-start.36 = (bf16[512,128]{1,0:T(8,128)(2,1)S(1)}, bf16[512,128]{1,0:T(8,128)(2,1)S(1)}, u32[]{:S(2)}, u32[]{:S(2)}) collective-permute-start(bf16[512,128]{1,0:T(8,128)(2,1)S(1)} %shard_map.92), channel_id=1, source_target_pairs={{0,0},{1,32},{2,2},{3,34},{4,4},{5,36},{6,6},{7,38},{8,64},{9,96},... | collective-permute-start | bytes 393224 | tf_op jit(solution)/shard_map/ppermute | solution.py:38
  324.6 4.2 %collective-permute-done.36 = bf16[512,128]{1,0:T(8,128)(2,1)S(1)} collective-permute-done((bf16[512,128]{1,0:T(8,128)(2,1)S(1)}, bf16[512,128]{1,0:T(8,128)(2,1)S(1)}, u32[]{:S(2)}, u32[]{:S(2)}) %collective-permute-start.36) | collective-permute-done | bytes 131104 | tf_op jit(solution)/shard_map/ppermute | solution.py:38
  (73 shorter events, 6.2 us)
Async XLA Ops:
  6.5 156.8 %all-gather.3.cloned.1.call-start = ((), (), s32[]{:S(2)}) async-start(), calls=%async_computation | async-start | bytes 4866048 | tf_op jit(solution)/shard_map/all_gather | solution.py:138
  8.1 7.6 %collective-permute-start = (bf16[528,128]{1,0:T(8,128)(2,1)S(1)}, bf16[528,128]{1,0:T(8,128)(2,1)S(1)}, u32[]{:S(2)}, u32[]{:S(2)}) collective-permute-start(bf16[528,128]{1,0:T(8,128)(2,1)S(1)} %fusion.1), channel_id=1, source_target_pairs={{0,0},{1,32},{2,2},{3,34},{4,4},{5,36},{6,6},{7,38},{8,64},{9,96},... | collective-permute-start | bytes 405512 | tf_op jit(solution)/shard_map/ppermute | solution.py:38
  15.7 14.7 %collective-permute-start.3 = (bf16[528,128]{1,0:T(8,128)(2,1)S(1)}, bf16[528,128]{1,0:T(8,128)(2,1)S(1)}, u32[]{:S(2)}, u32[]{:S(2)}) collective-permute-start(bf16[528,128]{1,0:T(8,128)(2,1)S(1)} %collective-permute-done.refs_0_), channel_id=1, source_target_pairs={{0,96},{32,0},{64,32},{96,64},{1,97},{33,1},{65,33},{97,65},{2,98}... | collective-permute-start | bytes 405512 | tf_op jit(solution)/shard_map/ppermute | solution.py:137
  26.3 12.6 %collective-permute-start.2 = (bf16[528,128]{1,0:T(8,128)(2,1)S(1)}, bf16[528,128]{1,0:T(8,128)(2,1)S(1)}, u32[]{:S(2)}, u32[]{:S(2)}) collective-permute-start(bf16[528,128]{1,0:T(8,128)(2,1)S(1)} %collective-permute-done.refs_0_), channel_id=1, source_target_pairs={{0,64},{32,96},{64,0},{96,32},{1,65},{33,97},{65,1},{97,33},{2,66}... | collective-permute-start | bytes 405512 | tf_op jit(solution)/shard_map/ppermute | solution.py:137
  28.2 10.7 %collective-permute-start.1 = (bf16[528,128]{1,0:T(8,128)(2,1)S(1)}, bf16[528,128]{1,0:T(8,128)(2,1)S(1)}, u32[]{:S(2)}, u32[]{:S(2)}) collective-permute-start(bf16[528,128]{1,0:T(8,128)(2,1)S(1)} %collective-permute-done.refs_0_), channel_id=1, source_target_pairs={{0,32},{32,64},{64,96},{96,0},{1,33},{33,65},{65,97},{97,1},{2,34}... | collective-permute-start | bytes 405512 | tf_op jit(solution)/shard_map/ppermute | solution.py:137
  39.8 267.5 %all-gather.5.cloned.1.call-start = ((), (), s32[]{:S(2)}) async-start(), calls=%async_computation.1 | async-start | bytes 4718592 | tf_op jit(solution)/shard_map/all_gather | solution.py:138
  39.9 22.2 %collective-permute-start.6 = (bf16[528,128]{1,0:T(8,128)(2,1)S(1)}, bf16[528,128]{1,0:T(8,128)(2,1)S(1)}, u32[]{:S(2)}, u32[]{:S(2)}) collective-permute-start(bf16[528,128]{1,0:T(8,128)(2,1)S(1)} %fusion.1), channel_id=1, source_target_pairs={{0,128},{1,160},{2,130},{3,162},{4,132},{5,164},{6,134},{7,166},{8... | collective-permute-start | bytes 405512 | tf_op jit(solution)/shard_map/ppermute | solution.py:38
  49.2 20.7 %collective-permute-start.7 = (bf16[528,128]{1,0:T(8,128)(2,1)S(1)}, bf16[528,128]{1,0:T(8,128)(2,1)S(1)}, u32[]{:S(2)}, u32[]{:S(2)}) collective-permute-start(bf16[528,128]{1,0:T(8,128)(2,1)S(1)} %fusion.1), channel_id=1, source_target_pairs={{0,897},{1,929},{2,899},{3,931},{4,901},{5,933},{6,903},{7,935},{8... | collective-permute-start | bytes 405512 | tf_op jit(solution)/shard_map/ppermute | solution.py:38
  69.9 27.8 %collective-permute-start.10 = (bf16[1056,128]{1,0:T(8,128)(2,1)S(1)}, bf16[1056,128]{1,0:T(8,128)(2,1)S(1)}, u32[]{:S(2)}, u32[]{:S(2)}) collective-permute-start(bf16[1056,128]{1,0:T(8,128)(2,1)S(1)} %get-tuple-element.9), channel_id=1, source_target_pairs={{0,128},{1,897},{2,130},{3,899},{4,132},{5,901},{6,134},{7,903},{8... | collective-permute-start | bytes 811016 | tf_op jit(solution)/shard_map/ppermute | solution.py:38
  77.5 36.9 %collective-permute-start.8 = (bf16[1056,128]{1,0:T(8,128)(2,1)S(1)}, bf16[1056,128]{1,0:T(8,128)(2,1)S(1)}, u32[]{:S(2)}, u32[]{:S(2)}) collective-permute-start(bf16[1056,128]{1,0:T(8,128)(2,1)S(1)} %get-tuple-element.9), channel_id=1, source_target_pairs={{0,8},{8,0},{1,9},{9,1},{2,10},{10,2},{3,11},{11,3},{4,12},{12,4},... | collective-permute-start | bytes 811016 | tf_op jit(solution)/shard_map/ppermute | solution.py:42
  79.4 4.4 %collective-permute-start.4 = (bf16[528,128]{1,0:T(8,128)(2,1)S(1)}, bf16[528,128]{1,0:T(8,128)(2,1)S(1)}, u32[]{:S(2)}, u32[]{:S(2)}) collective-permute-start(bf16[528,128]{1,0:T(8,128)(2,1)S(1)} %fusion.1), channel_id=1, source_target_pairs={{0,1},{1,33},{2,3},{3,35},{4,5},{5,37},{6,7},{7,39},{8,65},{9,97},... | collective-permute-start | bytes 405512 | tf_op jit(solution)/shard_map/ppermute | solution.py:38
  83.9 73.8 %collective-permute-start.5 = (bf16[1056,128]{1,0:T(8,128)(2,1)S(1)}, bf16[1056,128]{1,0:T(8,128)(2,1)}, u32[]{:S(2)}, u32[]{:S(2)}) collective-permute-start(bf16[1056,128]{1,0:T(8,128)(2,1)S(1)} %constant_dynamic-update-slice_fusion.refs_2_), channel_id=1, source_target_pairs={{0,8},{8,0},{1,9},{9,1},{2,10},{10,2},{3,11},{11,3},{4,12},{12,4},... | collective-permute-start | bytes 811016 | tf_op jit(solution)/shard_map/ppermute | solution.py:42
  97.7 26.6 %collective-permute-start.13 = (bf16[1056,128]{1,0:T(8,128)(2,1)S(1)}, bf16[1056,128]{1,0:T(8,128)(2,1)S(1)}, u32[]{:S(2)}, u32[]{:S(2)}) collective-permute-start(bf16[1056,128]{1,0:T(8,128)(2,1)S(1)} %collective-permute-done.10), channel_id=1, source_target_pairs={{0,128},{1,897},{2,130},{3,899},{4,132},{5,901},{6,134},{7,903},{8... | collective-permute-start | bytes 811016 | tf_op jit(solution)/shard_map/ppermute | solution.py:38
  112.4 19.7 %collective-permute-start.11 = (bf16[1056,128]{1,0:T(8,128)(2,1)S(1)}, bf16[1056,128]{1,0:T(8,128)(2,1)S(1)}, u32[]{:S(2)}, u32[]{:S(2)}) collective-permute-start(bf16[1056,128]{1,0:T(8,128)(2,1)S(1)} %collective-permute-done.10), channel_id=1, source_target_pairs={{0,8},{8,0},{1,9},{9,1},{2,10},{10,2},{3,11},{11,3},{4,12},{12,4},... | collective-permute-start | bytes 811016 | tf_op jit(solution)/shard_map/ppermute | solution.py:42
  114.4 43.3 %collective-permute-start.9 = (bf16[2112,128]{1,0:T(8,128)(2,1)S(1)}, bf16[2112,128]{1,0:T(8,128)(2,1)S(1)}, u32[]{:S(2)}, u32[]{:S(2)}) collective-permute-start(bf16[2112,128]{1,0:T(8,128)(2,1)S(1)} %constant_dynamic-update-slice_fusion.4.refs_4_), channel_id=1, source_target_pairs={{0,1},{1,0},{2,3},{3,2},{4,5},{5,4},{6,7},{7,6},{8,9},{9,8},{10,11... | collective-permute-start | bytes 1622024 | tf_op jit(solution)/shard_map/ppermute | solution.py:42
  124.2 32.7 %copy-start.9 = (s32[32]{0:T(128)S(1)}, s32[32]{0:T(128)}, u32[]{:S(2)}) copy-start(s32[32]{0:T(128)} %constant.159.clone) | copy-start | bytes 388
  124.3 32.7 %copy-start.10 = (s32[32]{0:T(128)S(1)}, s32[32]{0:T(128)}, u32[]{:S(2)}) copy-start(s32[32]{0:T(128)} %constant.158.clone) | copy-start | bytes 388
  124.3 32.7 %copy-start.11 = (s32[32]{0:T(128)S(1)}, s32[32]{0:T(128)}, u32[]{:S(2)}) copy-start(s32[32]{0:T(128)} %constant.157.clone) | copy-start | bytes 388
  124.3 32.8 %copy-start.8 = (s32[2]{0:T(128)S(1)}, s32[2]{0:T(128)}, u32[]{:S(2)}) copy-start(s32[2]{0:T(128)} %param.11) | copy-start | bytes 28
  124.3 11.9 %collective-permute-start.16 = (bf16[528,128]{1,0:T(8,128)(2,1)S(1)}, bf16[528,128]{1,0:T(8,128)(2,1)S(1)}, u32[]{:S(2)}, u32[]{:S(2)}) collective-permute-start(bf16[528,128]{1,0:T(8,128)(2,1)S(1)} %slice.16), channel_id=1, source_target_pairs={{0,128},{1,897},{2,130},{3,899},{4,132},{5,901},{6,134},{7,903},{8... | collective-permute-start | bytes 405512 | tf_op jit(solution)/shard_map/ppermute | solution.py:38
  132.2 25.5 %collective-permute-start.12 = (bf16[2112,128]{1,0:T(8,128)(2,1)S(1)}, bf16[2112,128]{1,0:T(8,128)(2,1)S(1)}, u32[]{:S(2)}, u32[]{:S(2)}) collective-permute-start(bf16[2112,128]{1,0:T(8,128)(2,1)S(1)} %constant_dynamic-update-slice_fusion.7.refs_6_), channel_id=1, source_target_pairs={{0,1},{1,0},{2,3},{3,2},{4,5},{5,4},{6,7},{7,6},{8,9},{9,8},{10,11... | collective-permute-start | bytes 1622024 | tf_op jit(solution)/shard_map/ppermute | solution.py:42
  134.1 15.9 %collective-permute-start.14 = (bf16[1056,128]{1,0:T(8,128)(2,1)S(1)}, bf16[1056,128]{1,0:T(8,128)(2,1)S(1)}, u32[]{:S(2)}, u32[]{:S(2)}) collective-permute-start(bf16[1056,128]{1,0:T(8,128)(2,1)S(1)} %collective-permute-done.13), channel_id=1, source_target_pairs={{0,8},{8,0},{1,9},{9,1},{2,10},{10,2},{3,11},{11,3},{4,12},{12,4},... | collective-permute-start | bytes 811016 | tf_op jit(solution)/shard_map/ppermute | solution.py:42
  136.2 18.2 %collective-permute-start.17 = (bf16[528,128]{1,0:T(8,128)(2,1)S(1)}, bf16[528,128]{1,0:T(8,128)(2,1)S(1)}, u32[]{:S(2)}, u32[]{:S(2)}) collective-permute-start(bf16[528,128]{1,0:T(8,128)(2,1)S(1)} %collective-permute-done.16), channel_id=1, source_target_pairs={{0,8},{8,0},{1,9},{9,1},{2,10},{10,2},{3,11},{11,3},{4,12},{12,4},... | collective-permute-start | bytes 405512 | tf_op jit(solution)/shard_map/ppermute | solution.py:42
  150.1 8.1 %collective-permute-start.15 = (bf16[2112,128]{1,0:T(8,128)(2,1)S(1)}, bf16[2112,128]{1,0:T(8,128)(2,1)}, u32[]{:S(2)}, u32[]{:S(2)}) collective-permute-start(bf16[2112,128]{1,0:T(8,128)(2,1)S(1)} %constant_dynamic-update-slice_fusion.9.refs_8_), channel_id=1, source_target_pairs={{0,1},{1,0},{2,3},{3,2},{4,5},{5,4},{6,7},{7,6},{8,9},{9,8},{10,11... | collective-permute-start | bytes 1622024 | tf_op jit(solution)/shard_map/ppermute | solution.py:42
  154.4 3.8 %collective-permute-start.18 = (bf16[1056,128]{1,0:T(8,128)(2,1)S(1)}, bf16[1056,128]{1,0:T(8,128)(2,1)}, u32[]{:S(2)}, u32[]{:S(2)}) collective-permute-start(bf16[1056,128]{1,0:T(8,128)(2,1)S(1)} %constant_dynamic-update-slice_fusion.11.refs_10_), channel_id=1, source_target_pairs={{0,1},{1,0},{2,3},{3,2},{4,5},{5,4},{6,7},{7,6},{8,9},{9,8},{10,11... | collective-permute-start | bytes 811016 | tf_op jit(solution)/shard_map/ppermute | solution.py:42
  163.3 2.2 copy-start
  173.6 11.8 %collective-permute-start.21 = (bf16[512,128]{1,0:T(8,128)(2,1)S(1)}, bf16[512,128]{1,0:T(8,128)(2,1)S(1)}, u32[]{:S(2)}, u32[]{:S(2)}) collective-permute-start(bf16[512,128]{1,0:T(8,128)(2,1)S(1)} %get-tuple-element.8.refs_1_), channel_id=1, source_target_pairs={{0,96},{32,0},{64,32},{96,64},{1,97},{33,1},{65,33},{97,65},{2,98}... | collective-permute-start | bytes 393224 | tf_op jit(solution)/shard_map/ppermute | solution.py:137
  181.1 12.6 %collective-permute-start.20 = (bf16[512,128]{1,0:T(8,128)(2,1)S(1)}, bf16[512,128]{1,0:T(8,128)(2,1)S(1)}, u32[]{:S(2)}, u32[]{:S(2)}) collective-permute-start(bf16[512,128]{1,0:T(8,128)(2,1)S(1)} %get-tuple-element.8.refs_1_), channel_id=1, source_target_pairs={{0,64},{32,96},{64,0},{96,32},{1,65},{33,97},{65,1},{97,33},{2,66}... | collective-permute-start | bytes 393224 | tf_op jit(solution)/shard_map/ppermute | solution.py:137
  183.0 10.7 %collective-permute-start.19 = (bf16[512,128]{1,0:T(8,128)(2,1)S(1)}, bf16[512,128]{1,0:T(8,128)(2,1)S(1)}, u32[]{:S(2)}, u32[]{:S(2)}) collective-permute-start(bf16[512,128]{1,0:T(8,128)(2,1)S(1)} %get-tuple-element.8.refs_1_), channel_id=1, source_target_pairs={{0,32},{32,64},{64,96},{96,0},{1,33},{33,65},{65,97},{97,1},{2,34}... | collective-permute-start | bytes 393224 | tf_op jit(solution)/shard_map/ppermute | solution.py:137
  194.6 3.4 %collective-permute-start.22 = (bf16[512,128]{1,0:T(8,128)(2,1)S(1)}, bf16[512,128]{1,0:T(8,128)(2,1)S(1)}, u32[]{:S(2)}, u32[]{:S(2)}) collective-permute-start(bf16[512,128]{1,0:T(8,128)(2,1)S(1)} %get-tuple-element.8.refs_1_), channel_id=1, source_target_pairs={{0,1},{1,0},{2,3},{3,2},{4,5},{5,4},{6,7},{7,6},{8,9},{9,8},{10,11... | collective-permute-start | bytes 393224 | tf_op jit(solution)/shard_map/ppermute | solution.py:42
  198.1 19.6 %collective-permute-start.24 = (bf16[1024,128]{1,0:T(8,128)(2,1)S(1)}, bf16[1024,128]{1,0:T(8,128)(2,1)S(1)}, u32[]{:S(2)}, u32[]{:S(2)}) collective-permute-start(bf16[1024,128]{1,0:T(8,128)(2,1)S(1)} %constant_dynamic-update-slice_fusion.13.refs_3_), channel_id=1, source_target_pairs={{0,128},{1,897},{2,130},{3,899},{4,132},{5,901},{6,134},{7,903},{8... | collective-permute-start | bytes 786440 | tf_op jit(solution)/shard_map/ppermute | solution.py:38
  217.7 16.3 %collective-permute-start.27 = (bf16[1024,128]{1,0:T(8,128)(2,1)S(1)}, bf16[1024,128]{1,0:T(8,128)(2,1)S(1)}, u32[]{:S(2)}, u32[]{:S(2)}) collective-permute-start(bf16[1024,128]{1,0:T(8,128)(2,1)S(1)} %collective-permute-done.24), channel_id=1, source_target_pairs={{0,128},{1,897},{2,130},{3,899},{4,132},{5,901},{6,134},{7,903},{8... | collective-permute-start | bytes 786440 | tf_op jit(solution)/shard_map/ppermute | solution.py:38
  224.4 14.8 %collective-permute-start.25 = (bf16[1024,128]{1,0:T(8,128)(2,1)S(1)}, bf16[1024,128]{1,0:T(8,128)(2,1)S(1)}, u32[]{:S(2)}, u32[]{:S(2)}) collective-permute-start(bf16[1024,128]{1,0:T(8,128)(2,1)S(1)} %collective-permute-done.24), channel_id=1, source_target_pairs={{0,8},{8,0},{1,9},{9,1},{2,10},{10,2},{3,11},{11,3},{4,12},{12,4},... | collective-permute-start | bytes 786440 | tf_op jit(solution)/shard_map/ppermute | solution.py:42
  234.0 16.3 %collective-permute-start.30 = (bf16[1024,128]{1,0:T(8,128)(2,1)S(1)}, bf16[1024,128]{1,0:T(8,128)(2,1)S(1)}, u32[]{:S(2)}, u32[]{:S(2)}) collective-permute-start(bf16[1024,128]{1,0:T(8,128)(2,1)S(1)} %collective-permute-done.27), channel_id=1, source_target_pairs={{0,128},{1,897},{2,130},{3,899},{4,132},{5,901},{6,134},{7,903},{8... | collective-permute-start | bytes 786440 | tf_op jit(solution)/shard_map/ppermute | solution.py:38
  237.0 17.4 %collective-permute-start.28 = (bf16[1024,128]{1,0:T(8,128)(2,1)S(1)}, bf16[1024,128]{1,0:T(8,128)(2,1)S(1)}, u32[]{:S(2)}, u32[]{:S(2)}) collective-permute-start(bf16[1024,128]{1,0:T(8,128)(2,1)S(1)} %collective-permute-done.27), channel_id=1, source_target_pairs={{0,8},{8,0},{1,9},{9,1},{2,10},{10,2},{3,11},{11,3},{4,12},{12,4},... | collective-permute-start | bytes 786440 | tf_op jit(solution)/shard_map/ppermute | solution.py:42
  239.3 47.2 %collective-permute-start.26 = (bf16[2048,128]{1,0:T(8,128)(2,1)S(1)}, bf16[2048,128]{1,0:T(8,128)(2,1)S(1)}, u32[]{:S(2)}, u32[]{:S(2)}) collective-permute-start(bf16[2048,128]{1,0:T(8,128)(2,1)S(1)} %constant_dynamic-update-slice_fusion.15.refs_5_), channel_id=1, source_target_pairs={{0,1},{1,0},{2,3},{3,2},{4,5},{5,4},{6,7},{7,6},{8,9},{9,8},{10,11... | collective-permute-start | bytes 1572872 | tf_op jit(solution)/shard_map/ppermute | solution.py:42
  250.3 9.8 %collective-permute-start.31 = (bf16[1024,128]{1,0:T(8,128)(2,1)S(1)}, bf16[1024,128]{1,0:T(8,128)(2,1)S(1)}, u32[]{:S(2)}, u32[]{:S(2)}) collective-permute-start(bf16[1024,128]{1,0:T(8,128)(2,1)S(1)} %collective-permute-done.30), channel_id=1, source_target_pairs={{0,8},{8,0},{1,9},{9,1},{2,10},{10,2},{3,11},{11,3},{4,12},{12,4},... | collective-permute-start | bytes 786440 | tf_op jit(solution)/shard_map/ppermute | solution.py:42
  252.5 12.5 %collective-permute-start.33 = (bf16[512,128]{1,0:T(8,128)(2,1)S(1)}, bf16[512,128]{1,0:T(8,128)(2,1)S(1)}, u32[]{:S(2)}, u32[]{:S(2)}) collective-permute-start(bf16[512,128]{1,0:T(8,128)(2,1)S(1)} %slice.17), channel_id=1, source_target_pairs={{0,128},{1,897},{2,130},{3,899},{4,132},{5,901},{6,134},{7,903},{8... | collective-permute-start | bytes 393224 | tf_op jit(solution)/shard_map/ppermute | solution.py:38
  254.5 32.7 %collective-permute-start.29 = (bf16[2048,128]{1,0:T(8,128)(2,1)S(1)}, bf16[2048,128]{1,0:T(8,128)(2,1)S(1)}, u32[]{:S(2)}, u32[]{:S(2)}) collective-permute-start(bf16[2048,128]{1,0:T(8,128)(2,1)S(1)} %constant_dynamic-update-slice_fusion.17.refs_7_), channel_id=1, source_target_pairs={{0,1},{1,0},{2,3},{3,2},{4,5},{5,4},{6,7},{7,6},{8,9},{9,8},{10,11... | collective-permute-start | bytes 1572872 | tf_op jit(solution)/shard_map/ppermute | solution.py:42
  260.2 27.1 %collective-permute-start.32 = (bf16[2048,128]{1,0:T(8,128)(2,1)S(1)}, bf16[2048,128]{1,0:T(8,128)(2,1)S(1)}, u32[]{:S(2)}, u32[]{:S(2)}) collective-permute-start(bf16[2048,128]{1,0:T(8,128)(2,1)S(1)} %constant_dynamic-update-slice_fusion.19.refs_9_), channel_id=1, source_target_pairs={{0,1},{1,0},{2,3},{3,2},{4,5},{5,4},{6,7},{7,6},{8,9},{9,8},{10,11... | collective-permute-start | bytes 1572872 | tf_op jit(solution)/shard_map/ppermute | solution.py:42
  265.0 10.3 %collective-permute-start.34 = (bf16[512,128]{1,0:T(8,128)(2,1)S(1)}, bf16[512,128]{1,0:T(8,128)(2,1)S(1)}, u32[]{:S(2)}, u32[]{:S(2)}) collective-permute-start(bf16[512,128]{1,0:T(8,128)(2,1)S(1)} %collective-permute-done.33), channel_id=1, source_target_pairs={{0,8},{8,0},{1,9},{9,1},{2,10},{10,2},{3,11},{11,3},{4,12},{12,4},... | collective-permute-start | bytes 393224 | tf_op jit(solution)/shard_map/ppermute | solution.py:42
  268.1 17.7 %collective-permute-start.23 = (bf16[1024,128]{1,0:T(8,128)(2,1)S(1)}, bf16[1024,128]{1,0:T(8,128)(2,1)S(1)}, u32[]{:S(2)}, u32[]{:S(2)}) collective-permute-start(bf16[1024,128]{1,0:T(8,128)(2,1)S(1)} %constant_dynamic-update-slice_fusion.13.refs_3_), channel_id=1, source_target_pairs={{0,8},{8,0},{1,9},{9,1},{2,10},{10,2},{3,11},{11,3},{4,12},{12,4},... | collective-permute-start | bytes 786440 | tf_op jit(solution)/shard_map/ppermute | solution.py:42
  275.3 11.2 %collective-permute-start.35 = (bf16[1024,128]{1,0:T(8,128)(2,1)S(1)}, bf16[1024,128]{1,0:T(8,128)(2,1)S(1)}, u32[]{:S(2)}, u32[]{:S(2)}) collective-permute-start(bf16[1024,128]{1,0:T(8,128)(2,1)S(1)} %constant_dynamic-update-slice_fusion.21.refs_11_), channel_id=1, source_target_pairs={{0,1},{1,0},{2,3},{3,2},{4,5},{5,4},{6,7},{7,6},{8,9},{9,8},{10,11... | collective-permute-start | bytes 786440 | tf_op jit(solution)/shard_map/ppermute | solution.py:42
  285.8 0.7 copy-start.4
  286.5 0.7 copy-start.6
  287.2 0.8 copy-start.2
  307.3 2.2 copy-start.1
  309.5 1.0 copy-start.3
  310.6 0.9 copy-start.5
  311.5 0.9 copy-start.7
  318.6 10.2 %collective-permute-start.36 = (bf16[512,128]{1,0:T(8,128)(2,1)S(1)}, bf16[512,128]{1,0:T(8,128)(2,1)S(1)}, u32[]{:S(2)}, u32[]{:S(2)}) collective-permute-start(bf16[512,128]{1,0:T(8,128)(2,1)S(1)} %shard_map.92), channel_id=1, source_target_pairs={{0,0},{1,32},{2,2},{3,34},{4,4},{5,36},{6,6},{7,38},{8,64},{9,96},... | collective-permute-start | bytes 393224 | tf_op jit(solution)/shard_map/ppermute | solution.py:38
Sparse Core Ops, SparseCore 0:
  40.0 123.3 all-gather.2
  194.7 112.5 all-gather.4

commit v4 on v3

v4 whole, which is shorter than its diff:
```python
import functools

import jax
import jax.numpy as jnp
import numpy as np
from jax import lax
from jax.experimental import pallas as pl
from jax.experimental.pallas import tpu as pltpu
from jax.sharding import Mesh, PartitionSpec as P

STEPS = 2
BS = 128
ROWS = 4 * BS
TAIL = 16
AXES = ("zh", "zl", "x", "y", "core")
SIZES = (8, 4, 4, 4, 2)


def swap(zh, zl, x, y, core):
    return zh, x, zl, y, core


def hop(zh, zl, x, y, core):
    return (zh + 1 - 2 * core) % 8, zl, x, y, core


def flip(zh, zl, x, y, core):
    return zh, zl, x, y, 1 - core


def move(part, *steps):
    pairs = []
    for i in range(1024):
        place = tuple(int(k) for k in np.unravel_index(i, SIZES))
        for step in steps:
            place = step(*place)
        pairs.append((i, int(np.ravel_multi_index(place, SIZES))))
    return lax.ppermute(part, AXES, pairs)


def across(part, axis, mask):
    size = SIZES[AXES.index(axis)]
    return lax.ppermute(part, axis, [(i, i ^ mask) for i in range(size)])


def kernel(rows, picks, first, branch, tab, *refs):
    slots, refs = (None, refs) if first else (refs[0], refs[1:])
    own, a_hbm, refs = refs[0], refs[1], refs[2:]
    parts, refs = refs[: len(picks)], refs[len(picks) :]
    if first:
        out, slots_out, a_all, b_all, acc, sems, slots, sem = refs
    else:
        out, a_all, b_all, acc, sems = refs
    copies = [pltpu.make_async_copy(a_hbm, a_all, sems.at[0])]
    for part, wanted in zip(parts, picks):
        for k in wanted:
            at = len(copies)
            copies.append(
                pltpu.make_async_copy(
                    part.at[pl.ds(k * rows, rows)],
                    b_all.at[pl.ds((at - 1) * rows, rows)],
                    sems.at[at],
                )
            )
    for copy in copies:
        copy.start()
    nothing = 32 * rows
    b_all[nothing : nothing + BS, :] = jnp.zeros((BS, BS), jnp.bfloat16)
    acc[...] = jnp.zeros_like(acc)
    for copy in copies:
        copy.wait()
    if first:
        for base, whole in ((0, a_all), (32, b_all)):
            for k in range(32):
                row = whole[k * rows + ROWS : (k + 1) * rows, :].astype(jnp.float32)[0:1]
                slots_out[base + k : base + k + 1, :] = row.astype(jnp.int32)
        copy = pltpu.make_async_copy(slots_out, slots, sem)
        copy.start()
        copy.wait()
    mine = [slots[tab[32], j] for j in range(4)]

    def pair(t, carry):
        las = [tab[2 * t + k] for k in range(2)]
        for j in range(4):
            lefts, rights = [], []
            for k in range(2):
                m = slots[las[k], j]
                hit = slots[32 + 2 * t + k, m] == mine[j]
                right = jnp.where(hit, (2 * t + k) * rows + m * BS, nothing)
                rights.append(b_all[pl.ds(pl.multiple_of(right, 16), BS), :])
                left = las[k] * rows + j * BS
                lefts.append(a_all[pl.ds(pl.multiple_of(left, 16), BS), :])
            acc[j * BS : (j + 1) * BS, :] += jnp.dot(
                jnp.concatenate(lefts, 1),
                jnp.concatenate(rights, 0),
                preferred_element_type=jnp.float32,
            )
        return carry

    lax.fori_loop(0, 16, pair, 0)
    square = acc[...]
    twice = 2.0 * own[:ROWS, :].astype(jnp.float32) - square
    out[...] = jnp.where(branch[0] == 1, twice, square).astype(out.dtype)


def multiply(branch, tab, slots, own, a_all, placed):
    first, rows = slots is None, own.shape[0]
    parts = [part for part, _ in placed]
    picks = [list(names) for _, names in placed]
    smem = pl.BlockSpec(memory_space=pltpu.SMEM)
    vmem = pl.BlockSpec(memory_space=pltpu.VMEM)
    anywhere = pl.BlockSpec(memory_space=pl.ANY)
    out_shape = [jax.ShapeDtypeStruct((ROWS, BS), jnp.bfloat16)]
    scratch = [
        pltpu.VMEM((32 * rows, BS), jnp.bfloat16),
        pltpu.VMEM((32 * rows + BS, BS), jnp.bfloat16),
        pltpu.VMEM((ROWS, BS), jnp.float32),
        pltpu.SemaphoreType.DMA((33,)),
    ]
    if first:
        out_shape.append(jax.ShapeDtypeStruct((64, BS), jnp.int32))
        scratch += [pltpu.SMEM((64, BS), jnp.int32), pltpu.SemaphoreType.DMA]
    done = pl.pallas_call(
        functools.partial(kernel, rows, picks, first),
        out_shape=out_shape,
        in_specs=[smem] * (2 if first else 3) + [vmem] + [anywhere] * (1 + len(parts)),
        out_specs=[vmem] * len(out_shape),
        scratch_shapes=scratch,
        compiler_params=pltpu.CompilerParams(vmem_limit_bytes=52 * 1024 * 1024),
        cost_estimate=pl.CostEstimate(
            flops=2 * 128 * BS**3, bytes_accessed=64 * ROWS * BS * 2, transcendentals=0
        ),
    )(branch, tab, *([] if first else [slots]), own, a_all, *parts)
    return done[0], done[1] if first else slots


def together(*parts):
    return lax.optimization_barrier(parts)


def gather(unit, up, down):
    rows = unit.shape[0]
    near = [unit]
    for by in (1, 2, 3):
        near.append(lax.ppermute(unit, "zl", [(i, (i + by) % 4) for i in range(4)]))
    near = jnp.concatenate(near)
    near, up, down = together(near, up, down)
    a_all = lax.all_gather(near, ("y", "core"), axis=0, tiled=True)
    hop1 = jnp.concatenate([up, down])
    hop2 = move(hop1, hop)
    one0, one1 = across(unit, "x", 1), across(hop1, "x", 1)
    hop2, one0, one1 = together(hop2, one0, one1)

    hop3 = move(hop2, hop)
    two0 = across(jnp.concatenate([unit, one0]), "x", 3)
    two1 = across(jnp.concatenate([hop1, one1]), "x", 3)
    one2 = across(hop2, "x", 1)
    hop3, two0, two1, one2 = together(hop3, two0, two1, one2)

    hop4 = move(hop3[:rows], hop)
    two2, one3 = across(jnp.concatenate([hop2, one2]), "x", 3), across(hop3, "x", 1)
    far1 = to_other(rows, hop1, one1, two1)
    hop4, two2, one3, far1 = together(hop4, two2, one3, far1)

    two3 = across(jnp.concatenate([hop3, one3]), "x", 3)
    last = [across(hop4, "x", f) for f in (1, 3, 2)]
    far2 = to_other(rows, hop2, one2, two2)
    two3, far2, *last = together(two3, far2, *last)

    far3 = to_other(rows, hop3, one3, two3)
    placed = [(unit, {0: (0, 0)}), (one0, {0: (0, 1)}), (two0, {0: (0, 3), 1: (0, 2)})]
    for k, one, two, three, far in ((1, hop1, one1, two1, far1), (2, hop2, one2, two2, far2)):
        placed += parted(k, one, two, three, far)
    placed += [(hop4, {0: (4, 0)})] + [(q, {0: (4, f)}) for q, f in zip(last, (1, 3, 2))]
    placed += parted(3, hop3, one3, two3, far3)
    return a_all, placed


def to_other(rows, got, one, two):
    theirs = [got[rows:], one[rows:], two[rows : 2 * rows], two[3 * rows :]]
    return across(jnp.concatenate(theirs), "core", 1)


def parted(k, got, one, two, far):
    return [
        (got, {0: (k, 0)}),
        (one, {0: (k, 1)}),
        (two, {0: (k, 3), 2: (k, 2)}),
        (far, {i: (-k, f) for i, f in enumerate((0, 1, 3, 2))}),
    ]


def table(placed):
    zh, zl, x, y, core = (lax.axis_index(name) for name in AXES)
    names = np.concatenate([np.array(list(n.values())) for _, n in placed])
    p = (zh - (1 - 2 * core) * names[:, 0]) % 8 * 4 + (x ^ names[:, 1])
    la = p % 8 * 4 + (zl - p // 8) % 4
    return jnp.concatenate([la, jnp.reshape((y * 2 + core) * 4, (1,))]).astype(jnp.int32)


def body(values, column_slot_index, branches):
    flat = values.reshape(ROWS, BS)
    tail = column_slot_index[:, 0].astype(jnp.bfloat16)[None]
    start = jnp.concatenate([flat, jnp.pad(tail, ((0, TAIL - 1), (0, BS - 4)))])
    unit, up, down = (move(start, swap, *more) for more in ((), (hop,), (flip, hop)))
    slots = None
    for step in range(STEPS):
        if step:
            up, down = move(unit, hop), move(unit, flip, hop)
        a_all, placed = gather(unit, up, down)
        unit, slots = multiply(
            branches[step : step + 1], table(placed), slots, unit, a_all, placed
        )
    return move(unit, swap).reshape(values.shape)


def solution(mesh):
    fine = Mesh(mesh.devices.reshape(SIZES), AXES)
    split = (("zh", "zl"), ("x", "y", "core"))
    in_specs = (P(*split, None, None), P(*split), P())
    return jax.shard_map(
        body, mesh=fine, in_specs=in_specs, out_specs=P(*split, None, None), check_vma=False
    )
```

time: 339 us -> 341 us (level)
  the two profiles are of different devices: /device:TPU:1 before, /device:TPU:26 now
where the time goes in v4:
time: 341 us; the launch traced here: 340 us
  starting transfers between devices  196 us (57%)
  waiting for transfers between devices  102 us (30%)
  Pallas kernels  18.8 us (6%)
  between operations  14.4 us (4%)
  other arithmetic  4.83 us (1%)
  local copies, waits for them, and re-layouts  4.28 us (1%)
    ppermute x28, starting transfers between devices, across(): return lax.ppermute(part, axis, [(i, i ^ mask) for i in range(size)])  103 us
    ppermute x12, starting transfers between devices, move(): return lax.ppermute(part, AXES, pairs)  72.1 us
    ppermute x12, waiting for transfers between devices, move(): return lax.ppermute(part, AXES, pairs)  66.4 us
    ppermute x28, waiting for transfers between devices, across(): return lax.ppermute(part, axis, [(i, i ^ mask) for i in range(size)])  35.1 us
    ppermute x6, starting transfers between devices, gather(): near.append(lax.ppermute(unit, 'zl', [(i, (i + by) % 4) for i in range(4)]))  20.1 us
    pallas_call x2, Pallas kernels, multiply(): pl.pallas_call(functools.partial(kernel, rows, picks, first), out_shape=o...  18.8 us
  transfers between devices with their start and end apart: 48, of which 16 were waited for; matrix products, arithmetic and copies ran while one was open for 1% of the time, Pallas kernels for 0%

profile of v4, /device:TPU:26, one launch (start us, length us, event | category | flops | bytes accessed | tf_op | source)
XLA Modules:
  0.0 339.5 jit_solution(3688293772886344294)
XLA Ops:
  8.1 3.8 %collective-permute-start = (bf16[528,128]{1,0:T(8,128)(2,1)S(1)}, bf16[528,128]{1,0:T(8,128)(2,1)S(1)}, u32[]{:S(2)}, u32[]{:S(2)}) collective-permute-start(bf16[528,128]{1,0:T(8,128)(2,1)S(1)} %fusion.1), channel_id=1, source_target_pairs={{0,0},{1,1},{2,2},{3,3},{4,4},{5,5},{6,6},{7,7},{8,32},{9,33},{10,... | collective-permute-start | bytes 405512 | tf_op jit(solution)/shard_map/ppermute | solution.py:38
  11.9 10.1 %collective-permute-done.refs_0_.refs_2_ = bf16[528,128]{1,0:T(8,128)(2,1)S(1)} collective-permute-done((bf16[528,128]{1,0:T(8,128)(2,1)S(1)}, bf16[528,128]{1,0:T(8,128)(2,1)S(1)}, u32[]{:S(2)}, u32[]{:S(2)}) %collective-permute-start) | collective-permute-done | bytes 135200 | tf_op jit(solution)/shard_map/ppermute | solution.py:38
  22.0 1.9 collective-permute-start.1
  23.9 6.7 %collective-permute-start.2 = (bf16[528,128]{1,0:T(8,128)(2,1)S(1)}, bf16[528,128]{1,0:T(8,128)(2,1)S(1)}, u32[]{:S(2)}, u32[]{:S(2)}) collective-permute-start(bf16[528,128]{1,0:T(8,128)(2,1)S(1)} %collective-permute-done.refs_0_.refs_2_), channel_id=1, source_target_pairs={{0,64},{32,96},{64,0},{96,32},{1,65},{33,97},{65,1},{97,33},{2,66}... | collective-permute-start | bytes 405512 | tf_op jit(solution)/shard_map/ppermute | solution.py:145
  30.6 1.9 collective-permute-start.3
  32.5 8.4 %collective-permute-start.4 = (bf16[528,128]{1,0:T(8,128)(2,1)S(1)}, bf16[528,128]{1,0:T(8,128)(2,1)S(1)}, u32[]{:S(2)}, u32[]{:S(2)}) collective-permute-start(bf16[528,128]{1,0:T(8,128)(2,1)S(1)} %fusion.1), channel_id=1, source_target_pairs={{0,128},{1,897},{2,130},{3,899},{4,132},{5,901},{6,134},{7,903},{8... | collective-permute-start | bytes 405512 | tf_op jit(solution)/shard_map/ppermute | solution.py:38
  40.9 14.0 %collective-permute-start.5 = (bf16[528,128]{1,0:T(8,128)(2,1)S(1)}, bf16[528,128]{1,0:T(8,128)(2,1)S(1)}, u32[]{:S(2)}, u32[]{:S(2)}) collective-permute-start(bf16[528,128]{1,0:T(8,128)(2,1)S(1)} %fusion.1), channel_id=1, source_target_pairs={{0,897},{1,128},{2,899},{3,130},{4,901},{5,132},{6,903},{7,134},{8... | collective-permute-start | bytes 405512 | tf_op jit(solution)/shard_map/ppermute | solution.py:38
  55.8 1.6 collective-permute-done.4
  57.4 2.7 collective-permute-done.5
  60.3 3.3 collective-permute-start.6
  63.6 1.9 collective-permute-start.8
  65.5 3.9 %collective-permute-start.7 = (bf16[528,128]{1,0:T(8,128)(2,1)S(1)}, bf16[528,128]{1,0:T(8,128)(2,1)S(1)}, u32[]{:S(2)}, u32[]{:S(2)}) collective-permute-start(bf16[528,128]{1,0:T(8,128)(2,1)S(1)} %collective-permute-done.refs_0_.refs_2_), channel_id=1, source_target_pairs={{0,8},{8,0},{16,24},{24,16},{1,9},{9,1},{17,25},{25,17},{2,10},{10... | collective-permute-start | bytes 405512 | tf_op jit(solution)/shard_map/ppermute | solution.py:43
  69.5 3.9 %collective-permute-done.7.refs_3_ = bf16[528,128]{1,0:T(8,128)(2,1)S(1)} collective-permute-done((bf16[528,128]{1,0:T(8,128)(2,1)S(1)}, bf16[528,128]{1,0:T(8,128)(2,1)S(1)}, u32[]{:S(2)}, u32[]{:S(2)}) %collective-permute-start.7) | collective-permute-done | bytes 135200 | tf_op jit(solution)/shard_map/ppermute | solution.py:43
  73.5 7.2 %collective-permute-start.11 = (bf16[2112,128]{1,0:T(8,128)(2,1)S(1)}, bf16[2112,128]{1,0:T(8,128)(2,1)S(1)}, u32[]{:S(2)}, u32[]{:S(2)}) collective-permute-start(bf16[2112,128]{1,0:T(8,128)(2,1)S(1)} %pad_maximum_fusion.1), channel_id=1, source_target_pairs={{0,24},{8,16},{16,8},{24,0},{1,25},{9,17},{17,9},{25,1},{2,26},{10... | collective-permute-start | bytes 1622024 | tf_op jit(solution)/shard_map/ppermute | solution.py:43
  80.7 1.9 collective-permute-start.10
  82.6 4.0 %collective-permute-start.12 = (bf16[1056,128]{1,0:T(8,128)(2,1)S(1)}, bf16[1056,128]{1,0:T(8,128)(2,1)S(1)}, u32[]{:S(2)}, u32[]{:S(2)}) collective-permute-start(bf16[1056,128]{1,0:T(8,128)(2,1)S(1)} %collective-permute-done.6.refs_9_), channel_id=1, source_target_pairs={{0,8},{8,0},{16,24},{24,16},{1,9},{9,1},{17,25},{25,17},{2,10},{10... | collective-permute-start | bytes 811016 | tf_op jit(solution)/shard_map/ppermute | solution.py:43
  86.7 9.6 %collective-permute-start.9 = (bf16[1056,128]{1,0:T(8,128)(2,1)S(1)}, bf16[1056,128]{1,0:T(8,128)(2,1)S(1)}, u32[]{:S(2)}, u32[]{:S(2)}) collective-permute-start(bf16[1056,128]{1,0:T(8,128)(2,1)S(1)} %collective-permute-done.6.refs_9_), channel_id=1, source_target_pairs={{0,128},{1,897},{2,130},{3,899},{4,132},{5,901},{6,134},{7,903},{8... | collective-permute-start | bytes 811016 | tf_op jit(solution)/shard_map/ppermute | solution.py:38
  96.3 3.9 %collective-permute-done.9.refs_17_ = bf16[1056,128]{1,0:T(8,128)(2,1)S(1)} collective-permute-done((bf16[1056,128]{1,0:T(8,128)(2,1)S(1)}, bf16[1056,128]{1,0:T(8,128)(2,1)S(1)}, u32[]{:S(2)}, u32[]{:S(2)}) %collective-permute-start.9) | collective-permute-done | bytes 270368 | tf_op jit(solution)/shard_map/ppermute | solution.py:38
  100.3 17.7 %collective-permute-start.16 = (bf16[2112,128]{1,0:T(8,128)(2,1)S(1)}, bf16[2112,128]{1,0:T(8,128)(2,1)S(1)}, u32[]{:S(2)}, u32[]{:S(2)}) collective-permute-start(bf16[2112,128]{1,0:T(8,128)(2,1)S(1)} %pad_maximum_fusion.3), channel_id=1, source_target_pairs={{0,1},{1,0},{2,3},{3,2},{4,5},{5,4},{6,7},{7,6},{8,9},{9,8},{10,11... | collective-permute-start | bytes 1622024 | tf_op jit(solution)/shard_map/ppermute | solution.py:43
  118.1 3.1 collective-permute-start.14
  121.3 2.8 collective-permute-start.15
  124.1 1.9 collective-permute-start.13
  126.1 11.9 %collective-permute-done.13.refs_13_ = bf16[528,128]{1,0:T(8,128)(2,1)S(1)} collective-permute-done((bf16[528,128]{1,0:T(8,128)(2,1)S(1)}, bf16[528,128]{1,0:T(8,128)(2,1)S(1)}, u32[]{:S(2)}, u32[]{:S(2)}) %collective-permute-start.13) | collective-permute-done | bytes 135200 | tf_op jit(solution)/shard_map/ppermute | solution.py:38
  139.1 1.9 collective-permute-start.18
  141.1 2.1 collective-permute-start.17
  143.2 1.9 collective-permute-start.19
  145.1 4.2 %collective-permute-start.20 = (bf16[528,128]{1,0:T(8,128)(2,1)S(1)}, bf16[528,128]{1,0:T(8,128)(2,1)S(1)}, u32[]{:S(2)}, u32[]{:S(2)}) collective-permute-start(bf16[528,128]{1,0:T(8,128)(2,1)S(1)} %collective-permute-done.13.refs_13_), channel_id=1, source_target_pairs={{0,24},{8,16},{16,8},{24,0},{1,25},{9,17},{17,9},{25,1},{2,26},{10... | collective-permute-start | bytes 405512 | tf_op jit(solution)/shard_map/ppermute | solution.py:43
  149.3 3.7 %collective-permute-start.21 = (bf16[528,128]{1,0:T(8,128)(2,1)S(1)}, bf16[528,128]{1,0:T(8,128)(2,1)S(1)}, u32[]{:S(2)}, u32[]{:S(2)}) collective-permute-start(bf16[528,128]{1,0:T(8,128)(2,1)S(1)} %collective-permute-done.13.refs_13_), channel_id=1, source_target_pairs={{0,16},{8,24},{16,0},{24,8},{1,17},{9,25},{17,1},{25,9},{2,18},{10... | collective-permute-start | bytes 405512 | tf_op jit(solution)/shard_map/ppermute | solution.py:43
  153.0 10.6 %collective-permute-done.20.refs_15_ = bf16[528,128]{1,0:T(8,128)(2,1)S(1)} collective-permute-done((bf16[528,128]{1,0:T(8,128)(2,1)S(1)}, bf16[528,128]{1,0:T(8,128)(2,1)S(1)}, u32[]{:S(2)}, u32[]{:S(2)}) %collective-permute-start.20) | collective-permute-done | bytes 135200 | tf_op jit(solution)/shard_map/ppermute | solution.py:43
  164.6 1.9 collective-permute-start.22
  167.3 1.4 collective-permute-done.22.refs_20_
  169.5 9.7 %shard_map.73 = (bf16[512,128]{1,0:T(8,128)(2,1)S(1)}, s32[64,128]{1,0:T(8,128)S(1)}) custom-call(s32[1]{0:T(128)} %get-tuple-element.101.branch, s32[33]{0:T(128)S(1)} %pad_add_fusion.tab, bf16[528,128]{1,0:T(8,128)(2,1)S(1)} %collective-permute-done.refs_0_.refs_2_, bf16[16896,128]{1,0:T(8,128)(2,1)} %all-gather.3.cloned.1.call-done.refs_1_, ...), custom_call_target="tpu_custom_call" | custom-call | flops 536870912 | bytes 8388608 | tf_op jit(solution)/shard_map/pallas_call | solution.py:123
  179.2 1.9 collective-permute-start.23
  181.2 5.4 %collective-permute-start.24 = (bf16[512,128]{1,0:T(8,128)(2,1)S(1)}, bf16[512,128]{1,0:T(8,128)(2,1)S(1)}, u32[]{:S(2)}, u32[]{:S(2)}) collective-permute-start(bf16[512,128]{1,0:T(8,128)(2,1)S(1)} %get-tuple-element.65.refs_1_.refs_3_), channel_id=1, source_target_pairs={{0,64},{32,96},{64,0},{96,32},{1,65},{33,97},{65,1},{97,33},{2,66}... | collective-permute-start | bytes 393224 | tf_op jit(solution)/shard_map/ppermute | solution.py:145
  186.6 2.2 collective-permute-start.25
  188.8 6.3 %collective-permute-start.26 = (bf16[512,128]{1,0:T(8,128)(2,1)S(1)}, bf16[512,128]{1,0:T(8,128)(2,1)S(1)}, u32[]{:S(2)}, u32[]{:S(2)}) collective-permute-start(bf16[512,128]{1,0:T(8,128)(2,1)S(1)} %get-tuple-element.65.refs_1_.refs_3_), channel_id=1, source_target_pairs={{0,128},{1,897},{2,130},{3,899},{4,132},{5,901},{6,134},{7,903},{8... | collective-permute-start | bytes 393224 | tf_op jit(solution)/shard_map/ppermute | solution.py:38
  195.1 5.0 %collective-permute-start.27 = (bf16[512,128]{1,0:T(8,128)(2,1)S(1)}, bf16[512,128]{1,0:T(8,128)(2,1)S(1)}, u32[]{:S(2)}, u32[]{:S(2)}) collective-permute-start(bf16[512,128]{1,0:T(8,128)(2,1)S(1)} %get-tuple-element.65.refs_1_.refs_3_), channel_id=1, source_target_pairs={{0,897},{1,128},{2,899},{3,130},{4,901},{5,132},{6,903},{7,134},{8... | collective-permute-start | bytes 393224 | tf_op jit(solution)/shard_map/ppermute | solution.py:38
  201.0 6.4 %collective-permute-done.27 = bf16[512,128]{1,0:T(8,128)(2,1)S(1)} collective-permute-done((bf16[512,128]{1,0:T(8,128)(2,1)S(1)}, bf16[512,128]{1,0:T(8,128)(2,1)S(1)}, u32[]{:S(2)}, u32[]{:S(2)}) %collective-permute-start.27) | collective-permute-done | bytes 131104 | tf_op jit(solution)/shard_map/ppermute | solution.py:38
  207.4 8.5 %collective-permute-start.28 = (bf16[1024,128]{1,0:T(8,128)(2,1)S(1)}, bf16[1024,128]{1,0:T(8,128)(2,1)S(1)}, u32[]{:S(2)}, u32[]{:S(2)}) collective-permute-start(bf16[1024,128]{1,0:T(8,128)(2,1)S(1)} %constant_dynamic-update-slice_fusion.2.refs_6_), channel_id=1, source_target_pairs={{0,128},{1,897},{2,130},{3,899},{4,132},{5,901},{6,134},{7,903},{8... | collective-permute-start | bytes 786440 | tf_op jit(solution)/shard_map/ppermute | solution.py:38
  215.9 6.5 %collective-permute-start.30 = (bf16[1024,128]{1,0:T(8,128)(2,1)S(1)}, bf16[1024,128]{1,0:T(8,128)(2,1)S(1)}, u32[]{:S(2)}, u32[]{:S(2)}) collective-permute-start(bf16[1024,128]{1,0:T(8,128)(2,1)S(1)} %constant_dynamic-update-slice_fusion.2.refs_6_), channel_id=1, source_target_pairs={{0,8},{8,0},{16,24},{24,16},{1,9},{9,1},{17,25},{25,17},{2,10},{10... | collective-permute-start | bytes 786440 | tf_op jit(solution)/shard_map/ppermute | solution.py:43
  222.4 1.9 collective-permute-start.29
  224.3 4.9 %collective-permute-done.29.refs_4_ = bf16[512,128]{1,0:T(8,128)(2,1)S(1)} collective-permute-done((bf16[512,128]{1,0:T(8,128)(2,1)S(1)}, bf16[512,128]{1,0:T(8,128)(2,1)S(1)}, u32[]{:S(2)}, u32[]{:S(2)}) %collective-permute-start.29) | collective-permute-done | bytes 131104 | tf_op jit(solution)/shard_map/ppermute | solution.py:43
  229.3 3.1 collective-permute-start.33
  232.4 2.7 collective-permute-start.32
  235.2 6.6 %collective-permute-start.31 = (bf16[1024,128]{1,0:T(8,128)(2,1)S(1)}, bf16[1024,128]{1,0:T(8,128)(2,1)S(1)}, u32[]{:S(2)}, u32[]{:S(2)}) collective-permute-start(bf16[1024,128]{1,0:T(8,128)(2,1)S(1)} %collective-permute-done.28.refs_10_), channel_id=1, source_target_pairs={{0,128},{1,897},{2,130},{3,899},{4,132},{5,901},{6,134},{7,903},{8... | collective-permute-start | bytes 786440 | tf_op jit(solution)/shard_map/ppermute | solution.py:38
  241.8 5.3 %collective-permute-start.34 = (bf16[1024,128]{1,0:T(8,128)(2,1)S(1)}, bf16[1024,128]{1,0:T(8,128)(2,1)S(1)}, u32[]{:S(2)}, u32[]{:S(2)}) collective-permute-start(bf16[1024,128]{1,0:T(8,128)(2,1)S(1)} %collective-permute-done.28.refs_10_), channel_id=1, source_target_pairs={{0,8},{8,0},{16,24},{24,16},{1,9},{9,1},{17,25},{25,17},{2,10},{10... | collective-permute-start | bytes 786440 | tf_op jit(solution)/shard_map/ppermute | solution.py:43
  247.1 2.2 collective-permute-done.32.refs_5_
  249.3 6.4 %collective-permute-done.31.refs_18_ = bf16[1024,128]{1,0:T(8,128)(2,1)S(1)} collective-permute-done((bf16[1024,128]{1,0:T(8,128)(2,1)S(1)}, bf16[1024,128]{1,0:T(8,128)(2,1)S(1)}, u32[]{:S(2)}, u32[]{:S(2)}) %collective-permute-start.31) | collective-permute-done | bytes 262176 | tf_op jit(solution)/shard_map/ppermute | solution.py:38
  255.8 1.9 collective-permute-start.38
  257.8 3.1 collective-permute-start.36
  260.9 5.0 %collective-permute-start.37 = (bf16[1024,128]{1,0:T(8,128)(2,1)S(1)}, bf16[1024,128]{1,0:T(8,128)(2,1)S(1)}, u32[]{:S(2)}, u32[]{:S(2)}) collective-permute-start(bf16[1024,128]{1,0:T(8,128)(2,1)S(1)} %collective-permute-done.31.refs_18_), channel_id=1, source_target_pairs={{0,8},{8,0},{16,24},{24,16},{1,9},{9,1},{17,25},{25,17},{2,10},{10... | collective-permute-start | bytes 786440 | tf_op jit(solution)/shard_map/ppermute | solution.py:43
  265.9 2.8 collective-permute-start.35
  268.8 11.4 %collective-permute-done.35.refs_14_ = bf16[512,128]{1,0:T(8,128)(2,1)S(1)} collective-permute-done((bf16[512,128]{1,0:T(8,128)(2,1)S(1)}, bf16[512,128]{1,0:T(8,128)(2,1)S(1)}, u32[]{:S(2)}, u32[]{:S(2)}) %collective-permute-start.35) | collective-permute-done | bytes 131104 | tf_op jit(solution)/shard_map/ppermute | solution.py:38
  281.1 1.9 collective-permute-start.40
  283.1 1.9 collective-permute-start.39
  285.0 3.0 collective-permute-start.41
  288.1 3.4 %collective-permute-start.42 = (bf16[512,128]{1,0:T(8,128)(2,1)S(1)}, bf16[512,128]{1,0:T(8,128)(2,1)S(1)}, u32[]{:S(2)}, u32[]{:S(2)}) collective-permute-start(bf16[512,128]{1,0:T(8,128)(2,1)S(1)} %collective-permute-done.35.refs_14_), channel_id=1, source_target_pairs={{0,24},{8,16},{16,8},{24,0},{1,25},{9,17},{17,9},{25,1},{2,26},{10... | collective-permute-start | bytes 393224 | tf_op jit(solution)/shard_map/ppermute | solution.py:43
  291.5 3.4 collective-permute-start.43
  294.9 10.0 %collective-permute-done.42.refs_16_ = bf16[512,128]{1,0:T(8,128)(2,1)S(1)} collective-permute-done((bf16[512,128]{1,0:T(8,128)(2,1)S(1)}, bf16[512,128]{1,0:T(8,128)(2,1)S(1)}, u32[]{:S(2)}, u32[]{:S(2)}) %collective-permute-start.42) | collective-permute-done | bytes 131104 | tf_op jit(solution)/shard_map/ppermute | solution.py:43
  305.0 1.9 collective-permute-start.44
  307.0 2.0 collective-permute-done.44.refs_21_
  309.0 9.1 %shard_map.74 = bf16[512,128]{1,0:T(8,128)(2,1)S(1)} custom-call(s32[1]{0:T(128)} %get-tuple-element.102.branch, s32[33]{0:T(128)S(1)} %pad_add_fusion.tab, s32[64,128]{1,0:T(8,128)S(1)} %get-tuple-element.64.refs_0_, bf16[512,128]{1,0:T(8,128)(2,1)S(1)} %get-tuple-element.65.refs_1_.refs_3_, bf16[16384,128]{1,0:T(8,128)(2,1)} %all-gather.5.cloned.1.call-done.refs_2_, ...), custom_call_target="tpu_custom_call" | custom-call | flops 536870912 | bytes 8388608 | tf_op jit(solution)/shard_map/pallas_call | solution.py:123
  318.1 1.9 collective-permute-start.45
  320.0 12.0 %collective-permute-done.45 = bf16[512,128]{1,0:T(8,128)(2,1)S(1)} collective-permute-done((bf16[512,128]{1,0:T(8,128)(2,1)S(1)}, bf16[512,128]{1,0:T(8,128)(2,1)S(1)}, u32[]{:S(2)}, u32[]{:S(2)}) %collective-permute-start.45) | collective-permute-done | bytes 131104 | tf_op jit(solution)/shard_map/ppermute | solution.py:38
  (120 shorter events, 9.3 us)
Async XLA Ops:
  6.5 162.1 %all-gather.3.cloned.1.call-start = ((), (), s32[]{:S(2)}) async-start(), calls=%async_computation | async-start | bytes 4866048 | tf_op jit(solution)/shard_map/all_gather | solution.py:148
  8.1 13.9 %collective-permute-start = (bf16[528,128]{1,0:T(8,128)(2,1)S(1)}, bf16[528,128]{1,0:T(8,128)(2,1)S(1)}, u32[]{:S(2)}, u32[]{:S(2)}) collective-permute-start(bf16[528,128]{1,0:T(8,128)(2,1)S(1)} %fusion.1), channel_id=1, source_target_pairs={{0,0},{1,1},{2,2},{3,3},{4,4},{5,5},{6,6},{7,7},{8,32},{9,33},{10,... | collective-permute-start | bytes 405512 | tf_op jit(solution)/shard_map/ppermute | solution.py:38
  22.0 32.9 %collective-permute-start.1 = (bf16[528,128]{1,0:T(8,128)(2,1)S(1)}, bf16[528,128]{1,0:T(8,128)(2,1)S(1)}, u32[]{:S(2)}, u32[]{:S(2)}) collective-permute-start(bf16[528,128]{1,0:T(8,128)(2,1)S(1)} %collective-permute-done.refs_0_.refs_2_), channel_id=1, source_target_pairs={{0,32},{32,64},{64,96},{96,0},{1,33},{33,65},{65,97},{97,1},{2,34}... | collective-permute-start | bytes 405512 | tf_op jit(solution)/shard_map/ppermute | solution.py:145
  23.9 31.0 %collective-permute-start.2 = (bf16[528,128]{1,0:T(8,128)(2,1)S(1)}, bf16[528,128]{1,0:T(8,128)(2,1)S(1)}, u32[]{:S(2)}, u32[]{:S(2)}) collective-permute-start(bf16[528,128]{1,0:T(8,128)(2,1)S(1)} %collective-permute-done.refs_0_.refs_2_), channel_id=1, source_target_pairs={{0,64},{32,96},{64,0},{96,32},{1,65},{33,97},{65,1},{97,33},{2,66}... | collective-permute-start | bytes 405512 | tf_op jit(solution)/shard_map/ppermute | solution.py:145
  30.6 24.4 %collective-permute-start.3 = (bf16[528,128]{1,0:T(8,128)(2,1)S(1)}, bf16[528,128]{1,0:T(8,128)(2,1)S(1)}, u32[]{:S(2)}, u32[]{:S(2)}) collective-permute-start(bf16[528,128]{1,0:T(8,128)(2,1)S(1)} %collective-permute-done.refs_0_.refs_2_), channel_id=1, source_target_pairs={{0,96},{32,0},{64,32},{96,64},{1,97},{33,1},{65,33},{97,65},{2,98}... | collective-permute-start | bytes 405512 | tf_op jit(solution)/shard_map/ppermute | solution.py:145
  32.5 24.9 %collective-permute-start.4 = (bf16[528,128]{1,0:T(8,128)(2,1)S(1)}, bf16[528,128]{1,0:T(8,128)(2,1)S(1)}, u32[]{:S(2)}, u32[]{:S(2)}) collective-permute-start(bf16[528,128]{1,0:T(8,128)(2,1)S(1)} %fusion.1), channel_id=1, source_target_pairs={{0,128},{1,897},{2,130},{3,899},{4,132},{5,901},{6,134},{7,903},{8... | collective-permute-start | bytes 405512 | tf_op jit(solution)/shard_map/ppermute | solution.py:38
  40.9 19.2 %collective-permute-start.5 = (bf16[528,128]{1,0:T(8,128)(2,1)S(1)}, bf16[528,128]{1,0:T(8,128)(2,1)S(1)}, u32[]{:S(2)}, u32[]{:S(2)}) collective-permute-start(bf16[528,128]{1,0:T(8,128)(2,1)S(1)} %fusion.1), channel_id=1, source_target_pairs={{0,897},{1,128},{2,899},{3,130},{4,901},{5,132},{6,903},{7,134},{8... | collective-permute-start | bytes 405512 | tf_op jit(solution)/shard_map/ppermute | solution.py:38
  60.2 248.8 %all-gather.5.cloned.1.call-start = ((), (), s32[]{:S(2)}) async-start(), calls=%async_computation.1 | async-start | bytes 4718592 | tf_op jit(solution)/shard_map/all_gather | solution.py:148
  60.3 13.2 %collective-permute-start.6 = (bf16[1056,128]{1,0:T(8,128)(2,1)S(1)}, bf16[1056,128]{1,0:T(8,128)(2,1)S(1)}, u32[]{:S(2)}, u32[]{:S(2)}) collective-permute-start(bf16[1056,128]{1,0:T(8,128)(2,1)S(1)} %constant_dynamic-update-slice_fusion.refs_5_), channel_id=1, source_target_pairs={{0,128},{1,897},{2,130},{3,899},{4,132},{5,901},{6,134},{7,903},{8... | collective-permute-start | bytes 811016 | tf_op jit(solution)/shard_map/ppermute | solution.py:38
  63.6 9.8 %collective-permute-start.8 = (bf16[1056,128]{1,0:T(8,128)(2,1)S(1)}, bf16[1056,128]{1,0:T(8,128)(2,1)S(1)}, u32[]{:S(2)}, u32[]{:S(2)}) collective-permute-start(bf16[1056,128]{1,0:T(8,128)(2,1)S(1)} %constant_dynamic-update-slice_fusion.refs_5_), channel_id=1, source_target_pairs={{0,8},{8,0},{16,24},{24,16},{1,9},{9,1},{17,25},{25,17},{2,10},{10... | collective-permute-start | bytes 811016 | tf_op jit(solution)/shard_map/ppermute | solution.py:43
  65.5 7.9 %collective-permute-start.7 = (bf16[528,128]{1,0:T(8,128)(2,1)S(1)}, bf16[528,128]{1,0:T(8,128)(2,1)S(1)}, u32[]{:S(2)}, u32[]{:S(2)}) collective-permute-start(bf16[528,128]{1,0:T(8,128)(2,1)S(1)} %collective-permute-done.refs_0_.refs_2_), channel_id=1, source_target_pairs={{0,8},{8,0},{16,24},{24,16},{1,9},{9,1},{17,25},{25,17},{2,10},{10... | collective-permute-start | bytes 405512 | tf_op jit(solution)/shard_map/ppermute | solution.py:43
  73.4 52.6 %copy-start.2 = (bf16[1056,128]{1,0:T(8,128)(2,1)}, bf16[1056,128]{1,0:T(8,128)(2,1)S(1)}, u32[]{:S(2)}) copy-start(bf16[1056,128]{1,0:T(8,128)(2,1)S(1)} %collective-permute-done.6.refs_9_) | copy-start | bytes 811012
  73.5 26.8 %collective-permute-start.11 = (bf16[2112,128]{1,0:T(8,128)(2,1)S(1)}, bf16[2112,128]{1,0:T(8,128)(2,1)S(1)}, u32[]{:S(2)}, u32[]{:S(2)}) collective-permute-start(bf16[2112,128]{1,0:T(8,128)(2,1)S(1)} %pad_maximum_fusion.1), channel_id=1, source_target_pairs={{0,24},{8,16},{16,8},{24,0},{1,25},{9,17},{17,9},{25,1},{2,26},{10... | collective-permute-start | bytes 1622024 | tf_op jit(solution)/shard_map/ppermute | solution.py:43
  80.7 15.6 %collective-permute-start.10 = (bf16[1056,128]{1,0:T(8,128)(2,1)S(1)}, bf16[1056,128]{1,0:T(8,128)(2,1)S(1)}, u32[]{:S(2)}, u32[]{:S(2)}) collective-permute-start(bf16[1056,128]{1,0:T(8,128)(2,1)S(1)} %pad_maximum_fusion.14), channel_id=1, source_target_pairs={{0,24},{8,16},{16,8},{24,0},{1,25},{9,17},{17,9},{25,1},{2,26},{10... | collective-permute-start | bytes 811016 | tf_op jit(solution)/shard_map/ppermute | solution.py:43
  82.6 13.7 %collective-permute-start.12 = (bf16[1056,128]{1,0:T(8,128)(2,1)S(1)}, bf16[1056,128]{1,0:T(8,128)(2,1)S(1)}, u32[]{:S(2)}, u32[]{:S(2)}) collective-permute-start(bf16[1056,128]{1,0:T(8,128)(2,1)S(1)} %collective-permute-done.6.refs_9_), channel_id=1, source_target_pairs={{0,8},{8,0},{16,24},{24,16},{1,9},{9,1},{17,25},{25,17},{2,10},{10... | collective-permute-start | bytes 811016 | tf_op jit(solution)/shard_map/ppermute | solution.py:43
  86.7 13.6 %collective-permute-start.9 = (bf16[1056,128]{1,0:T(8,128)(2,1)S(1)}, bf16[1056,128]{1,0:T(8,128)(2,1)S(1)}, u32[]{:S(2)}, u32[]{:S(2)}) collective-permute-start(bf16[1056,128]{1,0:T(8,128)(2,1)S(1)} %collective-permute-done.6.refs_9_), channel_id=1, source_target_pairs={{0,128},{1,897},{2,130},{3,899},{4,132},{5,901},{6,134},{7,903},{8... | collective-permute-start | bytes 811016 | tf_op jit(solution)/shard_map/ppermute | solution.py:38
  96.3 29.7 %copy-start.3 = (bf16[1056,128]{1,0:T(8,128)(2,1)}, bf16[1056,128]{1,0:T(8,128)(2,1)S(1)}, u32[]{:S(2)}) copy-start(bf16[1056,128]{1,0:T(8,128)(2,1)S(1)} %collective-permute-done.12.refs_10_) | copy-start | bytes 811012
  100.3 40.8 %copy-start = (bf16[1056,128]{1,0:T(8,128)(2,1)}, bf16[1056,128]{1,0:T(8,128)(2,1)S(1)}, u32[]{:S(2)}) copy-start(bf16[1056,128]{1,0:T(8,128)(2,1)S(1)} %collective-permute-done.9.refs_17_) | copy-start | bytes 811012
  100.3 17.9 %copy-start.7 = (bf16[2112,128]{1,0:T(8,128)(2,1)}, bf16[2112,128]{1,0:T(8,128)(2,1)S(1)}, u32[]{:S(2)}) copy-start(bf16[2112,128]{1,0:T(8,128)(2,1)S(1)} %collective-permute-done.11.refs_7_) | copy-start | bytes 1622020
  100.3 37.7 %collective-permute-start.16 = (bf16[2112,128]{1,0:T(8,128)(2,1)S(1)}, bf16[2112,128]{1,0:T(8,128)(2,1)S(1)}, u32[]{:S(2)}, u32[]{:S(2)}) collective-permute-start(bf16[2112,128]{1,0:T(8,128)(2,1)S(1)} %pad_maximum_fusion.3), channel_id=1, source_target_pairs={{0,1},{1,0},{2,3},{3,2},{4,5},{5,4},{6,7},{7,6},{8,9},{9,8},{10,11... | collective-permute-start | bytes 1622024 | tf_op jit(solution)/shard_map/ppermute | solution.py:43
  118.1 19.9 %collective-permute-start.14 = (bf16[2112,128]{1,0:T(8,128)(2,1)S(1)}, bf16[2112,128]{1,0:T(8,128)(2,1)S(1)}, u32[]{:S(2)}, u32[]{:S(2)}) collective-permute-start(bf16[2112,128]{1,0:T(8,128)(2,1)S(1)} %pad_maximum_fusion.2), channel_id=1, source_target_pairs={{0,24},{8,16},{16,8},{24,0},{1,25},{9,17},{17,9},{25,1},{2,26},{10... | collective-permute-start | bytes 1622024 | tf_op jit(solution)/shard_map/ppermute | solution.py:43
  121.3 16.7 %collective-permute-start.15 = (bf16[1056,128]{1,0:T(8,128)(2,1)S(1)}, bf16[1056,128]{1,0:T(8,128)(2,1)S(1)}, u32[]{:S(2)}, u32[]{:S(2)}) collective-permute-start(bf16[1056,128]{1,0:T(8,128)(2,1)S(1)} %collective-permute-done.9.refs_17_), channel_id=1, source_target_pairs={{0,8},{8,0},{16,24},{24,16},{1,9},{9,1},{17,25},{25,17},{2,10},{10... | collective-permute-start | bytes 811016 | tf_op jit(solution)/shard_map/ppermute | solution.py:43
  124.1 13.9 %collective-permute-start.13 = (bf16[528,128]{1,0:T(8,128)(2,1)S(1)}, bf16[528,128]{1,0:T(8,128)(2,1)S(1)}, u32[]{:S(2)}, u32[]{:S(2)}) collective-permute-start(bf16[528,128]{1,0:T(8,128)(2,1)S(1)} %get-tuple-element.98), channel_id=1, source_target_pairs={{0,128},{1,897},{2,130},{3,899},{4,132},{5,901},{6,134},{7,903},{8... | collective-permute-start | bytes 405512 | tf_op jit(solution)/shard_map/ppermute | solution.py:38
  138.0 15.0 %copy-start.4 = (bf16[1056,128]{1,0:T(8,128)(2,1)}, bf16[1056,128]{1,0:T(8,128)(2,1)S(1)}, u32[]{:S(2)}) copy-start(bf16[1056,128]{1,0:T(8,128)(2,1)S(1)} %collective-permute-done.15.refs_18_) | copy-start | bytes 811012
  139.1 24.5 %collective-permute-start.18 = (bf16[2112,128]{1,0:T(8,128)(2,1)S(1)}, bf16[2112,128]{1,0:T(8,128)(2,1)S(1)}, u32[]{:S(2)}, u32[]{:S(2)}) collective-permute-start(bf16[2112,128]{1,0:T(8,128)(2,1)S(1)} %pad_maximum_fusion.5), channel_id=1, source_target_pairs={{0,1},{1,0},{2,3},{3,2},{4,5},{5,4},{6,7},{7,6},{8,9},{9,8},{10,11... | collective-permute-start | bytes 1622024 | tf_op jit(solution)/shard_map/ppermute | solution.py:43
  141.1 25.5 %copy-start.19 = (s32[32]{0:T(128)S(1)}, s32[32]{0:T(128)}, u32[]{:S(2)}) copy-start(s32[32]{0:T(128)} %constant.95.clone) | copy-start | bytes 388
  141.1 25.5 %copy-start.20 = (s32[32]{0:T(128)S(1)}, s32[32]{0:T(128)}, u32[]{:S(2)}) copy-start(s32[32]{0:T(128)} %constant.96.clone) | copy-start | bytes 388
  141.1 25.6 %copy-start.18 = (s32[2]{0:T(128)S(1)}, s32[2]{0:T(128)}, u32[]{:S(2)}) copy-start(s32[2]{0:T(128)} %param.9) | copy-start | bytes 28
  141.1 22.5 %collective-permute-start.17 = (bf16[2112,128]{1,0:T(8,128)(2,1)S(1)}, bf16[2112,128]{1,0:T(8,128)(2,1)S(1)}, u32[]{:S(2)}, u32[]{:S(2)}) collective-permute-start(bf16[2112,128]{1,0:T(8,128)(2,1)S(1)} %pad_maximum_fusion.4), channel_id=1, source_target_pairs={{0,24},{8,16},{16,8},{24,0},{1,25},{9,17},{17,9},{25,1},{2,26},{10... | collective-permute-start | bytes 1622024 | tf_op jit(solution)/shard_map/ppermute | solution.py:43
  143.2 9.9 %collective-permute-start.19 = (bf16[528,128]{1,0:T(8,128)(2,1)S(1)}, bf16[528,128]{1,0:T(8,128)(2,1)S(1)}, u32[]{:S(2)}, u32[]{:S(2)}) collective-permute-start(bf16[528,128]{1,0:T(8,128)(2,1)S(1)} %collective-permute-done.13.refs_13_), channel_id=1, source_target_pairs={{0,8},{8,0},{16,24},{24,16},{1,9},{9,1},{17,25},{25,17},{2,10},{10... | collective-permute-start | bytes 405512 | tf_op jit(solution)/shard_map/ppermute | solution.py:43
  145.1 18.5 %collective-permute-start.20 = (bf16[528,128]{1,0:T(8,128)(2,1)S(1)}, bf16[528,128]{1,0:T(8,128)(2,1)S(1)}, u32[]{:S(2)}, u32[]{:S(2)}) collective-permute-start(bf16[528,128]{1,0:T(8,128)(2,1)S(1)} %collective-permute-done.13.refs_13_), channel_id=1, source_target_pairs={{0,24},{8,16},{16,8},{24,0},{1,25},{9,17},{17,9},{25,1},{2,26},{10... | collective-permute-start | bytes 405512 | tf_op jit(solution)/shard_map/ppermute | solution.py:43
  149.3 14.3 %collective-permute-start.21 = (bf16[528,128]{1,0:T(8,128)(2,1)S(1)}, bf16[528,128]{1,0:T(8,128)(2,1)S(1)}, u32[]{:S(2)}, u32[]{:S(2)}) collective-permute-start(bf16[528,128]{1,0:T(8,128)(2,1)S(1)} %collective-permute-done.13.refs_13_), channel_id=1, source_target_pairs={{0,16},{8,24},{16,0},{24,8},{1,17},{9,25},{17,1},{25,9},{2,18},{10... | collective-permute-start | bytes 405512 | tf_op jit(solution)/shard_map/ppermute | solution.py:43
  163.6 5.1 %copy-start.14 = (bf16[2112,128]{1,0:T(8,128)(2,1)}, bf16[2112,128]{1,0:T(8,128)(2,1)S(1)}, u32[]{:S(2)}) copy-start(bf16[2112,128]{1,0:T(8,128)(2,1)S(1)} %collective-permute-done.18.refs_12_) | copy-start | bytes 1622020
  163.6 5.1 %copy-start.9 = (bf16[2112,128]{1,0:T(8,128)(2,1)}, bf16[2112,128]{1,0:T(8,128)(2,1)S(1)}, u32[]{:S(2)}) copy-start(bf16[2112,128]{1,0:T(8,128)(2,1)S(1)} %collective-permute-done.17.refs_19_) | copy-start | bytes 1622020
  164.6 4.0 %collective-permute-start.22 = (bf16[2112,128]{1,0:T(8,128)(2,1)}, bf16[2112,128]{1,0:T(8,128)(2,1)S(1)}, u32[]{:S(2)}, u32[]{:S(2)}) collective-permute-start(bf16[2112,128]{1,0:T(8,128)(2,1)} %pad_maximum_fusion.6), channel_id=1, source_target_pairs={{0,1},{1,0},{2,3},{3,2},{4,5},{5,4},{6,7},{7,6},{8,9},{9,8},{10,11... | collective-permute-start | bytes 1622024 | tf_op jit(solution)/shard_map/ppermute | solution.py:43
  179.2 20.8 %collective-permute-start.23 = (bf16[512,128]{1,0:T(8,128)(2,1)S(1)}, bf16[512,128]{1,0:T(8,128)(2,1)S(1)}, u32[]{:S(2)}, u32[]{:S(2)}) collective-permute-start(bf16[512,128]{1,0:T(8,128)(2,1)S(1)} %get-tuple-element.65.refs_1_.refs_3_), channel_id=1, source_target_pairs={{0,32},{32,64},{64,96},{96,0},{1,33},{33,65},{65,97},{97,1},{2,34}... | collective-permute-start | bytes 393224 | tf_op jit(solution)/shard_map/ppermute | solution.py:145
  181.2 18.9 %collective-permute-start.24 = (bf16[512,128]{1,0:T(8,128)(2,1)S(1)}, bf16[512,128]{1,0:T(8,128)(2,1)S(1)}, u32[]{:S(2)}, u32[]{:S(2)}) collective-permute-start(bf16[512,128]{1,0:T(8,128)(2,1)S(1)} %get-tuple-element.65.refs_1_.refs_3_), channel_id=1, source_target_pairs={{0,64},{32,96},{64,0},{96,32},{1,65},{33,97},{65,1},{97,33},{2,66}... | collective-permute-start | bytes 393224 | tf_op jit(solution)/shard_map/ppermute | solution.py:145
  186.6 13.5 %collective-permute-start.25 = (bf16[512,128]{1,0:T(8,128)(2,1)S(1)}, bf16[512,128]{1,0:T(8,128)(2,1)S(1)}, u32[]{:S(2)}, u32[]{:S(2)}) collective-permute-start(bf16[512,128]{1,0:T(8,128)(2,1)S(1)} %get-tuple-element.65.refs_1_.refs_3_), channel_id=1, source_target_pairs={{0,96},{32,0},{64,32},{96,64},{1,97},{33,1},{65,33},{97,65},{2,98}... | collective-permute-start | bytes 393224 | tf_op jit(solution)/shard_map/ppermute | solution.py:145
  188.8 12.1 %collective-permute-start.26 = (bf16[512,128]{1,0:T(8,128)(2,1)S(1)}, bf16[512,128]{1,0:T(8,128)(2,1)S(1)}, u32[]{:S(2)}, u32[]{:S(2)}) collective-permute-start(bf16[512,128]{1,0:T(8,128)(2,1)S(1)} %get-tuple-element.65.refs_1_.refs_3_), channel_id=1, source_target_pairs={{0,128},{1,897},{2,130},{3,899},{4,132},{5,901},{6,134},{7,903},{8... | collective-permute-start | bytes 393224 | tf_op jit(solution)/shard_map/ppermute | solution.py:38
  195.1 12.2 %collective-permute-start.27 = (bf16[512,128]{1,0:T(8,128)(2,1)S(1)}, bf16[512,128]{1,0:T(8,128)(2,1)S(1)}, u32[]{:S(2)}, u32[]{:S(2)}) collective-permute-start(bf16[512,128]{1,0:T(8,128)(2,1)S(1)} %get-tuple-element.65.refs_1_.refs_3_), channel_id=1, source_target_pairs={{0,897},{1,128},{2,899},{3,130},{4,901},{5,132},{6,903},{7,134},{8... | collective-permute-start | bytes 393224 | tf_op jit(solution)/shard_map/ppermute | solution.py:38
  207.4 21.8 %collective-permute-start.28 = (bf16[1024,128]{1,0:T(8,128)(2,1)S(1)}, bf16[1024,128]{1,0:T(8,128)(2,1)S(1)}, u32[]{:S(2)}, u32[]{:S(2)}) collective-permute-start(bf16[1024,128]{1,0:T(8,128)(2,1)S(1)} %constant_dynamic-update-slice_fusion.2.refs_6_), channel_id=1, source_target_pairs={{0,128},{1,897},{2,130},{3,899},{4,132},{5,901},{6,134},{7,903},{8... | collective-permute-start | bytes 786440 | tf_op jit(solution)/shard_map/ppermute | solution.py:38
  215.9 13.3 %collective-permute-start.30 = (bf16[1024,128]{1,0:T(8,128)(2,1)S(1)}, bf16[1024,128]{1,0:T(8,128)(2,1)S(1)}, u32[]{:S(2)}, u32[]{:S(2)}) collective-permute-start(bf16[1024,128]{1,0:T(8,128)(2,1)S(1)} %constant_dynamic-update-slice_fusion.2.refs_6_), channel_id=1, source_target_pairs={{0,8},{8,0},{16,24},{24,16},{1,9},{9,1},{17,25},{25,17},{2,10},{10... | collective-permute-start | bytes 786440 | tf_op jit(solution)/shard_map/ppermute | solution.py:43
  222.4 6.9 %collective-permute-start.29 = (bf16[512,128]{1,0:T(8,128)(2,1)S(1)}, bf16[512,128]{1,0:T(8,128)(2,1)S(1)}, u32[]{:S(2)}, u32[]{:S(2)}) collective-permute-start(bf16[512,128]{1,0:T(8,128)(2,1)S(1)} %get-tuple-element.65.refs_1_.refs_3_), channel_id=1, source_target_pairs={{0,8},{8,0},{16,24},{24,16},{1,9},{9,1},{17,25},{25,17},{2,10},{10... | collective-permute-start | bytes 393224 | tf_op jit(solution)/shard_map/ppermute | solution.py:43
  229.3 26.4 %collective-permute-start.33 = (bf16[2048,128]{1,0:T(8,128)(2,1)S(1)}, bf16[2048,128]{1,0:T(8,128)(2,1)S(1)}, u32[]{:S(2)}, u32[]{:S(2)}) collective-permute-start(bf16[2048,128]{1,0:T(8,128)(2,1)S(1)} %pad_maximum_fusion.8), channel_id=1, source_target_pairs={{0,24},{8,16},{16,8},{24,0},{1,25},{9,17},{17,9},{25,1},{2,26},{10... | collective-permute-start | bytes 1572872 | tf_op jit(solution)/shard_map/ppermute | solution.py:43
  232.4 16.9 %collective-permute-start.32 = (bf16[1024,128]{1,0:T(8,128)(2,1)S(1)}, bf16[1024,128]{1,0:T(8,128)(2,1)S(1)}, u32[]{:S(2)}, u32[]{:S(2)}) collective-permute-start(bf16[1024,128]{1,0:T(8,128)(2,1)S(1)} %pad_maximum_fusion.15), channel_id=1, source_target_pairs={{0,24},{8,16},{16,8},{24,0},{1,25},{9,17},{17,9},{25,1},{2,26},{10... | collective-permute-start | bytes 786440 | tf_op jit(solution)/shard_map/ppermute | solution.py:43
  235.2 20.5 %collective-permute-start.31 = (bf16[1024,128]{1,0:T(8,128)(2,1)S(1)}, bf16[1024,128]{1,0:T(8,128)(2,1)S(1)}, u32[]{:S(2)}, u32[]{:S(2)}) collective-permute-start(bf16[1024,128]{1,0:T(8,128)(2,1)S(1)} %collective-permute-done.28.refs_10_), channel_id=1, source_target_pairs={{0,128},{1,897},{2,130},{3,899},{4,132},{5,901},{6,134},{7,903},{8... | collective-permute-start | bytes 786440 | tf_op jit(solution)/shard_map/ppermute | solution.py:38
  241.8 13.9 %collective-permute-start.34 = (bf16[1024,128]{1,0:T(8,128)(2,1)S(1)}, bf16[1024,128]{1,0:T(8,128)(2,1)S(1)}, u32[]{:S(2)}, u32[]{:S(2)}) collective-permute-start(bf16[1024,128]{1,0:T(8,128)(2,1)S(1)} %collective-permute-done.28.refs_10_), channel_id=1, source_target_pairs={{0,8},{8,0},{16,24},{24,16},{1,9},{9,1},{17,25},{25,17},{2,10},{10... | collective-permute-start | bytes 786440 | tf_op jit(solution)/shard_map/ppermute | solution.py:43
  255.7 27.4 %copy-start.1 = (bf16[1024,128]{1,0:T(8,128)(2,1)}, bf16[1024,128]{1,0:T(8,128)(2,1)S(1)}, u32[]{:S(2)}) copy-start(bf16[1024,128]{1,0:T(8,128)(2,1)S(1)} %collective-permute-done.31.refs_18_) | copy-start | bytes 786436
  255.7 13.0 %copy-start.5 = (bf16[1024,128]{1,0:T(8,128)(2,1)}, bf16[1024,128]{1,0:T(8,128)(2,1)S(1)}, u32[]{:S(2)}) copy-start(bf16[1024,128]{1,0:T(8,128)(2,1)S(1)} %collective-permute-done.34.refs_11_) | copy-start | bytes 786436
  255.8 24.4 %collective-permute-start.38 = (bf16[2048,128]{1,0:T(8,128)(2,1)S(1)}, bf16[2048,128]{1,0:T(8,128)(2,1)S(1)}, u32[]{:S(2)}, u32[]{:S(2)}) collective-permute-start(bf16[2048,128]{1,0:T(8,128)(2,1)S(1)} %pad_maximum_fusion.10), channel_id=1, source_target_pairs={{0,1},{1,0},{2,3},{3,2},{4,5},{5,4},{6,7},{7,6},{8,9},{9,8},{10,11... | collective-permute-start | bytes 1572872 | tf_op jit(solution)/shard_map/ppermute | solution.py:43
  257.8 22.4 %collective-permute-start.36 = (bf16[2048,128]{1,0:T(8,128)(2,1)S(1)}, bf16[2048,128]{1,0:T(8,128)(2,1)S(1)}, u32[]{:S(2)}, u32[]{:S(2)}) collective-permute-start(bf16[2048,128]{1,0:T(8,128)(2,1)S(1)} %pad_maximum_fusion.9), channel_id=1, source_target_pairs={{0,24},{8,16},{16,8},{24,0},{1,25},{9,17},{17,9},{25,1},{2,26},{10... | collective-permute-start | bytes 1572872 | tf_op jit(solution)/shard_map/ppermute | solution.py:43
  260.9 19.3 %collective-permute-start.37 = (bf16[1024,128]{1,0:T(8,128)(2,1)S(1)}, bf16[1024,128]{1,0:T(8,128)(2,1)S(1)}, u32[]{:S(2)}, u32[]{:S(2)}) collective-permute-start(bf16[1024,128]{1,0:T(8,128)(2,1)S(1)} %collective-permute-done.31.refs_18_), channel_id=1, source_target_pairs={{0,8},{8,0},{16,24},{24,16},{1,9},{9,1},{17,25},{25,17},{2,10},{10... | collective-permute-start | bytes 786440 | tf_op jit(solution)/shard_map/ppermute | solution.py:43
  265.9 14.3 %collective-permute-start.35 = (bf16[512,128]{1,0:T(8,128)(2,1)S(1)}, bf16[512,128]{1,0:T(8,128)(2,1)S(1)}, u32[]{:S(2)}, u32[]{:S(2)}) collective-permute-start(bf16[512,128]{1,0:T(8,128)(2,1)S(1)} %get-tuple-element.100), channel_id=1, source_target_pairs={{0,128},{1,897},{2,130},{3,899},{4,132},{5,901},{6,134},{7,903},{8... | collective-permute-start | bytes 393224 | tf_op jit(solution)/shard_map/ppermute | solution.py:38
  280.2 14.7 %copy-start.6 = (bf16[1024,128]{1,0:T(8,128)(2,1)}, bf16[1024,128]{1,0:T(8,128)(2,1)S(1)}, u32[]{:S(2)}) copy-start(bf16[1024,128]{1,0:T(8,128)(2,1)S(1)} %collective-permute-done.37.refs_19_) | copy-start | bytes 786436
  280.2 26.8 %copy-start.16 = (bf16[2048,128]{1,0:T(8,128)(2,1)}, bf16[2048,128]{1,0:T(8,128)(2,1)S(1)}, u32[]{:S(2)}) copy-start(bf16[2048,128]{1,0:T(8,128)(2,1)S(1)} %collective-permute-done.38.refs_9_) | copy-start | bytes 1572868
  281.1 23.8 %collective-permute-start.40 = (bf16[2048,128]{1,0:T(8,128)(2,1)S(1)}, bf16[2048,128]{1,0:T(8,128)(2,1)S(1)}, u32[]{:S(2)}, u32[]{:S(2)}) collective-permute-start(bf16[2048,128]{1,0:T(8,128)(2,1)S(1)} %pad_maximum_fusion.12), channel_id=1, source_target_pairs={{0,1},{1,0},{2,3},{3,2},{4,5},{5,4},{6,7},{7,6},{8,9},{9,8},{10,11... | collective-permute-start | bytes 1572872 | tf_op jit(solution)/shard_map/ppermute | solution.py:43
  283.1 21.9 %collective-permute-start.39 = (bf16[2048,128]{1,0:T(8,128)(2,1)S(1)}, bf16[2048,128]{1,0:T(8,128)(2,1)S(1)}, u32[]{:S(2)}, u32[]{:S(2)}) collective-permute-start(bf16[2048,128]{1,0:T(8,128)(2,1)S(1)} %pad_maximum_fusion.11), channel_id=1, source_target_pairs={{0,24},{8,16},{16,8},{24,0},{1,25},{9,17},{17,9},{25,1},{2,26},{10... | collective-permute-start | bytes 1572872 | tf_op jit(solution)/shard_map/ppermute | solution.py:43
  285.0 9.9 %collective-permute-start.41 = (bf16[512,128]{1,0:T(8,128)(2,1)S(1)}, bf16[512,128]{1,0:T(8,128)(2,1)S(1)}, u32[]{:S(2)}, u32[]{:S(2)}) collective-permute-start(bf16[512,128]{1,0:T(8,128)(2,1)S(1)} %collective-permute-done.35.refs_14_), channel_id=1, source_target_pairs={{0,8},{8,0},{16,24},{24,16},{1,9},{9,1},{17,25},{25,17},{2,10},{10... | collective-permute-start | bytes 393224 | tf_op jit(solution)/shard_map/ppermute | solution.py:43
  288.1 16.9 %collective-permute-start.42 = (bf16[512,128]{1,0:T(8,128)(2,1)S(1)}, bf16[512,128]{1,0:T(8,128)(2,1)S(1)}, u32[]{:S(2)}, u32[]{:S(2)}) collective-permute-start(bf16[512,128]{1,0:T(8,128)(2,1)S(1)} %collective-permute-done.35.refs_14_), channel_id=1, source_target_pairs={{0,24},{8,16},{16,8},{24,0},{1,25},{9,17},{17,9},{25,1},{2,26},{10... | collective-permute-start | bytes 393224 | tf_op jit(solution)/shard_map/ppermute | solution.py:43
  291.5 13.4 %collective-permute-start.43 = (bf16[512,128]{1,0:T(8,128)(2,1)S(1)}, bf16[512,128]{1,0:T(8,128)(2,1)S(1)}, u32[]{:S(2)}, u32[]{:S(2)}) collective-permute-start(bf16[512,128]{1,0:T(8,128)(2,1)S(1)} %collective-permute-done.35.refs_14_), channel_id=1, source_target_pairs={{0,16},{8,24},{16,0},{24,8},{1,17},{9,25},{17,1},{25,9},{2,18},{10... | collective-permute-start | bytes 393224 | tf_op jit(solution)/shard_map/ppermute | solution.py:43
  304.9 4.0 %copy-start.17 = (bf16[2048,128]{1,0:T(8,128)(2,1)}, bf16[2048,128]{1,0:T(8,128)(2,1)S(1)}, u32[]{:S(2)}) copy-start(bf16[2048,128]{1,0:T(8,128)(2,1)S(1)} %collective-permute-done.40.refs_13_) | copy-start | bytes 1572868
  305.0 4.0 %copy-start.12 = (bf16[2048,128]{1,0:T(8,128)(2,1)}, bf16[2048,128]{1,0:T(8,128)(2,1)S(1)}, u32[]{:S(2)}) copy-start(bf16[2048,128]{1,0:T(8,128)(2,1)S(1)} %collective-permute-done.39.refs_20_) | copy-start | bytes 1572868
  305.0 3.9 %collective-permute-start.44 = (bf16[2048,128]{1,0:T(8,128)(2,1)S(1)}, bf16[2048,128]{1,0:T(8,128)(2,1)}, u32[]{:S(2)}, u32[]{:S(2)}) collective-permute-start(bf16[2048,128]{1,0:T(8,128)(2,1)S(1)} %pad_maximum_fusion.13), channel_id=1, source_target_pairs={{0,1},{1,0},{2,3},{3,2},{4,5},{5,4},{6,7},{7,6},{8,9},{9,8},{10,11... | collective-permute-start | bytes 1572872 | tf_op jit(solution)/shard_map/ppermute | solution.py:43
  318.1 13.9 %collective-permute-start.45 = (bf16[512,128]{1,0:T(8,128)(2,1)S(1)}, bf16[512,128]{1,0:T(8,128)(2,1)S(1)}, u32[]{:S(2)}, u32[]{:S(2)}) collective-permute-start(bf16[512,128]{1,0:T(8,128)(2,1)S(1)} %shard_map.74), channel_id=1, source_target_pairs={{0,0},{1,1},{2,2},{3,3},{4,4},{5,5},{6,6},{7,7},{8,32},{9,33},{10,... | collective-permute-start | bytes 393224 | tf_op jit(solution)/shard_map/ppermute | solution.py:38
  (5 other events, 5.6 us)
Sparse Core Ops, SparseCore 0:
  60.3 63.8 all-gather.2
  207.5 45.5 all-gather.4

commit v5 on v3

v5 whole, which is shorter than its diff:
```python
import functools

import jax
import jax.numpy as jnp
import numpy as np
from jax import lax
from jax.experimental import pallas as pl
from jax.experimental.pallas import tpu as pltpu
from jax.sharding import Mesh, PartitionSpec as P

STEPS = 2
BS = 128
ROWS = 4 * BS
LIST = 40
TAIL = 16
AXES = ("zh", "zl", "x", "y", "core")
SIZES = (16, 2, 4, 4, 2)


def swap(zh, zl, x, y, core):
    return zh, core, x, y, zl


def hop(zh, zl, x, y, core):
    return (zh + 1 - 2 * core) % 16, zl, x, y, core


def pair(zh, zl, x, y, core):
    return zh, 1 - zl, x, y, core


def flip(zh, zl, x, y, core):
    return zh, zl, x, y, 1 - core


def move(part, *steps):
    pairs = []
    for i in range(1024):
        place = tuple(int(k) for k in np.unravel_index(i, SIZES))
        for step in steps:
            place = step(*place)
        pairs.append((i, int(np.ravel_multi_index(place, SIZES))))
    return lax.ppermute(part, AXES, pairs)


def across(part, axis, mask):
    size = SIZES[AXES.index(axis)]
    return lax.ppermute(part, axis, [(i, i ^ mask) for i in range(size)])


def kernel(rows, units, first, branch, tab, *refs):
    slots, refs = (None, refs) if first else (refs[0], refs[1:])
    own, a_hbm, refs = refs[0], refs[1], refs[2:]
    parts, refs = refs[: len(units)], refs[len(units) :]
    if first:
        out, slots_out, a_all, b_all, lefts, rights, sems, slots, sem = refs
    else:
        out, a_all, b_all, lefts, rights, sems = refs
    copies = [pltpu.make_async_copy(a_hbm, a_all, sems.at[0])]
    at = 0
    for part, n in zip(parts, units):
        copies.append(
            pltpu.make_async_copy(
                part, b_all.at[pl.ds(at * rows, n * rows)], sems.at[len(copies)]
            )
        )
        at += n
    for copy in copies:
        copy.start()
    nothing = 32 * rows
    b_all[nothing : nothing + BS, :] = jnp.zeros((BS, BS), jnp.bfloat16)

    def listed():
        mine = [slots[tab[32], j] for j in range(4)]

        def scan(p, counts):
            la, more = tab[p], []
            for j in range(4):
                m = slots[la, j]
                lefts[j * LIST + counts[j]] = la * rows + j * BS
                rights[j * LIST + counts[j]] = p * rows + m * BS
                more.append(counts[j] + (slots[32 + p, m] == mine[j]).astype(jnp.int32))
            return tuple(more)

        counts = lax.fori_loop(0, 32, scan, (jnp.int32(0),) * 4)
        for j in range(4):
            for k in range(3):
                lefts[j * LIST + counts[j] + k] = 0
                rights[j * LIST + counts[j] + k] = nothing
        return counts

    if not first:
        counts = listed()
    for copy in copies:
        copy.wait()
    if first:
        for base, whole in ((0, a_all), (32, b_all)):
            for k in range(32):
                row = whole[k * rows + ROWS : (k + 1) * rows, :].astype(jnp.float32)[0:1]
                slots_out[base + k : base + k + 1, :] = row.astype(jnp.int32)
        copy = pltpu.make_async_copy(slots_out, slots, sem)
        copy.start()
        copy.wait()
        counts = listed()

    for j in range(4):

        def four(t, total):
            at = [j * LIST + 4 * t + k for k in range(4)]
            left = [a_all[pl.ds(pl.multiple_of(lefts[i], 16), BS), :] for i in at]
            right = [b_all[pl.ds(pl.multiple_of(rights[i], 16), BS), :] for i in at]
            return total + jnp.dot(
                jnp.concatenate(left, 1),
                jnp.concatenate(right, 0),
                preferred_element_type=jnp.float32,
            )

        square = lax.fori_loop(0, (counts[j] + 3) // 4, four, jnp.zeros((BS, BS), jnp.float32))
        block = pl.ds(j * BS, BS)
        twice = 2.0 * own[block, :].astype(jnp.float32) - square
        out[block, :] = jnp.where(branch[0] == 1, twice, square).astype(out.dtype)


def multiply(branch, tab, slots, own, a_all, placed):
    first, rows = slots is None, own.shape[0]
    parts = [part for part, _ in placed]
    units = [len(names) for _, names in placed]
    smem = pl.BlockSpec(memory_space=pltpu.SMEM)
    vmem = pl.BlockSpec(memory_space=pltpu.VMEM)
    anywhere = pl.BlockSpec(memory_space=pl.ANY)
    out_shape = [jax.ShapeDtypeStruct((ROWS, BS), jnp.bfloat16)]
    scratch = [
        pltpu.VMEM((32 * rows, BS), jnp.bfloat16),
        pltpu.VMEM((32 * rows + BS, BS), jnp.bfloat16),
        pltpu.SMEM((4 * LIST,), jnp.int32),
        pltpu.SMEM((4 * LIST,), jnp.int32),
        pltpu.SemaphoreType.DMA((1 + len(parts),)),
    ]
    if first:
        out_shape.append(jax.ShapeDtypeStruct((64, BS), jnp.int32))
        scratch += [pltpu.SMEM((64, BS), jnp.int32), pltpu.SemaphoreType.DMA]
    done = pl.pallas_call(
        functools.partial(kernel, rows, units, first),
        out_shape=out_shape,
        in_specs=[smem] * (2 if first else 3) + [vmem] + [anywhere] * (1 + len(parts)),
        out_specs=[vmem] * len(out_shape),
        scratch_shapes=scratch,
        compiler_params=pltpu.CompilerParams(vmem_limit_bytes=52 * 1024 * 1024),
        cost_estimate=pl.CostEstimate(
            flops=2 * 128 * BS**3, bytes_accessed=64 * ROWS * BS * 2, transcendentals=0
        ),
    )(branch, tab, *([] if first else [slots]), own, a_all, *parts)
    return done[0], done[1] if first else slots


def gather(unit, pal, sibling, up, down):
    rows = unit.shape[0]
    near = jnp.concatenate([unit, pal])
    near, sibling, up, down = lax.optimization_barrier((near, sibling, up, down))
    a_all = lax.all_gather(near, ("x", "y"), axis=0, tiled=True)
    chains, first, second = ring(up, down)
    last = move(chains[0][6], hop)
    final = across(jnp.concatenate([chains[0][6], chains[1][6], last]), "core", 1)
    placed = [(unit, {0: (0, 0)}), (sibling, {0: (0, 1)})]
    for k in range(7):
        placed += [(chain[k], {0: (k + 1, w)}) for w, chain in enumerate(chains)]
    for part, start in ((first, 1), (second, 4)):
        placed.append((part, {i: (-(i // 2 + start), 1 - i % 2) for i in range(6)}))
    placed += [(last, {0: (8, 0)}), (final, {0: (-7, 1), 1: (-7, 0), 2: (8, 1)})]
    return a_all, placed


def ring(up, down):
    chains = [[up], [down]]

    def on():
        for chain in chains:
            chain.append(move(chain[-1], hop))

    def to_other(a, b):
        return across(jnp.concatenate([chain[k] for k in range(a, b) for chain in chains]), "core", 1)

    for _ in range(4):
        on()
    first = to_other(0, 3)
    on()
    chains[0][5], chains[1][5], first = lax.optimization_barrier((chains[0][5], chains[1][5], first))
    on()
    second = to_other(3, 6)
    chains[0][6], chains[1][6], second = lax.optimization_barrier((chains[0][6], chains[1][6], second))
    return chains, first, second


def table(placed):
    zh, zl, x, y, core = (lax.axis_index(name) for name in AXES)
    names = np.concatenate([np.array(list(n.values())) for _, n in placed])
    p = (zh - (1 - 2 * core) * names[:, 0]) % 16 * 2 + (core ^ names[:, 1])
    la = p // 2 * 2 + (p % 2 ^ zl)
    return jnp.concatenate([la, jnp.reshape((x * 4 + y) * 2, (1,))]).astype(jnp.int32)


def body(values, column_slot_index, branches):
    flat = values.reshape(ROWS, BS)
    tail = column_slot_index[:, 0].astype(jnp.bfloat16)[None]
    start = jnp.concatenate([flat, jnp.pad(tail, ((0, TAIL - 1), (0, BS - 4)))])
    def firsts(part, *steps):
        return [move(part, *steps, *more) for more in ((pair,), (flip,), (hop,), (flip, hop))]

    unit, others = move(start, swap), firsts(start, swap)
    slots = None
    for step in range(STEPS):
        if step:
            others = firsts(unit)
        a_all, placed = gather(unit, *others)
        unit, slots = multiply(
            branches[step : step + 1], table(placed), slots, unit, a_all, placed
        )
    return move(unit, swap).reshape(values.shape)


def solution(mesh):
    fine = Mesh(mesh.devices.reshape(SIZES), AXES)
    split = (("zh", "zl"), ("x", "y", "core"))
    in_specs = (P(*split, None, None), P(*split), P())
    return jax.shard_map(
        body, mesh=fine, in_specs=in_specs, out_specs=P(*split, None, None), check_vma=False
    )
```

time: 339 us -> 274 us (0.81)
  waiting for transfers between devices: 123 us -> 61.3 us
  local copies, waits for them, and re-layouts: 11.4 us -> 1.7 us
    ppermute x12 -> x36, starting transfers between devices: 85.5 us -> 148 us  [move(): return lax.ppermute(part, AXES, pairs)]
    ppermute x25 -> x6, starting transfers between devices: 84.8 us -> 25.9 us  [across(): return lax.ppermute(part, axis, [(i, i ^ mask) for i in range(size)])]
    ppermute x25 -> x6, waiting for transfers between devices: 43.2 us -> 2.59 us  [across(): return lax.ppermute(part, axis, [(i, i ^ mask) for i in range(size)])]
    all_gather x2, waiting for transfers between devices: 24.4 us -> 0.01 us  [gather(): a_all = lax.all_gather(near, ('x', 'y'), axis=0, tiled=True)]
    unnamed x35 -> x45, local copies, waits for them, and re-layouts: 10.4 us -> 1.05 us
    ppermute x12 -> x36, waiting for transfers between devices: 55.3 us -> 58.6 us  [move(): return lax.ppermute(part, AXES, pairs)]
  transfers between devices with their start and end apart: 39 -> 44, of which waited for: 19 -> 23; matrix products, arithmetic and copies ran while one was open for 0% -> 1% of each run, Pallas kernels for 0% -> 0%
where the time goes in v5:
time: 274 us; the launch traced here: 272 us
  starting transfers between devices  173 us (63%)
  waiting for transfers between devices  61.3 us (22%)
  Pallas kernels  17.5 us (6%)
  between operations  14.1 us (5%)
  other arithmetic  4.19 us (2%)
    ppermute x36, starting transfers between devices, move(): return lax.ppermute(part, AXES, pairs)  148 us
    ppermute x36, waiting for transfers between devices, move(): return lax.ppermute(part, AXES, pairs)  58.6 us
    ppermute x6, starting transfers between devices, across(): return lax.ppermute(part, axis, [(i, i ^ mask) for i in range(size)])  25.9 us
    pallas_call x2, Pallas kernels, multiply(): pl.pallas_call(functools.partial(kernel, rows, units, first), out_shape=o...  17.5 us
  transfers between devices with their start and end apart: 44, of which 23 were waited for; matrix products, arithmetic and copies ran while one was open for 1% of the time, Pallas kernels for 0%

profile of v5, /device:TPU:1, one launch (start us, length us, event | category | flops | bytes accessed | tf_op | source)
XLA Modules:
  0.0 272.2 jit_solution(10107134776996504266)
XLA Ops:
  8.2 4.9 %collective-permute-start = (bf16[528,128]{1,0:T(8,128)(2,1)S(1)}, bf16[528,128]{1,0:T(8,128)(2,1)S(1)}, u32[]{:S(2)}, u32[]{:S(2)}) collective-permute-start(bf16[528,128]{1,0:T(8,128)(2,1)S(1)} %fusion.1), channel_id=1, source_target_pairs={{0,0},{1,32},{2,2},{3,34},{4,4},{5,36},{6,6},{7,38},{8,8},{9,40},{... | collective-permute-start | bytes 405512 | tf_op jit(solution)/shard_map/ppermute | solution.py:43
  13.1 11.8 %collective-permute-start.1 = (bf16[528,128]{1,0:T(8,128)(2,1)S(1)}, bf16[528,128]{1,0:T(8,128)(2,1)S(1)}, u32[]{:S(2)}, u32[]{:S(2)}) collective-permute-start(bf16[528,128]{1,0:T(8,128)(2,1)S(1)} %fusion.1), channel_id=1, source_target_pairs={{0,32},{1,0},{2,34},{3,2},{4,36},{5,4},{6,38},{7,6},{8,40},{9,8},{... | collective-permute-start | bytes 405512 | tf_op jit(solution)/shard_map/ppermute | solution.py:43
  24.9 1.9 collective-permute-start.2
  26.8 1.9 collective-permute-start.3
  28.8 9.5 %collective-permute-start.4 = (bf16[528,128]{1,0:T(8,128)(2,1)S(1)}, bf16[528,128]{1,0:T(8,128)(2,1)S(1)}, u32[]{:S(2)}, u32[]{:S(2)}) collective-permute-start(bf16[528,128]{1,0:T(8,128)(2,1)S(1)} %fusion.1), channel_id=1, source_target_pairs={{0,961},{1,993},{2,963},{3,995},{4,965},{5,997},{6,967},{7,999},{8... | collective-permute-start | bytes 405512 | tf_op jit(solution)/shard_map/ppermute | solution.py:43
  39.0 3.6 %collective-permute-done.4.refs_5_ = bf16[528,128]{1,0:T(8,128)(2,1)S(1)} collective-permute-done((bf16[528,128]{1,0:T(8,128)(2,1)S(1)}, bf16[528,128]{1,0:T(8,128)(2,1)S(1)}, u32[]{:S(2)}, u32[]{:S(2)}) %collective-permute-start.4) | collective-permute-done | bytes 135200 | tf_op jit(solution)/shard_map/ppermute | solution.py:43
  42.7 6.0 %collective-permute-start.5 = (bf16[528,128]{1,0:T(8,128)(2,1)S(1)}, bf16[528,128]{1,0:T(8,128)(2,1)S(1)}, u32[]{:S(2)}, u32[]{:S(2)}) collective-permute-start(bf16[528,128]{1,0:T(8,128)(2,1)S(1)} %collective-permute-done.3.refs_4_), channel_id=1, source_target_pairs={{0,64},{1,961},{2,66},{3,963},{4,68},{5,965},{6,70},{7,967},{8,72}... | collective-permute-start | bytes 405512 | tf_op jit(solution)/shard_map/ppermute | solution.py:43
  48.7 2.2 collective-permute-start.6
  50.9 2.6 collective-permute-done.5.refs_6_
  53.5 5.9 %collective-permute-start.7 = (bf16[528,128]{1,0:T(8,128)(2,1)S(1)}, bf16[528,128]{1,0:T(8,128)(2,1)S(1)}, u32[]{:S(2)}, u32[]{:S(2)}) collective-permute-start(bf16[528,128]{1,0:T(8,128)(2,1)S(1)} %collective-permute-done.5.refs_6_), channel_id=1, source_target_pairs={{0,64},{1,961},{2,66},{3,963},{4,68},{5,965},{6,70},{7,967},{8,72}... | collective-permute-start | bytes 405512 | tf_op jit(solution)/shard_map/ppermute | solution.py:43
  59.5 1.9 collective-permute-start.8
  61.4 1.6 collective-permute-done.7.refs_8_
  63.0 3.1 %collective-permute-done.8.refs_9_ = bf16[528,128]{1,0:T(8,128)(2,1)S(1)} collective-permute-done((bf16[528,128]{1,0:T(8,128)(2,1)S(1)}, bf16[528,128]{1,0:T(8,128)(2,1)S(1)}, u32[]{:S(2)}, u32[]{:S(2)}) %collective-permute-start.8) | collective-permute-done | bytes 135200 | tf_op jit(solution)/shard_map/ppermute | solution.py:43
  66.2 1.9 collective-permute-start.15
  68.1 4.2 %collective-permute-start.9 = (bf16[528,128]{1,0:T(8,128)(2,1)S(1)}, bf16[528,128]{1,0:T(8,128)(2,1)S(1)}, u32[]{:S(2)}, u32[]{:S(2)}) collective-permute-start(bf16[528,128]{1,0:T(8,128)(2,1)S(1)} %collective-permute-done.7.refs_8_), channel_id=1, source_target_pairs={{0,64},{1,961},{2,66},{3,963},{4,68},{5,965},{6,70},{7,967},{8,72}... | collective-permute-start | bytes 405512 | tf_op jit(solution)/shard_map/ppermute | solution.py:43
  72.3 2.9 %collective-permute-start.10 = (bf16[528,128]{1,0:T(8,128)(2,1)S(1)}, bf16[528,128]{1,0:T(8,128)(2,1)S(1)}, u32[]{:S(2)}, u32[]{:S(2)}) collective-permute-start(bf16[528,128]{1,0:T(8,128)(2,1)S(1)} %collective-permute-done.8.refs_9_), channel_id=1, source_target_pairs={{0,64},{1,961},{2,66},{3,963},{4,68},{5,965},{6,70},{7,967},{8,72}... | collective-permute-start | bytes 405512 | tf_op jit(solution)/shard_map/ppermute | solution.py:43
  75.2 6.4 %collective-permute-start.11 = (bf16[528,128]{1,0:T(8,128)(2,1)S(1)}, bf16[528,128]{1,0:T(8,128)(2,1)S(1)}, u32[]{:S(2)}, u32[]{:S(2)}) collective-permute-start(bf16[528,128]{1,0:T(8,128)(2,1)S(1)} %collective-permute-done.9.refs_10_), channel_id=1, source_target_pairs={{0,64},{1,961},{2,66},{3,963},{4,68},{5,965},{6,70},{7,967},{8,72}... | collective-permute-start | bytes 405512 | tf_op jit(solution)/shard_map/ppermute | solution.py:43
  81.6 1.9 collective-permute-start.12
  83.6 1.4 collective-permute-done.11.refs_12_
  85.0 5.9 %collective-permute-start.13 = (bf16[528,128]{1,0:T(8,128)(2,1)S(1)}, bf16[528,128]{1,0:T(8,128)(2,1)S(1)}, u32[]{:S(2)}, u32[]{:S(2)}) collective-permute-start(bf16[528,128]{1,0:T(8,128)(2,1)S(1)} %collective-permute-done.11.refs_12_), channel_id=1, source_target_pairs={{0,64},{1,961},{2,66},{3,963},{4,68},{5,965},{6,70},{7,967},{8,72}... | collective-permute-start | bytes 405512 | tf_op jit(solution)/shard_map/ppermute | solution.py:43
  90.9 1.9 collective-permute-start.14
  93.6 5.1 %collective-permute-done.14.refs_15_ = bf16[528,128]{1,0:T(8,128)(2,1)S(1)} collective-permute-done((bf16[528,128]{1,0:T(8,128)(2,1)S(1)}, bf16[528,128]{1,0:T(8,128)(2,1)S(1)}, u32[]{:S(2)}, u32[]{:S(2)}) %collective-permute-start.14) | collective-permute-done | bytes 135200 | tf_op jit(solution)/shard_map/ppermute | solution.py:43
  98.8 3.5 %collective-permute-start.18 = (bf16[3168,128]{1,0:T(8,128)(2,1)S(1)}, bf16[3168,128]{1,0:T(8,128)(2,1)S(1)}, u32[]{:S(2)}, u32[]{:S(2)}) collective-permute-start(bf16[3168,128]{1,0:T(8,128)(2,1)S(1)} %constant_dynamic-update-slice_fusion.6), channel_id=1, source_target_pairs={{0,1},{1,0},{2,3},{3,2},{4,5},{5,4},{6,7},{7,6},{8,9},{9,8},{10,11... | collective-permute-start | bytes 2433032 | tf_op jit(solution)/shard_map/ppermute | solution.py:48
  102.3 5.4 %collective-permute-start.16 = (bf16[528,128]{1,0:T(8,128)(2,1)S(1)}, bf16[528,128]{1,0:T(8,128)(2,1)}, u32[]{:S(2)}, u32[]{:S(2)}) collective-permute-start(bf16[528,128]{1,0:T(8,128)(2,1)S(1)} %collective-permute-done.13.refs_14_), channel_id=1, source_target_pairs={{0,64},{1,961},{2,66},{3,963},{4,68},{5,965},{6,70},{7,967},{8,72}... | collective-permute-start | bytes 405512 | tf_op jit(solution)/shard_map/ppermute | solution.py:43
  107.8 4.1 %collective-permute-start.17 = (bf16[528,128]{1,0:T(8,128)(2,1)S(1)}, bf16[528,128]{1,0:T(8,128)(2,1)S(1)}, u32[]{:S(2)}, u32[]{:S(2)}) collective-permute-start(bf16[528,128]{1,0:T(8,128)(2,1)S(1)} %collective-permute-done.14.refs_15_), channel_id=1, source_target_pairs={{0,64},{1,961},{2,66},{3,963},{4,68},{5,965},{6,70},{7,967},{8,72}... | collective-permute-start | bytes 405512 | tf_op jit(solution)/shard_map/ppermute | solution.py:43
  111.9 4.8 %collective-permute-done.17.refs_17_ = bf16[528,128]{1,0:T(8,128)(2,1)S(1)} collective-permute-done((bf16[528,128]{1,0:T(8,128)(2,1)S(1)}, bf16[528,128]{1,0:T(8,128)(2,1)S(1)}, u32[]{:S(2)}, u32[]{:S(2)}) %collective-permute-start.17) | collective-permute-done | bytes 135200 | tf_op jit(solution)/shard_map/ppermute | solution.py:43
  116.8 4.0 %collective-permute-start.19 = (bf16[528,128]{1,0:T(8,128)(2,1)}, bf16[528,128]{1,0:T(8,128)(2,1)}, u32[]{:S(2)}, u32[]{:S(2)}) collective-permute-start(bf16[528,128]{1,0:T(8,128)(2,1)} %collective-permute-done.16.refs_16_), channel_id=1, source_target_pairs={{0,64},{1,961},{2,66},{3,963},{4,68},{5,965},{6,70},{7,967},{8,72}... | collective-permute-start | bytes 405512 | tf_op jit(solution)/shard_map/ppermute | solution.py:43
  120.8 4.7 %collective-permute-done.19.refs_20_ = bf16[528,128]{1,0:T(8,128)(2,1)} collective-permute-done((bf16[528,128]{1,0:T(8,128)(2,1)}, bf16[528,128]{1,0:T(8,128)(2,1)}, u32[]{:S(2)}, u32[]{:S(2)}) %collective-permute-start.19) | collective-permute-done | bytes 135200 | tf_op jit(solution)/shard_map/ppermute | solution.py:43
  126.5 1.9 collective-permute-start.20
  129.1 1.1 collective-permute-done.20.refs_21_
  130.3 9.6 %shard_map.73 = (bf16[512,128]{1,0:T(8,128)(2,1)S(1)}, s32[64,128]{1,0:T(8,128)S(1)}) custom-call(s32[1]{0:T(128)} %get-tuple-element.49.branch, s32[33]{0:T(128)S(1)} %pad_add_fusion.tab, bf16[528,128]{1,0:T(8,128)(2,1)S(1)} %collective-permute-done.refs_0_.refs_2_, bf16[16896,128]{1,0:T(8,128)(2,1)} %all-gather.3.cloned.1.call-done.refs_1_, ...), custom_call_target="tpu_custom_call" | custom-call | flops 536870912 | bytes 8388608 | tf_op jit(solution)/shard_map/pallas_call | solution.py:142
  139.9 4.3 %collective-permute-start.21 = (bf16[512,128]{1,0:T(8,128)(2,1)S(1)}, bf16[512,128]{1,0:T(8,128)(2,1)S(1)}, u32[]{:S(2)}, u32[]{:S(2)}) collective-permute-start(bf16[512,128]{1,0:T(8,128)(2,1)S(1)} %get-tuple-element.38.refs_1_.refs_3_), channel_id=1, source_target_pairs={{0,32},{1,33},{2,34},{3,35},{4,36},{5,37},{6,38},{7,39},{8,40},{9,... | collective-permute-start | bytes 393224 | tf_op jit(solution)/shard_map/ppermute | solution.py:43
  144.2 2.4 collective-permute-start.22
  146.6 3.2 %collective-permute-start.23 = (bf16[512,128]{1,0:T(8,128)(2,1)S(1)}, bf16[512,128]{1,0:T(8,128)(2,1)S(1)}, u32[]{:S(2)}, u32[]{:S(2)}) collective-permute-start(bf16[512,128]{1,0:T(8,128)(2,1)S(1)} %get-tuple-element.38.refs_1_.refs_3_), channel_id=1, source_target_pairs={{0,64},{1,961},{2,66},{3,963},{4,68},{5,965},{6,70},{7,967},{8,72}... | collective-permute-start | bytes 393224 | tf_op jit(solution)/shard_map/ppermute | solution.py:43
  149.8 7.5 %collective-permute-start.24 = (bf16[512,128]{1,0:T(8,128)(2,1)S(1)}, bf16[512,128]{1,0:T(8,128)(2,1)S(1)}, u32[]{:S(2)}, u32[]{:S(2)}) collective-permute-start(bf16[512,128]{1,0:T(8,128)(2,1)S(1)} %get-tuple-element.38.refs_1_.refs_3_), channel_id=1, source_target_pairs={{0,961},{1,64},{2,963},{3,66},{4,965},{5,68},{6,967},{7,70},{8,969... | collective-permute-start | bytes 393224 | tf_op jit(solution)/shard_map/ppermute | solution.py:43
  158.0 2.9 %collective-permute-done.24.refs_6_ = bf16[512,128]{1,0:T(8,128)(2,1)S(1)} collective-permute-done((bf16[512,128]{1,0:T(8,128)(2,1)S(1)}, bf16[512,128]{1,0:T(8,128)(2,1)S(1)}, u32[]{:S(2)}, u32[]{:S(2)}) %collective-permute-start.24) | collective-permute-done | bytes 131104 | tf_op jit(solution)/shard_map/ppermute | solution.py:43
  161.0 3.4 %collective-permute-start.25 = (bf16[512,128]{1,0:T(8,128)(2,1)S(1)}, bf16[512,128]{1,0:T(8,128)(2,1)S(1)}, u32[]{:S(2)}, u32[]{:S(2)}) collective-permute-start(bf16[512,128]{1,0:T(8,128)(2,1)S(1)} %collective-permute-done.23.refs_5_), channel_id=1, source_target_pairs={{0,64},{1,961},{2,66},{3,963},{4,68},{5,965},{6,70},{7,967},{8,72}... | collective-permute-start | bytes 393224 | tf_op jit(solution)/shard_map/ppermute | solution.py:43
  164.4 1.9 collective-permute-start.26
  166.3 3.0 %collective-permute-done.25.refs_7_ = bf16[512,128]{1,0:T(8,128)(2,1)S(1)} collective-permute-done((bf16[512,128]{1,0:T(8,128)(2,1)S(1)}, bf16[512,128]{1,0:T(8,128)(2,1)S(1)}, u32[]{:S(2)}, u32[]{:S(2)}) %collective-permute-start.25) | collective-permute-done | bytes 131104 | tf_op jit(solution)/shard_map/ppermute | solution.py:43
  169.3 4.0 %collective-permute-start.27 = (bf16[512,128]{1,0:T(8,128)(2,1)S(1)}, bf16[512,128]{1,0:T(8,128)(2,1)S(1)}, u32[]{:S(2)}, u32[]{:S(2)}) collective-permute-start(bf16[512,128]{1,0:T(8,128)(2,1)S(1)} %collective-permute-done.25.refs_7_), channel_id=1, source_target_pairs={{0,64},{1,961},{2,66},{3,963},{4,68},{5,965},{6,70},{7,967},{8,72}... | collective-permute-start | bytes 393224 | tf_op jit(solution)/shard_map/ppermute | solution.py:43
  173.3 2.9 %collective-permute-start.28 = (bf16[512,128]{1,0:T(8,128)(2,1)S(1)}, bf16[512,128]{1,0:T(8,128)(2,1)S(1)}, u32[]{:S(2)}, u32[]{:S(2)}) collective-permute-start(bf16[512,128]{1,0:T(8,128)(2,1)S(1)} %collective-permute-done.26.refs_8_), channel_id=1, source_target_pairs={{0,64},{1,961},{2,66},{3,963},{4,68},{5,965},{6,70},{7,967},{8,72}... | collective-permute-start | bytes 393224 | tf_op jit(solution)/shard_map/ppermute | solution.py:43
  176.5 3.7 %collective-permute-done.28.refs_10_ = bf16[512,128]{1,0:T(8,128)(2,1)S(1)} collective-permute-done((bf16[512,128]{1,0:T(8,128)(2,1)S(1)}, bf16[512,128]{1,0:T(8,128)(2,1)S(1)}, u32[]{:S(2)}, u32[]{:S(2)}) %collective-permute-start.28) | collective-permute-done | bytes 131104 | tf_op jit(solution)/shard_map/ppermute | solution.py:43
  180.2 6.6 %collective-permute-start.35 = (bf16[3072,128]{1,0:T(8,128)(2,1)S(1)}, bf16[3072,128]{1,0:T(8,128)(2,1)S(1)}, u32[]{:S(2)}, u32[]{:S(2)}) collective-permute-start(bf16[3072,128]{1,0:T(8,128)(2,1)S(1)} %constant_dynamic-update-slice_fusion.12), channel_id=1, source_target_pairs={{0,1},{1,0},{2,3},{3,2},{4,5},{5,4},{6,7},{7,6},{8,9},{9,8},{10,11... | collective-permute-start | bytes 2359304 | tf_op jit(solution)/shard_map/ppermute | solution.py:48
  186.8 4.1 %collective-permute-start.29 = (bf16[512,128]{1,0:T(8,128)(2,1)S(1)}, bf16[512,128]{1,0:T(8,128)(2,1)S(1)}, u32[]{:S(2)}, u32[]{:S(2)}) collective-permute-start(bf16[512,128]{1,0:T(8,128)(2,1)S(1)} %collective-permute-done.27.refs_9_), channel_id=1, source_target_pairs={{0,64},{1,961},{2,66},{3,963},{4,68},{5,965},{6,70},{7,967},{8,72}... | collective-permute-start | bytes 393224 | tf_op jit(solution)/shard_map/ppermute | solution.py:43
  190.9 1.9 collective-permute-start.30
  193.5 8.0 %collective-permute-start.31 = (bf16[512,128]{1,0:T(8,128)(2,1)S(1)}, bf16[512,128]{1,0:T(8,128)(2,1)S(1)}, u32[]{:S(2)}, u32[]{:S(2)}) collective-permute-start(bf16[512,128]{1,0:T(8,128)(2,1)S(1)} %collective-permute-done.29.refs_11_), channel_id=1, source_target_pairs={{0,64},{1,961},{2,66},{3,963},{4,68},{5,965},{6,70},{7,967},{8,72}... | collective-permute-start | bytes 393224 | tf_op jit(solution)/shard_map/ppermute | solution.py:43
  201.5 1.9 collective-permute-start.32
  203.5 1.3 collective-permute-done.31.refs_13_
  204.8 5.9 %collective-permute-start.33 = (bf16[512,128]{1,0:T(8,128)(2,1)S(1)}, bf16[512,128]{1,0:T(8,128)(2,1)S(1)}, u32[]{:S(2)}, u32[]{:S(2)}) collective-permute-start(bf16[512,128]{1,0:T(8,128)(2,1)S(1)} %collective-permute-done.31.refs_13_), channel_id=1, source_target_pairs={{0,64},{1,961},{2,66},{3,963},{4,68},{5,965},{6,70},{7,967},{8,72}... | collective-permute-start | bytes 393224 | tf_op jit(solution)/shard_map/ppermute | solution.py:43
  210.8 1.9 collective-permute-start.34
  212.8 1.2 collective-permute-done.33.refs_15_
  214.0 3.9 %collective-permute-done.34.refs_16_ = bf16[512,128]{1,0:T(8,128)(2,1)S(1)} collective-permute-done((bf16[512,128]{1,0:T(8,128)(2,1)S(1)}, bf16[512,128]{1,0:T(8,128)(2,1)S(1)}, u32[]{:S(2)}, u32[]{:S(2)}) %collective-permute-start.34) | collective-permute-done | bytes 131104 | tf_op jit(solution)/shard_map/ppermute | solution.py:43
  218.0 4.0 %collective-permute-start.38 = (bf16[3072,128]{1,0:T(8,128)(2,1)S(1)}, bf16[3072,128]{1,0:T(8,128)(2,1)S(1)}, u32[]{:S(2)}, u32[]{:S(2)}) collective-permute-start(bf16[3072,128]{1,0:T(8,128)(2,1)S(1)} %constant_dynamic-update-slice_fusion.18), channel_id=1, source_target_pairs={{0,1},{1,0},{2,3},{3,2},{4,5},{5,4},{6,7},{7,6},{8,9},{9,8},{10,11... | collective-permute-start | bytes 2359304 | tf_op jit(solution)/shard_map/ppermute | solution.py:48
  222.0 2.0 collective-permute-start.36
  224.0 3.5 %collective-permute-start.37 = (bf16[512,128]{1,0:T(8,128)(2,1)S(1)}, bf16[512,128]{1,0:T(8,128)(2,1)S(1)}, u32[]{:S(2)}, u32[]{:S(2)}) collective-permute-start(bf16[512,128]{1,0:T(8,128)(2,1)S(1)} %collective-permute-done.34.refs_16_), channel_id=1, source_target_pairs={{0,64},{1,961},{2,66},{3,963},{4,68},{5,965},{6,70},{7,967},{8,72}... | collective-permute-start | bytes 393224 | tf_op jit(solution)/shard_map/ppermute | solution.py:43
  227.5 3.6 %collective-permute-done.36.refs_17_ = bf16[512,128]{1,0:T(8,128)(2,1)S(1)} collective-permute-done((bf16[512,128]{1,0:T(8,128)(2,1)S(1)}, bf16[512,128]{1,0:T(8,128)(2,1)S(1)}, u32[]{:S(2)}, u32[]{:S(2)}) %collective-permute-start.36) | collective-permute-done | bytes 131104 | tf_op jit(solution)/shard_map/ppermute | solution.py:43
  231.1 1.4 collective-permute-done.37.refs_18_
  232.6 4.0 %collective-permute-start.39 = (bf16[512,128]{1,0:T(8,128)(2,1)S(1)}, bf16[512,128]{1,0:T(8,128)(2,1)S(1)}, u32[]{:S(2)}, u32[]{:S(2)}) collective-permute-start(bf16[512,128]{1,0:T(8,128)(2,1)S(1)} %collective-permute-done.36.refs_17_), channel_id=1, source_target_pairs={{0,64},{1,961},{2,66},{3,963},{4,68},{5,965},{6,70},{7,967},{8,72}... | collective-permute-start | bytes 393224 | tf_op jit(solution)/shard_map/ppermute | solution.py:43
  236.6 4.5 %collective-permute-done.39.refs_21_ = bf16[512,128]{1,0:T(8,128)(2,1)S(1)} collective-permute-done((bf16[512,128]{1,0:T(8,128)(2,1)S(1)}, bf16[512,128]{1,0:T(8,128)(2,1)S(1)}, u32[]{:S(2)}, u32[]{:S(2)}) %collective-permute-start.39) | collective-permute-done | bytes 131104 | tf_op jit(solution)/shard_map/ppermute | solution.py:43
  241.1 7.9 %collective-permute-start.40 = (bf16[1536,128]{1,0:T(8,128)(2,1)S(1)}, bf16[1536,128]{1,0:T(8,128)(2,1)}, u32[]{:S(2)}, u32[]{:S(2)}) collective-permute-start(bf16[1536,128]{1,0:T(8,128)(2,1)S(1)} %pad_maximum_fusion.1), channel_id=1, source_target_pairs={{0,1},{1,0},{2,3},{3,2},{4,5},{5,4},{6,7},{7,6},{8,9},{9,8},{10,11... | collective-permute-start | bytes 1179656 | tf_op jit(solution)/shard_map/ppermute | solution.py:48
  249.1 1.4 collective-permute-done.40.refs_22_
  250.6 7.9 %shard_map.74 = bf16[512,128]{1,0:T(8,128)(2,1)S(1)} custom-call(s32[1]{0:T(128)} %get-tuple-element.50.branch, s32[33]{0:T(128)S(1)} %pad_add_fusion.tab, s32[64,128]{1,0:T(8,128)S(1)} %get-tuple-element.37.refs_0_, bf16[512,128]{1,0:T(8,128)(2,1)S(1)} %get-tuple-element.38.refs_1_.refs_3_, bf16[16384,128]{1,0:T(8,128)(2,1)} %all-gather.5.cloned.1.call-done.refs_2_, ...), custom_call_target="tpu_custom_call" | custom-call | flops 536870912 | bytes 8388608 | tf_op jit(solution)/shard_map/pallas_call | solution.py:142
  258.4 1.9 collective-permute-start.41
  260.3 4.4 %collective-permute-done.41 = bf16[512,128]{1,0:T(8,128)(2,1)S(1)} collective-permute-done((bf16[512,128]{1,0:T(8,128)(2,1)S(1)}, bf16[512,128]{1,0:T(8,128)(2,1)S(1)}, u32[]{:S(2)}, u32[]{:S(2)}) %collective-permute-start.41) | collective-permute-done | bytes 131104 | tf_op jit(solution)/shard_map/ppermute | solution.py:43
  (86 shorter events, 7.7 us)
Async XLA Ops:
  6.5 121.9 %copy-start.10 = (s32[32]{0:T(128)S(1)}, s32[32]{0:T(128)}, u32[]{:S(2)}) copy-start(s32[32]{0:T(128)} %constant.86.clone) | copy-start | bytes 388
  6.5 121.9 %copy-start.11 = (s32[32]{0:T(128)S(1)}, s32[32]{0:T(128)}, u32[]{:S(2)}) copy-start(s32[32]{0:T(128)} %constant.87.clone) | copy-start | bytes 388
  6.5 122.0 %copy-start.9 = (s32[2]{0:T(128)S(1)}, s32[2]{0:T(128)}, u32[]{:S(2)}) copy-start(s32[2]{0:T(128)} %param.9) | copy-start | bytes 28
  6.5 123.7 %all-gather.3.cloned.1.call-start = ((), (), s32[]{:S(2)}) async-start(), calls=%async_computation | async-start | bytes 4595712 | tf_op jit(solution)/shard_map/all_gather | solution.py:160
  8.2 30.1 %collective-permute-start = (bf16[528,128]{1,0:T(8,128)(2,1)S(1)}, bf16[528,128]{1,0:T(8,128)(2,1)S(1)}, u32[]{:S(2)}, u32[]{:S(2)}) collective-permute-start(bf16[528,128]{1,0:T(8,128)(2,1)S(1)} %fusion.1), channel_id=1, source_target_pairs={{0,0},{1,32},{2,2},{3,34},{4,4},{5,36},{6,6},{7,38},{8,8},{9,40},{... | collective-permute-start | bytes 405512 | tf_op jit(solution)/shard_map/ppermute | solution.py:43
  13.1 25.2 %collective-permute-start.1 = (bf16[528,128]{1,0:T(8,128)(2,1)S(1)}, bf16[528,128]{1,0:T(8,128)(2,1)S(1)}, u32[]{:S(2)}, u32[]{:S(2)}) collective-permute-start(bf16[528,128]{1,0:T(8,128)(2,1)S(1)} %fusion.1), channel_id=1, source_target_pairs={{0,32},{1,0},{2,34},{3,2},{4,36},{5,4},{6,38},{7,6},{8,40},{9,8},{... | collective-permute-start | bytes 405512 | tf_op jit(solution)/shard_map/ppermute | solution.py:43
  24.9 14.1 %collective-permute-start.2 = (bf16[528,128]{1,0:T(8,128)(2,1)S(1)}, bf16[528,128]{1,0:T(8,128)(2,1)S(1)}, u32[]{:S(2)}, u32[]{:S(2)}) collective-permute-start(bf16[528,128]{1,0:T(8,128)(2,1)S(1)} %fusion.1), channel_id=1, source_target_pairs={{0,1},{1,33},{2,3},{3,35},{4,5},{5,37},{6,7},{7,39},{8,9},{9,41},{... | collective-permute-start | bytes 405512 | tf_op jit(solution)/shard_map/ppermute | solution.py:43
  26.8 12.2 %collective-permute-start.3 = (bf16[528,128]{1,0:T(8,128)(2,1)S(1)}, bf16[528,128]{1,0:T(8,128)(2,1)S(1)}, u32[]{:S(2)}, u32[]{:S(2)}) collective-permute-start(bf16[528,128]{1,0:T(8,128)(2,1)S(1)} %fusion.1), channel_id=1, source_target_pairs={{0,64},{1,96},{2,66},{3,98},{4,68},{5,100},{6,70},{7,102},{8,72},{... | collective-permute-start | bytes 405512 | tf_op jit(solution)/shard_map/ppermute | solution.py:43
  28.8 13.8 %collective-permute-start.4 = (bf16[528,128]{1,0:T(8,128)(2,1)S(1)}, bf16[528,128]{1,0:T(8,128)(2,1)S(1)}, u32[]{:S(2)}, u32[]{:S(2)}) collective-permute-start(bf16[528,128]{1,0:T(8,128)(2,1)S(1)} %fusion.1), channel_id=1, source_target_pairs={{0,961},{1,993},{2,963},{3,995},{4,965},{5,997},{6,967},{7,999},{8... | collective-permute-start | bytes 405512 | tf_op jit(solution)/shard_map/ppermute | solution.py:43
  42.6 207.9 %all-gather.5.cloned.1.call-start = ((), (), s32[]{:S(2)}) async-start(), calls=%async_computation.1 | async-start | bytes 4456448 | tf_op jit(solution)/shard_map/all_gather | solution.py:160
  42.7 10.8 %collective-permute-start.5 = (bf16[528,128]{1,0:T(8,128)(2,1)S(1)}, bf16[528,128]{1,0:T(8,128)(2,1)S(1)}, u32[]{:S(2)}, u32[]{:S(2)}) collective-permute-start(bf16[528,128]{1,0:T(8,128)(2,1)S(1)} %collective-permute-done.3.refs_4_), channel_id=1, source_target_pairs={{0,64},{1,961},{2,66},{3,963},{4,68},{5,965},{6,70},{7,967},{8,72}... | collective-permute-start | bytes 405512 | tf_op jit(solution)/shard_map/ppermute | solution.py:43
  48.7 10.8 %collective-permute-start.6 = (bf16[528,128]{1,0:T(8,128)(2,1)S(1)}, bf16[528,128]{1,0:T(8,128)(2,1)S(1)}, u32[]{:S(2)}, u32[]{:S(2)}) collective-permute-start(bf16[528,128]{1,0:T(8,128)(2,1)S(1)} %collective-permute-done.4.refs_5_), channel_id=1, source_target_pairs={{0,64},{1,961},{2,66},{3,963},{4,68},{5,965},{6,70},{7,967},{8,72}... | collective-permute-start | bytes 405512 | tf_op jit(solution)/shard_map/ppermute | solution.py:43
  53.5 9.5 %collective-permute-start.7 = (bf16[528,128]{1,0:T(8,128)(2,1)S(1)}, bf16[528,128]{1,0:T(8,128)(2,1)S(1)}, u32[]{:S(2)}, u32[]{:S(2)}) collective-permute-start(bf16[528,128]{1,0:T(8,128)(2,1)S(1)} %collective-permute-done.5.refs_6_), channel_id=1, source_target_pairs={{0,64},{1,961},{2,66},{3,963},{4,68},{5,965},{6,70},{7,967},{8,72}... | collective-permute-start | bytes 405512 | tf_op jit(solution)/shard_map/ppermute | solution.py:43
  59.5 6.7 %collective-permute-start.8 = (bf16[528,128]{1,0:T(8,128)(2,1)S(1)}, bf16[528,128]{1,0:T(8,128)(2,1)S(1)}, u32[]{:S(2)}, u32[]{:S(2)}) collective-permute-start(bf16[528,128]{1,0:T(8,128)(2,1)S(1)} %collective-permute-done.6.refs_7_), channel_id=1, source_target_pairs={{0,64},{1,961},{2,66},{3,963},{4,68},{5,965},{6,70},{7,967},{8,72}... | collective-permute-start | bytes 405512 | tf_op jit(solution)/shard_map/ppermute | solution.py:43
  66.2 32.6 %collective-permute-start.15 = (bf16[3168,128]{1,0:T(8,128)(2,1)S(1)}, bf16[3168,128]{1,0:T(8,128)(2,1)S(1)}, u32[]{:S(2)}, u32[]{:S(2)}) collective-permute-start(bf16[3168,128]{1,0:T(8,128)(2,1)S(1)} %constant_dynamic-update-slice_fusion), channel_id=1, source_target_pairs={{0,1},{1,0},{2,3},{3,2},{4,5},{5,4},{6,7},{7,6},{8,9},{9,8},{10,11... | collective-permute-start | bytes 2433032 | tf_op jit(solution)/shard_map/ppermute | solution.py:48
  68.1 7.1 %collective-permute-start.9 = (bf16[528,128]{1,0:T(8,128)(2,1)S(1)}, bf16[528,128]{1,0:T(8,128)(2,1)S(1)}, u32[]{:S(2)}, u32[]{:S(2)}) collective-permute-start(bf16[528,128]{1,0:T(8,128)(2,1)S(1)} %collective-permute-done.7.refs_8_), channel_id=1, source_target_pairs={{0,64},{1,961},{2,66},{3,963},{4,68},{5,965},{6,70},{7,967},{8,72}... | collective-permute-start | bytes 405512 | tf_op jit(solution)/shard_map/ppermute | solution.py:43
  72.3 9.3 %collective-permute-start.10 = (bf16[528,128]{1,0:T(8,128)(2,1)S(1)}, bf16[528,128]{1,0:T(8,128)(2,1)S(1)}, u32[]{:S(2)}, u32[]{:S(2)}) collective-permute-start(bf16[528,128]{1,0:T(8,128)(2,1)S(1)} %collective-permute-done.8.refs_9_), channel_id=1, source_target_pairs={{0,64},{1,961},{2,66},{3,963},{4,68},{5,965},{6,70},{7,967},{8,72}... | collective-permute-start | bytes 405512 | tf_op jit(solution)/shard_map/ppermute | solution.py:43
  75.2 9.8 %collective-permute-start.11 = (bf16[528,128]{1,0:T(8,128)(2,1)S(1)}, bf16[528,128]{1,0:T(8,128)(2,1)S(1)}, u32[]{:S(2)}, u32[]{:S(2)}) collective-permute-start(bf16[528,128]{1,0:T(8,128)(2,1)S(1)} %collective-permute-done.9.refs_10_), channel_id=1, source_target_pairs={{0,64},{1,961},{2,66},{3,963},{4,68},{5,965},{6,70},{7,967},{8,72}... | collective-permute-start | bytes 405512 | tf_op jit(solution)/shard_map/ppermute | solution.py:43
  81.6 9.3 %collective-permute-start.12 = (bf16[528,128]{1,0:T(8,128)(2,1)S(1)}, bf16[528,128]{1,0:T(8,128)(2,1)S(1)}, u32[]{:S(2)}, u32[]{:S(2)}) collective-permute-start(bf16[528,128]{1,0:T(8,128)(2,1)S(1)} %collective-permute-done.10.refs_11_), channel_id=1, source_target_pairs={{0,64},{1,961},{2,66},{3,963},{4,68},{5,965},{6,70},{7,967},{8,72}... | collective-permute-start | bytes 405512 | tf_op jit(solution)/shard_map/ppermute | solution.py:43
  85.0 8.6 %collective-permute-start.13 = (bf16[528,128]{1,0:T(8,128)(2,1)S(1)}, bf16[528,128]{1,0:T(8,128)(2,1)S(1)}, u32[]{:S(2)}, u32[]{:S(2)}) collective-permute-start(bf16[528,128]{1,0:T(8,128)(2,1)S(1)} %collective-permute-done.11.refs_12_), channel_id=1, source_target_pairs={{0,64},{1,961},{2,66},{3,963},{4,68},{5,965},{6,70},{7,967},{8,72}... | collective-permute-start | bytes 405512 | tf_op jit(solution)/shard_map/ppermute | solution.py:43
  90.9 7.8 %collective-permute-start.14 = (bf16[528,128]{1,0:T(8,128)(2,1)S(1)}, bf16[528,128]{1,0:T(8,128)(2,1)S(1)}, u32[]{:S(2)}, u32[]{:S(2)}) collective-permute-start(bf16[528,128]{1,0:T(8,128)(2,1)S(1)} %collective-permute-done.12.refs_13_), channel_id=1, source_target_pairs={{0,64},{1,961},{2,66},{3,963},{4,68},{5,965},{6,70},{7,967},{8,72}... | collective-permute-start | bytes 405512 | tf_op jit(solution)/shard_map/ppermute | solution.py:43
  98.7 18.0 %copy-start.5 = (bf16[528,128]{1,0:T(8,128)(2,1)}, bf16[528,128]{1,0:T(8,128)(2,1)S(1)}, u32[]{:S(2)}) copy-start(bf16[528,128]{1,0:T(8,128)(2,1)S(1)} %collective-permute-done.14.refs_15_) | copy-start | bytes 405508
  98.7 31.5 %copy-start = (bf16[3168,128]{1,0:T(8,128)(2,1)}, bf16[3168,128]{1,0:T(8,128)(2,1)S(1)}, u32[]{:S(2)}) copy-start(bf16[3168,128]{1,0:T(8,128)(2,1)S(1)} %collective-permute-done.15.refs_18_) | copy-start | bytes 2433028
  98.8 17.9 %collective-permute-start.18 = (bf16[3168,128]{1,0:T(8,128)(2,1)S(1)}, bf16[3168,128]{1,0:T(8,128)(2,1)S(1)}, u32[]{:S(2)}, u32[]{:S(2)}) collective-permute-start(bf16[3168,128]{1,0:T(8,128)(2,1)S(1)} %constant_dynamic-update-slice_fusion.6), channel_id=1, source_target_pairs={{0,1},{1,0},{2,3},{3,2},{4,5},{5,4},{6,7},{7,6},{8,9},{9,8},{10,11... | collective-permute-start | bytes 2433032 | tf_op jit(solution)/shard_map/ppermute | solution.py:48
  102.3 9.6 %collective-permute-start.16 = (bf16[528,128]{1,0:T(8,128)(2,1)S(1)}, bf16[528,128]{1,0:T(8,128)(2,1)}, u32[]{:S(2)}, u32[]{:S(2)}) collective-permute-start(bf16[528,128]{1,0:T(8,128)(2,1)S(1)} %collective-permute-done.13.refs_14_), channel_id=1, source_target_pairs={{0,64},{1,961},{2,66},{3,963},{4,68},{5,965},{6,70},{7,967},{8,72}... | collective-permute-start | bytes 405512 | tf_op jit(solution)/shard_map/ppermute | solution.py:43
  107.8 9.0 %collective-permute-start.17 = (bf16[528,128]{1,0:T(8,128)(2,1)S(1)}, bf16[528,128]{1,0:T(8,128)(2,1)S(1)}, u32[]{:S(2)}, u32[]{:S(2)}) collective-permute-start(bf16[528,128]{1,0:T(8,128)(2,1)S(1)} %collective-permute-done.14.refs_15_), channel_id=1, source_target_pairs={{0,64},{1,961},{2,66},{3,963},{4,68},{5,965},{6,70},{7,967},{8,72}... | collective-permute-start | bytes 405512 | tf_op jit(solution)/shard_map/ppermute | solution.py:43
  116.7 13.5 %copy-start.4 = (bf16[528,128]{1,0:T(8,128)(2,1)}, bf16[528,128]{1,0:T(8,128)(2,1)S(1)}, u32[]{:S(2)}) copy-start(bf16[528,128]{1,0:T(8,128)(2,1)S(1)} %collective-permute-done.17.refs_17_) | copy-start | bytes 405508
  116.8 13.5 %copy-start.1 = (bf16[3168,128]{1,0:T(8,128)(2,1)}, bf16[3168,128]{1,0:T(8,128)(2,1)S(1)}, u32[]{:S(2)}) copy-start(bf16[3168,128]{1,0:T(8,128)(2,1)S(1)} %collective-permute-done.18.refs_19_) | copy-start | bytes 2433028
  116.8 8.7 %collective-permute-start.19 = (bf16[528,128]{1,0:T(8,128)(2,1)}, bf16[528,128]{1,0:T(8,128)(2,1)}, u32[]{:S(2)}, u32[]{:S(2)}) collective-permute-start(bf16[528,128]{1,0:T(8,128)(2,1)} %collective-permute-done.16.refs_16_), channel_id=1, source_target_pairs={{0,64},{1,961},{2,66},{3,963},{4,68},{5,965},{6,70},{7,967},{8,72}... | collective-permute-start | bytes 405512 | tf_op jit(solution)/shard_map/ppermute | solution.py:43
  126.5 3.8 %collective-permute-start.20 = (bf16[1584,128]{1,0:T(8,128)(2,1)S(1)}, bf16[1584,128]{1,0:T(8,128)(2,1)}, u32[]{:S(2)}, u32[]{:S(2)}) collective-permute-start(bf16[1584,128]{1,0:T(8,128)(2,1)S(1)} %pad_maximum_fusion), channel_id=1, source_target_pairs={{0,1},{1,0},{2,3},{3,2},{4,5},{5,4},{6,7},{7,6},{8,9},{9,8},{10,11... | collective-permute-start | bytes 1216520 | tf_op jit(solution)/shard_map/ppermute | solution.py:48
  139.9 17.4 %collective-permute-start.21 = (bf16[512,128]{1,0:T(8,128)(2,1)S(1)}, bf16[512,128]{1,0:T(8,128)(2,1)S(1)}, u32[]{:S(2)}, u32[]{:S(2)}) collective-permute-start(bf16[512,128]{1,0:T(8,128)(2,1)S(1)} %get-tuple-element.38.refs_1_.refs_3_), channel_id=1, source_target_pairs={{0,32},{1,33},{2,34},{3,35},{4,36},{5,37},{6,38},{7,39},{8,40},{9,... | collective-permute-start | bytes 393224 | tf_op jit(solution)/shard_map/ppermute | solution.py:43
  144.2 13.9 %collective-permute-start.22 = (bf16[512,128]{1,0:T(8,128)(2,1)S(1)}, bf16[512,128]{1,0:T(8,128)(2,1)S(1)}, u32[]{:S(2)}, u32[]{:S(2)}) collective-permute-start(bf16[512,128]{1,0:T(8,128)(2,1)S(1)} %get-tuple-element.38.refs_1_.refs_3_), channel_id=1, source_target_pairs={{0,1},{1,0},{2,3},{3,2},{4,5},{5,4},{6,7},{7,6},{8,9},{9,8},{10,11... | collective-permute-start | bytes 393224 | tf_op jit(solution)/shard_map/ppermute | solution.py:43
  146.6 11.5 %collective-permute-start.23 = (bf16[512,128]{1,0:T(8,128)(2,1)S(1)}, bf16[512,128]{1,0:T(8,128)(2,1)S(1)}, u32[]{:S(2)}, u32[]{:S(2)}) collective-permute-start(bf16[512,128]{1,0:T(8,128)(2,1)S(1)} %get-tuple-element.38.refs_1_.refs_3_), channel_id=1, source_target_pairs={{0,64},{1,961},{2,66},{3,963},{4,68},{5,965},{6,70},{7,967},{8,72}... | collective-permute-start | bytes 393224 | tf_op jit(solution)/shard_map/ppermute | solution.py:43
  149.8 11.1 %collective-permute-start.24 = (bf16[512,128]{1,0:T(8,128)(2,1)S(1)}, bf16[512,128]{1,0:T(8,128)(2,1)S(1)}, u32[]{:S(2)}, u32[]{:S(2)}) collective-permute-start(bf16[512,128]{1,0:T(8,128)(2,1)S(1)} %get-tuple-element.38.refs_1_.refs_3_), channel_id=1, source_target_pairs={{0,961},{1,64},{2,963},{3,66},{4,965},{5,68},{6,967},{7,70},{8,969... | collective-permute-start | bytes 393224 | tf_op jit(solution)/shard_map/ppermute | solution.py:43
  161.0 8.3 %collective-permute-start.25 = (bf16[512,128]{1,0:T(8,128)(2,1)S(1)}, bf16[512,128]{1,0:T(8,128)(2,1)S(1)}, u32[]{:S(2)}, u32[]{:S(2)}) collective-permute-start(bf16[512,128]{1,0:T(8,128)(2,1)S(1)} %collective-permute-done.23.refs_5_), channel_id=1, source_target_pairs={{0,64},{1,961},{2,66},{3,963},{4,68},{5,965},{6,70},{7,967},{8,72}... | collective-permute-start | bytes 393224 | tf_op jit(solution)/shard_map/ppermute | solution.py:43
  164.4 8.9 %collective-permute-start.26 = (bf16[512,128]{1,0:T(8,128)(2,1)S(1)}, bf16[512,128]{1,0:T(8,128)(2,1)S(1)}, u32[]{:S(2)}, u32[]{:S(2)}) collective-permute-start(bf16[512,128]{1,0:T(8,128)(2,1)S(1)} %collective-permute-done.24.refs_6_), channel_id=1, source_target_pairs={{0,64},{1,961},{2,66},{3,963},{4,68},{5,965},{6,70},{7,967},{8,72}... | collective-permute-start | bytes 393224 | tf_op jit(solution)/shard_map/ppermute | solution.py:43
  169.3 7.2 %collective-permute-start.27 = (bf16[512,128]{1,0:T(8,128)(2,1)S(1)}, bf16[512,128]{1,0:T(8,128)(2,1)S(1)}, u32[]{:S(2)}, u32[]{:S(2)}) collective-permute-start(bf16[512,128]{1,0:T(8,128)(2,1)S(1)} %collective-permute-done.25.refs_7_), channel_id=1, source_target_pairs={{0,64},{1,961},{2,66},{3,963},{4,68},{5,965},{6,70},{7,967},{8,72}... | collective-permute-start | bytes 393224 | tf_op jit(solution)/shard_map/ppermute | solution.py:43
  173.3 6.9 %collective-permute-start.28 = (bf16[512,128]{1,0:T(8,128)(2,1)S(1)}, bf16[512,128]{1,0:T(8,128)(2,1)S(1)}, u32[]{:S(2)}, u32[]{:S(2)}) collective-permute-start(bf16[512,128]{1,0:T(8,128)(2,1)S(1)} %collective-permute-done.26.refs_8_), channel_id=1, source_target_pairs={{0,64},{1,961},{2,66},{3,963},{4,68},{5,965},{6,70},{7,967},{8,72}... | collective-permute-start | bytes 393224 | tf_op jit(solution)/shard_map/ppermute | solution.py:43
  180.2 37.7 %collective-permute-start.35 = (bf16[3072,128]{1,0:T(8,128)(2,1)S(1)}, bf16[3072,128]{1,0:T(8,128)(2,1)S(1)}, u32[]{:S(2)}, u32[]{:S(2)}) collective-permute-start(bf16[3072,128]{1,0:T(8,128)(2,1)S(1)} %constant_dynamic-update-slice_fusion.12), channel_id=1, source_target_pairs={{0,1},{1,0},{2,3},{3,2},{4,5},{5,4},{6,7},{7,6},{8,9},{9,8},{10,11... | collective-permute-start | bytes 2359304 | tf_op jit(solution)/shard_map/ppermute | solution.py:48
  186.8 6.7 %collective-permute-start.29 = (bf16[512,128]{1,0:T(8,128)(2,1)S(1)}, bf16[512,128]{1,0:T(8,128)(2,1)S(1)}, u32[]{:S(2)}, u32[]{:S(2)}) collective-permute-start(bf16[512,128]{1,0:T(8,128)(2,1)S(1)} %collective-permute-done.27.refs_9_), channel_id=1, source_target_pairs={{0,64},{1,961},{2,66},{3,963},{4,68},{5,965},{6,70},{7,967},{8,72}... | collective-permute-start | bytes 393224 | tf_op jit(solution)/shard_map/ppermute | solution.py:43
  190.9 10.6 %collective-permute-start.30 = (bf16[512,128]{1,0:T(8,128)(2,1)S(1)}, bf16[512,128]{1,0:T(8,128)(2,1)S(1)}, u32[]{:S(2)}, u32[]{:S(2)}) collective-permute-start(bf16[512,128]{1,0:T(8,128)(2,1)S(1)} %collective-permute-done.28.refs_10_), channel_id=1, source_target_pairs={{0,64},{1,961},{2,66},{3,963},{4,68},{5,965},{6,70},{7,967},{8,72}... | collective-permute-start | bytes 393224 | tf_op jit(solution)/shard_map/ppermute | solution.py:43
  193.5 11.3 %collective-permute-start.31 = (bf16[512,128]{1,0:T(8,128)(2,1)S(1)}, bf16[512,128]{1,0:T(8,128)(2,1)S(1)}, u32[]{:S(2)}, u32[]{:S(2)}) collective-permute-start(bf16[512,128]{1,0:T(8,128)(2,1)S(1)} %collective-permute-done.29.refs_11_), channel_id=1, source_target_pairs={{0,64},{1,961},{2,66},{3,963},{4,68},{5,965},{6,70},{7,967},{8,72}... | collective-permute-start | bytes 393224 | tf_op jit(solution)/shard_map/ppermute | solution.py:43
  201.5 9.2 %collective-permute-start.32 = (bf16[512,128]{1,0:T(8,128)(2,1)S(1)}, bf16[512,128]{1,0:T(8,128)(2,1)S(1)}, u32[]{:S(2)}, u32[]{:S(2)}) collective-permute-start(bf16[512,128]{1,0:T(8,128)(2,1)S(1)} %collective-permute-done.30.refs_12_), channel_id=1, source_target_pairs={{0,64},{1,961},{2,66},{3,963},{4,68},{5,965},{6,70},{7,967},{8,72}... | collective-permute-start | bytes 393224 | tf_op jit(solution)/shard_map/ppermute | solution.py:43
  204.8 9.2 %collective-permute-start.33 = (bf16[512,128]{1,0:T(8,128)(2,1)S(1)}, bf16[512,128]{1,0:T(8,128)(2,1)S(1)}, u32[]{:S(2)}, u32[]{:S(2)}) collective-permute-start(bf16[512,128]{1,0:T(8,128)(2,1)S(1)} %collective-permute-done.31.refs_13_), channel_id=1, source_target_pairs={{0,64},{1,961},{2,66},{3,963},{4,68},{5,965},{6,70},{7,967},{8,72}... | collective-permute-start | bytes 393224 | tf_op jit(solution)/shard_map/ppermute | solution.py:43
  210.8 7.2 %collective-permute-start.34 = (bf16[512,128]{1,0:T(8,128)(2,1)S(1)}, bf16[512,128]{1,0:T(8,128)(2,1)S(1)}, u32[]{:S(2)}, u32[]{:S(2)}) collective-permute-start(bf16[512,128]{1,0:T(8,128)(2,1)S(1)} %collective-permute-done.32.refs_14_), channel_id=1, source_target_pairs={{0,64},{1,961},{2,66},{3,963},{4,68},{5,965},{6,70},{7,967},{8,72}... | collective-permute-start | bytes 393224 | tf_op jit(solution)/shard_map/ppermute | solution.py:43
  217.9 32.6 %copy-start.2 = (bf16[3072,128]{1,0:T(8,128)(2,1)}, bf16[3072,128]{1,0:T(8,128)(2,1)S(1)}, u32[]{:S(2)}) copy-start(bf16[3072,128]{1,0:T(8,128)(2,1)S(1)} %collective-permute-done.35.refs_19_) | copy-start | bytes 2359300
  218.0 14.6 %collective-permute-start.38 = (bf16[3072,128]{1,0:T(8,128)(2,1)S(1)}, bf16[3072,128]{1,0:T(8,128)(2,1)S(1)}, u32[]{:S(2)}, u32[]{:S(2)}) collective-permute-start(bf16[3072,128]{1,0:T(8,128)(2,1)S(1)} %constant_dynamic-update-slice_fusion.18), channel_id=1, source_target_pairs={{0,1},{1,0},{2,3},{3,2},{4,5},{5,4},{6,7},{7,6},{8,9},{9,8},{10,11... | collective-permute-start | bytes 2359304 | tf_op jit(solution)/shard_map/ppermute | solution.py:48
  222.0 9.1 %collective-permute-start.36 = (bf16[512,128]{1,0:T(8,128)(2,1)S(1)}, bf16[512,128]{1,0:T(8,128)(2,1)S(1)}, u32[]{:S(2)}, u32[]{:S(2)}) collective-permute-start(bf16[512,128]{1,0:T(8,128)(2,1)S(1)} %collective-permute-done.33.refs_15_), channel_id=1, source_target_pairs={{0,64},{1,961},{2,66},{3,963},{4,68},{5,965},{6,70},{7,967},{8,72}... | collective-permute-start | bytes 393224 | tf_op jit(solution)/shard_map/ppermute | solution.py:43
  224.0 8.6 %collective-permute-start.37 = (bf16[512,128]{1,0:T(8,128)(2,1)S(1)}, bf16[512,128]{1,0:T(8,128)(2,1)S(1)}, u32[]{:S(2)}, u32[]{:S(2)}) collective-permute-start(bf16[512,128]{1,0:T(8,128)(2,1)S(1)} %collective-permute-done.34.refs_16_), channel_id=1, source_target_pairs={{0,64},{1,961},{2,66},{3,963},{4,68},{5,965},{6,70},{7,967},{8,72}... | collective-permute-start | bytes 393224 | tf_op jit(solution)/shard_map/ppermute | solution.py:43
  231.1 10.0 %copy-start.6 = (bf16[512,128]{1,0:T(8,128)(2,1)}, bf16[512,128]{1,0:T(8,128)(2,1)S(1)}, u32[]{:S(2)}) copy-start(bf16[512,128]{1,0:T(8,128)(2,1)S(1)} %collective-permute-done.36.refs_17_) | copy-start | bytes 393220
  232.6 8.6 %copy-start.7 = (bf16[512,128]{1,0:T(8,128)(2,1)}, bf16[512,128]{1,0:T(8,128)(2,1)S(1)}, u32[]{:S(2)}) copy-start(bf16[512,128]{1,0:T(8,128)(2,1)S(1)} %collective-permute-done.37.refs_18_) | copy-start | bytes 393220
  232.6 18.0 %copy-start.3 = (bf16[3072,128]{1,0:T(8,128)(2,1)}, bf16[3072,128]{1,0:T(8,128)(2,1)S(1)}, u32[]{:S(2)}) copy-start(bf16[3072,128]{1,0:T(8,128)(2,1)S(1)} %collective-permute-done.38.refs_20_) | copy-start | bytes 2359300
  232.6 8.5 %collective-permute-start.39 = (bf16[512,128]{1,0:T(8,128)(2,1)S(1)}, bf16[512,128]{1,0:T(8,128)(2,1)S(1)}, u32[]{:S(2)}, u32[]{:S(2)}) collective-permute-start(bf16[512,128]{1,0:T(8,128)(2,1)S(1)} %collective-permute-done.36.refs_17_), channel_id=1, source_target_pairs={{0,64},{1,961},{2,66},{3,963},{4,68},{5,965},{6,70},{7,967},{8,72}... | collective-permute-start | bytes 393224 | tf_op jit(solution)/shard_map/ppermute | solution.py:43
  241.1 8.0 %copy-start.8 = (bf16[512,128]{1,0:T(8,128)(2,1)}, bf16[512,128]{1,0:T(8,128)(2,1)S(1)}, u32[]{:S(2)}) copy-start(bf16[512,128]{1,0:T(8,128)(2,1)S(1)} %collective-permute-done.39.refs_21_) | copy-start | bytes 393220
  241.1 9.4 %collective-permute-start.40 = (bf16[1536,128]{1,0:T(8,128)(2,1)S(1)}, bf16[1536,128]{1,0:T(8,128)(2,1)}, u32[]{:S(2)}, u32[]{:S(2)}) collective-permute-start(bf16[1536,128]{1,0:T(8,128)(2,1)S(1)} %pad_maximum_fusion.1), channel_id=1, source_target_pairs={{0,1},{1,0},{2,3},{3,2},{4,5},{5,4},{6,7},{7,6},{8,9},{9,8},{10,11... | collective-permute-start | bytes 1179656 | tf_op jit(solution)/shard_map/ppermute | solution.py:48
  258.4 6.3 %collective-permute-start.41 = (bf16[512,128]{1,0:T(8,128)(2,1)S(1)}, bf16[512,128]{1,0:T(8,128)(2,1)S(1)}, u32[]{:S(2)}, u32[]{:S(2)}) collective-permute-start(bf16[512,128]{1,0:T(8,128)(2,1)S(1)} %shard_map.74), channel_id=1, source_target_pairs={{0,0},{1,32},{2,2},{3,34},{4,4},{5,36},{6,6},{7,38},{8,8},{9,40},{... | collective-permute-start | bytes 393224 | tf_op jit(solution)/shard_map/ppermute | solution.py:43
Sparse Core Ops, SparseCore 0:
  42.7 84.6 all-gather.2
  161.1 80.8 all-gather.4

commit v6 on v5

--- a/solution.py
+++ b/solution.py
@@ -156,9 +156,9 @@
 def gather(unit, pal, sibling, up, down):
     rows = unit.shape[0]
     near = jnp.concatenate([unit, pal])
-    near, sibling, up, down = lax.optimization_barrier((near, sibling, up, down))
+    near, up, down = lax.optimization_barrier((near, up, down))
     a_all = lax.all_gather(near, ("x", "y"), axis=0, tiled=True)
-    chains, first, second = ring(up, down)
+    chains, first, second, sibling = ring(up, down, sibling)
     last = move(chains[0][6], hop)
     final = across(jnp.concatenate([chains[0][6], chains[1][6], last]), "core", 1)
     placed = [(unit, {0: (0, 0)}), (sibling, {0: (0, 1)})]
@@ -170,7 +170,7 @@
     return a_all, placed
 
 
-def ring(up, down):
+def ring(up, down, sibling):
     chains = [[up], [down]]
 
     def on():
@@ -184,11 +184,13 @@
         on()
     first = to_other(0, 3)
     on()
-    chains[0][5], chains[1][5], first = lax.optimization_barrier((chains[0][5], chains[1][5], first))
+    chains[0][5], chains[1][5], first, sibling = lax.optimization_barrier(
+        (chains[0][5], chains[1][5], first, sibling)
+    )
     on()
     second = to_other(3, 6)
     chains[0][6], chains[1][6], second = lax.optimization_barrier((chains[0][6], chains[1][6], second))
-    return chains, first, second
+    return chains, first, second, sibling
 
 
 def table(placed):

time: 274 us -> 269 us (0.982); the launches traced: 272 us -> 264 us
  waiting for transfers between devices: 61.3 us -> 55.1 us
    ppermute x36, waiting for transfers between devices: 58.6 us -> 52.8 us  [move(): return lax.ppermute(part, AXES, pairs)]
  transfers between devices with their start and end apart: 44 -> 44, of which waited for: 23 -> 22; matrix products, arithmetic and copies ran while one was open for 1% -> 1% of each run, Pallas kernels for 0% -> 0%
where the time goes in v6:
time: 269 us; the launch traced here: 264 us
  starting transfers between devices  171 us (64%)
  waiting for transfers between devices  55.1 us (20%)
  Pallas kernels  17.9 us (7%)
  between operations  14.1 us (5%)
  other arithmetic  4.19 us (2%)
    ppermute x36, starting transfers between devices, move(): return lax.ppermute(part, AXES, pairs)  145 us
    ppermute x36, waiting for transfers between devices, move(): return lax.ppermute(part, AXES, pairs)  52.8 us
    ppermute x6, starting transfers between devices, across(): return lax.ppermute(part, axis, [(i, i ^ mask) for i in range(size)])  25.9 us
    pallas_call x2, Pallas kernels, multiply(): pl.pallas_call(functools.partial(kernel, rows, units, first), out_shape=o...  17.9 us
  transfers between devices with their start and end apart: 44, of which 22 were waited for; matrix products, arithmetic and copies ran while one was open for 1% of the time, Pallas kernels for 0%

profile of v6, /device:TPU:1, one launch (start us, length us, event | category | flops | bytes accessed | tf_op | source)
XLA Modules:
  0.0 264.2 jit_solution(2391303984039159421)
XLA Ops:
  7.2 0.9 fusion.1
  8.2 4.9 %collective-permute-start = (bf16[528,128]{1,0:T(8,128)(2,1)S(1)}, bf16[528,128]{1,0:T(8,128)(2,1)S(1)}, u32[]{:S(2)}, u32[]{:S(2)}) collective-permute-start(bf16[528,128]{1,0:T(8,128)(2,1)S(1)} %fusion.1), channel_id=1, source_target_pairs={{0,0},{1,32},{2,2},{3,34},{4,4},{5,36},{6,6},{7,38},{8,8},{9,40},{... | collective-permute-start | bytes 405512 | tf_op jit(solution)/shard_map/ppermute | solution.py:43
  13.1 11.8 %collective-permute-start.1 = (bf16[528,128]{1,0:T(8,128)(2,1)S(1)}, bf16[528,128]{1,0:T(8,128)(2,1)S(1)}, u32[]{:S(2)}, u32[]{:S(2)}) collective-permute-start(bf16[528,128]{1,0:T(8,128)(2,1)S(1)} %fusion.1), channel_id=1, source_target_pairs={{0,32},{1,0},{2,34},{3,2},{4,36},{5,4},{6,38},{7,6},{8,40},{9,8},{... | collective-permute-start | bytes 405512 | tf_op jit(solution)/shard_map/ppermute | solution.py:43
  24.9 1.9 collective-permute-start.2
  26.8 9.5 %collective-permute-start.3 = (bf16[528,128]{1,0:T(8,128)(2,1)S(1)}, bf16[528,128]{1,0:T(8,128)(2,1)S(1)}, u32[]{:S(2)}, u32[]{:S(2)}) collective-permute-start(bf16[528,128]{1,0:T(8,128)(2,1)S(1)} %fusion.1), channel_id=1, source_target_pairs={{0,961},{1,993},{2,963},{3,995},{4,965},{5,997},{6,967},{7,999},{8... | collective-permute-start | bytes 405512 | tf_op jit(solution)/shard_map/ppermute | solution.py:43
  37.1 3.4 %collective-permute-done.3.refs_5_ = bf16[528,128]{1,0:T(8,128)(2,1)S(1)} collective-permute-done((bf16[528,128]{1,0:T(8,128)(2,1)S(1)}, bf16[528,128]{1,0:T(8,128)(2,1)S(1)}, u32[]{:S(2)}, u32[]{:S(2)}) %collective-permute-start.3) | collective-permute-done | bytes 135200 | tf_op jit(solution)/shard_map/ppermute | solution.py:43
  40.6 5.8 %collective-permute-start.4 = (bf16[528,128]{1,0:T(8,128)(2,1)S(1)}, bf16[528,128]{1,0:T(8,128)(2,1)S(1)}, u32[]{:S(2)}, u32[]{:S(2)}) collective-permute-start(bf16[528,128]{1,0:T(8,128)(2,1)S(1)} %collective-permute-done.2.refs_4_), channel_id=1, source_target_pairs={{0,64},{1,961},{2,66},{3,963},{4,68},{5,965},{6,70},{7,967},{8,72}... | collective-permute-start | bytes 405512 | tf_op jit(solution)/shard_map/ppermute | solution.py:43
  46.4 2.2 collective-permute-start.9
  48.6 2.6 collective-permute-done.4.refs_6_
  51.2 6.0 %collective-permute-start.5 = (bf16[528,128]{1,0:T(8,128)(2,1)S(1)}, bf16[528,128]{1,0:T(8,128)(2,1)S(1)}, u32[]{:S(2)}, u32[]{:S(2)}) collective-permute-start(bf16[528,128]{1,0:T(8,128)(2,1)S(1)} %collective-permute-done.4.refs_6_), channel_id=1, source_target_pairs={{0,64},{1,961},{2,66},{3,963},{4,68},{5,965},{6,70},{7,967},{8,72}... | collective-permute-start | bytes 405512 | tf_op jit(solution)/shard_map/ppermute | solution.py:43
  57.3 2.4 collective-permute-start.10
  59.8 1.3 collective-permute-done.5.refs_8_
  61.0 3.2 %collective-permute-done.10.refs_9_ = bf16[528,128]{1,0:T(8,128)(2,1)S(1)} collective-permute-done((bf16[528,128]{1,0:T(8,128)(2,1)S(1)}, bf16[528,128]{1,0:T(8,128)(2,1)S(1)}, u32[]{:S(2)}, u32[]{:S(2)}) %collective-permute-start.10) | collective-permute-done | bytes 135200 | tf_op jit(solution)/shard_map/ppermute | solution.py:43
  64.2 4.6 %collective-permute-start.14 = (bf16[3168,128]{1,0:T(8,128)(2,1)S(1)}, bf16[3168,128]{1,0:T(8,128)(2,1)S(1)}, u32[]{:S(2)}, u32[]{:S(2)}) collective-permute-start(bf16[3168,128]{1,0:T(8,128)(2,1)S(1)} %constant_dynamic-update-slice_fusion), channel_id=1, source_target_pairs={{0,1},{1,0},{2,3},{3,2},{4,5},{5,4},{6,7},{7,6},{8,9},{9,8},{10,11... | collective-permute-start | bytes 2433032 | tf_op jit(solution)/shard_map/ppermute | solution.py:48
  68.9 1.9 collective-permute-start.11
  70.8 3.6 %collective-permute-start.6 = (bf16[528,128]{1,0:T(8,128)(2,1)S(1)}, bf16[528,128]{1,0:T(8,128)(2,1)S(1)}, u32[]{:S(2)}, u32[]{:S(2)}) collective-permute-start(bf16[528,128]{1,0:T(8,128)(2,1)S(1)} %collective-permute-done.5.refs_8_), channel_id=1, source_target_pairs={{0,64},{1,961},{2,66},{3,963},{4,68},{5,965},{6,70},{7,967},{8,72}... | collective-permute-start | bytes 405512 | tf_op jit(solution)/shard_map/ppermute | solution.py:43
  74.4 4.6 %collective-permute-start.15 = (bf16[528,128]{1,0:T(8,128)(2,1)S(1)}, bf16[528,128]{1,0:T(8,128)(2,1)S(1)}, u32[]{:S(2)}, u32[]{:S(2)}) collective-permute-start(bf16[528,128]{1,0:T(8,128)(2,1)S(1)} %fusion.1), channel_id=1, source_target_pairs={{0,1},{1,33},{2,3},{3,35},{4,5},{5,37},{6,7},{7,39},{8,9},{9,41},{... | collective-permute-start | bytes 405512 | tf_op jit(solution)/shard_map/ppermute | solution.py:43
  79.0 3.6 %collective-permute-start.12 = (bf16[528,128]{1,0:T(8,128)(2,1)S(1)}, bf16[528,128]{1,0:T(8,128)(2,1)S(1)}, u32[]{:S(2)}, u32[]{:S(2)}) collective-permute-start(bf16[528,128]{1,0:T(8,128)(2,1)S(1)} %collective-permute-done.11.refs_11_), channel_id=1, source_target_pairs={{0,64},{1,961},{2,66},{3,963},{4,68},{5,965},{6,70},{7,967},{8,72}... | collective-permute-start | bytes 405512 | tf_op jit(solution)/shard_map/ppermute | solution.py:43
  82.7 4.2 %collective-permute-start.7 = (bf16[528,128]{1,0:T(8,128)(2,1)S(1)}, bf16[528,128]{1,0:T(8,128)(2,1)S(1)}, u32[]{:S(2)}, u32[]{:S(2)}) collective-permute-start(bf16[528,128]{1,0:T(8,128)(2,1)S(1)} %collective-permute-done.6.refs_10_), channel_id=1, source_target_pairs={{0,64},{1,961},{2,66},{3,963},{4,68},{5,965},{6,70},{7,967},{8,72}... | collective-permute-start | bytes 405512 | tf_op jit(solution)/shard_map/ppermute | solution.py:43
  87.1 4.6 %collective-permute-start.13 = (bf16[528,128]{1,0:T(8,128)(2,1)S(1)}, bf16[528,128]{1,0:T(8,128)(2,1)S(1)}, u32[]{:S(2)}, u32[]{:S(2)}) collective-permute-start(bf16[528,128]{1,0:T(8,128)(2,1)S(1)} %collective-permute-done.12.refs_13_), channel_id=1, source_target_pairs={{0,64},{1,961},{2,66},{3,963},{4,68},{5,965},{6,70},{7,967},{8,72}... | collective-permute-start | bytes 405512 | tf_op jit(solution)/shard_map/ppermute | solution.py:43
  91.8 3.6 %collective-permute-start.8 = (bf16[528,128]{1,0:T(8,128)(2,1)S(1)}, bf16[528,128]{1,0:T(8,128)(2,1)S(1)}, u32[]{:S(2)}, u32[]{:S(2)}) collective-permute-start(bf16[528,128]{1,0:T(8,128)(2,1)S(1)} %collective-permute-done.7.refs_12_), channel_id=1, source_target_pairs={{0,64},{1,961},{2,66},{3,963},{4,68},{5,965},{6,70},{7,967},{8,72}... | collective-permute-start | bytes 405512 | tf_op jit(solution)/shard_map/ppermute | solution.py:43
  95.5 3.6 %collective-permute-done.8.refs_14_ = bf16[528,128]{1,0:T(8,128)(2,1)S(1)} collective-permute-done((bf16[528,128]{1,0:T(8,128)(2,1)S(1)}, bf16[528,128]{1,0:T(8,128)(2,1)S(1)}, u32[]{:S(2)}, u32[]{:S(2)}) %collective-permute-start.8) | collective-permute-done | bytes 135200 | tf_op jit(solution)/shard_map/ppermute | solution.py:43
  99.2 5.8 %collective-permute-start.18 = (bf16[3168,128]{1,0:T(8,128)(2,1)S(1)}, bf16[3168,128]{1,0:T(8,128)(2,1)S(1)}, u32[]{:S(2)}, u32[]{:S(2)}) collective-permute-start(bf16[3168,128]{1,0:T(8,128)(2,1)S(1)} %constant_dynamic-update-slice_fusion.6), channel_id=1, source_target_pairs={{0,1},{1,0},{2,3},{3,2},{4,5},{5,4},{6,7},{7,6},{8,9},{9,8},{10,11... | collective-permute-start | bytes 2433032 | tf_op jit(solution)/shard_map/ppermute | solution.py:48
  104.9 5.0 %collective-permute-start.16 = (bf16[528,128]{1,0:T(8,128)(2,1)S(1)}, bf16[528,128]{1,0:T(8,128)(2,1)}, u32[]{:S(2)}, u32[]{:S(2)}) collective-permute-start(bf16[528,128]{1,0:T(8,128)(2,1)S(1)} %collective-permute-done.8.refs_14_), channel_id=1, source_target_pairs={{0,64},{1,961},{2,66},{3,963},{4,68},{5,965},{6,70},{7,967},{8,72}... | collective-permute-start | bytes 405512 | tf_op jit(solution)/shard_map/ppermute | solution.py:43
  110.0 1.9 collective-permute-start.17
  112.0 5.1 %collective-permute-done.17.refs_17_ = bf16[528,128]{1,0:T(8,128)(2,1)S(1)} collective-permute-done((bf16[528,128]{1,0:T(8,128)(2,1)S(1)}, bf16[528,128]{1,0:T(8,128)(2,1)S(1)}, u32[]{:S(2)}, u32[]{:S(2)}) %collective-permute-start.17) | collective-permute-done | bytes 135200 | tf_op jit(solution)/shard_map/ppermute | solution.py:43
  117.1 4.2 %collective-permute-start.19 = (bf16[528,128]{1,0:T(8,128)(2,1)}, bf16[528,128]{1,0:T(8,128)(2,1)}, u32[]{:S(2)}, u32[]{:S(2)}) collective-permute-start(bf16[528,128]{1,0:T(8,128)(2,1)} %collective-permute-done.16.refs_16_), channel_id=1, source_target_pairs={{0,64},{1,961},{2,66},{3,963},{4,68},{5,965},{6,70},{7,967},{8,72}... | collective-permute-start | bytes 405512 | tf_op jit(solution)/shard_map/ppermute | solution.py:43
  121.3 2.8 %collective-permute-done.19.refs_20_ = bf16[528,128]{1,0:T(8,128)(2,1)} collective-permute-done((bf16[528,128]{1,0:T(8,128)(2,1)}, bf16[528,128]{1,0:T(8,128)(2,1)}, u32[]{:S(2)}, u32[]{:S(2)}) %collective-permute-start.19) | collective-permute-done | bytes 135200 | tf_op jit(solution)/shard_map/ppermute | solution.py:43
  124.1 1.0 pad_maximum_fusion
  125.2 4.1 %collective-permute-start.20 = (bf16[1584,128]{1,0:T(8,128)(2,1)S(1)}, bf16[1584,128]{1,0:T(8,128)(2,1)}, u32[]{:S(2)}, u32[]{:S(2)}) collective-permute-start(bf16[1584,128]{1,0:T(8,128)(2,1)S(1)} %pad_maximum_fusion), channel_id=1, source_target_pairs={{0,1},{1,0},{2,3},{3,2},{4,5},{5,4},{6,7},{7,6},{8,9},{9,8},{10,11... | collective-permute-start | bytes 1216520 | tf_op jit(solution)/shard_map/ppermute | solution.py:48
  130.0 0.8 collective-permute-done.20.refs_21_
  130.8 9.8 %shard_map.73 = (bf16[512,128]{1,0:T(8,128)(2,1)S(1)}, s32[64,128]{1,0:T(8,128)S(1)}) custom-call(s32[1]{0:T(128)} %get-tuple-element.49.branch, s32[33]{0:T(128)S(1)} %pad_add_fusion.tab, bf16[528,128]{1,0:T(8,128)(2,1)S(1)} %collective-permute-done.refs_0_.refs_2_, bf16[16896,128]{1,0:T(8,128)(2,1)} %all-gather.3.cloned.1.call-done.refs_1_, ...), custom_call_target="tpu_custom_call" | custom-call | flops 536870912 | bytes 8388608 | tf_op jit(solution)/shard_map/pallas_call | solution.py:142
  140.6 1.9 collective-permute-start.21
  142.5 5.6 %collective-permute-start.22 = (bf16[512,128]{1,0:T(8,128)(2,1)S(1)}, bf16[512,128]{1,0:T(8,128)(2,1)S(1)}, u32[]{:S(2)}, u32[]{:S(2)}) collective-permute-start(bf16[512,128]{1,0:T(8,128)(2,1)S(1)} %get-tuple-element.38.refs_1_.refs_3_), channel_id=1, source_target_pairs={{0,64},{1,961},{2,66},{3,963},{4,68},{5,965},{6,70},{7,967},{8,72}... | collective-permute-start | bytes 393224 | tf_op jit(solution)/shard_map/ppermute | solution.py:43
  148.1 1.9 collective-permute-start.23
  150.8 5.9 %collective-permute-done.23.refs_6_ = bf16[512,128]{1,0:T(8,128)(2,1)S(1)} collective-permute-done((bf16[512,128]{1,0:T(8,128)(2,1)S(1)}, bf16[512,128]{1,0:T(8,128)(2,1)S(1)}, u32[]{:S(2)}, u32[]{:S(2)}) %collective-permute-start.23) | collective-permute-done | bytes 131104 | tf_op jit(solution)/shard_map/ppermute | solution.py:43
  156.7 5.5 %collective-permute-start.24 = (bf16[512,128]{1,0:T(8,128)(2,1)S(1)}, bf16[512,128]{1,0:T(8,128)(2,1)S(1)}, u32[]{:S(2)}, u32[]{:S(2)}) collective-permute-start(bf16[512,128]{1,0:T(8,128)(2,1)S(1)} %collective-permute-done.22.refs_5_), channel_id=1, source_target_pairs={{0,64},{1,961},{2,66},{3,963},{4,68},{5,965},{6,70},{7,967},{8,72}... | collective-permute-start | bytes 393224 | tf_op jit(solution)/shard_map/ppermute | solution.py:43
  162.2 1.9 collective-permute-start.29
  164.2 2.7 %collective-permute-done.24.refs_7_ = bf16[512,128]{1,0:T(8,128)(2,1)S(1)} collective-permute-done((bf16[512,128]{1,0:T(8,128)(2,1)S(1)}, bf16[512,128]{1,0:T(8,128)(2,1)S(1)}, u32[]{:S(2)}, u32[]{:S(2)}) %collective-permute-start.24) | collective-permute-done | bytes 131104 | tf_op jit(solution)/shard_map/ppermute | solution.py:43
  166.9 5.9 %collective-permute-start.25 = (bf16[512,128]{1,0:T(8,128)(2,1)S(1)}, bf16[512,128]{1,0:T(8,128)(2,1)S(1)}, u32[]{:S(2)}, u32[]{:S(2)}) collective-permute-start(bf16[512,128]{1,0:T(8,128)(2,1)S(1)} %collective-permute-done.24.refs_7_), channel_id=1, source_target_pairs={{0,64},{1,961},{2,66},{3,963},{4,68},{5,965},{6,70},{7,967},{8,72}... | collective-permute-start | bytes 393224 | tf_op jit(solution)/shard_map/ppermute | solution.py:43
  172.8 1.9 collective-permute-start.30
  174.8 2.2 collective-permute-done.25.refs_9_
  177.0 2.5 collective-permute-done.30.refs_10_
  179.5 1.9 collective-permute-start.34
  181.5 4.8 %collective-permute-start.26 = (bf16[512,128]{1,0:T(8,128)(2,1)S(1)}, bf16[512,128]{1,0:T(8,128)(2,1)S(1)}, u32[]{:S(2)}, u32[]{:S(2)}) collective-permute-start(bf16[512,128]{1,0:T(8,128)(2,1)S(1)} %collective-permute-done.25.refs_9_), channel_id=1, source_target_pairs={{0,64},{1,961},{2,66},{3,963},{4,68},{5,965},{6,70},{7,967},{8,72}... | collective-permute-start | bytes 393224 | tf_op jit(solution)/shard_map/ppermute | solution.py:43
  186.3 1.9 collective-permute-start.31
  188.2 3.0 %collective-permute-start.35 = (bf16[512,128]{1,0:T(8,128)(2,1)S(1)}, bf16[512,128]{1,0:T(8,128)(2,1)S(1)}, u32[]{:S(2)}, u32[]{:S(2)}) collective-permute-start(bf16[512,128]{1,0:T(8,128)(2,1)S(1)} %get-tuple-element.38.refs_1_.refs_3_), channel_id=1, source_target_pairs={{0,1},{1,0},{2,3},{3,2},{4,5},{5,4},{6,7},{7,6},{8,9},{9,8},{10,11... | collective-permute-start | bytes 393224 | tf_op jit(solution)/shard_map/ppermute | solution.py:43
  191.2 4.2 %collective-permute-start.27 = (bf16[512,128]{1,0:T(8,128)(2,1)S(1)}, bf16[512,128]{1,0:T(8,128)(2,1)S(1)}, u32[]{:S(2)}, u32[]{:S(2)}) collective-permute-start(bf16[512,128]{1,0:T(8,128)(2,1)S(1)} %collective-permute-done.26.refs_11_), channel_id=1, source_target_pairs={{0,64},{1,961},{2,66},{3,963},{4,68},{5,965},{6,70},{7,967},{8,72}... | collective-permute-start | bytes 393224 | tf_op jit(solution)/shard_map/ppermute | solution.py:43
  195.4 3.4 %collective-permute-start.32 = (bf16[512,128]{1,0:T(8,128)(2,1)S(1)}, bf16[512,128]{1,0:T(8,128)(2,1)S(1)}, u32[]{:S(2)}, u32[]{:S(2)}) collective-permute-start(bf16[512,128]{1,0:T(8,128)(2,1)S(1)} %collective-permute-done.31.refs_12_), channel_id=1, source_target_pairs={{0,64},{1,961},{2,66},{3,963},{4,68},{5,965},{6,70},{7,967},{8,72}... | collective-permute-start | bytes 393224 | tf_op jit(solution)/shard_map/ppermute | solution.py:43
  199.5 5.2 %collective-permute-start.28 = (bf16[512,128]{1,0:T(8,128)(2,1)S(1)}, bf16[512,128]{1,0:T(8,128)(2,1)S(1)}, u32[]{:S(2)}, u32[]{:S(2)}) collective-permute-start(bf16[512,128]{1,0:T(8,128)(2,1)S(1)} %collective-permute-done.27.refs_13_), channel_id=1, source_target_pairs={{0,64},{1,961},{2,66},{3,963},{4,68},{5,965},{6,70},{7,967},{8,72}... | collective-permute-start | bytes 393224 | tf_op jit(solution)/shard_map/ppermute | solution.py:43
  204.7 2.0 collective-permute-start.33
  206.8 1.2 collective-permute-done.28.refs_15_
  208.0 4.5 %collective-permute-done.33.refs_16_ = bf16[512,128]{1,0:T(8,128)(2,1)S(1)} collective-permute-done((bf16[512,128]{1,0:T(8,128)(2,1)S(1)}, bf16[512,128]{1,0:T(8,128)(2,1)S(1)}, u32[]{:S(2)}, u32[]{:S(2)}) %collective-permute-start.33) | collective-permute-done | bytes 131104 | tf_op jit(solution)/shard_map/ppermute | solution.py:43
  212.5 4.7 %collective-permute-start.38 = (bf16[3072,128]{1,0:T(8,128)(2,1)S(1)}, bf16[3072,128]{1,0:T(8,128)(2,1)S(1)}, u32[]{:S(2)}, u32[]{:S(2)}) collective-permute-start(bf16[3072,128]{1,0:T(8,128)(2,1)S(1)} %constant_dynamic-update-slice_fusion.18), channel_id=1, source_target_pairs={{0,1},{1,0},{2,3},{3,2},{4,5},{5,4},{6,7},{7,6},{8,9},{9,8},{10,11... | collective-permute-start | bytes 2359304 | tf_op jit(solution)/shard_map/ppermute | solution.py:48
  217.2 2.8 %collective-permute-start.36 = (bf16[512,128]{1,0:T(8,128)(2,1)S(1)}, bf16[512,128]{1,0:T(8,128)(2,1)S(1)}, u32[]{:S(2)}, u32[]{:S(2)}) collective-permute-start(bf16[512,128]{1,0:T(8,128)(2,1)S(1)} %collective-permute-done.28.refs_15_), channel_id=1, source_target_pairs={{0,64},{1,961},{2,66},{3,963},{4,68},{5,965},{6,70},{7,967},{8,72}... | collective-permute-start | bytes 393224 | tf_op jit(solution)/shard_map/ppermute | solution.py:43
  220.0 3.7 %collective-permute-start.37 = (bf16[512,128]{1,0:T(8,128)(2,1)S(1)}, bf16[512,128]{1,0:T(8,128)(2,1)S(1)}, u32[]{:S(2)}, u32[]{:S(2)}) collective-permute-start(bf16[512,128]{1,0:T(8,128)(2,1)S(1)} %collective-permute-done.33.refs_16_), channel_id=1, source_target_pairs={{0,64},{1,961},{2,66},{3,963},{4,68},{5,965},{6,70},{7,967},{8,72}... | collective-permute-start | bytes 393224 | tf_op jit(solution)/shard_map/ppermute | solution.py:43
  224.2 4.3 %collective-permute-done.37.refs_18_ = bf16[512,128]{1,0:T(8,128)(2,1)S(1)} collective-permute-done((bf16[512,128]{1,0:T(8,128)(2,1)S(1)}, bf16[512,128]{1,0:T(8,128)(2,1)S(1)}, u32[]{:S(2)}, u32[]{:S(2)}) %collective-permute-start.37) | collective-permute-done | bytes 131104 | tf_op jit(solution)/shard_map/ppermute | solution.py:43
  228.5 3.4 %collective-permute-start.39 = (bf16[512,128]{1,0:T(8,128)(2,1)S(1)}, bf16[512,128]{1,0:T(8,128)(2,1)S(1)}, u32[]{:S(2)}, u32[]{:S(2)}) collective-permute-start(bf16[512,128]{1,0:T(8,128)(2,1)S(1)} %collective-permute-done.36.refs_17_), channel_id=1, source_target_pairs={{0,64},{1,961},{2,66},{3,963},{4,68},{5,965},{6,70},{7,967},{8,72}... | collective-permute-start | bytes 393224 | tf_op jit(solution)/shard_map/ppermute | solution.py:43
  231.9 3.6 %collective-permute-done.39.refs_21_ = bf16[512,128]{1,0:T(8,128)(2,1)S(1)} collective-permute-done((bf16[512,128]{1,0:T(8,128)(2,1)S(1)}, bf16[512,128]{1,0:T(8,128)(2,1)S(1)}, u32[]{:S(2)}, u32[]{:S(2)}) %collective-permute-start.39) | collective-permute-done | bytes 131104 | tf_op jit(solution)/shard_map/ppermute | solution.py:43
  235.6 4.7 %collective-permute-start.40 = (bf16[1536,128]{1,0:T(8,128)(2,1)S(1)}, bf16[1536,128]{1,0:T(8,128)(2,1)}, u32[]{:S(2)}, u32[]{:S(2)}) collective-permute-start(bf16[1536,128]{1,0:T(8,128)(2,1)S(1)} %pad_maximum_fusion.1), channel_id=1, source_target_pairs={{0,1},{1,0},{2,3},{3,2},{4,5},{5,4},{6,7},{7,6},{8,9},{9,8},{10,11... | collective-permute-start | bytes 1179656 | tf_op jit(solution)/shard_map/ppermute | solution.py:48
  240.3 1.4 collective-permute-done.40.refs_22_
  241.8 8.0 %shard_map.74 = bf16[512,128]{1,0:T(8,128)(2,1)S(1)} custom-call(s32[1]{0:T(128)} %get-tuple-element.50.branch, s32[33]{0:T(128)S(1)} %pad_add_fusion.tab, s32[64,128]{1,0:T(8,128)S(1)} %get-tuple-element.37.refs_0_, bf16[512,128]{1,0:T(8,128)(2,1)S(1)} %get-tuple-element.38.refs_1_.refs_3_, bf16[16384,128]{1,0:T(8,128)(2,1)} %all-gather.5.cloned.1.call-done.refs_2_, ...), custom_call_target="tpu_custom_call" | custom-call | flops 536870912 | bytes 8388608 | tf_op jit(solution)/shard_map/pallas_call | solution.py:142
  249.8 4.2 %collective-permute-start.41 = (bf16[512,128]{1,0:T(8,128)(2,1)S(1)}, bf16[512,128]{1,0:T(8,128)(2,1)S(1)}, u32[]{:S(2)}, u32[]{:S(2)}) collective-permute-start(bf16[512,128]{1,0:T(8,128)(2,1)S(1)} %shard_map.74), channel_id=1, source_target_pairs={{0,0},{1,32},{2,2},{3,34},{4,4},{5,36},{6,6},{7,38},{8,8},{9,40},{... | collective-permute-start | bytes 393224 | tf_op jit(solution)/shard_map/ppermute | solution.py:43
  254.0 2.6 collective-permute-done.41
  (86 shorter events, 5.5 us)
Async XLA Ops:
  6.5 122.7 %copy-start.10 = (s32[32]{0:T(128)S(1)}, s32[32]{0:T(128)}, u32[]{:S(2)}) copy-start(s32[32]{0:T(128)} %constant.86.clone) | copy-start | bytes 388
  6.5 122.7 %copy-start.11 = (s32[32]{0:T(128)S(1)}, s32[32]{0:T(128)}, u32[]{:S(2)}) copy-start(s32[32]{0:T(128)} %constant.87.clone) | copy-start | bytes 388
  6.5 122.9 %copy-start.9 = (s32[2]{0:T(128)S(1)}, s32[2]{0:T(128)}, u32[]{:S(2)}) copy-start(s32[2]{0:T(128)} %param.9) | copy-start | bytes 28
  6.5 124.2 %all-gather.3.cloned.1.call-start = ((), (), s32[]{:S(2)}) async-start(), calls=%async_computation | async-start | bytes 4595712 | tf_op jit(solution)/shard_map/all_gather | solution.py:160
  8.2 28.2 %collective-permute-start = (bf16[528,128]{1,0:T(8,128)(2,1)S(1)}, bf16[528,128]{1,0:T(8,128)(2,1)S(1)}, u32[]{:S(2)}, u32[]{:S(2)}) collective-permute-start(bf16[528,128]{1,0:T(8,128)(2,1)S(1)} %fusion.1), channel_id=1, source_target_pairs={{0,0},{1,32},{2,2},{3,34},{4,4},{5,36},{6,6},{7,38},{8,8},{9,40},{... | collective-permute-start | bytes 405512 | tf_op jit(solution)/shard_map/ppermute | solution.py:43
  13.1 23.3 %collective-permute-start.1 = (bf16[528,128]{1,0:T(8,128)(2,1)S(1)}, bf16[528,128]{1,0:T(8,128)(2,1)S(1)}, u32[]{:S(2)}, u32[]{:S(2)}) collective-permute-start(bf16[528,128]{1,0:T(8,128)(2,1)S(1)} %fusion.1), channel_id=1, source_target_pairs={{0,32},{1,0},{2,34},{3,2},{4,36},{5,4},{6,38},{7,6},{8,40},{9,8},{... | collective-permute-start | bytes 405512 | tf_op jit(solution)/shard_map/ppermute | solution.py:43
  24.9 12.2 %collective-permute-start.2 = (bf16[528,128]{1,0:T(8,128)(2,1)S(1)}, bf16[528,128]{1,0:T(8,128)(2,1)S(1)}, u32[]{:S(2)}, u32[]{:S(2)}) collective-permute-start(bf16[528,128]{1,0:T(8,128)(2,1)S(1)} %fusion.1), channel_id=1, source_target_pairs={{0,64},{1,96},{2,66},{3,98},{4,68},{5,100},{6,70},{7,102},{8,72},{... | collective-permute-start | bytes 405512 | tf_op jit(solution)/shard_map/ppermute | solution.py:43
  26.8 13.7 %collective-permute-start.3 = (bf16[528,128]{1,0:T(8,128)(2,1)S(1)}, bf16[528,128]{1,0:T(8,128)(2,1)S(1)}, u32[]{:S(2)}, u32[]{:S(2)}) collective-permute-start(bf16[528,128]{1,0:T(8,128)(2,1)S(1)} %fusion.1), channel_id=1, source_target_pairs={{0,961},{1,993},{2,963},{3,995},{4,965},{5,997},{6,967},{7,999},{8... | collective-permute-start | bytes 405512 | tf_op jit(solution)/shard_map/ppermute | solution.py:43
  40.5 201.2 %all-gather.5.cloned.1.call-start = ((), (), s32[]{:S(2)}) async-start(), calls=%async_computation.1 | async-start | bytes 4456448 | tf_op jit(solution)/shard_map/all_gather | solution.py:160
  40.6 10.6 %collective-permute-start.4 = (bf16[528,128]{1,0:T(8,128)(2,1)S(1)}, bf16[528,128]{1,0:T(8,128)(2,1)S(1)}, u32[]{:S(2)}, u32[]{:S(2)}) collective-permute-start(bf16[528,128]{1,0:T(8,128)(2,1)S(1)} %collective-permute-done.2.refs_4_), channel_id=1, source_target_pairs={{0,64},{1,961},{2,66},{3,963},{4,68},{5,965},{6,70},{7,967},{8,72}... | collective-permute-start | bytes 405512 | tf_op jit(solution)/shard_map/ppermute | solution.py:43
  46.4 10.9 %collective-permute-start.9 = (bf16[528,128]{1,0:T(8,128)(2,1)S(1)}, bf16[528,128]{1,0:T(8,128)(2,1)S(1)}, u32[]{:S(2)}, u32[]{:S(2)}) collective-permute-start(bf16[528,128]{1,0:T(8,128)(2,1)S(1)} %collective-permute-done.3.refs_5_), channel_id=1, source_target_pairs={{0,64},{1,961},{2,66},{3,963},{4,68},{5,965},{6,70},{7,967},{8,72}... | collective-permute-start | bytes 405512 | tf_op jit(solution)/shard_map/ppermute | solution.py:43
  51.2 9.8 %collective-permute-start.5 = (bf16[528,128]{1,0:T(8,128)(2,1)S(1)}, bf16[528,128]{1,0:T(8,128)(2,1)S(1)}, u32[]{:S(2)}, u32[]{:S(2)}) collective-permute-start(bf16[528,128]{1,0:T(8,128)(2,1)S(1)} %collective-permute-done.4.refs_6_), channel_id=1, source_target_pairs={{0,64},{1,961},{2,66},{3,963},{4,68},{5,965},{6,70},{7,967},{8,72}... | collective-permute-start | bytes 405512 | tf_op jit(solution)/shard_map/ppermute | solution.py:43
  57.3 6.9 %collective-permute-start.10 = (bf16[528,128]{1,0:T(8,128)(2,1)S(1)}, bf16[528,128]{1,0:T(8,128)(2,1)S(1)}, u32[]{:S(2)}, u32[]{:S(2)}) collective-permute-start(bf16[528,128]{1,0:T(8,128)(2,1)S(1)} %collective-permute-done.9.refs_7_), channel_id=1, source_target_pairs={{0,64},{1,961},{2,66},{3,963},{4,68},{5,965},{6,70},{7,967},{8,72}... | collective-permute-start | bytes 405512 | tf_op jit(solution)/shard_map/ppermute | solution.py:43
  64.2 34.9 %collective-permute-start.14 = (bf16[3168,128]{1,0:T(8,128)(2,1)S(1)}, bf16[3168,128]{1,0:T(8,128)(2,1)S(1)}, u32[]{:S(2)}, u32[]{:S(2)}) collective-permute-start(bf16[3168,128]{1,0:T(8,128)(2,1)S(1)} %constant_dynamic-update-slice_fusion), channel_id=1, source_target_pairs={{0,1},{1,0},{2,3},{3,2},{4,5},{5,4},{6,7},{7,6},{8,9},{9,8},{10,11... | collective-permute-start | bytes 2433032 | tf_op jit(solution)/shard_map/ppermute | solution.py:48
  68.9 10.1 %collective-permute-start.11 = (bf16[528,128]{1,0:T(8,128)(2,1)S(1)}, bf16[528,128]{1,0:T(8,128)(2,1)S(1)}, u32[]{:S(2)}, u32[]{:S(2)}) collective-permute-start(bf16[528,128]{1,0:T(8,128)(2,1)S(1)} %collective-permute-done.10.refs_9_), channel_id=1, source_target_pairs={{0,64},{1,961},{2,66},{3,963},{4,68},{5,965},{6,70},{7,967},{8,72}... | collective-permute-start | bytes 405512 | tf_op jit(solution)/shard_map/ppermute | solution.py:43
  70.8 11.8 %collective-permute-start.6 = (bf16[528,128]{1,0:T(8,128)(2,1)S(1)}, bf16[528,128]{1,0:T(8,128)(2,1)S(1)}, u32[]{:S(2)}, u32[]{:S(2)}) collective-permute-start(bf16[528,128]{1,0:T(8,128)(2,1)S(1)} %collective-permute-done.5.refs_8_), channel_id=1, source_target_pairs={{0,64},{1,961},{2,66},{3,963},{4,68},{5,965},{6,70},{7,967},{8,72}... | collective-permute-start | bytes 405512 | tf_op jit(solution)/shard_map/ppermute | solution.py:43
  74.4 21.1 %collective-permute-start.15 = (bf16[528,128]{1,0:T(8,128)(2,1)S(1)}, bf16[528,128]{1,0:T(8,128)(2,1)S(1)}, u32[]{:S(2)}, u32[]{:S(2)}) collective-permute-start(bf16[528,128]{1,0:T(8,128)(2,1)S(1)} %fusion.1), channel_id=1, source_target_pairs={{0,1},{1,33},{2,3},{3,35},{4,5},{5,37},{6,7},{7,39},{8,9},{9,41},{... | collective-permute-start | bytes 405512 | tf_op jit(solution)/shard_map/ppermute | solution.py:43
  79.0 8.1 %collective-permute-start.12 = (bf16[528,128]{1,0:T(8,128)(2,1)S(1)}, bf16[528,128]{1,0:T(8,128)(2,1)S(1)}, u32[]{:S(2)}, u32[]{:S(2)}) collective-permute-start(bf16[528,128]{1,0:T(8,128)(2,1)S(1)} %collective-permute-done.11.refs_11_), channel_id=1, source_target_pairs={{0,64},{1,961},{2,66},{3,963},{4,68},{5,965},{6,70},{7,967},{8,72}... | collective-permute-start | bytes 405512 | tf_op jit(solution)/shard_map/ppermute | solution.py:43
  82.7 9.1 %collective-permute-start.7 = (bf16[528,128]{1,0:T(8,128)(2,1)S(1)}, bf16[528,128]{1,0:T(8,128)(2,1)S(1)}, u32[]{:S(2)}, u32[]{:S(2)}) collective-permute-start(bf16[528,128]{1,0:T(8,128)(2,1)S(1)} %collective-permute-done.6.refs_10_), channel_id=1, source_target_pairs={{0,64},{1,961},{2,66},{3,963},{4,68},{5,965},{6,70},{7,967},{8,72}... | collective-permute-start | bytes 405512 | tf_op jit(solution)/shard_map/ppermute | solution.py:43
  87.1 8.4 %collective-permute-start.13 = (bf16[528,128]{1,0:T(8,128)(2,1)S(1)}, bf16[528,128]{1,0:T(8,128)(2,1)S(1)}, u32[]{:S(2)}, u32[]{:S(2)}) collective-permute-start(bf16[528,128]{1,0:T(8,128)(2,1)S(1)} %collective-permute-done.12.refs_13_), channel_id=1, source_target_pairs={{0,64},{1,961},{2,66},{3,963},{4,68},{5,965},{6,70},{7,967},{8,72}... | collective-permute-start | bytes 405512 | tf_op jit(solution)/shard_map/ppermute | solution.py:43
  91.8 7.3 %collective-permute-start.8 = (bf16[528,128]{1,0:T(8,128)(2,1)S(1)}, bf16[528,128]{1,0:T(8,128)(2,1)S(1)}, u32[]{:S(2)}, u32[]{:S(2)}) collective-permute-start(bf16[528,128]{1,0:T(8,128)(2,1)S(1)} %collective-permute-done.7.refs_12_), channel_id=1, source_target_pairs={{0,64},{1,961},{2,66},{3,963},{4,68},{5,965},{6,70},{7,967},{8,72}... | collective-permute-start | bytes 405512 | tf_op jit(solution)/shard_map/ppermute | solution.py:43
  95.5 21.6 %copy-start.5 = (bf16[528,128]{1,0:T(8,128)(2,1)}, bf16[528,128]{1,0:T(8,128)(2,1)S(1)}, u32[]{:S(2)}) copy-start(bf16[528,128]{1,0:T(8,128)(2,1)S(1)} %collective-permute-done.13.refs_15_) | copy-start | bytes 405508
  99.1 31.6 %copy-start = (bf16[3168,128]{1,0:T(8,128)(2,1)}, bf16[3168,128]{1,0:T(8,128)(2,1)S(1)}, u32[]{:S(2)}) copy-start(bf16[3168,128]{1,0:T(8,128)(2,1)S(1)} %collective-permute-done.14.refs_18_) | copy-start | bytes 2433028
  99.2 17.9 %collective-permute-start.18 = (bf16[3168,128]{1,0:T(8,128)(2,1)S(1)}, bf16[3168,128]{1,0:T(8,128)(2,1)S(1)}, u32[]{:S(2)}, u32[]{:S(2)}) collective-permute-start(bf16[3168,128]{1,0:T(8,128)(2,1)S(1)} %constant_dynamic-update-slice_fusion.6), channel_id=1, source_target_pairs={{0,1},{1,0},{2,3},{3,2},{4,5},{5,4},{6,7},{7,6},{8,9},{9,8},{10,11... | collective-permute-start | bytes 2433032 | tf_op jit(solution)/shard_map/ppermute | solution.py:48
  104.9 7.1 %collective-permute-start.16 = (bf16[528,128]{1,0:T(8,128)(2,1)S(1)}, bf16[528,128]{1,0:T(8,128)(2,1)}, u32[]{:S(2)}, u32[]{:S(2)}) collective-permute-start(bf16[528,128]{1,0:T(8,128)(2,1)S(1)} %collective-permute-done.8.refs_14_), channel_id=1, source_target_pairs={{0,64},{1,961},{2,66},{3,963},{4,68},{5,965},{6,70},{7,967},{8,72}... | collective-permute-start | bytes 405512 | tf_op jit(solution)/shard_map/ppermute | solution.py:43
  110.0 7.1 %collective-permute-start.17 = (bf16[528,128]{1,0:T(8,128)(2,1)S(1)}, bf16[528,128]{1,0:T(8,128)(2,1)S(1)}, u32[]{:S(2)}, u32[]{:S(2)}) collective-permute-start(bf16[528,128]{1,0:T(8,128)(2,1)S(1)} %collective-permute-done.13.refs_15_), channel_id=1, source_target_pairs={{0,64},{1,961},{2,66},{3,963},{4,68},{5,965},{6,70},{7,967},{8,72}... | collective-permute-start | bytes 405512 | tf_op jit(solution)/shard_map/ppermute | solution.py:43
  117.1 13.7 %copy-start.4 = (bf16[528,128]{1,0:T(8,128)(2,1)}, bf16[528,128]{1,0:T(8,128)(2,1)S(1)}, u32[]{:S(2)}) copy-start(bf16[528,128]{1,0:T(8,128)(2,1)S(1)} %collective-permute-done.17.refs_17_) | copy-start | bytes 405508
  117.1 13.7 %copy-start.1 = (bf16[3168,128]{1,0:T(8,128)(2,1)}, bf16[3168,128]{1,0:T(8,128)(2,1)S(1)}, u32[]{:S(2)}) copy-start(bf16[3168,128]{1,0:T(8,128)(2,1)S(1)} %collective-permute-done.18.refs_19_) | copy-start | bytes 2433028
  117.1 7.1 %collective-permute-start.19 = (bf16[528,128]{1,0:T(8,128)(2,1)}, bf16[528,128]{1,0:T(8,128)(2,1)}, u32[]{:S(2)}, u32[]{:S(2)}) collective-permute-start(bf16[528,128]{1,0:T(8,128)(2,1)} %collective-permute-done.16.refs_16_), channel_id=1, source_target_pairs={{0,64},{1,961},{2,66},{3,963},{4,68},{5,965},{6,70},{7,967},{8,72}... | collective-permute-start | bytes 405512 | tf_op jit(solution)/shard_map/ppermute | solution.py:43
  125.2 5.6 %collective-permute-start.20 = (bf16[1584,128]{1,0:T(8,128)(2,1)S(1)}, bf16[1584,128]{1,0:T(8,128)(2,1)}, u32[]{:S(2)}, u32[]{:S(2)}) collective-permute-start(bf16[1584,128]{1,0:T(8,128)(2,1)S(1)} %pad_maximum_fusion), channel_id=1, source_target_pairs={{0,1},{1,0},{2,3},{3,2},{4,5},{5,4},{6,7},{7,6},{8,9},{9,8},{10,11... | collective-permute-start | bytes 1216520 | tf_op jit(solution)/shard_map/ppermute | solution.py:48
  140.6 9.4 %collective-permute-start.21 = (bf16[512,128]{1,0:T(8,128)(2,1)S(1)}, bf16[512,128]{1,0:T(8,128)(2,1)S(1)}, u32[]{:S(2)}, u32[]{:S(2)}) collective-permute-start(bf16[512,128]{1,0:T(8,128)(2,1)S(1)} %get-tuple-element.38.refs_1_.refs_3_), channel_id=1, source_target_pairs={{0,32},{1,33},{2,34},{3,35},{4,36},{5,37},{6,38},{7,39},{8,40},{9,... | collective-permute-start | bytes 393224 | tf_op jit(solution)/shard_map/ppermute | solution.py:43
  142.5 8.3 %collective-permute-start.22 = (bf16[512,128]{1,0:T(8,128)(2,1)S(1)}, bf16[512,128]{1,0:T(8,128)(2,1)S(1)}, u32[]{:S(2)}, u32[]{:S(2)}) collective-permute-start(bf16[512,128]{1,0:T(8,128)(2,1)S(1)} %get-tuple-element.38.refs_1_.refs_3_), channel_id=1, source_target_pairs={{0,64},{1,961},{2,66},{3,963},{4,68},{5,965},{6,70},{7,967},{8,72}... | collective-permute-start | bytes 393224 | tf_op jit(solution)/shard_map/ppermute | solution.py:43
  148.1 8.6 %collective-permute-start.23 = (bf16[512,128]{1,0:T(8,128)(2,1)S(1)}, bf16[512,128]{1,0:T(8,128)(2,1)S(1)}, u32[]{:S(2)}, u32[]{:S(2)}) collective-permute-start(bf16[512,128]{1,0:T(8,128)(2,1)S(1)} %get-tuple-element.38.refs_1_.refs_3_), channel_id=1, source_target_pairs={{0,961},{1,64},{2,963},{3,66},{4,965},{5,68},{6,967},{7,70},{8,969... | collective-permute-start | bytes 393224 | tf_op jit(solution)/shard_map/ppermute | solution.py:43
  156.7 10.2 %collective-permute-start.24 = (bf16[512,128]{1,0:T(8,128)(2,1)S(1)}, bf16[512,128]{1,0:T(8,128)(2,1)S(1)}, u32[]{:S(2)}, u32[]{:S(2)}) collective-permute-start(bf16[512,128]{1,0:T(8,128)(2,1)S(1)} %collective-permute-done.22.refs_5_), channel_id=1, source_target_pairs={{0,64},{1,961},{2,66},{3,963},{4,68},{5,965},{6,70},{7,967},{8,72}... | collective-permute-start | bytes 393224 | tf_op jit(solution)/shard_map/ppermute | solution.py:43
  162.2 10.6 %collective-permute-start.29 = (bf16[512,128]{1,0:T(8,128)(2,1)S(1)}, bf16[512,128]{1,0:T(8,128)(2,1)S(1)}, u32[]{:S(2)}, u32[]{:S(2)}) collective-permute-start(bf16[512,128]{1,0:T(8,128)(2,1)S(1)} %collective-permute-done.23.refs_6_), channel_id=1, source_target_pairs={{0,64},{1,961},{2,66},{3,963},{4,68},{5,965},{6,70},{7,967},{8,72}... | collective-permute-start | bytes 393224 | tf_op jit(solution)/shard_map/ppermute | solution.py:43
  166.9 10.1 %collective-permute-start.25 = (bf16[512,128]{1,0:T(8,128)(2,1)S(1)}, bf16[512,128]{1,0:T(8,128)(2,1)S(1)}, u32[]{:S(2)}, u32[]{:S(2)}) collective-permute-start(bf16[512,128]{1,0:T(8,128)(2,1)S(1)} %collective-permute-done.24.refs_7_), channel_id=1, source_target_pairs={{0,64},{1,961},{2,66},{3,963},{4,68},{5,965},{6,70},{7,967},{8,72}... | collective-permute-start | bytes 393224 | tf_op jit(solution)/shard_map/ppermute | solution.py:43
  172.8 6.7 %collective-permute-start.30 = (bf16[512,128]{1,0:T(8,128)(2,1)S(1)}, bf16[512,128]{1,0:T(8,128)(2,1)S(1)}, u32[]{:S(2)}, u32[]{:S(2)}) collective-permute-start(bf16[512,128]{1,0:T(8,128)(2,1)S(1)} %collective-permute-done.29.refs_8_), channel_id=1, source_target_pairs={{0,64},{1,961},{2,66},{3,963},{4,68},{5,965},{6,70},{7,967},{8,72}... | collective-permute-start | bytes 393224 | tf_op jit(solution)/shard_map/ppermute | solution.py:43
  179.5 32.9 %collective-permute-start.34 = (bf16[3072,128]{1,0:T(8,128)(2,1)S(1)}, bf16[3072,128]{1,0:T(8,128)(2,1)S(1)}, u32[]{:S(2)}, u32[]{:S(2)}) collective-permute-start(bf16[3072,128]{1,0:T(8,128)(2,1)S(1)} %constant_dynamic-update-slice_fusion.12), channel_id=1, source_target_pairs={{0,1},{1,0},{2,3},{3,2},{4,5},{5,4},{6,7},{7,6},{8,9},{9,8},{10,11... | collective-permute-start | bytes 2359304 | tf_op jit(solution)/shard_map/ppermute | solution.py:48
  181.5 9.8 %collective-permute-start.26 = (bf16[512,128]{1,0:T(8,128)(2,1)S(1)}, bf16[512,128]{1,0:T(8,128)(2,1)S(1)}, u32[]{:S(2)}, u32[]{:S(2)}) collective-permute-start(bf16[512,128]{1,0:T(8,128)(2,1)S(1)} %collective-permute-done.25.refs_9_), channel_id=1, source_target_pairs={{0,64},{1,961},{2,66},{3,963},{4,68},{5,965},{6,70},{7,967},{8,72}... | collective-permute-start | bytes 393224 | tf_op jit(solution)/shard_map/ppermute | solution.py:43
  186.3 9.1 %collective-permute-start.31 = (bf16[512,128]{1,0:T(8,128)(2,1)S(1)}, bf16[512,128]{1,0:T(8,128)(2,1)S(1)}, u32[]{:S(2)}, u32[]{:S(2)}) collective-permute-start(bf16[512,128]{1,0:T(8,128)(2,1)S(1)} %collective-permute-done.30.refs_10_), channel_id=1, source_target_pairs={{0,64},{1,961},{2,66},{3,963},{4,68},{5,965},{6,70},{7,967},{8,72}... | collective-permute-start | bytes 393224 | tf_op jit(solution)/shard_map/ppermute | solution.py:43
  188.2 18.6 %collective-permute-start.35 = (bf16[512,128]{1,0:T(8,128)(2,1)S(1)}, bf16[512,128]{1,0:T(8,128)(2,1)S(1)}, u32[]{:S(2)}, u32[]{:S(2)}) collective-permute-start(bf16[512,128]{1,0:T(8,128)(2,1)S(1)} %get-tuple-element.38.refs_1_.refs_3_), channel_id=1, source_target_pairs={{0,1},{1,0},{2,3},{3,2},{4,5},{5,4},{6,7},{7,6},{8,9},{9,8},{10,11... | collective-permute-start | bytes 393224 | tf_op jit(solution)/shard_map/ppermute | solution.py:43
  191.2 8.3 %collective-permute-start.27 = (bf16[512,128]{1,0:T(8,128)(2,1)S(1)}, bf16[512,128]{1,0:T(8,128)(2,1)S(1)}, u32[]{:S(2)}, u32[]{:S(2)}) collective-permute-start(bf16[512,128]{1,0:T(8,128)(2,1)S(1)} %collective-permute-done.26.refs_11_), channel_id=1, source_target_pairs={{0,64},{1,961},{2,66},{3,963},{4,68},{5,965},{6,70},{7,967},{8,72}... | collective-permute-start | bytes 393224 | tf_op jit(solution)/shard_map/ppermute | solution.py:43
  195.4 9.3 %collective-permute-start.32 = (bf16[512,128]{1,0:T(8,128)(2,1)S(1)}, bf16[512,128]{1,0:T(8,128)(2,1)S(1)}, u32[]{:S(2)}, u32[]{:S(2)}) collective-permute-start(bf16[512,128]{1,0:T(8,128)(2,1)S(1)} %collective-permute-done.31.refs_12_), channel_id=1, source_target_pairs={{0,64},{1,961},{2,66},{3,963},{4,68},{5,965},{6,70},{7,967},{8,72}... | collective-permute-start | bytes 393224 | tf_op jit(solution)/shard_map/ppermute | solution.py:43
  199.5 8.4 %collective-permute-start.28 = (bf16[512,128]{1,0:T(8,128)(2,1)S(1)}, bf16[512,128]{1,0:T(8,128)(2,1)S(1)}, u32[]{:S(2)}, u32[]{:S(2)}) collective-permute-start(bf16[512,128]{1,0:T(8,128)(2,1)S(1)} %collective-permute-done.27.refs_13_), channel_id=1, source_target_pairs={{0,64},{1,961},{2,66},{3,963},{4,68},{5,965},{6,70},{7,967},{8,72}... | collective-permute-start | bytes 393224 | tf_op jit(solution)/shard_map/ppermute | solution.py:43
  204.7 7.7 %collective-permute-start.33 = (bf16[512,128]{1,0:T(8,128)(2,1)S(1)}, bf16[512,128]{1,0:T(8,128)(2,1)S(1)}, u32[]{:S(2)}, u32[]{:S(2)}) collective-permute-start(bf16[512,128]{1,0:T(8,128)(2,1)S(1)} %collective-permute-done.32.refs_14_), channel_id=1, source_target_pairs={{0,64},{1,961},{2,66},{3,963},{4,68},{5,965},{6,70},{7,967},{8,72}... | collective-permute-start | bytes 393224 | tf_op jit(solution)/shard_map/ppermute | solution.py:43
  212.4 29.3 %copy-start.2 = (bf16[3072,128]{1,0:T(8,128)(2,1)}, bf16[3072,128]{1,0:T(8,128)(2,1)S(1)}, u32[]{:S(2)}) copy-start(bf16[3072,128]{1,0:T(8,128)(2,1)S(1)} %collective-permute-done.34.refs_19_) | copy-start | bytes 2359300
  212.5 16.0 %collective-permute-start.38 = (bf16[3072,128]{1,0:T(8,128)(2,1)S(1)}, bf16[3072,128]{1,0:T(8,128)(2,1)S(1)}, u32[]{:S(2)}, u32[]{:S(2)}) collective-permute-start(bf16[3072,128]{1,0:T(8,128)(2,1)S(1)} %constant_dynamic-update-slice_fusion.18), channel_id=1, source_target_pairs={{0,1},{1,0},{2,3},{3,2},{4,5},{5,4},{6,7},{7,6},{8,9},{9,8},{10,11... | collective-permute-start | bytes 2359304 | tf_op jit(solution)/shard_map/ppermute | solution.py:48
  217.2 7.0 %collective-permute-start.36 = (bf16[512,128]{1,0:T(8,128)(2,1)S(1)}, bf16[512,128]{1,0:T(8,128)(2,1)S(1)}, u32[]{:S(2)}, u32[]{:S(2)}) collective-permute-start(bf16[512,128]{1,0:T(8,128)(2,1)S(1)} %collective-permute-done.28.refs_15_), channel_id=1, source_target_pairs={{0,64},{1,961},{2,66},{3,963},{4,68},{5,965},{6,70},{7,967},{8,72}... | collective-permute-start | bytes 393224 | tf_op jit(solution)/shard_map/ppermute | solution.py:43
  220.0 8.5 %collective-permute-start.37 = (bf16[512,128]{1,0:T(8,128)(2,1)S(1)}, bf16[512,128]{1,0:T(8,128)(2,1)S(1)}, u32[]{:S(2)}, u32[]{:S(2)}) collective-permute-start(bf16[512,128]{1,0:T(8,128)(2,1)S(1)} %collective-permute-done.33.refs_16_), channel_id=1, source_target_pairs={{0,64},{1,961},{2,66},{3,963},{4,68},{5,965},{6,70},{7,967},{8,72}... | collective-permute-start | bytes 393224 | tf_op jit(solution)/shard_map/ppermute | solution.py:43
  224.2 11.3 %copy-start.6 = (bf16[512,128]{1,0:T(8,128)(2,1)}, bf16[512,128]{1,0:T(8,128)(2,1)S(1)}, u32[]{:S(2)}) copy-start(bf16[512,128]{1,0:T(8,128)(2,1)S(1)} %collective-permute-done.36.refs_17_) | copy-start | bytes 393220
  228.5 7.1 %copy-start.7 = (bf16[512,128]{1,0:T(8,128)(2,1)}, bf16[512,128]{1,0:T(8,128)(2,1)S(1)}, u32[]{:S(2)}) copy-start(bf16[512,128]{1,0:T(8,128)(2,1)S(1)} %collective-permute-done.37.refs_18_) | copy-start | bytes 393220
  228.5 13.3 %copy-start.3 = (bf16[3072,128]{1,0:T(8,128)(2,1)}, bf16[3072,128]{1,0:T(8,128)(2,1)S(1)}, u32[]{:S(2)}) copy-start(bf16[3072,128]{1,0:T(8,128)(2,1)S(1)} %collective-permute-done.38.refs_20_) | copy-start | bytes 2359300
  228.5 7.0 %collective-permute-start.39 = (bf16[512,128]{1,0:T(8,128)(2,1)S(1)}, bf16[512,128]{1,0:T(8,128)(2,1)S(1)}, u32[]{:S(2)}, u32[]{:S(2)}) collective-permute-start(bf16[512,128]{1,0:T(8,128)(2,1)S(1)} %collective-permute-done.36.refs_17_), channel_id=1, source_target_pairs={{0,64},{1,961},{2,66},{3,963},{4,68},{5,965},{6,70},{7,967},{8,72}... | collective-permute-start | bytes 393224 | tf_op jit(solution)/shard_map/ppermute | solution.py:43
  235.5 4.8 %copy-start.8 = (bf16[512,128]{1,0:T(8,128)(2,1)}, bf16[512,128]{1,0:T(8,128)(2,1)S(1)}, u32[]{:S(2)}) copy-start(bf16[512,128]{1,0:T(8,128)(2,1)S(1)} %collective-permute-done.39.refs_21_) | copy-start | bytes 393220
  235.6 6.2 %collective-permute-start.40 = (bf16[1536,128]{1,0:T(8,128)(2,1)S(1)}, bf16[1536,128]{1,0:T(8,128)(2,1)}, u32[]{:S(2)}, u32[]{:S(2)}) collective-permute-start(bf16[1536,128]{1,0:T(8,128)(2,1)S(1)} %pad_maximum_fusion.1), channel_id=1, source_target_pairs={{0,1},{1,0},{2,3},{3,2},{4,5},{5,4},{6,7},{7,6},{8,9},{9,8},{10,11... | collective-permute-start | bytes 1179656 | tf_op jit(solution)/shard_map/ppermute | solution.py:48
  249.8 6.9 %collective-permute-start.41 = (bf16[512,128]{1,0:T(8,128)(2,1)S(1)}, bf16[512,128]{1,0:T(8,128)(2,1)S(1)}, u32[]{:S(2)}, u32[]{:S(2)}) collective-permute-start(bf16[512,128]{1,0:T(8,128)(2,1)S(1)} %shard_map.74), channel_id=1, source_target_pairs={{0,0},{1,32},{2,2},{3,34},{4,4},{5,36},{6,6},{7,38},{8,8},{9,40},{... | collective-permute-start | bytes 393224 | tf_op jit(solution)/shard_map/ppermute | solution.py:43
Sparse Core Ops, SparseCore 0:
  40.7 82.7 all-gather.2
  156.8 79.3 all-gather.4

commit v7 on v6

--- a/solution.py
+++ b/solution.py
@@ -160,13 +160,15 @@
     a_all = lax.all_gather(near, ("x", "y"), axis=0, tiled=True)
     chains, first, second, sibling = ring(up, down, sibling)
     last = move(chains[0][6], hop)
-    final = across(jnp.concatenate([chains[0][6], chains[1][6], last]), "core", 1)
+    seven = across(jnp.concatenate([chains[0][6], chains[1][6]]), "core", 1)
+    last, seven = lax.optimization_barrier((last, seven))
+    eight = across(last, "core", 1)
     placed = [(unit, {0: (0, 0)}), (sibling, {0: (0, 1)})]
     for k in range(7):
         placed += [(chain[k], {0: (k + 1, w)}) for w, chain in enumerate(chains)]
     for part, start in ((first, 1), (second, 4)):
         placed.append((part, {i: (-(i // 2 + start), 1 - i % 2) for i in range(6)}))
-    placed += [(last, {0: (8, 0)}), (final, {0: (-7, 1), 1: (-7, 0), 2: (8, 1)})]
+    placed += [(last, {0: (8, 0)}), (seven, {0: (-7, 1), 1: (-7, 0)}), (eight, {0: (8, 1)})]
     return a_all, placed
 
 

time: 269 us -> 272 us (1.011); the launches traced: 264 us -> 271 us
  starting transfers between devices: 171 us -> 175 us
    ppermute x6 -> x8, starting transfers between devices: 25.9 us -> 35 us  [across(): return lax.ppermute(part, axis, [(i, i ^ mask) for i in range(size)])]
    ppermute x36, starting transfers between devices: 145 us -> 140 us  [move(): return lax.ppermute(part, AXES, pairs)]
    ppermute x36, waiting for transfers between devices: 52.8 us -> 56.2 us  [move(): return lax.ppermute(part, AXES, pairs)]
  transfers between devices with their start and end apart: 44 -> 46, of which waited for: 22 -> 23; matrix products, arithmetic and copies ran while one was open for 1% -> 1% of each run, Pallas kernels for 0% -> 0%
where the time goes in v7:
time: 272 us; the launch traced here: 271 us
  starting transfers between devices  175 us (64%)
  waiting for transfers between devices  57.7 us (21%)
  Pallas kernels  17.6 us (6%)
  between operations  14.1 us (5%)
  other arithmetic  3.98 us (1%)
    ppermute x36, starting transfers between devices, move(): return lax.ppermute(part, AXES, pairs)  140 us
    ppermute x36, waiting for transfers between devices, move(): return lax.ppermute(part, AXES, pairs)  56.2 us
    ppermute x8, starting transfers between devices, across(): return lax.ppermute(part, axis, [(i, i ^ mask) for i in range(size)])  35 us
    pallas_call x2, Pallas kernels, multiply(): pl.pallas_call(functools.partial(kernel, rows, units, first), out_shape=o...  17.6 us
  transfers between devices with their start and end apart: 46, of which 23 were waited for; matrix products, arithmetic and copies ran while one was open for 1% of the time, Pallas kernels for 0%

profile of v7, /device:TPU:1, one launch (start us, length us, event | category | flops | bytes accessed | tf_op | source)
XLA Modules:
  0.0 270.8 jit_solution(14894734309330192785)
XLA Ops:
  8.2 4.9 %collective-permute-start = (bf16[528,128]{1,0:T(8,128)(2,1)S(1)}, bf16[528,128]{1,0:T(8,128)(2,1)S(1)}, u32[]{:S(2)}, u32[]{:S(2)}) collective-permute-start(bf16[528,128]{1,0:T(8,128)(2,1)S(1)} %fusion.1), channel_id=1, source_target_pairs={{0,0},{1,32},{2,2},{3,34},{4,4},{5,36},{6,6},{7,38},{8,8},{9,40},{... | collective-permute-start | bytes 405512 | tf_op jit(solution)/shard_map/ppermute | solution.py:43
  13.1 11.8 %collective-permute-start.1 = (bf16[528,128]{1,0:T(8,128)(2,1)S(1)}, bf16[528,128]{1,0:T(8,128)(2,1)S(1)}, u32[]{:S(2)}, u32[]{:S(2)}) collective-permute-start(bf16[528,128]{1,0:T(8,128)(2,1)S(1)} %fusion.1), channel_id=1, source_target_pairs={{0,32},{1,0},{2,34},{3,2},{4,36},{5,4},{6,38},{7,6},{8,40},{9,8},{... | collective-permute-start | bytes 405512 | tf_op jit(solution)/shard_map/ppermute | solution.py:43
  24.9 1.9 collective-permute-start.2
  26.8 9.5 %collective-permute-start.3 = (bf16[528,128]{1,0:T(8,128)(2,1)S(1)}, bf16[528,128]{1,0:T(8,128)(2,1)S(1)}, u32[]{:S(2)}, u32[]{:S(2)}) collective-permute-start(bf16[528,128]{1,0:T(8,128)(2,1)S(1)} %fusion.1), channel_id=1, source_target_pairs={{0,961},{1,993},{2,963},{3,995},{4,965},{5,997},{6,967},{7,999},{8... | collective-permute-start | bytes 405512 | tf_op jit(solution)/shard_map/ppermute | solution.py:43
  37.1 3.4 %collective-permute-done.3.refs_5_ = bf16[528,128]{1,0:T(8,128)(2,1)S(1)} collective-permute-done((bf16[528,128]{1,0:T(8,128)(2,1)S(1)}, bf16[528,128]{1,0:T(8,128)(2,1)S(1)}, u32[]{:S(2)}, u32[]{:S(2)}) %collective-permute-start.3) | collective-permute-done | bytes 135200 | tf_op jit(solution)/shard_map/ppermute | solution.py:43
  40.6 5.8 %collective-permute-start.4 = (bf16[528,128]{1,0:T(8,128)(2,1)S(1)}, bf16[528,128]{1,0:T(8,128)(2,1)S(1)}, u32[]{:S(2)}, u32[]{:S(2)}) collective-permute-start(bf16[528,128]{1,0:T(8,128)(2,1)S(1)} %collective-permute-done.2.refs_4_), channel_id=1, source_target_pairs={{0,64},{1,961},{2,66},{3,963},{4,68},{5,965},{6,70},{7,967},{8,72}... | collective-permute-start | bytes 405512 | tf_op jit(solution)/shard_map/ppermute | solution.py:43
  46.4 2.2 collective-permute-start.9
  48.6 2.6 collective-permute-done.4.refs_6_
  51.2 6.0 %collective-permute-start.5 = (bf16[528,128]{1,0:T(8,128)(2,1)S(1)}, bf16[528,128]{1,0:T(8,128)(2,1)S(1)}, u32[]{:S(2)}, u32[]{:S(2)}) collective-permute-start(bf16[528,128]{1,0:T(8,128)(2,1)S(1)} %collective-permute-done.4.refs_6_), channel_id=1, source_target_pairs={{0,64},{1,961},{2,66},{3,963},{4,68},{5,965},{6,70},{7,967},{8,72}... | collective-permute-start | bytes 405512 | tf_op jit(solution)/shard_map/ppermute | solution.py:43
  57.3 2.4 collective-permute-start.10
  59.8 1.3 collective-permute-done.5.refs_8_
  61.0 3.2 %collective-permute-done.10.refs_9_ = bf16[528,128]{1,0:T(8,128)(2,1)S(1)} collective-permute-done((bf16[528,128]{1,0:T(8,128)(2,1)S(1)}, bf16[528,128]{1,0:T(8,128)(2,1)S(1)}, u32[]{:S(2)}, u32[]{:S(2)}) %collective-permute-start.10) | collective-permute-done | bytes 135200 | tf_op jit(solution)/shard_map/ppermute | solution.py:43
  64.2 4.6 %collective-permute-start.14 = (bf16[3168,128]{1,0:T(8,128)(2,1)S(1)}, bf16[3168,128]{1,0:T(8,128)(2,1)S(1)}, u32[]{:S(2)}, u32[]{:S(2)}) collective-permute-start(bf16[3168,128]{1,0:T(8,128)(2,1)S(1)} %constant_dynamic-update-slice_fusion), channel_id=1, source_target_pairs={{0,1},{1,0},{2,3},{3,2},{4,5},{5,4},{6,7},{7,6},{8,9},{9,8},{10,11... | collective-permute-start | bytes 2433032 | tf_op jit(solution)/shard_map/ppermute | solution.py:48
  68.9 1.9 collective-permute-start.11
  70.8 3.6 %collective-permute-start.6 = (bf16[528,128]{1,0:T(8,128)(2,1)S(1)}, bf16[528,128]{1,0:T(8,128)(2,1)S(1)}, u32[]{:S(2)}, u32[]{:S(2)}) collective-permute-start(bf16[528,128]{1,0:T(8,128)(2,1)S(1)} %collective-permute-done.5.refs_8_), channel_id=1, source_target_pairs={{0,64},{1,961},{2,66},{3,963},{4,68},{5,965},{6,70},{7,967},{8,72}... | collective-permute-start | bytes 405512 | tf_op jit(solution)/shard_map/ppermute | solution.py:43
  74.4 4.6 %collective-permute-start.15 = (bf16[528,128]{1,0:T(8,128)(2,1)S(1)}, bf16[528,128]{1,0:T(8,128)(2,1)S(1)}, u32[]{:S(2)}, u32[]{:S(2)}) collective-permute-start(bf16[528,128]{1,0:T(8,128)(2,1)S(1)} %fusion.1), channel_id=1, source_target_pairs={{0,1},{1,33},{2,3},{3,35},{4,5},{5,37},{6,7},{7,39},{8,9},{9,41},{... | collective-permute-start | bytes 405512 | tf_op jit(solution)/shard_map/ppermute | solution.py:43
  79.0 3.6 %collective-permute-start.12 = (bf16[528,128]{1,0:T(8,128)(2,1)S(1)}, bf16[528,128]{1,0:T(8,128)(2,1)S(1)}, u32[]{:S(2)}, u32[]{:S(2)}) collective-permute-start(bf16[528,128]{1,0:T(8,128)(2,1)S(1)} %collective-permute-done.11.refs_11_), channel_id=1, source_target_pairs={{0,64},{1,961},{2,66},{3,963},{4,68},{5,965},{6,70},{7,967},{8,72}... | collective-permute-start | bytes 405512 | tf_op jit(solution)/shard_map/ppermute | solution.py:43
  82.7 4.2 %collective-permute-start.7 = (bf16[528,128]{1,0:T(8,128)(2,1)S(1)}, bf16[528,128]{1,0:T(8,128)(2,1)S(1)}, u32[]{:S(2)}, u32[]{:S(2)}) collective-permute-start(bf16[528,128]{1,0:T(8,128)(2,1)S(1)} %collective-permute-done.6.refs_10_), channel_id=1, source_target_pairs={{0,64},{1,961},{2,66},{3,963},{4,68},{5,965},{6,70},{7,967},{8,72}... | collective-permute-start | bytes 405512 | tf_op jit(solution)/shard_map/ppermute | solution.py:43
  87.1 4.6 %collective-permute-start.13 = (bf16[528,128]{1,0:T(8,128)(2,1)S(1)}, bf16[528,128]{1,0:T(8,128)(2,1)S(1)}, u32[]{:S(2)}, u32[]{:S(2)}) collective-permute-start(bf16[528,128]{1,0:T(8,128)(2,1)S(1)} %collective-permute-done.12.refs_13_), channel_id=1, source_target_pairs={{0,64},{1,961},{2,66},{3,963},{4,68},{5,965},{6,70},{7,967},{8,72}... | collective-permute-start | bytes 405512 | tf_op jit(solution)/shard_map/ppermute | solution.py:43
  91.8 3.6 %collective-permute-start.8 = (bf16[528,128]{1,0:T(8,128)(2,1)S(1)}, bf16[528,128]{1,0:T(8,128)(2,1)S(1)}, u32[]{:S(2)}, u32[]{:S(2)}) collective-permute-start(bf16[528,128]{1,0:T(8,128)(2,1)S(1)} %collective-permute-done.7.refs_12_), channel_id=1, source_target_pairs={{0,64},{1,961},{2,66},{3,963},{4,68},{5,965},{6,70},{7,967},{8,72}... | collective-permute-start | bytes 405512 | tf_op jit(solution)/shard_map/ppermute | solution.py:43
  95.5 3.6 %collective-permute-done.8.refs_14_ = bf16[528,128]{1,0:T(8,128)(2,1)S(1)} collective-permute-done((bf16[528,128]{1,0:T(8,128)(2,1)S(1)}, bf16[528,128]{1,0:T(8,128)(2,1)S(1)}, u32[]{:S(2)}, u32[]{:S(2)}) %collective-permute-start.8) | collective-permute-done | bytes 135200 | tf_op jit(solution)/shard_map/ppermute | solution.py:43
  99.2 5.8 %collective-permute-start.18 = (bf16[3168,128]{1,0:T(8,128)(2,1)S(1)}, bf16[3168,128]{1,0:T(8,128)(2,1)S(1)}, u32[]{:S(2)}, u32[]{:S(2)}) collective-permute-start(bf16[3168,128]{1,0:T(8,128)(2,1)S(1)} %constant_dynamic-update-slice_fusion.6), channel_id=1, source_target_pairs={{0,1},{1,0},{2,3},{3,2},{4,5},{5,4},{6,7},{7,6},{8,9},{9,8},{10,11... | collective-permute-start | bytes 2433032 | tf_op jit(solution)/shard_map/ppermute | solution.py:48
  104.9 5.0 %collective-permute-start.16 = (bf16[528,128]{1,0:T(8,128)(2,1)S(1)}, bf16[528,128]{1,0:T(8,128)(2,1)S(1)}, u32[]{:S(2)}, u32[]{:S(2)}) collective-permute-start(bf16[528,128]{1,0:T(8,128)(2,1)S(1)} %collective-permute-done.8.refs_14_), channel_id=1, source_target_pairs={{0,64},{1,961},{2,66},{3,963},{4,68},{5,965},{6,70},{7,967},{8,72}... | collective-permute-start | bytes 405512 | tf_op jit(solution)/shard_map/ppermute | solution.py:43
  110.0 1.9 collective-permute-start.17
  112.0 5.1 %collective-permute-done.17.refs_17_ = bf16[528,128]{1,0:T(8,128)(2,1)S(1)} collective-permute-done((bf16[528,128]{1,0:T(8,128)(2,1)S(1)}, bf16[528,128]{1,0:T(8,128)(2,1)S(1)}, u32[]{:S(2)}, u32[]{:S(2)}) %collective-permute-start.17) | collective-permute-done | bytes 135200 | tf_op jit(solution)/shard_map/ppermute | solution.py:43
  117.9 1.9 collective-permute-start.20
  119.8 5.4 %collective-permute-start.19 = (bf16[528,128]{1,0:T(8,128)(2,1)}, bf16[528,128]{1,0:T(8,128)(2,1)S(1)}, u32[]{:S(2)}, u32[]{:S(2)}) collective-permute-start(bf16[528,128]{1,0:T(8,128)(2,1)} %copy-done.5), channel_id=1, source_target_pairs={{0,64},{1,961},{2,66},{3,963},{4,68},{5,965},{6,70},{7,967},{8,72}... | collective-permute-start | bytes 405512 | tf_op jit(solution)/shard_map/ppermute | solution.py:43
  125.2 2.8 %collective-permute-done.19.refs_20_ = bf16[528,128]{1,0:T(8,128)(2,1)S(1)} collective-permute-done((bf16[528,128]{1,0:T(8,128)(2,1)}, bf16[528,128]{1,0:T(8,128)(2,1)S(1)}, u32[]{:S(2)}, u32[]{:S(2)}) %collective-permute-start.19) | collective-permute-done | bytes 135200 | tf_op jit(solution)/shard_map/ppermute | solution.py:43
  128.0 3.7 %collective-permute-start.21 = (bf16[528,128]{1,0:T(8,128)(2,1)S(1)}, bf16[528,128]{1,0:T(8,128)(2,1)}, u32[]{:S(2)}, u32[]{:S(2)}) collective-permute-start(bf16[528,128]{1,0:T(8,128)(2,1)S(1)} %collective-permute-done.19.refs_20_), channel_id=1, source_target_pairs={{0,1},{1,0},{2,3},{3,2},{4,5},{5,4},{6,7},{7,6},{8,9},{9,8},{10,11... | collective-permute-start | bytes 405512 | tf_op jit(solution)/shard_map/ppermute | solution.py:48
  132.8 9.7 %shard_map.73 = (bf16[512,128]{1,0:T(8,128)(2,1)S(1)}, s32[64,128]{1,0:T(8,128)S(1)}) custom-call(s32[1]{0:T(128)} %get-tuple-element.57.branch, s32[33]{0:T(128)S(1)} %pad_add_fusion.tab, bf16[528,128]{1,0:T(8,128)(2,1)S(1)} %collective-permute-done.refs_0_.refs_2_, bf16[16896,128]{1,0:T(8,128)(2,1)} %all-gather.3.cloned.1.call-done.refs_1_, ...), custom_call_target="tpu_custom_call" | custom-call | flops 536870912 | bytes 8388608 | tf_op jit(solution)/shard_map/pallas_call | solution.py:142
  142.5 1.9 collective-permute-start.22
  144.5 4.5 %collective-permute-start.23 = (bf16[512,128]{1,0:T(8,128)(2,1)S(1)}, bf16[512,128]{1,0:T(8,128)(2,1)S(1)}, u32[]{:S(2)}, u32[]{:S(2)}) collective-permute-start(bf16[512,128]{1,0:T(8,128)(2,1)S(1)} %get-tuple-element.44.refs_1_.refs_3_), channel_id=1, source_target_pairs={{0,64},{1,961},{2,66},{3,963},{4,68},{5,965},{6,70},{7,967},{8,72}... | collective-permute-start | bytes 393224 | tf_op jit(solution)/shard_map/ppermute | solution.py:43
  148.9 2.3 collective-permute-start.24
  152.0 4.4 %collective-permute-done.24.refs_6_ = bf16[512,128]{1,0:T(8,128)(2,1)S(1)} collective-permute-done((bf16[512,128]{1,0:T(8,128)(2,1)S(1)}, bf16[512,128]{1,0:T(8,128)(2,1)S(1)}, u32[]{:S(2)}, u32[]{:S(2)}) %collective-permute-start.24) | collective-permute-done | bytes 131104 | tf_op jit(solution)/shard_map/ppermute | solution.py:43
  156.5 6.6 %collective-permute-start.25 = (bf16[512,128]{1,0:T(8,128)(2,1)S(1)}, bf16[512,128]{1,0:T(8,128)(2,1)S(1)}, u32[]{:S(2)}, u32[]{:S(2)}) collective-permute-start(bf16[512,128]{1,0:T(8,128)(2,1)S(1)} %collective-permute-done.23.refs_5_), channel_id=1, source_target_pairs={{0,64},{1,961},{2,66},{3,963},{4,68},{5,965},{6,70},{7,967},{8,72}... | collective-permute-start | bytes 393224 | tf_op jit(solution)/shard_map/ppermute | solution.py:43
  163.1 2.0 collective-permute-start.30
  165.1 2.5 collective-permute-done.25.refs_7_
  167.7 5.9 %collective-permute-start.26 = (bf16[512,128]{1,0:T(8,128)(2,1)S(1)}, bf16[512,128]{1,0:T(8,128)(2,1)S(1)}, u32[]{:S(2)}, u32[]{:S(2)}) collective-permute-start(bf16[512,128]{1,0:T(8,128)(2,1)S(1)} %collective-permute-done.25.refs_7_), channel_id=1, source_target_pairs={{0,64},{1,961},{2,66},{3,963},{4,68},{5,965},{6,70},{7,967},{8,72}... | collective-permute-start | bytes 393224 | tf_op jit(solution)/shard_map/ppermute | solution.py:43
  173.6 1.9 collective-permute-start.31
  175.6 1.8 collective-permute-done.26.refs_9_
  177.4 2.8 %collective-permute-done.31.refs_10_ = bf16[512,128]{1,0:T(8,128)(2,1)S(1)} collective-permute-done((bf16[512,128]{1,0:T(8,128)(2,1)S(1)}, bf16[512,128]{1,0:T(8,128)(2,1)S(1)}, u32[]{:S(2)}, u32[]{:S(2)}) %collective-permute-start.31) | collective-permute-done | bytes 131104 | tf_op jit(solution)/shard_map/ppermute | solution.py:43
  180.2 1.9 collective-permute-start.35
  182.1 4.5 %collective-permute-start.27 = (bf16[512,128]{1,0:T(8,128)(2,1)S(1)}, bf16[512,128]{1,0:T(8,128)(2,1)S(1)}, u32[]{:S(2)}, u32[]{:S(2)}) collective-permute-start(bf16[512,128]{1,0:T(8,128)(2,1)S(1)} %collective-permute-done.26.refs_9_), channel_id=1, source_target_pairs={{0,64},{1,961},{2,66},{3,963},{4,68},{5,965},{6,70},{7,967},{8,72}... | collective-permute-start | bytes 393224 | tf_op jit(solution)/shard_map/ppermute | solution.py:43
  186.7 2.4 collective-permute-start.32
  189.1 4.4 %collective-permute-start.36 = (bf16[512,128]{1,0:T(8,128)(2,1)S(1)}, bf16[512,128]{1,0:T(8,128)(2,1)S(1)}, u32[]{:S(2)}, u32[]{:S(2)}) collective-permute-start(bf16[512,128]{1,0:T(8,128)(2,1)S(1)} %get-tuple-element.44.refs_1_.refs_3_), channel_id=1, source_target_pairs={{0,1},{1,0},{2,3},{3,2},{4,5},{5,4},{6,7},{7,6},{8,9},{9,8},{10,11... | collective-permute-start | bytes 393224 | tf_op jit(solution)/shard_map/ppermute | solution.py:43
  193.6 2.4 collective-permute-start.28
  196.0 3.4 %collective-permute-start.33 = (bf16[512,128]{1,0:T(8,128)(2,1)S(1)}, bf16[512,128]{1,0:T(8,128)(2,1)S(1)}, u32[]{:S(2)}, u32[]{:S(2)}) collective-permute-start(bf16[512,128]{1,0:T(8,128)(2,1)S(1)} %collective-permute-done.32.refs_12_), channel_id=1, source_target_pairs={{0,64},{1,961},{2,66},{3,963},{4,68},{5,965},{6,70},{7,967},{8,72}... | collective-permute-start | bytes 393224 | tf_op jit(solution)/shard_map/ppermute | solution.py:43
  199.4 2.3 collective-permute-done.28.refs_13_
  201.8 2.1 collective-permute-start.29
  204.7 2.7 %collective-permute-start.34 = (bf16[512,128]{1,0:T(8,128)(2,1)S(1)}, bf16[512,128]{1,0:T(8,128)(2,1)S(1)}, u32[]{:S(2)}, u32[]{:S(2)}) collective-permute-start(bf16[512,128]{1,0:T(8,128)(2,1)S(1)} %collective-permute-done.33.refs_14_), channel_id=1, source_target_pairs={{0,64},{1,961},{2,66},{3,963},{4,68},{5,965},{6,70},{7,967},{8,72}... | collective-permute-start | bytes 393224 | tf_op jit(solution)/shard_map/ppermute | solution.py:43
  208.4 4.4 %collective-permute-done.34.refs_16_ = bf16[512,128]{1,0:T(8,128)(2,1)S(1)} collective-permute-done((bf16[512,128]{1,0:T(8,128)(2,1)S(1)}, bf16[512,128]{1,0:T(8,128)(2,1)S(1)}, u32[]{:S(2)}, u32[]{:S(2)}) %collective-permute-start.34) | collective-permute-done | bytes 131104 | tf_op jit(solution)/shard_map/ppermute | solution.py:43
  212.8 5.4 %collective-permute-start.39 = (bf16[3072,128]{1,0:T(8,128)(2,1)S(1)}, bf16[3072,128]{1,0:T(8,128)(2,1)S(1)}, u32[]{:S(2)}, u32[]{:S(2)}) collective-permute-start(bf16[3072,128]{1,0:T(8,128)(2,1)S(1)} %constant_dynamic-update-slice_fusion.18), channel_id=1, source_target_pairs={{0,1},{1,0},{2,3},{3,2},{4,5},{5,4},{6,7},{7,6},{8,9},{9,8},{10,11... | collective-permute-start | bytes 2359304 | tf_op jit(solution)/shard_map/ppermute | solution.py:48
  218.2 3.5 %collective-permute-start.37 = (bf16[512,128]{1,0:T(8,128)(2,1)S(1)}, bf16[512,128]{1,0:T(8,128)(2,1)S(1)}, u32[]{:S(2)}, u32[]{:S(2)}) collective-permute-start(bf16[512,128]{1,0:T(8,128)(2,1)S(1)} %collective-permute-done.29.refs_15_), channel_id=1, source_target_pairs={{0,64},{1,961},{2,66},{3,963},{4,68},{5,965},{6,70},{7,967},{8,72}... | collective-permute-start | bytes 393224 | tf_op jit(solution)/shard_map/ppermute | solution.py:43
  221.6 2.1 collective-permute-start.38
  223.7 3.6 %collective-permute-done.37.refs_17_ = bf16[512,128]{1,0:T(8,128)(2,1)S(1)} collective-permute-done((bf16[512,128]{1,0:T(8,128)(2,1)S(1)}, bf16[512,128]{1,0:T(8,128)(2,1)S(1)}, u32[]{:S(2)}, u32[]{:S(2)}) %collective-permute-start.37) | collective-permute-done | bytes 131104 | tf_op jit(solution)/shard_map/ppermute | solution.py:43
  227.3 1.5 collective-permute-done.38.refs_18_
  228.8 6.9 %collective-permute-start.41 = (bf16[1024,128]{1,0:T(8,128)(2,1)S(1)}, bf16[1024,128]{1,0:T(8,128)(2,1)S(1)}, u32[]{:S(2)}, u32[]{:S(2)}) collective-permute-start(bf16[1024,128]{1,0:T(8,128)(2,1)S(1)} %pad_maximum_fusion.3), channel_id=1, source_target_pairs={{0,1},{1,0},{2,3},{3,2},{4,5},{5,4},{6,7},{7,6},{8,9},{9,8},{10,11... | collective-permute-start | bytes 786440 | tf_op jit(solution)/shard_map/ppermute | solution.py:48
  235.7 1.9 collective-permute-start.40
  237.6 4.7 %collective-permute-done.40.refs_21_ = bf16[512,128]{1,0:T(8,128)(2,1)S(1)} collective-permute-done((bf16[512,128]{1,0:T(8,128)(2,1)S(1)}, bf16[512,128]{1,0:T(8,128)(2,1)S(1)}, u32[]{:S(2)}, u32[]{:S(2)}) %collective-permute-start.40) | collective-permute-done | bytes 131104 | tf_op jit(solution)/shard_map/ppermute | solution.py:43
  243.1 4.8 %collective-permute-start.42 = (bf16[512,128]{1,0:T(8,128)(2,1)S(1)}, bf16[512,128]{1,0:T(8,128)(2,1)}, u32[]{:S(2)}, u32[]{:S(2)}) collective-permute-start(bf16[512,128]{1,0:T(8,128)(2,1)S(1)} %collective-permute-done.40.refs_21_), channel_id=1, source_target_pairs={{0,1},{1,0},{2,3},{3,2},{4,5},{5,4},{6,7},{7,6},{8,9},{9,8},{10,11... | collective-permute-start | bytes 393224 | tf_op jit(solution)/shard_map/ppermute | solution.py:48
  247.9 1.1 collective-permute-done.42.refs_23_
  249.0 7.9 %shard_map.74 = bf16[512,128]{1,0:T(8,128)(2,1)S(1)} custom-call(s32[1]{0:T(128)} %get-tuple-element.58.branch, s32[33]{0:T(128)S(1)} %pad_add_fusion.tab, s32[64,128]{1,0:T(8,128)S(1)} %get-tuple-element.43.refs_0_, bf16[512,128]{1,0:T(8,128)(2,1)S(1)} %get-tuple-element.44.refs_1_.refs_3_, bf16[16384,128]{1,0:T(8,128)(2,1)} %all-gather.5.cloned.1.call-done.refs_2_, ...), custom_call_target="tpu_custom_call" | custom-call | flops 536870912 | bytes 8388608 | tf_op jit(solution)/shard_map/pallas_call | solution.py:142
  257.0 1.9 collective-permute-start.43
  258.9 4.4 %collective-permute-done.43 = bf16[512,128]{1,0:T(8,128)(2,1)S(1)} collective-permute-done((bf16[512,128]{1,0:T(8,128)(2,1)S(1)}, bf16[512,128]{1,0:T(8,128)(2,1)S(1)}, u32[]{:S(2)}, u32[]{:S(2)}) %collective-permute-start.43) | collective-permute-done | bytes 131104 | tf_op jit(solution)/shard_map/ppermute | solution.py:43
  (96 shorter events, 9.0 us)
Async XLA Ops:
  6.5 118.7 %copy-start.13 = (s32[32]{0:T(128)S(1)}, s32[32]{0:T(128)}, u32[]{:S(2)}) copy-start(s32[32]{0:T(128)} %constant.86.clone) | copy-start | bytes 388
  6.5 118.7 %copy-start.14 = (s32[32]{0:T(128)S(1)}, s32[32]{0:T(128)}, u32[]{:S(2)}) copy-start(s32[32]{0:T(128)} %constant.87.clone) | copy-start | bytes 388
  6.5 125.3 %copy-start.12 = (s32[2]{0:T(128)S(1)}, s32[2]{0:T(128)}, u32[]{:S(2)}) copy-start(s32[2]{0:T(128)} %param.9) | copy-start | bytes 28
  6.5 126.3 %all-gather.3.cloned.1.call-start = ((), (), s32[]{:S(2)}) async-start(), calls=%async_computation | async-start | bytes 4595712 | tf_op jit(solution)/shard_map/all_gather | solution.py:160
  8.2 28.2 %collective-permute-start = (bf16[528,128]{1,0:T(8,128)(2,1)S(1)}, bf16[528,128]{1,0:T(8,128)(2,1)S(1)}, u32[]{:S(2)}, u32[]{:S(2)}) collective-permute-start(bf16[528,128]{1,0:T(8,128)(2,1)S(1)} %fusion.1), channel_id=1, source_target_pairs={{0,0},{1,32},{2,2},{3,34},{4,4},{5,36},{6,6},{7,38},{8,8},{9,40},{... | collective-permute-start | bytes 405512 | tf_op jit(solution)/shard_map/ppermute | solution.py:43
  13.1 23.3 %collective-permute-start.1 = (bf16[528,128]{1,0:T(8,128)(2,1)S(1)}, bf16[528,128]{1,0:T(8,128)(2,1)S(1)}, u32[]{:S(2)}, u32[]{:S(2)}) collective-permute-start(bf16[528,128]{1,0:T(8,128)(2,1)S(1)} %fusion.1), channel_id=1, source_target_pairs={{0,32},{1,0},{2,34},{3,2},{4,36},{5,4},{6,38},{7,6},{8,40},{9,8},{... | collective-permute-start | bytes 405512 | tf_op jit(solution)/shard_map/ppermute | solution.py:43
  24.9 12.2 %collective-permute-start.2 = (bf16[528,128]{1,0:T(8,128)(2,1)S(1)}, bf16[528,128]{1,0:T(8,128)(2,1)S(1)}, u32[]{:S(2)}, u32[]{:S(2)}) collective-permute-start(bf16[528,128]{1,0:T(8,128)(2,1)S(1)} %fusion.1), channel_id=1, source_target_pairs={{0,64},{1,96},{2,66},{3,98},{4,68},{5,100},{6,70},{7,102},{8,72},{... | collective-permute-start | bytes 405512 | tf_op jit(solution)/shard_map/ppermute | solution.py:43
  26.8 13.7 %collective-permute-start.3 = (bf16[528,128]{1,0:T(8,128)(2,1)S(1)}, bf16[528,128]{1,0:T(8,128)(2,1)S(1)}, u32[]{:S(2)}, u32[]{:S(2)}) collective-permute-start(bf16[528,128]{1,0:T(8,128)(2,1)S(1)} %fusion.1), channel_id=1, source_target_pairs={{0,961},{1,993},{2,963},{3,995},{4,965},{5,997},{6,967},{7,999},{8... | collective-permute-start | bytes 405512 | tf_op jit(solution)/shard_map/ppermute | solution.py:43
  40.5 208.5 %all-gather.5.cloned.1.call-start = ((), (), s32[]{:S(2)}) async-start(), calls=%async_computation.1 | async-start | bytes 4456448 | tf_op jit(solution)/shard_map/all_gather | solution.py:160
  40.6 10.6 %collective-permute-start.4 = (bf16[528,128]{1,0:T(8,128)(2,1)S(1)}, bf16[528,128]{1,0:T(8,128)(2,1)S(1)}, u32[]{:S(2)}, u32[]{:S(2)}) collective-permute-start(bf16[528,128]{1,0:T(8,128)(2,1)S(1)} %collective-permute-done.2.refs_4_), channel_id=1, source_target_pairs={{0,64},{1,961},{2,66},{3,963},{4,68},{5,965},{6,70},{7,967},{8,72}... | collective-permute-start | bytes 405512 | tf_op jit(solution)/shard_map/ppermute | solution.py:43
  46.4 10.9 %collective-permute-start.9 = (bf16[528,128]{1,0:T(8,128)(2,1)S(1)}, bf16[528,128]{1,0:T(8,128)(2,1)S(1)}, u32[]{:S(2)}, u32[]{:S(2)}) collective-permute-start(bf16[528,128]{1,0:T(8,128)(2,1)S(1)} %collective-permute-done.3.refs_5_), channel_id=1, source_target_pairs={{0,64},{1,961},{2,66},{3,963},{4,68},{5,965},{6,70},{7,967},{8,72}... | collective-permute-start | bytes 405512 | tf_op jit(solution)/shard_map/ppermute | solution.py:43
  51.2 9.8 %collective-permute-start.5 = (bf16[528,128]{1,0:T(8,128)(2,1)S(1)}, bf16[528,128]{1,0:T(8,128)(2,1)S(1)}, u32[]{:S(2)}, u32[]{:S(2)}) collective-permute-start(bf16[528,128]{1,0:T(8,128)(2,1)S(1)} %collective-permute-done.4.refs_6_), channel_id=1, source_target_pairs={{0,64},{1,961},{2,66},{3,963},{4,68},{5,965},{6,70},{7,967},{8,72}... | collective-permute-start | bytes 405512 | tf_op jit(solution)/shard_map/ppermute | solution.py:43
  57.3 6.9 %collective-permute-start.10 = (bf16[528,128]{1,0:T(8,128)(2,1)S(1)}, bf16[528,128]{1,0:T(8,128)(2,1)S(1)}, u32[]{:S(2)}, u32[]{:S(2)}) collective-permute-start(bf16[528,128]{1,0:T(8,128)(2,1)S(1)} %collective-permute-done.9.refs_7_), channel_id=1, source_target_pairs={{0,64},{1,961},{2,66},{3,963},{4,68},{5,965},{6,70},{7,967},{8,72}... | collective-permute-start | bytes 405512 | tf_op jit(solution)/shard_map/ppermute | solution.py:43
  64.2 34.9 %collective-permute-start.14 = (bf16[3168,128]{1,0:T(8,128)(2,1)S(1)}, bf16[3168,128]{1,0:T(8,128)(2,1)S(1)}, u32[]{:S(2)}, u32[]{:S(2)}) collective-permute-start(bf16[3168,128]{1,0:T(8,128)(2,1)S(1)} %constant_dynamic-update-slice_fusion), channel_id=1, source_target_pairs={{0,1},{1,0},{2,3},{3,2},{4,5},{5,4},{6,7},{7,6},{8,9},{9,8},{10,11... | collective-permute-start | bytes 2433032 | tf_op jit(solution)/shard_map/ppermute | solution.py:48
  68.9 10.1 %collective-permute-start.11 = (bf16[528,128]{1,0:T(8,128)(2,1)S(1)}, bf16[528,128]{1,0:T(8,128)(2,1)S(1)}, u32[]{:S(2)}, u32[]{:S(2)}) collective-permute-start(bf16[528,128]{1,0:T(8,128)(2,1)S(1)} %collective-permute-done.10.refs_9_), channel_id=1, source_target_pairs={{0,64},{1,961},{2,66},{3,963},{4,68},{5,965},{6,70},{7,967},{8,72}... | collective-permute-start | bytes 405512 | tf_op jit(solution)/shard_map/ppermute | solution.py:43
  70.8 11.8 %collective-permute-start.6 = (bf16[528,128]{1,0:T(8,128)(2,1)S(1)}, bf16[528,128]{1,0:T(8,128)(2,1)S(1)}, u32[]{:S(2)}, u32[]{:S(2)}) collective-permute-start(bf16[528,128]{1,0:T(8,128)(2,1)S(1)} %collective-permute-done.5.refs_8_), channel_id=1, source_target_pairs={{0,64},{1,961},{2,66},{3,963},{4,68},{5,965},{6,70},{7,967},{8,72}... | collective-permute-start | bytes 405512 | tf_op jit(solution)/shard_map/ppermute | solution.py:43
  74.4 21.1 %collective-permute-start.15 = (bf16[528,128]{1,0:T(8,128)(2,1)S(1)}, bf16[528,128]{1,0:T(8,128)(2,1)S(1)}, u32[]{:S(2)}, u32[]{:S(2)}) collective-permute-start(bf16[528,128]{1,0:T(8,128)(2,1)S(1)} %fusion.1), channel_id=1, source_target_pairs={{0,1},{1,33},{2,3},{3,35},{4,5},{5,37},{6,7},{7,39},{8,9},{9,41},{... | collective-permute-start | bytes 405512 | tf_op jit(solution)/shard_map/ppermute | solution.py:43
  79.0 8.1 %collective-permute-start.12 = (bf16[528,128]{1,0:T(8,128)(2,1)S(1)}, bf16[528,128]{1,0:T(8,128)(2,1)S(1)}, u32[]{:S(2)}, u32[]{:S(2)}) collective-permute-start(bf16[528,128]{1,0:T(8,128)(2,1)S(1)} %collective-permute-done.11.refs_11_), channel_id=1, source_target_pairs={{0,64},{1,961},{2,66},{3,963},{4,68},{5,965},{6,70},{7,967},{8,72}... | collective-permute-start | bytes 405512 | tf_op jit(solution)/shard_map/ppermute | solution.py:43
  82.7 9.1 %collective-permute-start.7 = (bf16[528,128]{1,0:T(8,128)(2,1)S(1)}, bf16[528,128]{1,0:T(8,128)(2,1)S(1)}, u32[]{:S(2)}, u32[]{:S(2)}) collective-permute-start(bf16[528,128]{1,0:T(8,128)(2,1)S(1)} %collective-permute-done.6.refs_10_), channel_id=1, source_target_pairs={{0,64},{1,961},{2,66},{3,963},{4,68},{5,965},{6,70},{7,967},{8,72}... | collective-permute-start | bytes 405512 | tf_op jit(solution)/shard_map/ppermute | solution.py:43
  87.1 8.4 %collective-permute-start.13 = (bf16[528,128]{1,0:T(8,128)(2,1)S(1)}, bf16[528,128]{1,0:T(8,128)(2,1)S(1)}, u32[]{:S(2)}, u32[]{:S(2)}) collective-permute-start(bf16[528,128]{1,0:T(8,128)(2,1)S(1)} %collective-permute-done.12.refs_13_), channel_id=1, source_target_pairs={{0,64},{1,961},{2,66},{3,963},{4,68},{5,965},{6,70},{7,967},{8,72}... | collective-permute-start | bytes 405512 | tf_op jit(solution)/shard_map/ppermute | solution.py:43
  91.8 7.3 %collective-permute-start.8 = (bf16[528,128]{1,0:T(8,128)(2,1)S(1)}, bf16[528,128]{1,0:T(8,128)(2,1)S(1)}, u32[]{:S(2)}, u32[]{:S(2)}) collective-permute-start(bf16[528,128]{1,0:T(8,128)(2,1)S(1)} %collective-permute-done.7.refs_12_), channel_id=1, source_target_pairs={{0,64},{1,961},{2,66},{3,963},{4,68},{5,965},{6,70},{7,967},{8,72}... | collective-permute-start | bytes 405512 | tf_op jit(solution)/shard_map/ppermute | solution.py:43
  95.5 16.5 %copy-start.4 = (bf16[528,128]{1,0:T(8,128)(2,1)}, bf16[528,128]{1,0:T(8,128)(2,1)S(1)}, u32[]{:S(2)}) copy-start(bf16[528,128]{1,0:T(8,128)(2,1)S(1)} %collective-permute-done.13.refs_15_) | copy-start | bytes 405508
  99.1 33.7 %copy-start = (bf16[3168,128]{1,0:T(8,128)(2,1)}, bf16[3168,128]{1,0:T(8,128)(2,1)S(1)}, u32[]{:S(2)}) copy-start(bf16[3168,128]{1,0:T(8,128)(2,1)S(1)} %collective-permute-done.14.refs_18_) | copy-start | bytes 2433028
  99.2 17.9 %collective-permute-start.18 = (bf16[3168,128]{1,0:T(8,128)(2,1)S(1)}, bf16[3168,128]{1,0:T(8,128)(2,1)S(1)}, u32[]{:S(2)}, u32[]{:S(2)}) collective-permute-start(bf16[3168,128]{1,0:T(8,128)(2,1)S(1)} %constant_dynamic-update-slice_fusion.6), channel_id=1, source_target_pairs={{0,1},{1,0},{2,3},{3,2},{4,5},{5,4},{6,7},{7,6},{8,9},{9,8},{10,11... | collective-permute-start | bytes 2433032 | tf_op jit(solution)/shard_map/ppermute | solution.py:48
  104.9 7.1 %collective-permute-start.16 = (bf16[528,128]{1,0:T(8,128)(2,1)S(1)}, bf16[528,128]{1,0:T(8,128)(2,1)S(1)}, u32[]{:S(2)}, u32[]{:S(2)}) collective-permute-start(bf16[528,128]{1,0:T(8,128)(2,1)S(1)} %collective-permute-done.8.refs_14_), channel_id=1, source_target_pairs={{0,64},{1,961},{2,66},{3,963},{4,68},{5,965},{6,70},{7,967},{8,72}... | collective-permute-start | bytes 405512 | tf_op jit(solution)/shard_map/ppermute | solution.py:43
  110.0 7.1 %collective-permute-start.17 = (bf16[528,128]{1,0:T(8,128)(2,1)S(1)}, bf16[528,128]{1,0:T(8,128)(2,1)S(1)}, u32[]{:S(2)}, u32[]{:S(2)}) collective-permute-start(bf16[528,128]{1,0:T(8,128)(2,1)S(1)} %collective-permute-done.13.refs_15_), channel_id=1, source_target_pairs={{0,64},{1,961},{2,66},{3,963},{4,68},{5,965},{6,70},{7,967},{8,72}... | collective-permute-start | bytes 405512 | tf_op jit(solution)/shard_map/ppermute | solution.py:43
  112.0 5.1 %copy-start.5 = (bf16[528,128]{1,0:T(8,128)(2,1)}, bf16[528,128]{1,0:T(8,128)(2,1)S(1)}, u32[]{:S(2)}) copy-start(bf16[528,128]{1,0:T(8,128)(2,1)S(1)} %collective-permute-done.16.refs_16_) | copy-start | bytes 405508
  117.1 0.8 copy-start.6
  117.1 15.8 %copy-start.1 = (bf16[3168,128]{1,0:T(8,128)(2,1)}, bf16[3168,128]{1,0:T(8,128)(2,1)S(1)}, u32[]{:S(2)}) copy-start(bf16[3168,128]{1,0:T(8,128)(2,1)S(1)} %collective-permute-done.18.refs_19_) | copy-start | bytes 2433028
  117.9 10.2 %collective-permute-start.20 = (bf16[1056,128]{1,0:T(8,128)(2,1)}, bf16[1056,128]{1,0:T(8,128)(2,1)}, u32[]{:S(2)}, u32[]{:S(2)}) collective-permute-start(bf16[1056,128]{1,0:T(8,128)(2,1)} %pad_maximum_fusion.1), channel_id=1, source_target_pairs={{0,1},{1,0},{2,3},{3,2},{4,5},{5,4},{6,7},{7,6},{8,9},{9,8},{10,11... | collective-permute-start | bytes 811016 | tf_op jit(solution)/shard_map/ppermute | solution.py:48
  119.8 8.2 %collective-permute-start.19 = (bf16[528,128]{1,0:T(8,128)(2,1)}, bf16[528,128]{1,0:T(8,128)(2,1)S(1)}, u32[]{:S(2)}, u32[]{:S(2)}) collective-permute-start(bf16[528,128]{1,0:T(8,128)(2,1)} %copy-done.5), channel_id=1, source_target_pairs={{0,64},{1,961},{2,66},{3,963},{4,68},{5,965},{6,70},{7,967},{8,72}... | collective-permute-start | bytes 405512 | tf_op jit(solution)/shard_map/ppermute | solution.py:43
  128.0 4.8 %copy-start.10 = (bf16[528,128]{1,0:T(8,128)(2,1)}, bf16[528,128]{1,0:T(8,128)(2,1)S(1)}, u32[]{:S(2)}) copy-start(bf16[528,128]{1,0:T(8,128)(2,1)S(1)} %collective-permute-done.19.refs_20_) | copy-start | bytes 405508
  128.0 4.8 %collective-permute-start.21 = (bf16[528,128]{1,0:T(8,128)(2,1)S(1)}, bf16[528,128]{1,0:T(8,128)(2,1)}, u32[]{:S(2)}, u32[]{:S(2)}) collective-permute-start(bf16[528,128]{1,0:T(8,128)(2,1)S(1)} %collective-permute-done.19.refs_20_), channel_id=1, source_target_pairs={{0,1},{1,0},{2,3},{3,2},{4,5},{5,4},{6,7},{7,6},{8,9},{9,8},{10,11... | collective-permute-start | bytes 405512 | tf_op jit(solution)/shard_map/ppermute | solution.py:48
  142.5 8.7 %collective-permute-start.22 = (bf16[512,128]{1,0:T(8,128)(2,1)S(1)}, bf16[512,128]{1,0:T(8,128)(2,1)S(1)}, u32[]{:S(2)}, u32[]{:S(2)}) collective-permute-start(bf16[512,128]{1,0:T(8,128)(2,1)S(1)} %get-tuple-element.44.refs_1_.refs_3_), channel_id=1, source_target_pairs={{0,32},{1,33},{2,34},{3,35},{4,36},{5,37},{6,38},{7,39},{8,40},{9,... | collective-permute-start | bytes 393224 | tf_op jit(solution)/shard_map/ppermute | solution.py:43
  144.5 7.6 %collective-permute-start.23 = (bf16[512,128]{1,0:T(8,128)(2,1)S(1)}, bf16[512,128]{1,0:T(8,128)(2,1)S(1)}, u32[]{:S(2)}, u32[]{:S(2)}) collective-permute-start(bf16[512,128]{1,0:T(8,128)(2,1)S(1)} %get-tuple-element.44.refs_1_.refs_3_), channel_id=1, source_target_pairs={{0,64},{1,961},{2,66},{3,963},{4,68},{5,965},{6,70},{7,967},{8,72}... | collective-permute-start | bytes 393224 | tf_op jit(solution)/shard_map/ppermute | solution.py:43
  148.9 7.5 %collective-permute-start.24 = (bf16[512,128]{1,0:T(8,128)(2,1)S(1)}, bf16[512,128]{1,0:T(8,128)(2,1)S(1)}, u32[]{:S(2)}, u32[]{:S(2)}) collective-permute-start(bf16[512,128]{1,0:T(8,128)(2,1)S(1)} %get-tuple-element.44.refs_1_.refs_3_), channel_id=1, source_target_pairs={{0,961},{1,64},{2,963},{3,66},{4,965},{5,68},{6,967},{7,70},{8,969... | collective-permute-start | bytes 393224 | tf_op jit(solution)/shard_map/ppermute | solution.py:43
  156.5 11.2 %collective-permute-start.25 = (bf16[512,128]{1,0:T(8,128)(2,1)S(1)}, bf16[512,128]{1,0:T(8,128)(2,1)S(1)}, u32[]{:S(2)}, u32[]{:S(2)}) collective-permute-start(bf16[512,128]{1,0:T(8,128)(2,1)S(1)} %collective-permute-done.23.refs_5_), channel_id=1, source_target_pairs={{0,64},{1,961},{2,66},{3,963},{4,68},{5,965},{6,70},{7,967},{8,72}... | collective-permute-start | bytes 393224 | tf_op jit(solution)/shard_map/ppermute | solution.py:43
  163.1 10.5 %collective-permute-start.30 = (bf16[512,128]{1,0:T(8,128)(2,1)S(1)}, bf16[512,128]{1,0:T(8,128)(2,1)S(1)}, u32[]{:S(2)}, u32[]{:S(2)}) collective-permute-start(bf16[512,128]{1,0:T(8,128)(2,1)S(1)} %collective-permute-done.24.refs_6_), channel_id=1, source_target_pairs={{0,64},{1,961},{2,66},{3,963},{4,68},{5,965},{6,70},{7,967},{8,72}... | collective-permute-start | bytes 393224 | tf_op jit(solution)/shard_map/ppermute | solution.py:43
  167.7 9.7 %collective-permute-start.26 = (bf16[512,128]{1,0:T(8,128)(2,1)S(1)}, bf16[512,128]{1,0:T(8,128)(2,1)S(1)}, u32[]{:S(2)}, u32[]{:S(2)}) collective-permute-start(bf16[512,128]{1,0:T(8,128)(2,1)S(1)} %collective-permute-done.25.refs_7_), channel_id=1, source_target_pairs={{0,64},{1,961},{2,66},{3,963},{4,68},{5,965},{6,70},{7,967},{8,72}... | collective-permute-start | bytes 393224 | tf_op jit(solution)/shard_map/ppermute | solution.py:43
  173.6 6.6 %collective-permute-start.31 = (bf16[512,128]{1,0:T(8,128)(2,1)S(1)}, bf16[512,128]{1,0:T(8,128)(2,1)S(1)}, u32[]{:S(2)}, u32[]{:S(2)}) collective-permute-start(bf16[512,128]{1,0:T(8,128)(2,1)S(1)} %collective-permute-done.30.refs_8_), channel_id=1, source_target_pairs={{0,64},{1,961},{2,66},{3,963},{4,68},{5,965},{6,70},{7,967},{8,72}... | collective-permute-start | bytes 393224 | tf_op jit(solution)/shard_map/ppermute | solution.py:43
  180.2 32.5 %collective-permute-start.35 = (bf16[3072,128]{1,0:T(8,128)(2,1)S(1)}, bf16[3072,128]{1,0:T(8,128)(2,1)S(1)}, u32[]{:S(2)}, u32[]{:S(2)}) collective-permute-start(bf16[3072,128]{1,0:T(8,128)(2,1)S(1)} %constant_dynamic-update-slice_fusion.12), channel_id=1, source_target_pairs={{0,1},{1,0},{2,3},{3,2},{4,5},{5,4},{6,7},{7,6},{8,9},{9,8},{10,11... | collective-permute-start | bytes 2359304 | tf_op jit(solution)/shard_map/ppermute | solution.py:48
  182.1 11.4 %collective-permute-start.27 = (bf16[512,128]{1,0:T(8,128)(2,1)S(1)}, bf16[512,128]{1,0:T(8,128)(2,1)S(1)}, u32[]{:S(2)}, u32[]{:S(2)}) collective-permute-start(bf16[512,128]{1,0:T(8,128)(2,1)S(1)} %collective-permute-done.26.refs_9_), channel_id=1, source_target_pairs={{0,64},{1,961},{2,66},{3,963},{4,68},{5,965},{6,70},{7,967},{8,72}... | collective-permute-start | bytes 393224 | tf_op jit(solution)/shard_map/ppermute | solution.py:43
  186.7 9.3 %collective-permute-start.32 = (bf16[512,128]{1,0:T(8,128)(2,1)S(1)}, bf16[512,128]{1,0:T(8,128)(2,1)S(1)}, u32[]{:S(2)}, u32[]{:S(2)}) collective-permute-start(bf16[512,128]{1,0:T(8,128)(2,1)S(1)} %collective-permute-done.31.refs_10_), channel_id=1, source_target_pairs={{0,64},{1,961},{2,66},{3,963},{4,68},{5,965},{6,70},{7,967},{8,72}... | collective-permute-start | bytes 393224 | tf_op jit(solution)/shard_map/ppermute | solution.py:43
  189.1 18.4 %collective-permute-start.36 = (bf16[512,128]{1,0:T(8,128)(2,1)S(1)}, bf16[512,128]{1,0:T(8,128)(2,1)S(1)}, u32[]{:S(2)}, u32[]{:S(2)}) collective-permute-start(bf16[512,128]{1,0:T(8,128)(2,1)S(1)} %get-tuple-element.44.refs_1_.refs_3_), channel_id=1, source_target_pairs={{0,1},{1,0},{2,3},{3,2},{4,5},{5,4},{6,7},{7,6},{8,9},{9,8},{10,11... | collective-permute-start | bytes 393224 | tf_op jit(solution)/shard_map/ppermute | solution.py:43
  193.6 8.2 %collective-permute-start.28 = (bf16[512,128]{1,0:T(8,128)(2,1)S(1)}, bf16[512,128]{1,0:T(8,128)(2,1)S(1)}, u32[]{:S(2)}, u32[]{:S(2)}) collective-permute-start(bf16[512,128]{1,0:T(8,128)(2,1)S(1)} %collective-permute-done.27.refs_11_), channel_id=1, source_target_pairs={{0,64},{1,961},{2,66},{3,963},{4,68},{5,965},{6,70},{7,967},{8,72}... | collective-permute-start | bytes 393224 | tf_op jit(solution)/shard_map/ppermute | solution.py:43
  196.0 8.8 %collective-permute-start.33 = (bf16[512,128]{1,0:T(8,128)(2,1)S(1)}, bf16[512,128]{1,0:T(8,128)(2,1)S(1)}, u32[]{:S(2)}, u32[]{:S(2)}) collective-permute-start(bf16[512,128]{1,0:T(8,128)(2,1)S(1)} %collective-permute-done.32.refs_12_), channel_id=1, source_target_pairs={{0,64},{1,961},{2,66},{3,963},{4,68},{5,965},{6,70},{7,967},{8,72}... | collective-permute-start | bytes 393224 | tf_op jit(solution)/shard_map/ppermute | solution.py:43
  201.8 6.6 %collective-permute-start.29 = (bf16[512,128]{1,0:T(8,128)(2,1)S(1)}, bf16[512,128]{1,0:T(8,128)(2,1)S(1)}, u32[]{:S(2)}, u32[]{:S(2)}) collective-permute-start(bf16[512,128]{1,0:T(8,128)(2,1)S(1)} %collective-permute-done.28.refs_13_), channel_id=1, source_target_pairs={{0,64},{1,961},{2,66},{3,963},{4,68},{5,965},{6,70},{7,967},{8,72}... | collective-permute-start | bytes 393224 | tf_op jit(solution)/shard_map/ppermute | solution.py:43
  204.7 8.0 %collective-permute-start.34 = (bf16[512,128]{1,0:T(8,128)(2,1)S(1)}, bf16[512,128]{1,0:T(8,128)(2,1)S(1)}, u32[]{:S(2)}, u32[]{:S(2)}) collective-permute-start(bf16[512,128]{1,0:T(8,128)(2,1)S(1)} %collective-permute-done.33.refs_14_), channel_id=1, source_target_pairs={{0,64},{1,961},{2,66},{3,963},{4,68},{5,965},{6,70},{7,967},{8,72}... | collective-permute-start | bytes 393224 | tf_op jit(solution)/shard_map/ppermute | solution.py:43
  212.7 36.3 %copy-start.2 = (bf16[3072,128]{1,0:T(8,128)(2,1)}, bf16[3072,128]{1,0:T(8,128)(2,1)S(1)}, u32[]{:S(2)}) copy-start(bf16[3072,128]{1,0:T(8,128)(2,1)S(1)} %collective-permute-done.35.refs_19_) | copy-start | bytes 2359300
  212.8 16.0 %collective-permute-start.39 = (bf16[3072,128]{1,0:T(8,128)(2,1)S(1)}, bf16[3072,128]{1,0:T(8,128)(2,1)S(1)}, u32[]{:S(2)}, u32[]{:S(2)}) collective-permute-start(bf16[3072,128]{1,0:T(8,128)(2,1)S(1)} %constant_dynamic-update-slice_fusion.18), channel_id=1, source_target_pairs={{0,1},{1,0},{2,3},{3,2},{4,5},{5,4},{6,7},{7,6},{8,9},{9,8},{10,11... | collective-permute-start | bytes 2359304 | tf_op jit(solution)/shard_map/ppermute | solution.py:48
  218.2 9.1 %collective-permute-start.37 = (bf16[512,128]{1,0:T(8,128)(2,1)S(1)}, bf16[512,128]{1,0:T(8,128)(2,1)S(1)}, u32[]{:S(2)}, u32[]{:S(2)}) collective-permute-start(bf16[512,128]{1,0:T(8,128)(2,1)S(1)} %collective-permute-done.29.refs_15_), channel_id=1, source_target_pairs={{0,64},{1,961},{2,66},{3,963},{4,68},{5,965},{6,70},{7,967},{8,72}... | collective-permute-start | bytes 393224 | tf_op jit(solution)/shard_map/ppermute | solution.py:43
  221.6 7.2 %collective-permute-start.38 = (bf16[512,128]{1,0:T(8,128)(2,1)S(1)}, bf16[512,128]{1,0:T(8,128)(2,1)S(1)}, u32[]{:S(2)}, u32[]{:S(2)}) collective-permute-start(bf16[512,128]{1,0:T(8,128)(2,1)S(1)} %collective-permute-done.34.refs_16_), channel_id=1, source_target_pairs={{0,64},{1,961},{2,66},{3,963},{4,68},{5,965},{6,70},{7,967},{8,72}... | collective-permute-start | bytes 393224 | tf_op jit(solution)/shard_map/ppermute | solution.py:43
  227.3 8.4 %copy-start.7 = (bf16[512,128]{1,0:T(8,128)(2,1)}, bf16[512,128]{1,0:T(8,128)(2,1)S(1)}, u32[]{:S(2)}) copy-start(bf16[512,128]{1,0:T(8,128)(2,1)S(1)} %collective-permute-done.37.refs_17_) | copy-start | bytes 393220
  228.8 13.5 %copy-start.8 = (bf16[512,128]{1,0:T(8,128)(2,1)}, bf16[512,128]{1,0:T(8,128)(2,1)S(1)}, u32[]{:S(2)}) copy-start(bf16[512,128]{1,0:T(8,128)(2,1)S(1)} %collective-permute-done.38.refs_18_) | copy-start | bytes 393220
  228.8 20.2 %copy-start.3 = (bf16[3072,128]{1,0:T(8,128)(2,1)}, bf16[3072,128]{1,0:T(8,128)(2,1)S(1)}, u32[]{:S(2)}) copy-start(bf16[3072,128]{1,0:T(8,128)(2,1)S(1)} %collective-permute-done.39.refs_20_) | copy-start | bytes 2359300
  228.8 13.5 %collective-permute-start.41 = (bf16[1024,128]{1,0:T(8,128)(2,1)S(1)}, bf16[1024,128]{1,0:T(8,128)(2,1)S(1)}, u32[]{:S(2)}, u32[]{:S(2)}) collective-permute-start(bf16[1024,128]{1,0:T(8,128)(2,1)S(1)} %pad_maximum_fusion.3), channel_id=1, source_target_pairs={{0,1},{1,0},{2,3},{3,2},{4,5},{5,4},{6,7},{7,6},{8,9},{9,8},{10,11... | collective-permute-start | bytes 786440 | tf_op jit(solution)/shard_map/ppermute | solution.py:48
  235.7 6.6 %collective-permute-start.40 = (bf16[512,128]{1,0:T(8,128)(2,1)S(1)}, bf16[512,128]{1,0:T(8,128)(2,1)S(1)}, u32[]{:S(2)}, u32[]{:S(2)}) collective-permute-start(bf16[512,128]{1,0:T(8,128)(2,1)S(1)} %collective-permute-done.37.refs_17_), channel_id=1, source_target_pairs={{0,64},{1,961},{2,66},{3,963},{4,68},{5,965},{6,70},{7,967},{8,72}... | collective-permute-start | bytes 393224 | tf_op jit(solution)/shard_map/ppermute | solution.py:43
  242.3 5.6 %copy-start.11 = (bf16[512,128]{1,0:T(8,128)(2,1)}, bf16[512,128]{1,0:T(8,128)(2,1)S(1)}, u32[]{:S(2)}) copy-start(bf16[512,128]{1,0:T(8,128)(2,1)S(1)} %collective-permute-done.40.refs_21_) | copy-start | bytes 393220
  242.3 0.7 copy-start.9
  243.1 6.0 %collective-permute-start.42 = (bf16[512,128]{1,0:T(8,128)(2,1)S(1)}, bf16[512,128]{1,0:T(8,128)(2,1)}, u32[]{:S(2)}, u32[]{:S(2)}) collective-permute-start(bf16[512,128]{1,0:T(8,128)(2,1)S(1)} %collective-permute-done.40.refs_21_), channel_id=1, source_target_pairs={{0,1},{1,0},{2,3},{3,2},{4,5},{5,4},{6,7},{7,6},{8,9},{9,8},{10,11... | collective-permute-start | bytes 393224 | tf_op jit(solution)/shard_map/ppermute | solution.py:48
  257.0 6.3 %collective-permute-start.43 = (bf16[512,128]{1,0:T(8,128)(2,1)S(1)}, bf16[512,128]{1,0:T(8,128)(2,1)S(1)}, u32[]{:S(2)}, u32[]{:S(2)}) collective-permute-start(bf16[512,128]{1,0:T(8,128)(2,1)S(1)} %shard_map.74), channel_id=1, source_target_pairs={{0,0},{1,32},{2,2},{3,34},{4,4},{5,36},{6,6},{7,38},{8,8},{9,40},{... | collective-permute-start | bytes 393224 | tf_op jit(solution)/shard_map/ppermute | solution.py:43
Sparse Core Ops, SparseCore 0:
  40.7 82.7 all-gather.2
  156.6 81.4 all-gather.4
